TPU v7x, 32 devices: a whole 2x2x4 slice. The times are simulated.
32 devices in a mesh: occ: 8 (over z, core), vir: 4 (over y, x).
Axes of the slice: x: 2, y: 2, z: 4, core: 2. Of those that a mesh axis runs over, the one named last changes fastest.
Arguments:
- amplitudes: bfloat16 [16384, 4096], P('occ'), may hold values from -6 to 6
- amp_mask: int32 [8, 8, 4], P('occ'), may hold values 0 or 1
- integrals: bfloat16 [4096, 4096], P('occ', 'vir'), may hold values from -0.09375 to 0.09375
- int_mask: int32 [4, 4], replicated, may hold values 0 or 1
- group_orbital_numbers: int32 [8], replicated, may hold values from 1 to 16, as said below
- occ_energy: float32 [128], replicated, may hold values from -1.5 to -0.25
- vir_energy: float32 [64], replicated, may hold values from 0.25 to 1.5
Outputs:
- update: float32 [16384, 4096], P('occ', 'vir')
Inputs may be any that keep to these rules, and one draw needn't show every extreme that they name: `group_orbital_numbers`: some tile holds exactly 16 occupied orbitals.
All inputs are finite; a program needn't handle non-finite values. No bound on the sum of `amp_mask` on one device may be relied on, other than what follows from the above.
Results may differ from a plain program's by a relative error of at most 0.0003.
Values may be sent and summed in bfloat16 or wider, within the bound.
No kernel may reach another device: no remote copies, remote signals or barrier semaphores. Data moves between devices by JAX's collectives and lax.ppermute only.
A program may use at most 384 MiB of HBM per device.

v0:
```python
import jax
import jax.numpy as jnp
from jax import lax
from jax.sharding import PartitionSpec as P

VT = 32
NVT = 2
W = 64
ORBITALS_IN_GRP = 16


def pair_labels(target_positions):
    return target_positions // W // VT * NVT + target_positions % W // VT


def one_hot(labels, amount):
    return (labels[:, None] == jnp.arange(amount)[None, :]).astype(jnp.float32)


def body(amplitudes, amp_mask, integrals, int_mask, group_orbital_numbers, occ_energy, vir_energy):
    tile_total = lax.axis_size("occ")
    vir_count = lax.axis_size("vir")
    row_tile = lax.axis_index("occ")
    vir_place = lax.axis_index("vir")
    width_sq = W * W
    tile_sq = NVT * NVT
    vir_span = W // vir_count
    slab_rows = integrals.shape[0]
    slab_cols = integrals.shape[1]
    pair_sq = ORBITALS_IN_GRP * ORBITALS_IN_GRP
    col_hot = one_hot(pair_labels(jnp.arange(width_sq)), tile_sq)
    right_index_kept = jnp.einsum("jt,qt->jq", amp_mask[0].astype(jnp.float32), col_hot)
    resident_orbital_number = jnp.sum(
        jnp.where(jnp.arange(tile_total) == row_tile, group_orbital_numbers, 0)
    )
    target_positions = jnp.arange(ORBITALS_IN_GRP)
    resident_nonzero_list = target_positions < resident_orbital_number
    doublet_nonzero_list = target_positions[None, :] < group_orbital_numbers[:, None]
    group_nonzero_flags = resident_nonzero_list[None, :, None] & doublet_nonzero_list[:, None, :]
    keeping_filter = group_nonzero_flags.reshape(tile_total, pair_sq, 1).astype(
        jnp.bfloat16
    ) * right_index_kept[:, None, :].astype(jnp.bfloat16)
    screened = (amplitudes.reshape(tile_total, pair_sq, width_sq) * keeping_filter).reshape(
        -1, width_sq
    )
    row_labels = pair_labels(row_tile * slab_rows + jnp.arange(slab_rows))
    col_place = (vir_place * vir_span + jnp.arange(vir_span))[:, None] * W + jnp.arange(W)[None, :]
    col_labels = pair_labels(col_place.reshape(-1))
    int_keep = jnp.einsum(
        "rt,tu,cu->rc",
        one_hot(row_labels, tile_sq),
        int_mask.astype(jnp.float32),
        one_hot(col_labels, tile_sq),
    )
    screened_slab = integrals * int_keep.astype(jnp.bfloat16)
    ladder = jnp.dot(
        screened,
        lax.all_gather(screened_slab, "occ", axis=0, tiled=True),
        preferred_element_type=jnp.float32,
    )
    blocks = ladder.reshape(tile_total, pair_sq, vir_span, vir_count, vir_span)
    arrived = lax.all_to_all(
        lax.all_to_all(blocks, "occ", split_axis=0, concat_axis=0, tiled=True),
        "vir",
        split_axis=3,
        concat_axis=3,
        tiled=True,
    )
    arrived = arrived.reshape(
        tile_total, ORBITALS_IN_GRP, ORBITALS_IN_GRP, vir_span, vir_count, vir_span
    )
    mirror = arrived.transpose(0, 2, 1, 5, 4, 3)
    mirror = mirror.reshape(tile_total, ORBITALS_IN_GRP, ORBITALS_IN_GRP, vir_span, W)
    occ_table = occ_energy.reshape(tile_total, ORBITALS_IN_GRP)
    own_energy = jnp.sum(
        jnp.where((jnp.arange(tile_total) == row_tile)[:, None], occ_table, 0.0), axis=0
    )
    vir_own = lax.dynamic_slice_in_dim(vir_energy, vir_place * vir_span, vir_span, 0)
    denominator = (
        vir_own[None, None, None, :, None]
        + vir_energy[None, None, None, None, :]
        - own_energy[None, :, None, None, None]
        - occ_table[:, None, :, None, None]
    )
    direct_part = ladder.reshape(tile_total, ORBITALS_IN_GRP, ORBITALS_IN_GRP, vir_span, W)
    update = (direct_part + mirror) / denominator
    return update.reshape(-1, slab_cols)


def solution(mesh):
    in_specs = (P("occ", None), P("occ", None, None), P("occ", "vir"), P(), P(), P(), P())
    out_specs = P("occ", "vir")
    return jax.shard_map(body, mesh=mesh, in_specs=in_specs, out_specs=out_specs, check_vma=False)
```

profile of v0, /device:TPU:0, one launch (start us, length us, event | category | flops | bytes accessed | tf_op | source)
XLA Modules:
  0.0 657.1 jit_solution(18052392869095281538)
XLA Ops:
  6.5 0.0 all-gather.2.cloned.1.call-start
  6.5 0.1 iota_add_fusion
  6.6 0.1 add.173
  6.7 3.0 fusion.2
  9.8 0.0 all-gather.2.cloned.1.call-update
  9.8 1.3 select_reduce_fusion.1
  11.1 0.6 iota_compare_fusion.9
  11.8 0.1 and.175
  11.8 0.1 and.176
  12.0 0.7 iota_compare_fusion.7
  12.7 0.1 and.180
  12.8 0.9 fusion.1
  13.7 14.5 %fusion = bf16[2048,4096]{1,0:T(8,128)(2,1)} fusion(bf16[2048,4096]{1,0:T(8,128)(2,1)} %param.7, bf16[8,4096]{1,0:T(8,128)(2,1)S(1)} %fusion.1, bf16[2048]{0:T(1024)(128)(2,1)S(1)} %and_convert_fusion), kind=kLoop, calls=%fused_computation.1 | loop fusion | flops 16777216 | bytes 33624064 | tf_op jit(solution)/shard_map/mul | solution.py:43
  28.2 66.5 %all-gather.2.cloned.1.call-done = bf16[4096,1024]{1,0:T(8,128)(2,1)} async-done(((bf16[512,1024]{1,0:T(8,128)(2,1)}), bf16[4096,1024]{1,0:T(8,128)(2,1)}) %all-gather.2.cloned.1.call-update) | async-done | bytes 8388624 | tf_op jit(solution)/shard_map/all_gather | solution.py:58
  94.7 24.0 %fusion.48 = f32[2048,1024]{1,0:T(8,128)} fusion(bf16[2048,4096]{1,0:T(8,128)(2,1)} %fusion, bf16[4096,1024]{1,0:T(8,128)(2,1)} %all-gather.2.cloned.1.call-done), kind=kOutput, calls=%fused_computation.107 | convolution fusion | flops 17179869184 | bytes 33554432 | tf_op jit(solution)/shard_map/dot_general | solution.py:56
  118.7 9.1 %copy.16 = f32[2048,1024]{0,1:T(8,128)} copy(f32[2048,1024]{1,0:T(8,128)} %fusion.48) | data formatting | bytes 16777216 | tf_op jit(solution)/shard_map/dot_general | solution.py:56
  127.8 7.5 %copy.21 = f32[128,8,8,256]{3,2,1,0:T(8,128)S(1)} copy(f32[128,8,8,256]{3,1,2,0:T(8,128)} %bitcast.26) | data formatting | bytes 16777216
  135.3 2.7 copy.17
  138.0 186.7 %all_to_all.10 = f32[8,256,16,4,16]{1,4,3,2,0:T(8,128)S(1)} all-to-all(f32[8,256,16,4,16]{1,4,3,2,0:T(8,128)S(1)} %copy.17), channel_id=1, replica_groups=mesh['occ'=8,'vir'=4] {'occ'}, dimensions={0} | all-to-all | bytes 16777216 | tf_op jit(solution)/shard_map/all_to_all | solution.py:63
  324.7 11.3 %copy.18 = f32[8,256,16,4,16]{1,0,4,2,3:T(8,128)} copy(f32[8,256,16,4,16]{1,4,3,2,0:T(8,128)S(1)} %all_to_all.10) | data formatting | bytes 16777216 | tf_op jit(solution)/shard_map/all_to_all | solution.py:63
  336.0 0.0 copy-start
  336.0 0.0 copy-start.1
  336.0 6.0 all-to-all-start.1
  342.0 0.0 copy-done
  342.1 0.1 reshape.309
  342.1 0.0 copy-done.1
  342.1 0.1 dynamic_slice.3
  342.2 0.1 select_reduce_fusion
  342.3 0.1 broadcast_add_fusion
  342.4 0.1 broadcast_subtract_fusion
  342.5 7.5 %sub.92 = f32[8,16,16,16,64]{4,3,2,1,0:T(8,128)} broadcast(f32[16,16,64]{2,1,0:T(8,128)S(1)} %broadcast_subtract_fusion), dimensions={1,3,4} | broadcast | bytes 8454144 | tf_op jit(solution)/shard_map/sub | solution.py:80
  350.0 14.5 %sub.93 = f32[2048,1024]{1,0:T(8,128)} reshape(f32[8,16,16,16,64]{4,3,2,1,0:T(8,128)} %sub.92) | data formatting | bytes 16777216 | tf_op jit(solution)/shard_map/sub | solution.py:80
  364.4 0.1 sub.95
  364.5 69.6 %all-to-all-done.1 = f32[8,256,16,4,16]{1,0,4,2,3:T(8,128)} async-done(((f32[8,256,16,4,16]{1,0,4,2,3:T(8,128)}), f32[8,256,16,4,16]{1,0,4,2,3:T(8,128)}, u32[]{:S(2)}, u32[]{:S(2)}) %all-to-all-start.1) | async-done | bytes 8388640 | tf_op jit(solution)/shard_map/all_to_all | solution.py:62
  434.1 9.3 %copy.19 = f32[8,256,16,4,16]{1,4,3,2,0:T(8,128)} copy(f32[8,256,16,4,16]{1,0,4,2,3:T(8,128)} %all-to-all-done.1) | data formatting | bytes 16777216 | tf_op jit(solution)/shard_map/all_to_all | solution.py:62
  443.3 37.5 %reshape.307 = f32[8,16,16,16,4,16]{2,1,5,4,3,0:T(8,128)} reshape(f32[8,256,16,4,16]{1,4,3,2,0:T(8,128)} %copy.19) | data formatting | bytes 16777216 | tf_op jit(solution)/shard_map/reshape | solution.py:69
  480.8 86.3 %copy.20 = f32[8,16,16,16,4,16]{5,4,3,2,1,0:T(4,128)} copy(f32[8,16,16,16,4,16]{1,2,3,4,5,0:T(8,128)} %bitcast.3) | data formatting | bytes 16777216 | tf_op jit(solution)/shard_map/transpose | solution.py:72
  567.1 70.7 %reshape.308 = f32[2048,1024]{1,0:T(8,128)} reshape(f32[8,16,16,16,4,16]{5,4,3,2,1,0:T(4,128)} %copy.20) | data formatting | bytes 16777216 | tf_op jit(solution)/shard_map/reshape | solution.py:73
  637.8 12.4 %subtract_divide_fusion = f32[2048,1024]{1,0:T(8,128)} fusion(f32[2048,1024]{1,0:T(8,128)} %sub.93, f32[2048,1024]{1,0:T(8,128)} %fusion.48, f32[2048,1024]{1,0:T(8,128)} %reshape.308, f32[2048]{0:T(1024)S(1)} %sub.95), kind=kLoop, calls=%fused_computation.2 | loop fusion | flops 6291456 | bytes 33562624 | tf_op jit(solution)/shard_map/div | solution.py:86
  (10 shorter events, 0.1 us)
Async XLA Ops:
  6.5 88.2 %all-gather.2.cloned.1.call-start = ((), (), s32[]{:S(2)}) async-start(), calls=%async_computation.2 | async-start | bytes 9437184 | tf_op jit(solution)/shard_map/all_gather | solution.py:58
  336.0 6.0 copy-start
  336.0 6.1 copy-start.1
  336.0 98.0 %all-to-all-start.1 = ((f32[8,256,16,4,16]{1,0,4,2,3:T(8,128)}), f32[8,256,16,4,16]{1,0,4,2,3:T(8,128)}, u32[]{:S(2)}, u32[]{:S(2)}) async-start(f32[8,256,16,4,16]{1,0,4,2,3:T(8,128)} %copy.18), calls=%async_computation.1 | async-start | bytes 16777216 | tf_op jit(solution)/shard_map/all_to_all | solution.py:62
Sparse Core Ops, SparseCore 0:
  9.9 84.7 all-gather.1
where the time goes:
time: 661 us; the launch traced here: 657 us
  local copies, waits for them, and re-layouts  257 us (39%)
  blocking collectives  187 us (28%)
  waiting for transfers between devices  136 us (21%)
  other arithmetic  29.9 us (5%)
  matrix products  27.9 us (4%)
  between operations  13.5 us (2%)
    all_to_all x1, blocking collectives, body(): lax.all_to_all(blocks, 'occ', split_axis=0, concat_axis=0, tiled=True)  187 us
    transpose x1, local copies, waits for them, and re-layouts, body(): mirror = arrived.transpose(0, 2, 1, 5, 4, 3)  86.3 us
    reshape x1, local copies, waits for them, and re-layouts, body(): mirror.reshape(tile_total, ORBITALS_IN_GRP, ORBITALS_IN_GRP, vir_span, W)  70.7 us
    all_to_all x1, waiting for transfers between devices, body(): lax.all_to_all(lax.all_to_all(blocks, 'occ', split_axis=0, concat_axis=0,...  69.6 us
    all_gather x1, waiting for transfers between devices, body(): lax.all_gather(screened_slab, 'occ', axis=0, tiled=True)  66.5 us
    reshape x1, local copies, waits for them, and re-layouts, body(): arrived.reshape(tile_total, ORBITALS_IN_GRP, ORBITALS_IN_GRP, vir_span, v...  37.5 us
    dot_general x1, matrix products, body(): jnp.dot(screened, lax.all_gather(screened_slab, 'occ', axis=0, tiled=True...  24 us
    sub x4, local copies, waits for them, and re-layouts, body(): vir_own[None, None, None, :, None] + vir_energy[None, None, None, None, :]  22 us
  transfers between devices with their start and end apart: 2, of which 2 were waited for; matrix products, arithmetic and copies ran while one was open for 6% of the time, Pallas kernels for 0%

commit v1 on v0

v1 whole, which is shorter than its diff:
```python
import functools

import jax
import jax.numpy as jnp
from jax import lax
from jax.experimental import pallas as pl
from jax.experimental.pallas import tpu as pltpu
from jax.sharding import PartitionSpec as P

VT = 32
NVT = 2
W = 64
ORBITALS_IN_GRP = 16
PAIR_SQ = ORBITALS_IN_GRP * ORBITALS_IN_GRP
CODE_ROWS = 16
TOP = 32700.0
STEPS = 8.0
VMEM_LIMIT = 56 * 1024 * 1024


def one_hot_of(target, amount):
    return (target[:, None] == jnp.arange(amount)[None, :]).astype(jnp.bfloat16)


def split(values):
    high = values.astype(jnp.bfloat16)
    return high, (values - high.astype(jnp.float32)).astype(jnp.bfloat16)


def dot(left, right):
    return jnp.dot(left, right, preferred_element_type=jnp.float32)


def scale_of(code):
    return jnp.exp2(code * (1.0 / STEPS))


def ladder_kernel(vir_count, amp_mask, int_mask, place, numbers, rows_ref, slab_ref, swap_ref, perm_ref,
                  ladder_ref, packed_ref, slab_scr):
    tile = pl.program_id(0)
    cols = slab_ref.shape[1]

    @pl.when(tile == 0)
    def _():
        lane = lax.broadcasted_iota(jnp.int32, (1, cols), 1) % W
        second = lane >= VT
        first_pair = place[1] * NVT

        def screen(c, carry):
            for d_tile in range(NVT):
                label = c // VT * NVT + d_tile
                keep = jnp.where(second, int_mask[label, first_pair + 1], int_mask[label, first_pair])
                at = pl.ds(pl.multiple_of(c * W + d_tile * VT, VT), VT)
                slab_scr[at, :] = slab_ref[at, :] * keep.astype(jnp.float32).astype(jnp.bfloat16)
            return carry

        lax.fori_loop(0, W, screen, 0)

    lane = lax.broadcasted_iota(jnp.int32, (1, W * W), 1)
    low = lane < W * VT
    left = lane % W < VT
    keep = jnp.where(
        low,
        jnp.where(left, amp_mask[tile, 0], amp_mask[tile, 1]),
        jnp.where(left, amp_mask[tile, 2], amp_mask[tile, 3]),
    )
    screened = rows_ref[...] * keep.astype(jnp.float32).astype(jnp.bfloat16)
    ladder = dot(screened, slab_scr[...])
    pair = lax.broadcasted_iota(jnp.int32, (PAIR_SQ, 1), 0)
    nonzero = (pair // ORBITALS_IN_GRP < numbers[place[0]]) & (pair % ORBITALS_IN_GRP < numbers[tile])
    ladder = jnp.where(nonzero, ladder, 0.0)
    ladder_ref[...] = ladder
    high, low_part = split(ladder)
    mirror = dot(dot(swap_ref[...], high).astype(jnp.bfloat16), perm_ref[...]) + dot(
        dot(swap_ref[...], low_part).astype(jnp.bfloat16), perm_ref[...]
    )
    most = jnp.maximum(jnp.max(jnp.abs(mirror), axis=0, keepdims=True), 1e-30)
    code = jnp.ceil(jnp.log2(most) * STEPS)
    coded = jnp.round(mirror * (TOP / scale_of(code))).astype(jnp.int32).astype(jnp.int16)
    code_rows = jnp.broadcast_to(code.astype(jnp.int32), (CODE_ROWS, cols)).astype(jnp.int16)
    block = cols // vir_count
    for v in range(vir_count):
        packed_ref[0, v, :PAIR_SQ] = coded[:, v * block : (v + 1) * block]
        packed_ref[0, v, PAIR_SQ:] = code_rows[:, v * block : (v + 1) * block]


def ladder_call(tile_total, vir_count, chunk_cols, *args):
    block = chunk_cols // vir_count
    smem = pl.BlockSpec(memory_space=pltpu.SMEM)
    whole = lambda tile: (0, 0)
    flops = 2 * tile_total * PAIR_SQ * chunk_cols * (W * W + 2 * PAIR_SQ + 2 * chunk_cols)
    bytes_accessed = tile_total * PAIR_SQ * (W * W * 2 + chunk_cols * 6) + W * W * chunk_cols * 2
    return pl.pallas_call(
        functools.partial(ladder_kernel, vir_count),
        grid=(tile_total,),
        in_specs=[
            smem,
            smem,
            smem,
            smem,
            pl.BlockSpec((PAIR_SQ, W * W), lambda tile: (tile, 0)),
            pl.BlockSpec((W * W, chunk_cols), whole),
            pl.BlockSpec((PAIR_SQ, PAIR_SQ), whole),
            pl.BlockSpec((chunk_cols, chunk_cols), whole),
        ],
        out_specs=[
            pl.BlockSpec((PAIR_SQ, chunk_cols), lambda tile: (tile, 0)),
            pl.BlockSpec((1, vir_count, PAIR_SQ + CODE_ROWS, block), lambda tile: (tile, 0, 0, 0)),
        ],
        out_shape=[
            jax.ShapeDtypeStruct((tile_total * PAIR_SQ, chunk_cols), jnp.float32),
            jax.ShapeDtypeStruct((tile_total, vir_count, PAIR_SQ + CODE_ROWS, block), jnp.int16),
        ],
        scratch_shapes=[pltpu.VMEM((W * W, chunk_cols), jnp.bfloat16)],
        compiler_params=pltpu.CompilerParams(vmem_limit_bytes=VMEM_LIMIT),
        cost_estimate=pl.CostEstimate(flops=flops, bytes_accessed=bytes_accessed, transcendentals=0),
        name="ladder",
    )(*args)


def update_kernel(chunks, vir_count, vir_ref, occ_ref, spread_ref, *refs):
    ladders, arrived, update_ref = refs[:chunks], refs[chunks : 2 * chunks], refs[2 * chunks]
    highs, lows = [], []
    for c in range(chunks):
        for v in range(vir_count):
            code = arrived[c][0, v, PAIR_SQ:].astype(jnp.int32).astype(jnp.float32)[:1]
            values = arrived[c][0, v, :PAIR_SQ].astype(jnp.int32).astype(jnp.float32)
            high, low = split(values * (scale_of(code) * (1.0 / TOP)))
            highs.append(high)
            lows.append(low)
    mirror = dot(jnp.concatenate(highs, axis=1), spread_ref[...]) + dot(
        jnp.concatenate(lows, axis=1), spread_ref[...]
    )
    chunk_cols = ladders[0].shape[1]
    for c in range(chunks):
        at = slice(c * chunk_cols, (c + 1) * chunk_cols)
        denominator = vir_ref[:, at] - occ_ref[:, :1]
        update_ref[:, at] = (ladders[c][...] + mirror[:, at]) / denominator


def update_call(tile_total, vir_count, vir_sum, occ_sum, spread, ladders, arrived):
    chunks = len(ladders)
    chunk_cols = ladders[0].shape[1]
    block = chunk_cols // vir_count
    slab_cols = chunks * chunk_cols
    whole = lambda tile: (0, 0)
    rows = tile_total * PAIR_SQ
    return pl.pallas_call(
        functools.partial(update_kernel, chunks, vir_count),
        grid=(tile_total,),
        in_specs=[
            pl.BlockSpec((1, slab_cols), whole),
            pl.BlockSpec((PAIR_SQ, 128), lambda tile: (tile, 0)),
            pl.BlockSpec((slab_cols, slab_cols), whole),
        ]
        + [pl.BlockSpec((PAIR_SQ, chunk_cols), lambda tile: (tile, 0))] * chunks
        + [pl.BlockSpec((1, vir_count, PAIR_SQ + CODE_ROWS, block), lambda tile: (tile, 0, 0, 0))] * chunks,
        out_specs=pl.BlockSpec((PAIR_SQ, slab_cols), lambda tile: (tile, 0)),
        out_shape=jax.ShapeDtypeStruct((rows, slab_cols), jnp.float32),
        compiler_params=pltpu.CompilerParams(vmem_limit_bytes=VMEM_LIMIT),
        cost_estimate=pl.CostEstimate(
            flops=4 * rows * slab_cols * slab_cols, bytes_accessed=rows * slab_cols * 10, transcendentals=0
        ),
        name="update",
    )(vir_sum, occ_sum, spread, *ladders, *arrived)


def body(amplitudes, amp_mask, integrals, int_mask, group_orbital_numbers, occ_energy, vir_energy):
    tile_total = lax.axis_size("occ")
    vir_count = lax.axis_size("vir")
    row_tile = lax.axis_index("occ")
    vir_place = lax.axis_index("vir")
    vir_span = W // vir_count
    slab_cols = vir_span * W
    chunks = 2 if vir_span >= 16 else 1
    chunk_cols = slab_cols // chunks
    chunk_span = vir_span // chunks
    block = chunk_cols // vir_count

    slabs = [
        lax.all_gather(integrals[:, c * chunk_cols : (c + 1) * chunk_cols], "occ", axis=0, tiled=True)
        for c in range(chunks)
    ]

    pair = jnp.arange(PAIR_SQ)
    swap = one_hot_of(pair % ORBITALS_IN_GRP * ORBITALS_IN_GRP + pair // ORBITALS_IN_GRP, PAIR_SQ)
    col = jnp.arange(chunk_cols)
    a, b = col // W, col % W
    perm = one_hot_of(b // vir_span * block + b % vir_span * chunk_span + a, chunk_cols)
    place = jnp.arange(slab_cols)
    chunk, sender = place // chunk_cols, place % chunk_cols // block
    own, other = place % block // chunk_span, place % chunk_span
    spread = one_hot_of(own * W + sender * vir_span + chunk * chunk_span + other, slab_cols)

    where = jnp.stack([row_tile, vir_place * vir_span // VT]).astype(jnp.int32)
    occ_table = occ_energy.reshape(tile_total, ORBITALS_IN_GRP)
    own_energy = lax.dynamic_slice_in_dim(occ_table, row_tile, 1, 0)[0]
    occ_sum = jnp.broadcast_to(
        (own_energy[None, :, None] + occ_table[:, None, :]).reshape(-1, 1), (tile_total * PAIR_SQ, 128)
    )
    vir_own = lax.dynamic_slice_in_dim(vir_energy, vir_place * vir_span, vir_span, 0)
    vir_sum = (vir_own[:, None] + vir_energy[None, :]).reshape(1, -1)

    ladders, arrived = [], []
    for c in range(chunks):
        ladder, packed = ladder_call(
            tile_total, vir_count, chunk_cols, amp_mask[0], int_mask, where, group_orbital_numbers,
            amplitudes, slabs[c], swap, perm,
        )
        rows = PAIR_SQ + CODE_ROWS
        moved = lax.all_to_all(
            packed.reshape(tile_total * vir_count, rows, block), ("occ", "vir"), split_axis=0, concat_axis=0, tiled=True
        )
        ladders.append(ladder)
        arrived.append(moved.reshape(tile_total, vir_count, rows, block))
    return update_call(tile_total, vir_count, vir_sum, occ_sum, spread, ladders, arrived)


def solution(mesh):
    in_specs = (P("occ", None), P("occ", None, None), P("occ", "vir"), P(), P(), P(), P())
    out_specs = P("occ", "vir")
    return jax.shard_map(body, mesh=mesh, in_specs=in_specs, out_specs=out_specs, check_vma=False)
```

time: 661 us -> 233 us (0.35)
  local copies, waits for them, and re-layouts: 257 us -> 5.82 us
  blocking collectives: 187 us -> 0 us
  Pallas kernels: 0 us -> 57.7 us
  matrix products: 27.9 us -> 0 us
  other arithmetic: 29.9 us -> 4.29 us
  waiting for transfers between devices: 136 us -> 143 us
    all_to_all x1 -> x0, blocking collectives: 187 us -> none  [body(): lax.all_to_all(blocks, 'occ', split_axis=0, concat_axis=0, tiled=True)]
    reshape x3 -> x0, local copies, waits for them, and re-layouts: 111 us -> none  [the longest x1 70.7 us: body(): mirror.reshape(tile_total, ORBITALS_IN_GRP, ORBITALS_IN_GRP, vir_span, W)]
    transpose x1 -> x0, local copies, waits for them, and re-layouts: 86.3 us -> none  [body(): mirror = arrived.transpose(0, 2, 1, 5, 4, 3)]
    pallas_call x0 -> x3, Pallas kernels: none -> 57.7 us  [the longest x2 42.3 us: ladder_call(): pl.pallas_call(functools.partial(ladder_kernel, vir_count), grid=(tile_to...]
    dot_general x3 -> x0, matrix products: 27.9 us -> none  [the longest x1 24 us: body(): jnp.dot(screened, lax.all_gather(screened_slab, 'occ', axis=0, tiled=True...]
    all_gather x1 -> x2, waiting for transfers between devices: 66.5 us -> 93.5 us  [body(): lax.all_gather(integrals[:, c * chunk_cols:(c + 1) * chunk_cols], 'occ',...]
    sub x4 -> x0, local copies, waits for them, and re-layouts: 22 us -> none  [body(): vir_own[None, None, None, :, None] + vir_energy[None, None, None, None, :]]
    all_to_all x1 -> x2, waiting for transfers between devices: 69.6 us -> 48.7 us  [body(): lax.all_to_all(packed.reshape(tile_total * vir_count, rows, block), ('occ...]
  transfers between devices with their start and end apart: 2 -> 4, of which waited for: 2 -> 3; matrix products, arithmetic and copies ran while one was open for 6% -> 3% of each run, Pallas kernels for 0% -> 18%
where the time goes in v1:
time: 233 us; the launch traced here: 232 us
  waiting for transfers between devices  143 us (61%)
  Pallas kernels  57.7 us (25%)
  between operations  13.5 us (6%)
  starting transfers between devices  7.88 us (3%)
  local copies, waits for them, and re-layouts  5.82 us (2%)
  other arithmetic  4.29 us (2%)
    all_gather x2, waiting for transfers between devices, body(): lax.all_gather(integrals[:, c * chunk_cols:(c + 1) * chunk_cols], 'occ',...  93.5 us
    all_to_all x2, waiting for transfers between devices, body(): lax.all_to_all(packed.reshape(tile_total * vir_count, rows, block), ('occ...  48.7 us
    pallas_call x2, Pallas kernels, ladder_call(): pl.pallas_call(functools.partial(ladder_kernel, vir_count), grid=(tile_to...  42.3 us
    pallas_call x1, Pallas kernels, update_call(): pl.pallas_call(functools.partial(update_kernel, chunks, vir_count), grid=...  15.4 us
    all_to_all x2, starting transfers between devices, body(): lax.all_to_all(packed.reshape(tile_total * vir_count, rows, block), ('occ...  7.84 us
  transfers between devices with their start and end apart: 4, of which 3 were waited for; matrix products, arithmetic and copies ran while one was open for 3% of the time, Pallas kernels for 18%

profile of v1, /device:TPU:0, one launch (start us, length us, event | category | flops | bytes accessed | tf_op | source)
XLA Modules:
  0.0 232.1 jit_solution(3800269479472156974)
XLA Ops:
  6.5 0.0 all-gather.3.cloned.1.call-start
  6.5 2.2 fusion.53
  8.8 0.0 all-gather.3.cloned.1.call-update
  8.8 0.0 all-gather.5.cloned.1.call-start
  8.8 0.7 all-gather.5.cloned.1.call-update
  9.6 1.3 copy.8.amp_mask
  10.9 0.7 pad_add_fusion.place
  11.6 0.8 fusion.2.swap_ref
  12.3 0.9 fusion.1.perm_ref
  13.3 45.6 %all-gather.3.cloned.1.call-done.slab_ref = bf16[4096,512]{1,0:T(8,128)(2,1)} async-done(((bf16[512,512]{1,0:T(8,128)(2,1)}), bf16[4096,512]{1,0:T(8,128)(2,1)}) %all-gather.3.cloned.1.call-update) | async-done | bytes 4194320 | tf_op jit(solution)/shard_map/all_gather | solution.py:181
  58.8 21.1 %ladder.2 = (f32[2048,512]{1,0:T(8,128)}, s16[8,4,272,128]{3,2,1,0:T(8,128)(2,1)}) custom-call(s32[8,4]{1,0:T(8,128)} %copy.8.amp_mask, s32[4,4]{1,0:T(4,128)} %int_mask.3, s32[2]{0:T(128)} %pad_add_fusion.place, s32[8]{0:T(128)} %numbers.3, bf16[2048,4096]{1,0:T(8,128)(2,1)} %rows_ref.3, bf16[4096,512]{1,0:T(8,128)(2,1)} %all-gather.3.cloned.1.call-done.slab_ref, ...), custom_call_target="tpu_custom_call" | custom-call | flops 11811160064 | bytes 27262976 | tf_op jit(solution)/shard_map/ladder/pallas_call | solution.py:93
  80.0 3.3 %all-to-all-start = ((s16[32,272,128]{2,1,0:T(8,128)(2,1)}), s16[32,272,128]{2,1,0:T(8,128)(2,1)S(1)}, u32[]{:S(2)}, u32[]{:S(2)}) async-start(s16[32,272,128]{2,1,0:T(8,128)(2,1)} %bitcast.11), calls=%async_computation | async-start | bytes 4456448 | tf_op jit(solution)/shard_map/all_to_all | solution.py:211
  83.3 48.0 %all-gather.5.cloned.1.call-done.slab_ref = bf16[4096,512]{1,0:T(8,128)(2,1)} async-done(((bf16[512,512]{1,0:T(8,128)(2,1)}), bf16[4096,512]{1,0:T(8,128)(2,1)}) %all-gather.5.cloned.1.call-update) | async-done | bytes 4194320 | tf_op jit(solution)/shard_map/all_gather | solution.py:181
  131.3 21.2 %ladder.3 = (f32[2048,512]{1,0:T(8,128)}, s16[8,4,272,128]{3,2,1,0:T(8,128)(2,1)}) custom-call(s32[8,4]{1,0:T(8,128)} %copy.8.amp_mask, s32[4,4]{1,0:T(4,128)} %int_mask.3, s32[2]{0:T(128)} %pad_add_fusion.place, s32[8]{0:T(128)} %numbers.3, bf16[2048,4096]{1,0:T(8,128)(2,1)} %rows_ref.3, bf16[4096,512]{1,0:T(8,128)(2,1)} %all-gather.5.cloned.1.call-done.slab_ref, ...), custom_call_target="tpu_custom_call" | custom-call | flops 11811160064 | bytes 27262976 | tf_op jit(solution)/shard_map/ladder/pallas_call | solution.py:93
  152.5 0.0 copy-start.1
  152.5 0.0 copy-start.2
  152.5 0.0 all-to-all-done
  152.5 0.0 copy-start
  152.5 4.5 %all-to-all-start.1 = ((s16[32,272,128]{2,1,0:T(8,128)(2,1)}), s16[32,272,128]{2,1,0:T(8,128)(2,1)}, u32[]{:S(2)}, u32[]{:S(2)}) async-start(s16[32,272,128]{2,1,0:T(8,128)(2,1)} %bitcast.10), calls=%async_computation.1 | async-start | bytes 4456448 | tf_op jit(solution)/shard_map/all_to_all | solution.py:211
  157.0 0.0 copy-done.1
  157.0 0.1 reshape.199
  157.1 0.0 copy-done.2
  157.1 0.1 dynamic_slice.6
  157.2 0.1 broadcast_add_fusion.1
  157.3 0.7 add.194.vir_ref
  157.9 0.1 broadcast_add_fusion
  158.0 0.1 add.200
  158.1 1.8 fusion.spread_ref
  159.9 48.7 %all-to-all-done.1 = s16[32,272,128]{2,1,0:T(8,128)(2,1)} async-done(((s16[32,272,128]{2,1,0:T(8,128)(2,1)}), s16[32,272,128]{2,1,0:T(8,128)(2,1)}, u32[]{:S(2)}, u32[]{:S(2)}) %all-to-all-start.1) | async-done | bytes 2228256 | tf_op jit(solution)/shard_map/all_to_all | solution.py:211
  208.5 1.3 broadcast_in_dim.2.occ_ref
  209.8 0.0 copy-done
  209.8 15.4 %update.1 = f32[2048,1024]{1,0:T(8,128)} custom-call(f32[1,1024]{1,0:T(1,128)} %add.194.vir_ref, f32[2048,128]{1,0:T(8,128)} %broadcast_in_dim.2.occ_ref, bf16[1024,1024]{1,0:T(8,128)(2,1)} %fusion.spread_ref, f32[2048,512]{1,0:T(8,128)} %get-tuple-element.9.refs_0_, f32[2048,512]{1,0:T(8,128)} %get-tuple-element.10.refs_1_, ...), custom_call_target="tpu_custom_call" | custom-call | flops 8589934592 | bytes 20971520 | tf_op jit(solution)/shard_map/update/pallas_call | solution.py:148
  (4 shorter events, 0.0 us)
Async XLA Ops:
  6.5 52.3 %all-gather.3.cloned.1.call-start = ((), (), s32[]{:S(2)}) async-start(), calls=%async_computation.2 | async-start | bytes 4718592 | tf_op jit(solution)/shard_map/all_gather | solution.py:181
  8.8 122.5 %all-gather.5.cloned.1.call-start = ((), (), s32[]{:S(2)}) async-start(), calls=%async_computation.3 | async-start | bytes 4718592 | tf_op jit(solution)/shard_map/all_gather | solution.py:181
  80.0 72.5 %all-to-all-start = ((s16[32,272,128]{2,1,0:T(8,128)(2,1)}), s16[32,272,128]{2,1,0:T(8,128)(2,1)S(1)}, u32[]{:S(2)}, u32[]{:S(2)}) async-start(s16[32,272,128]{2,1,0:T(8,128)(2,1)} %bitcast.11), calls=%async_computation | async-start | bytes 4456448 | tf_op jit(solution)/shard_map/all_to_all | solution.py:211
  152.5 4.6 %copy-start.1 = (f32[128]{0:T(128)S(1)}, f32[128]{0:T(128)}, u32[]{:S(2)}) copy-start(f32[128]{0:T(128)} %param.12) | copy-start | bytes 1540
  152.5 4.6 %copy-start.2 = (f32[64]{0:T(128)S(1)}, f32[64]{0:T(128)}, u32[]{:S(2)}) copy-start(f32[64]{0:T(128)} %param.13) | copy-start | bytes 772
  152.5 57.4 %copy-start = (s16[32,272,128]{2,1,0:T(8,128)(2,1)}, s16[32,272,128]{2,1,0:T(8,128)(2,1)S(1)}, u32[]{:S(2)}) copy-start(s16[32,272,128]{2,1,0:T(8,128)(2,1)S(1)} %all-to-all-done) | copy-start | bytes 6684676
  152.5 56.0 %all-to-all-start.1 = ((s16[32,272,128]{2,1,0:T(8,128)(2,1)}), s16[32,272,128]{2,1,0:T(8,128)(2,1)}, u32[]{:S(2)}, u32[]{:S(2)}) async-start(s16[32,272,128]{2,1,0:T(8,128)(2,1)} %bitcast.10), calls=%async_computation.1 | async-start | bytes 4456448 | tf_op jit(solution)/shard_map/all_to_all | solution.py:211
Sparse Core Ops, SparseCore 0:
  9.0 49.8 all-gather.2
  60.4 70.8 all-gather.4

commit v2 on v1

v2 whole, which is shorter than its diff:
```python
import functools

import jax
import jax.numpy as jnp
from jax import lax
from jax.experimental import pallas as pl
from jax.experimental.pallas import tpu as pltpu
from jax.sharding import PartitionSpec as P

VT = 32
NVT = 2
W = 64
ORBITALS_IN_GRP = 16
PAIR_SQ = ORBITALS_IN_GRP * ORBITALS_IN_GRP
PIECES = 2
PIECE_SPAN = ORBITALS_IN_GRP // PIECES
PIECE_ROWS = PIECE_SPAN * ORBITALS_IN_GRP
TILES_AT_ONCE = 2
TOP = 32700.0
STEPS = 8.0
VMEM_LIMIT = 56 * 1024 * 1024


def one_hot_of(target, amount):
    return (target[:, None] == jnp.arange(amount)[None, :]).astype(jnp.bfloat16)


def split(values):
    high = values.astype(jnp.bfloat16)
    return high, (values - high.astype(jnp.float32)).astype(jnp.bfloat16)


def dot(left, right):
    return jnp.dot(left, right, preferred_element_type=jnp.float32)


def scale_of(code):
    return jnp.exp2(code * (1.0 / STEPS))


def screen_kernel(vir_count, int_mask, slab_ref, screened_ref):
    slab_rows, slab_cols = slab_ref.shape
    row_label = lax.axis_index("occ") * slab_rows // W // VT * NVT
    col_label = lax.axis_index("vir") * slab_cols // W // VT * NVT
    right = lax.broadcasted_iota(jnp.int32, (VT, slab_cols), 1) % W >= VT
    keep = []
    for d_tile in range(NVT):
        label = row_label + d_tile
        kept = jnp.where(right, int_mask[label, col_label + 1], int_mask[label, col_label])
        keep.append(kept.astype(jnp.float32).astype(jnp.bfloat16))
    for at in range(0, slab_rows, VT):
        screened_ref[at : at + VT, :] = slab_ref[at : at + VT, :] * keep[at // VT % NVT]


def screen_call(vir_count, int_mask, integrals):
    return pl.pallas_call(
        functools.partial(screen_kernel, vir_count),
        in_specs=[pl.BlockSpec(memory_space=pltpu.SMEM), pl.BlockSpec(memory_space=pltpu.VMEM)],
        out_specs=pl.BlockSpec(memory_space=pltpu.VMEM),
        out_shape=jax.ShapeDtypeStruct(integrals.shape, integrals.dtype),
        name="screen",
    )(int_mask, integrals)


def ladder_kernel(piece, vir_count, amp_mask, numbers, rows_ref, slab_ref, swap_ref, perm_ref,
                  ladder_ref, packed_ref, code_ref):
    tiles = rows_ref.shape[0]
    cols = slab_ref.shape[1]
    first = pl.program_id(1) * tiles
    lane = lax.broadcasted_iota(jnp.int32, (1, W * W), 1)
    low = lane < W * VT
    left = lane % W < VT
    pair = lax.broadcasted_iota(jnp.int32, (PIECE_ROWS, 1), 0)
    own_number = numbers[lax.axis_index("occ")]
    screened, nonzero = [], []
    for n in range(tiles):
        tile = first + n
        keep = jnp.where(
            low,
            jnp.where(left, amp_mask[tile, 0], amp_mask[tile, 1]),
            jnp.where(left, amp_mask[tile, 2], amp_mask[tile, 3]),
        )
        screened.append(rows_ref[n, 0] * keep.astype(jnp.float32).astype(jnp.bfloat16))
        nonzero.append(
            (pair // ORBITALS_IN_GRP + piece * PIECE_SPAN < own_number)
            & (pair % ORBITALS_IN_GRP < numbers[tile])
        )
    ladder = dot(jnp.concatenate(screened, axis=0), slab_ref[...])
    ladder = jnp.where(jnp.concatenate(nonzero, axis=0), ladder, 0.0)
    ladder_ref[...] = ladder.reshape(ladder_ref.shape)
    high, low_part = split(ladder)
    mirror = dot(dot(swap_ref[...], high).astype(jnp.bfloat16), perm_ref[...]) + dot(
        dot(swap_ref[...], low_part).astype(jnp.bfloat16), perm_ref[...]
    )
    block = cols // vir_count
    for n in range(tiles):
        part = mirror[n * PIECE_ROWS : (n + 1) * PIECE_ROWS]
        most = jnp.maximum(jnp.max(jnp.abs(part), axis=0, keepdims=True), 1e-30)
        code = jnp.ceil(jnp.log2(most) * STEPS)
        code_ref[0, n : n + 1, :] = code
        coded = jnp.round(part * (TOP / scale_of(code))).astype(jnp.int32).astype(jnp.int16)
        for v in range(vir_count):
            packed_ref[n, v] = coded[:, v * block : (v + 1) * block]


def ladder_call(piece, tile_total, vir_count, cut, amp_mask, numbers, amplitudes, slab, swap, perm):
    slab_cols = slab.shape[1]
    chunk = slab_cols // cut
    block = chunk // vir_count
    tiles = TILES_AT_ONCE
    smem = pl.BlockSpec(memory_space=pltpu.SMEM)
    whole = lambda c, t: (0, 0)
    rows = tile_total * PIECE_ROWS
    flops = 2 * rows * slab_cols * (W * W + 2 * tiles * PIECE_ROWS + 2 * chunk)
    bytes_accessed = rows * (W * W * 2 * cut + slab_cols * 6) + W * W * slab_cols * 2
    return pl.pallas_call(
        functools.partial(ladder_kernel, piece, vir_count),
        grid=(cut, tile_total // tiles),
        in_specs=[
            smem,
            smem,
            pl.BlockSpec((tiles, 1, PIECE_ROWS, W * W), lambda c, t: (t, piece, 0, 0)),
            pl.BlockSpec((W * W, chunk), lambda c, t: (0, c)),
            pl.BlockSpec(swap.shape, whole),
            pl.BlockSpec(perm.shape, whole),
        ],
        out_specs=[
            pl.BlockSpec((tiles, PIECE_ROWS, chunk), lambda c, t: (t, 0, c)),
            pl.BlockSpec((tiles, vir_count, PIECE_ROWS, block), lambda c, t: (t, 0, 0, c)),
            pl.BlockSpec((1, tiles, chunk), lambda c, t: (t, 0, c)),
        ],
        out_shape=[
            jax.ShapeDtypeStruct((tile_total, PIECE_ROWS, slab_cols), jnp.float32),
            jax.ShapeDtypeStruct((tile_total, vir_count, PIECE_ROWS, cut * block), jnp.int16),
            jax.ShapeDtypeStruct((tile_total // tiles, tiles, slab_cols), jnp.float32),
        ],
        compiler_params=pltpu.CompilerParams(vmem_limit_bytes=VMEM_LIMIT),
        cost_estimate=pl.CostEstimate(flops=flops, bytes_accessed=bytes_accessed, transcendentals=0),
        name="ladder",
    )(amp_mask, numbers, amplitudes, slab, swap, perm)


def update_kernel(vir_count, code_ref, vir_ref, occ_ref, spread_ref, arrived_ref, *refs):
    ladders, update_ref = refs[:PIECES], refs[-1]
    highs, lows = [], []
    for v in range(vir_count):
        values = arrived_ref[0, v].astype(jnp.int32).astype(jnp.float32)
        high, low = split(values * (scale_of(code_ref[0, v : v + 1, :]) * (1.0 / TOP)))
        highs.append(high)
        lows.append(low)
    mirror = dot(jnp.concatenate(highs, axis=1), spread_ref[...]) + dot(
        jnp.concatenate(lows, axis=1), spread_ref[...]
    )
    slab_cols = mirror.shape[1]
    ladder = jnp.concatenate([ref[...].reshape(-1, slab_cols) for ref in ladders], axis=0)
    denominator = vir_ref[...] - occ_ref[...].reshape(PIECE_ROWS, -1)[:, :1]
    update_ref[...] = ((ladder + mirror) / denominator).reshape(update_ref.shape)


def update_call(piece, tile_total, vir_count, code, vir_sum, occ_sum, spread, arrived, ladders, earlier):
    slab_cols = spread.shape[1]
    rows = tile_total * PIECE_ROWS
    of_piece = lambda span, lanes: pl.BlockSpec(
        (1, span, 1, PIECE_SPAN, lanes), lambda tile: (tile, 0, piece, 0, 0)
    )
    args = [code, vir_sum, occ_sum, spread, arrived, *ladders]
    in_specs = [
        pl.BlockSpec((1,) + code.shape[1:], lambda tile: (tile, 0, 0)),
        pl.BlockSpec((1, slab_cols), lambda tile: (0, 0)),
        of_piece(ORBITALS_IN_GRP, 128),
        pl.BlockSpec(spread.shape, lambda tile: (0, 0)),
        pl.BlockSpec((1,) + arrived.shape[1:], lambda tile: (tile, 0, 0, 0)),
    ] + [of_piece(PIECE_SPAN, slab_cols)] * PIECES
    aliases = {}
    if earlier is not None:
        aliases = {len(args): 0}
        args.append(earlier)
        in_specs.append(pl.BlockSpec(memory_space=pl.ANY))
    return pl.pallas_call(
        functools.partial(update_kernel, vir_count),
        grid=(tile_total,),
        in_specs=in_specs,
        out_specs=of_piece(ORBITALS_IN_GRP, slab_cols),
        out_shape=jax.ShapeDtypeStruct((tile_total, ORBITALS_IN_GRP, PIECES, PIECE_SPAN, slab_cols), jnp.float32),
        input_output_aliases=aliases,
        compiler_params=pltpu.CompilerParams(vmem_limit_bytes=VMEM_LIMIT),
        cost_estimate=pl.CostEstimate(
            flops=4 * rows * slab_cols * slab_cols, bytes_accessed=rows * slab_cols * 10, transcendentals=0
        ),
        name="update",
    )(*args)


def body(amplitudes, amp_mask, integrals, int_mask, group_orbital_numbers, occ_energy, vir_energy):
    tile_total = lax.axis_size("occ")
    vir_count = lax.axis_size("vir")
    row_tile = lax.axis_index("occ")
    vir_place = lax.axis_index("vir")
    vir_span = W // vir_count
    slab_cols = vir_span * W
    cut = 2 if vir_span >= 16 else 1
    chunk = slab_cols // cut
    chunk_span = vir_span // cut
    block = chunk // vir_count

    slab = lax.all_gather(screen_call(vir_count, int_mask, integrals), "occ", axis=0, tiled=True)

    rows = jnp.arange(TILES_AT_ONCE * PIECE_ROWS)
    in_tile = rows % PIECE_ROWS
    swap = one_hot_of(
        rows // PIECE_ROWS * PIECE_ROWS + in_tile % PIECE_SPAN * ORBITALS_IN_GRP + in_tile // PIECE_SPAN, rows.size
    )
    col = jnp.arange(chunk)
    a, b = col // W, col % W
    perm = one_hot_of(b // vir_span * block + b % vir_span * chunk_span + a, chunk)
    place = jnp.arange(slab_cols)
    sender, part = place // (cut * block), place // block % cut
    own, other = place % block // chunk_span, place % chunk_span
    spread = one_hot_of(own * W + sender * vir_span + part * chunk_span + other, slab_cols)

    occ_table = occ_energy.reshape(tile_total, ORBITALS_IN_GRP)
    own_energy = lax.dynamic_slice_in_dim(occ_table, row_tile, 1, 0)[0]
    occ_sum = jnp.broadcast_to(
        (own_energy[None, :, None] + occ_table[:, None, :]).reshape(
            tile_total, ORBITALS_IN_GRP, PIECES, PIECE_SPAN, 1
        ),
        (tile_total, ORBITALS_IN_GRP, PIECES, PIECE_SPAN, 128),
    )
    vir_own = lax.dynamic_slice_in_dim(vir_energy, vir_place * vir_span, vir_span, 0)
    vir_sum = (vir_own[:, None] + vir_energy[None, :]).reshape(1, -1)

    by_piece = amplitudes.reshape(tile_total, PIECES, PIECE_ROWS, W * W)
    ladders, arrived, codes = [], [], []
    for piece in range(PIECES):
        ladder, packed, code = ladder_call(
            piece, tile_total, vir_count, cut, amp_mask[0], group_orbital_numbers, by_piece, slab, swap, perm
        )
        moved = lax.all_to_all(
            packed.reshape(tile_total * vir_count, PIECE_ROWS, cut * block),
            ("occ", "vir"), split_axis=0, concat_axis=0, tiled=True,
        )
        all_codes = lax.all_gather(code, ("occ", "vir"), axis=0, tiled=False)
        all_codes = all_codes.reshape(tile_total, vir_count, tile_total, cut, vir_count, block)
        own_codes = lax.dynamic_slice(
            all_codes, (0, 0, row_tile, 0, vir_place, 0), (tile_total, vir_count, 1, cut, 1, block)
        )
        ladders.append(ladder.reshape(tile_total, PIECE_SPAN, PIECES, PIECE_SPAN, slab_cols))
        arrived.append(moved.reshape(tile_total, vir_count, PIECE_ROWS, cut * block))
        codes.append(own_codes.reshape(tile_total, vir_count, cut * block))
    update = None
    for piece in range(PIECES):
        update = update_call(
            piece, tile_total, vir_count, codes[piece], vir_sum, occ_sum, spread, arrived[piece], ladders, update
        )
    return update.reshape(tile_total * PAIR_SQ, slab_cols)


def solution(mesh):
    in_specs = (P("occ", None), P("occ", None, None), P("occ", "vir"), P(), P(), P(), P())
    out_specs = P("occ", "vir")
    return jax.shard_map(body, mesh=mesh, in_specs=in_specs, out_specs=out_specs, check_vma=False)
```

time: 233 us -> 274 us (1.18)
  waiting for transfers between devices: 143 us -> 174 us
  Pallas kernels: 57.7 us -> 65.6 us
  local copies, waits for them, and re-layouts: 5.82 us -> 9.46 us
    all_gather x2 -> x3, waiting for transfers between devices: 93.5 us -> 143 us  [the longest x1 81.8 us: body(): lax.all_gather(screen_call(vir_count, int_mask, integrals), 'occ', axis=0...]
    all_to_all x2, waiting for transfers between devices: 48.7 us -> 29 us  [body(): lax.all_to_all(packed.reshape(tile_total * vir_count, PIECE_ROWS, cut * b...]
    pallas_call x3 -> x5, Pallas kernels: 57.7 us -> 65.6 us  [the longest x2 41.9 us: ladder_call(): pl.pallas_call(functools.partial(ladder_kernel, piece, vir_count), grid=(...]
    reshape x0 -> x4, local copies, waits for them, and re-layouts: none -> 5.78 us  [the longest x2 4.49 us: body(): all_codes.reshape(tile_total, vir_count, tile_total, cut, vir_count, block)]
  transfers between devices with their start and end apart: 4 -> 5, of which waited for: 3 -> 4; matrix products, arithmetic and copies ran while one was open for 3% -> 5% of each run, Pallas kernels for 18% -> 12%
where the time goes in v2:
time: 274 us
  waiting for transfers between devices  174 us (64%)
  Pallas kernels  65.6 us (24%)
  between operations  13.2 us (5%)
  local copies, waits for them, and re-layouts  9.46 us (3%)
  starting transfers between devices  7.71 us (3%)
  other arithmetic  3.64 us (1%)
    all_gather x1, waiting for transfers between devices, body(): lax.all_gather(screen_call(vir_count, int_mask, integrals), 'occ', axis=0...  81.8 us
    all_gather x2, waiting for transfers between devices, body(): all_codes = lax.all_gather(code, ('occ', 'vir'), axis=0, tiled=False)  61.6 us
    pallas_call x2, Pallas kernels, ladder_call(): pl.pallas_call(functools.partial(ladder_kernel, piece, vir_count), grid=(...  41.9 us
    all_to_all x2, waiting for transfers between devices, body(): lax.all_to_all(packed.reshape(tile_total * vir_count, PIECE_ROWS, cut * b...  29 us
    pallas_call x2, Pallas kernels, update_call(): pl.pallas_call(functools.partial(update_kernel, vir_count), grid=(tile_to...  21.4 us
    all_to_all x2, starting transfers between devices, body(): lax.all_to_all(packed.reshape(tile_total * vir_count, PIECE_ROWS, cut * b...  7.62 us
  transfers between devices with their start and end apart: 5, of which 4 were waited for; matrix products, arithmetic and copies ran while one was open for 5% of the time, Pallas kernels for 12%

profile of v2, /device:TPU:0, one launch (start us, length us, event | category | flops | bytes accessed | tf_op | source)
XLA Modules:
  0.0 273.5 jit_solution(14022663111130207343)
XLA Ops:
  6.5 0.0 all-gather.6.cloned.1.call-start
  6.5 2.3 screen.1
  8.8 0.0 all-gather.6.cloned.1.call-update
  8.9 1.3 copy.13.amp_mask
  10.2 0.8 fusion.2.swap_ref
  11.0 0.9 fusion.1.perm_ref
  11.9 81.8 %all-gather.6.cloned.1.call-done.slab_ref = bf16[4096,1024]{1,0:T(8,128)(2,1)} async-done(((bf16[512,1024]{1,0:T(8,128)(2,1)}), bf16[4096,1024]{1,0:T(8,128)(2,1)}) %all-gather.6.cloned.1.call-update) | async-done | bytes 8388624 | tf_op jit(solution)/shard_map/all_gather | solution.py:206
  93.8 20.9 %ladder.3 = (f32[8,128,1024]{2,1,0:T(8,128)}, s16[8,4,128,256]{3,2,1,0:T(8,128)(2,1)}, f32[4,2,1024]{2,1,0:T(2,128)}) custom-call(s32[8,4]{1,0:T(8,128)} %copy.13.amp_mask, s32[8]{0:T(128)} %numbers.3, bf16[8,2,128,4096]{3,2,1,0:T(8,128)(2,1)} %bitcast.27, bf16[4096,1024]{1,0:T(8,128)(2,1)} %all-gather.6.cloned.1.call-done.slab_ref, ...), custom_call_target="tpu_custom_call" | custom-call | flops 11811160064 | bytes 31457280 | tf_op jit(solution)/shard_map/ladder/pallas_call | solution.py:116
  114.7 3.1 %all-to-all-start.1 = ((s16[32,128,256]{2,1,0:T(8,128)(2,1)}), s16[32,128,256]{2,1,0:T(8,128)(2,1)S(1)}, u32[]{:S(2)}, u32[]{:S(2)}) async-start(s16[32,128,256]{2,1,0:T(8,128)(2,1)} %bitcast.23), calls=%async_computation.1 | async-start | bytes 4194304 | tf_op jit(solution)/shard_map/all_to_all | solution.py:238
  117.8 0.0 all-gather.10.cloned.1.call-start
  117.9 0.7 all-gather.10.cloned.1.call-update
  118.6 21.0 %ladder.2 = (f32[8,128,1024]{2,1,0:T(8,128)}, s16[8,4,128,256]{3,2,1,0:T(8,128)(2,1)}, f32[4,2,1024]{2,1,0:T(2,128)}) custom-call(s32[8,4]{1,0:T(8,128)} %copy.13.amp_mask, s32[8]{0:T(128)} %numbers.3, bf16[8,2,128,4096]{3,2,1,0:T(8,128)(2,1)} %bitcast.28, bf16[4096,1024]{1,0:T(8,128)(2,1)} %all-gather.6.cloned.1.call-done.slab_ref, ...), custom_call_target="tpu_custom_call" | custom-call | flops 11811160064 | bytes 31457280 | tf_op jit(solution)/shard_map/ladder/pallas_call | solution.py:116
  139.6 0.0 copy-start.1
  139.6 0.0 copy-start.2
  139.6 29.0 %all-to-all-done.1 = s16[32,128,256]{2,1,0:T(8,128)(2,1)S(1)} async-done(((s16[32,128,256]{2,1,0:T(8,128)(2,1)}), s16[32,128,256]{2,1,0:T(8,128)(2,1)S(1)}, u32[]{:S(2)}, u32[]{:S(2)}) %all-to-all-start.1) | async-done | bytes 2097184 | tf_op jit(solution)/shard_map/all_to_all | solution.py:238
  168.7 0.0 copy-start
  168.7 4.5 %all-to-all-start = ((s16[32,128,256]{2,1,0:T(8,128)(2,1)}), s16[32,128,256]{2,1,0:T(8,128)(2,1)}, u32[]{:S(2)}, u32[]{:S(2)}) async-start(s16[32,128,256]{2,1,0:T(8,128)(2,1)} %bitcast.22), calls=%async_computation | async-start | bytes 4194304 | tf_op jit(solution)/shard_map/all_to_all | solution.py:238
  173.2 0.0 all-gather.8.cloned.1.call-start
  173.2 0.7 all-gather.8.cloned.1.call-update
  173.9 0.0 copy-done.1
  173.9 0.1 reshape.240
  174.0 0.1 add.247
  174.1 0.0 copy-done.2
  174.1 0.1 dynamic_slice.13
  174.2 0.1 broadcast_add_fusion.1
  174.3 0.7 add.244.vir_ref
  175.0 0.1 broadcast_add_fusion
  175.1 1.7 fusion.spread_ref
  176.8 4.1 %all-gather.10.cloned.1.call-done = f32[128,2,1024]{2,1,0:T(2,128)} async-done(((f32[4,2,1024]{2,1,0:T(2,128)}), f32[128,2,1024]{2,1,0:T(2,128)}) %all-gather.10.cloned.1.call-update) | async-done | bytes 1048592 | tf_op jit(solution)/shard_map/all_gather | solution.py:242
  180.9 2.2 reshape.245
  183.1 0.0 copy-done
  183.1 57.5 %all-gather.8.cloned.1.call-done = f32[128,2,1024]{2,1,0:T(2,128)} async-done(((f32[4,2,1024]{2,1,0:T(2,128)}), f32[128,2,1024]{2,1,0:T(2,128)}) %all-gather.8.cloned.1.call-update) | async-done | bytes 1048592 | tf_op jit(solution)/shard_map/all_gather | solution.py:242
  240.6 2.2 reshape.238
  242.9 0.1 constant_dynamic-slice_fusion
  243.0 0.6 reshape.246.code_ref
  243.6 0.6 reshape.239.code_ref
  244.3 1.3 broadcast_in_dim.2.occ_ref
  245.6 10.7 %update.2.refs_2_ = f32[8,16,2,8,1024]{4,3,2,1,0:T(8,128)} custom-call(f32[8,4,256]{2,1,0:T(4,128)} %reshape.246.code_ref, f32[1,1024]{1,0:T(1,128)} %add.244.vir_ref, f32[8,16,2,8,128]{4,3,2,1,0:T(8,128)} %broadcast_in_dim.2.occ_ref, bf16[1024,1024]{1,0:T(8,128)(2,1)} %fusion.spread_ref, s16[8,4,128,256]{3,2,1,0:T(8,128)(2,1)} %bitcast.21, ...), custom_call_target="tpu_custom_call" | custom-call | flops 4294967296 | bytes 10485760 | tf_op jit(solution)/shard_map/update/pallas_call | solution.py:179
  256.3 0.0 all-to-all-done
  256.3 10.7 %update.3 = f32[8,16,2,8,1024]{4,3,2,1,0:T(8,128)} custom-call(f32[8,4,256]{2,1,0:T(4,128)} %reshape.239.code_ref, f32[1,1024]{1,0:T(1,128)} %add.244.vir_ref, f32[8,16,2,8,128]{4,3,2,1,0:T(8,128)} %broadcast_in_dim.2.occ_ref, bf16[1024,1024]{1,0:T(8,128)(2,1)} %fusion.spread_ref, ...), custom_call_target="tpu_custom_call", output_to_operand_aliasing={{}: (7, {})} | custom-call | flops 4294967296 | bytes 10485760 | tf_op jit(solution)/shard_map/update/pallas_call | solution.py:179
  (4 shorter events, 0.0 us)
Async XLA Ops:
  6.5 87.3 %all-gather.6.cloned.1.call-start = ((), (), s32[]{:S(2)}) async-start(), calls=%async_computation.2 | async-start | bytes 9437184 | tf_op jit(solution)/shard_map/all_gather | solution.py:206
  114.7 53.9 %all-to-all-start.1 = ((s16[32,128,256]{2,1,0:T(8,128)(2,1)}), s16[32,128,256]{2,1,0:T(8,128)(2,1)S(1)}, u32[]{:S(2)}, u32[]{:S(2)}) async-start(s16[32,128,256]{2,1,0:T(8,128)(2,1)} %bitcast.23), calls=%async_computation.1 | async-start | bytes 4194304 | tf_op jit(solution)/shard_map/all_to_all | solution.py:238
  117.8 63.0 %all-gather.10.cloned.1.call-start = ((), (), s32[]{:S(2)}) async-start(), calls=%async_computation.4 | async-start | bytes 1081344 | tf_op jit(solution)/shard_map/all_gather | solution.py:242
  139.6 34.3 %copy-start.1 = (f32[128]{0:T(128)S(1)}, f32[128]{0:T(128)}, u32[]{:S(2)}) copy-start(f32[128]{0:T(128)} %param.12) | copy-start | bytes 1540
  139.6 34.5 %copy-start.2 = (f32[64]{0:T(128)S(1)}, f32[64]{0:T(128)}, u32[]{:S(2)}) copy-start(f32[64]{0:T(128)} %param.13) | copy-start | bytes 772
  168.7 14.5 %copy-start = (s16[32,128,256]{2,1,0:T(8,128)(2,1)}, s16[32,128,256]{2,1,0:T(8,128)(2,1)S(1)}, u32[]{:S(2)}) copy-start(s16[32,128,256]{2,1,0:T(8,128)(2,1)S(1)} %all-to-all-done.1) | copy-start | bytes 6291460
  168.7 87.6 %all-to-all-start = ((s16[32,128,256]{2,1,0:T(8,128)(2,1)}), s16[32,128,256]{2,1,0:T(8,128)(2,1)}, u32[]{:S(2)}, u32[]{:S(2)}) async-start(s16[32,128,256]{2,1,0:T(8,128)(2,1)} %bitcast.22), calls=%async_computation | async-start | bytes 4194304 | tf_op jit(solution)/shard_map/all_to_all | solution.py:238
  173.2 67.5 %all-gather.8.cloned.1.call-start = ((), (), s32[]{:S(2)}) async-start(), calls=%async_computation.3 | async-start | bytes 1081344 | tf_op jit(solution)/shard_map/all_gather | solution.py:242
Sparse Core Ops, SparseCore 0:
  9.0 84.7 all-gather.5
  121.7 59.1 all-gather.9
  183.9 56.7 all-gather.7

commit v3 on v2

v3 whole, which is shorter than its diff:
```python
import functools

import jax
import jax.numpy as jnp
from jax import lax
from jax.experimental import pallas as pl
from jax.experimental.pallas import tpu as pltpu
from jax.sharding import PartitionSpec as P

VT = 32
NVT = 2
W = 64
ORBITALS_IN_GRP = 16
PAIR_SQ = ORBITALS_IN_GRP * ORBITALS_IN_GRP
CODE_ROWS = 16
AT_ONCE = 2
TOP = 32700.0
STEPS = 8.0
VMEM_LIMIT = 56 * 1024 * 1024


def one_hot_of(target, amount):
    return (target[:, None] == jnp.arange(amount)[None, :]).astype(jnp.bfloat16)


def split(values):
    high = values.astype(jnp.bfloat16)
    return high, (values - high.astype(jnp.float32)).astype(jnp.bfloat16)


def dot(left, right):
    return jnp.dot(left, right, preferred_element_type=jnp.float32)


def scale_of(code):
    return jnp.exp2(code * (1.0 / STEPS))


def screen_kernel(int_mask, slab_ref, screened_ref):
    slab_rows, slab_cols = slab_ref.shape
    row_label = lax.axis_index("occ") * slab_rows // W // VT * NVT
    col_label = lax.axis_index("vir") * slab_cols // W // VT * NVT
    right = lax.broadcasted_iota(jnp.int32, (VT, slab_cols), 1) % W >= VT
    keep = []
    for d_tile in range(NVT):
        label = row_label + d_tile
        kept = jnp.where(right, int_mask[label, col_label + 1], int_mask[label, col_label])
        keep.append(kept.astype(jnp.float32).astype(jnp.bfloat16))
    for at in range(0, slab_rows, VT):
        screened_ref[at : at + VT, :] = slab_ref[at : at + VT, :] * keep[at // VT % NVT]


def screen_call(int_mask, integrals):
    return pl.pallas_call(
        screen_kernel,
        in_specs=[pl.BlockSpec(memory_space=pltpu.SMEM), pl.BlockSpec(memory_space=pltpu.VMEM)],
        out_specs=pl.BlockSpec(memory_space=pltpu.VMEM),
        out_shape=jax.ShapeDtypeStruct(integrals.shape, integrals.dtype),
        name="screen",
    )(int_mask, integrals)


def ladder_kernel(distances, vir_count, cut, own, amp_mask, numbers, *refs):
    count = len(distances)
    rows_refs, (slab_ref, swap_ref, perm_ref, ladder_ref), packed_refs = (
        refs[:count], refs[count : count + 4], refs[count + 4 :]
    )
    part = pl.program_id(0)
    cols = slab_ref.shape[1]
    block = cols // vir_count
    lane = lax.broadcasted_iota(jnp.int32, (1, W * W), 1)
    low = lane < W * VT
    left = lane % W < VT
    pair = lax.broadcasted_iota(jnp.int32, (PAIR_SQ, 1), 0)
    screened = []
    for n in range(count):
        tile = own[0] ^ distances[n]
        keep = jnp.where(
            low,
            jnp.where(left, amp_mask[tile, 0], amp_mask[tile, 1]),
            jnp.where(left, amp_mask[tile, 2], amp_mask[tile, 3]),
        )
        screened.append(rows_refs[n][...] * keep.astype(jnp.float32).astype(jnp.bfloat16))
    product = dot(jnp.concatenate(screened, axis=0), slab_ref[...])
    code_row = lax.broadcasted_iota(jnp.int32, (CODE_ROWS, block), 0) == part
    for n in range(count):
        tile = own[0] ^ distances[n]
        nonzero = (pair // ORBITALS_IN_GRP < numbers[own[0]]) & (pair % ORBITALS_IN_GRP < numbers[tile])
        ladder = jnp.where(nonzero, product[n * PAIR_SQ : (n + 1) * PAIR_SQ], 0.0)
        ladder_ref[n] = ladder
        high, low_part = split(ladder)
        mirror = dot(dot(swap_ref[...], high).astype(jnp.bfloat16), perm_ref[...]) + dot(
            dot(swap_ref[...], low_part).astype(jnp.bfloat16), perm_ref[...]
        )
        most = jnp.maximum(jnp.max(jnp.abs(mirror), axis=0, keepdims=True), 1e-30)
        code = jnp.ceil(jnp.log2(most) * STEPS)
        coded = jnp.round(mirror * (TOP / scale_of(code))).astype(jnp.int32).astype(jnp.int16)
        code_int = code.astype(jnp.int32)
        for v in range(vir_count):
            at = slice(v * block, (v + 1) * block)
            packed = packed_refs[n * vir_count + v]
            packed[pl.ds(pl.multiple_of(part * PAIR_SQ, PAIR_SQ), PAIR_SQ), :] = coded[:, at]
            before = packed[cut * PAIR_SQ :, :].astype(jnp.int32)
            packed[cut * PAIR_SQ :, :] = jnp.where(
                code_row, jnp.broadcast_to(code_int[:, at], (CODE_ROWS, block)), before
            ).astype(jnp.int16)


def ladder_call(distances, vir_count, cut, own, amp_mask, numbers, amplitudes, slab, swap, perm):
    slab_cols = slab.shape[1]
    chunk = slab_cols // cut
    block = chunk // vir_count
    count = len(distances)
    smem = pl.BlockSpec(memory_space=pltpu.SMEM)
    whole = lambda c, own: (0, 0)
    rows = count * PAIR_SQ
    packed_shape = (cut * PAIR_SQ + CODE_ROWS, block)
    flops = 2 * rows * slab_cols * (W * W + 2 * PAIR_SQ + 2 * chunk)
    bytes_accessed = rows * (W * W * 2 + slab_cols * 6) + W * W * slab_cols * 2
    return pl.pallas_call(
        functools.partial(ladder_kernel, distances, vir_count, cut),
        grid_spec=pltpu.PrefetchScalarGridSpec(
            num_scalar_prefetch=1,
            grid=(cut,),
            in_specs=[smem, smem]
            + [pl.BlockSpec((PAIR_SQ, W * W), lambda c, own, d=d: (own[0] ^ d, 0)) for d in distances]
            + [
                pl.BlockSpec((W * W, chunk), lambda c, own: (0, c)),
                pl.BlockSpec(swap.shape, whole),
                pl.BlockSpec(perm.shape, whole),
            ],
            out_specs=[pl.BlockSpec((count, PAIR_SQ, chunk), lambda c, own: (0, 0, c))]
            + [pl.BlockSpec(packed_shape, whole)] * (count * vir_count),
        ),
        out_shape=[jax.ShapeDtypeStruct((count, PAIR_SQ, slab_cols), jnp.float32)]
        + [jax.ShapeDtypeStruct(packed_shape, jnp.int16)] * (count * vir_count),
        compiler_params=pltpu.CompilerParams(vmem_limit_bytes=VMEM_LIMIT),
        cost_estimate=pl.CostEstimate(flops=flops, bytes_accessed=bytes_accessed, transcendentals=0),
        name="ladder",
    )(own, amp_mask, numbers, *[amplitudes] * count, slab, swap, perm)


def update_kernel(vir_count, cut, own, vir_ref, occ_ref, spread_ref, ladder_ref, *refs):
    arrived, update_ref = refs[:vir_count], refs[-1]
    highs, lows = [], []
    for ref in arrived:
        codes = ref[cut * PAIR_SQ :, :].astype(jnp.int32).astype(jnp.float32)
        for c in range(cut):
            values = ref[c * PAIR_SQ : (c + 1) * PAIR_SQ, :].astype(jnp.int32).astype(jnp.float32)
            high, low = split(values * (scale_of(codes[c : c + 1]) * (1.0 / TOP)))
            highs.append(high)
            lows.append(low)
    mirror = dot(jnp.concatenate(highs, axis=1), spread_ref[...]) + dot(
        jnp.concatenate(lows, axis=1), spread_ref[...]
    )
    update_ref[...] = (ladder_ref[0] + mirror) / (vir_ref[...] - occ_ref[:, :1])


def update_call(tile_total, distance, n, cut, own, vir_sum, occ_sum, spread, ladder, arrived, earlier):
    slab_cols = spread.shape[1]
    args = [vir_sum, occ_sum, spread, ladder, *arrived]
    in_specs = [
        pl.BlockSpec((1, slab_cols), lambda g, own: (0, 0)),
        pl.BlockSpec((PAIR_SQ, 128), lambda g, own: (own[0] ^ distance, 0)),
        pl.BlockSpec(spread.shape, lambda g, own: (0, 0)),
        pl.BlockSpec((1, PAIR_SQ, slab_cols), lambda g, own: (n, 0, 0)),
    ] + [pl.BlockSpec(arrived[0].shape, lambda g, own: (0, 0))] * len(arrived)
    aliases = {}
    if earlier is not None:
        aliases = {len(args) + 1: 0}
        args.append(earlier)
        in_specs.append(pl.BlockSpec(memory_space=pl.ANY))
    return pl.pallas_call(
        functools.partial(update_kernel, len(arrived), cut),
        grid_spec=pltpu.PrefetchScalarGridSpec(
            num_scalar_prefetch=1,
            grid=(1,),
            in_specs=in_specs,
            out_specs=pl.BlockSpec((PAIR_SQ, slab_cols), lambda g, own: (own[0] ^ distance, 0)),
        ),
        out_shape=jax.ShapeDtypeStruct((tile_total * PAIR_SQ, slab_cols), jnp.float32),
        input_output_aliases=aliases,
        compiler_params=pltpu.CompilerParams(vmem_limit_bytes=VMEM_LIMIT),
        cost_estimate=pl.CostEstimate(
            flops=4 * PAIR_SQ * slab_cols * slab_cols, bytes_accessed=PAIR_SQ * slab_cols * 10, transcendentals=0
        ),
        name="update",
    )(own, *args)


def body(amplitudes, amp_mask, integrals, int_mask, group_orbital_numbers, occ_energy, vir_energy):
    tile_total = lax.axis_size("occ")
    vir_count = lax.axis_size("vir")
    row_tile = lax.axis_index("occ")
    vir_place = lax.axis_index("vir")
    vir_span = W // vir_count
    slab_cols = vir_span * W
    cut = 2 if vir_span >= 16 else 1
    chunk = slab_cols // cut
    chunk_span = vir_span // cut
    block = chunk // vir_count

    slab = lax.all_gather(screen_call(int_mask, integrals), "occ", axis=0, tiled=True)

    own = row_tile.astype(jnp.int32).reshape(1)
    rows = jnp.arange(PAIR_SQ)
    swap = one_hot_of(rows % ORBITALS_IN_GRP * ORBITALS_IN_GRP + rows // ORBITALS_IN_GRP, PAIR_SQ)
    col = jnp.arange(chunk)
    a, b = col // W, col % W
    perm = one_hot_of((b // vir_span ^ vir_place) * block + b % vir_span * chunk_span + a, chunk)
    place = jnp.arange(slab_cols)
    sender, part = place // (cut * block) ^ vir_place, place // block % cut
    here, there = place % block // chunk_span, place % chunk_span
    spread = one_hot_of(here * W + sender * vir_span + part * chunk_span + there, slab_cols)

    occ_table = occ_energy.reshape(tile_total, ORBITALS_IN_GRP)
    own_energy = lax.dynamic_slice_in_dim(occ_table, row_tile, 1, 0)[0]
    occ_sum = jnp.broadcast_to(
        (own_energy[None, :, None] + occ_table[:, None, :]).reshape(-1, 1), (tile_total * PAIR_SQ, 128)
    )
    vir_own = lax.dynamic_slice_in_dim(vir_energy, vir_place * vir_span, vir_span, 0)
    vir_sum = (vir_own[:, None] + vir_energy[None, :]).reshape(1, -1)

    devices = tile_total * vir_count
    first = tile_total // 2
    order = list(range(first, tile_total)) + list(range(2, first)) + [0, 1]
    parts = []
    for at in range(0, tile_total, AT_ONCE):
        distances = order[at : at + AT_ONCE]
        ladder, *packed = ladder_call(
            distances, vir_count, cut, own, amp_mask[0], group_orbital_numbers, amplitudes, slab, swap, perm
        )
        for n, distance in enumerate(distances):
            arrived = []
            for v in range(vir_count):
                shift = distance * vir_count + v
                block_sent = packed[n * vir_count + v]
                if shift > 0:
                    block_sent = lax.ppermute(block_sent, ("occ", "vir"), [(s, s ^ shift) for s in range(devices)])
                arrived.append(block_sent)
            parts.append((distance, n, ladder, arrived))
    update = None
    for distance, n, ladder, arrived in parts[first:] + parts[:first]:
        update = update_call(
            tile_total, distance, n, cut, own, vir_sum, occ_sum, spread, ladder, arrived, update
        )
    return update


def solution(mesh):
    in_specs = (P("occ", None), P("occ", None, None), P("occ", "vir"), P(), P(), P(), P())
    out_specs = P("occ", "vir")
    return jax.shard_map(body, mesh=mesh, in_specs=in_specs, out_specs=out_specs, check_vma=False)
```

time: 274 us -> 264 us (0.964)
  the two profiles are of different devices: /device:TPU:0 before, /device:TPU:9 now
where the time goes in v3:
time: 264 us; the launch traced here: 263 us
  waiting for transfers between devices  109 us (41%)
  Pallas kernels  82.5 us (31%)
  starting transfers between devices  47.7 us (18%)
  between operations  13.8 us (5%)
  local copies, waits for them, and re-layouts  6.37 us (2%)
  other arithmetic  4.25 us (2%)
    all_gather x1, waiting for transfers between devices, body(): lax.all_gather(screen_call(int_mask, integrals), 'occ', axis=0, tiled=True)  73.5 us
    ppermute x31, starting transfers between devices, body(): lax.ppermute(block_sent, ('occ', 'vir'), [(s, s ^ shift) for s in range(d...  47.7 us
    pallas_call x4, Pallas kernels, ladder_call(): pl.pallas_call(functools.partial(ladder_kernel, distances, vir_count, cut...  45.8 us
    ppermute x31, waiting for transfers between devices, body(): lax.ppermute(block_sent, ('occ', 'vir'), [(s, s ^ shift) for s in range(d...  35.1 us
    pallas_call x8, Pallas kernels, update_call(): pl.pallas_call(functools.partial(update_kernel, len(arrived), cut), grid_...  34.4 us
  transfers between devices with their start and end apart: 32, of which 10 were waited for; matrix products, arithmetic and copies ran while one was open for 3% of the time, Pallas kernels for 25%

profile of v3, /device:TPU:9, one launch (start us, length us, event | category | flops | bytes accessed | tf_op | source)
XLA Modules:
  0.0 263.3 jit_solution(7957159393632004272)
XLA Ops:
  6.5 2.3 screen.1
  8.9 1.3 copy.15.amp_mask
  10.2 0.7 reshape.190
  11.0 0.7 dynamic_slice.6
  11.7 0.7 broadcast_add_fusion.1
  12.4 0.7 add.195.vir_ref
  13.1 0.8 fusion.2.refs_3_
  13.9 0.9 fusion.1.refs_4_
  14.8 1.7 fusion.spread_ref
  16.6 73.5 %all-gather.2.cloned.1.call-done.refs_2_ = bf16[4096,1024]{1,0:T(8,128)(2,1)} async-done(((bf16[512,1024]{1,0:T(8,128)(2,1)}), bf16[4096,1024]{1,0:T(8,128)(2,1)}) %all-gather.2.cloned.1.call-update) | async-done | bytes 8388624 | tf_op jit(solution)/shard_map/all_gather | solution.py:203
  90.0 11.4 %ladder.7 = (f32[2,256,1024]{2,1,0:T(8,128)}, s16[528,128]{1,0:T(8,128)(2,1)}, s16[528,128]{1,0:T(8,128)(2,1)}, s16[528,128]{1,0:T(8,128)(2,1)}, s16[528,128]{1,...) custom-call(s32[1]{0:T(128)} %bitcast.own, ...), custom_call_target="tpu_custom_call" | custom-call | flops 5905580032 | bytes 15728640 | tf_op jit(solution)/shard_map/ladder/pallas_call | solution.py:120
  101.4 3.1 %collective-permute-start.23 = (s16[528,128]{1,0:T(8,128)(2,1)}, s16[528,128]{1,0:T(8,128)(2,1)S(1)}, u32[]{:S(2)}, u32[]{:S(2)}) collective-permute-start(s16[528,128]{1,0:T(8,128)(2,1)} %get-tuple-element.69), channel_id=1, source_target_pairs={{0,12},{1,13},{2,14},{3,15},{4,8},{5,9},{6,10},{7,11},{8,4},{9,5},... | collective-permute-start | bytes 405512 | tf_op jit(solution)/shard_map/ppermute | solution.py:239
  104.6 0.1 broadcast_add_fusion
  104.6 0.1 add.201
  104.7 1.0 collective-permute-start.24
  105.7 2.6 %collective-permute-start.25 = (s16[528,128]{1,0:T(8,128)(2,1)}, s16[528,128]{1,0:T(8,128)(2,1)S(1)}, u32[]{:S(2)}, u32[]{:S(2)}) collective-permute-start(s16[528,128]{1,0:T(8,128)(2,1)} %get-tuple-element.71), channel_id=1, source_target_pairs={{0,14},{1,15},{2,12},{3,13},{4,10},{5,11},{6,8},{7,9},{8,6},{9,7},... | collective-permute-start | bytes 405512 | tf_op jit(solution)/shard_map/ppermute | solution.py:239
  108.4 1.5 collective-permute-start.27
  109.9 1.8 collective-permute-start.28
  111.7 11.5 %ladder.6 = (f32[2,256,1024]{2,1,0:T(8,128)}, s16[528,128]{1,0:T(8,128)(2,1)}, s16[528,128]{1,0:T(8,128)(2,1)}, s16[528,128]{1,0:T(8,128)(2,1)}, s16[528,128]{1,...) custom-call(s32[1]{0:T(128)} %bitcast.own, ...), custom_call_target="tpu_custom_call" | custom-call | flops 5905580032 | bytes 15728640 | tf_op jit(solution)/shard_map/ladder/pallas_call | solution.py:120
  123.3 1.7 collective-permute-start.29
  124.9 0.5 collective-permute-start.30
  125.4 0.9 collective-permute-start.16
  126.3 1.1 collective-permute-start.17
  127.5 1.6 collective-permute-start.18
  129.1 11.4 %ladder.5 = (f32[2,256,1024]{2,1,0:T(8,128)}, s16[528,128]{1,0:T(8,128)(2,1)}, s16[528,128]{1,0:T(8,128)(2,1)}, s16[528,128]{1,0:T(8,128)(2,1)}, s16[528,128]{1,...) custom-call(s32[1]{0:T(128)} %bitcast.own, ...), custom_call_target="tpu_custom_call" | custom-call | flops 5905580032 | bytes 15728640 | tf_op jit(solution)/shard_map/ladder/pallas_call | solution.py:120
  140.6 0.3 collective-permute-start.19
  140.9 1.2 collective-permute-start.20
  142.2 1.2 collective-permute-start.21
  143.4 0.4 collective-permute-start.22
  143.8 1.8 collective-permute-start.8
  145.6 11.4 %ladder.4 = (f32[2,256,1024]{2,1,0:T(8,128)}, s16[528,128]{1,0:T(8,128)(2,1)}, s16[528,128]{1,0:T(8,128)(2,1)}, s16[528,128]{1,0:T(8,128)(2,1)}, s16[528,128]{1,...) custom-call(s32[1]{0:T(128)} %bitcast.own, ...), custom_call_target="tpu_custom_call" | custom-call | flops 5905580032 | bytes 15728640 | tf_op jit(solution)/shard_map/ladder/pallas_call | solution.py:120
  157.1 1.8 collective-permute-start.9
  158.9 1.3 broadcast_in_dim.2.occ_ref
  160.2 4.3 %update.8.refs_4_ = f32[2048,1024]{1,0:T(8,128)} custom-call(s32[1]{0:T(128)} %bitcast.own, f32[1,1024]{1,0:T(1,128)} %add.195.vir_ref, f32[2048,128]{1,0:T(8,128)} %broadcast_in_dim.2.occ_ref, bf16[1024,1024]{1,0:T(8,128)(2,1)} %fusion.spread_ref, f32[2,256,1024]{2,1,0:T(8,128)} %get-tuple-element.68.ladder_ref, s16[528,128]{1,0:T(8,128)(2,1)} %copy-done.11, ...), custom_call_target="tpu_custom_call" | custom-call | flops 1073741824 | bytes 2621440 | tf_op jit(solution)/shard_map/update/pallas_call | solution.py:173
  164.5 3.0 %collective-permute-start.10 = (s16[528,128]{1,0:T(8,128)(2,1)S(1)}, s16[528,128]{1,0:T(8,128)(2,1)S(1)}, u32[]{:S(2)}, u32[]{:S(2)}) collective-permute-start(s16[528,128]{1,0:T(8,128)(2,1)S(1)} %copy-done.46), channel_id=1, source_target_pairs={{0,22},{1,23},{2,20},{3,21},{4,18},{5,19},{6,16},{7,17},{8,30},{9,... | collective-permute-start | bytes 405512 | tf_op jit(solution)/shard_map/ppermute | solution.py:239
  167.5 1.6 collective-permute-start.12
  169.1 0.9 collective-permute-start.13
  170.0 1.6 collective-permute-start.14
  171.6 4.3 %update.9.refs_4_ = f32[2048,1024]{1,0:T(8,128)} custom-call(s32[1]{0:T(128)} %bitcast.own, f32[1,1024]{1,0:T(1,128)} %add.195.vir_ref, f32[2048,128]{1,0:T(8,128)} %broadcast_in_dim.2.occ_ref, bf16[1024,1024]{1,0:T(8,128)(2,1)} %fusion.spread_ref, f32[2,256,1024]{2,1,0:T(8,128)} %get-tuple-element.68.ladder_ref, ...), custom_call_target="tpu_custom_call", output_to_operand_aliasing={{}: (9, {})} | custom-call | flops 1073741824 | bytes 2621440 | tf_op jit(solution)/shard_map/update/pallas_call | solution.py:173
  176.0 2.7 %collective-permute-start.15 = (s16[528,128]{1,0:T(8,128)(2,1)S(1)}, s16[528,128]{1,0:T(8,128)(2,1)S(1)}, u32[]{:S(2)}, u32[]{:S(2)}) collective-permute-start(s16[528,128]{1,0:T(8,128)(2,1)S(1)} %copy-done.37), channel_id=1, source_target_pairs={{0,19},{1,18},{2,17},{3,16},{4,23},{5,22},{6,21},{7,20},{8,27},{9,... | collective-permute-start | bytes 405512 | tf_op jit(solution)/shard_map/ppermute | solution.py:239
  178.6 4.3 %update.10.refs_4_ = f32[2048,1024]{1,0:T(8,128)} custom-call(s32[1]{0:T(128)} %bitcast.own, f32[1,1024]{1,0:T(1,128)} %add.195.vir_ref, f32[2048,128]{1,0:T(8,128)} %broadcast_in_dim.2.occ_ref, bf16[1024,1024]{1,0:T(8,128)(2,1)} %fusion.spread_ref, f32[2,256,1024]{2,1,0:T(8,128)} %get-tuple-element.59.ladder_ref, ...), custom_call_target="tpu_custom_call", output_to_operand_aliasing={{}: (9, {})} | custom-call | flops 1073741824 | bytes 2621440 | tf_op jit(solution)/shard_map/update/pallas_call | solution.py:173
  183.0 2.3 collective-permute-done.10.refs_2_
  185.3 4.3 %collective-permute-start.11 = (s16[528,128]{1,0:T(8,128)(2,1)S(1)}, s16[528,128]{1,0:T(8,128)(2,1)S(1)}, u32[]{:S(2)}, u32[]{:S(2)}) collective-permute-start(s16[528,128]{1,0:T(8,128)(2,1)S(1)} %copy-done.35), channel_id=1, source_target_pairs={{0,23},{1,22},{2,21},{3,20},{4,19},{5,18},{6,17},{7,16},{8,31},{9,... | collective-permute-start | bytes 405512 | tf_op jit(solution)/shard_map/ppermute | solution.py:239
  189.6 2.6 collective-permute-start.4
  192.2 1.8 collective-permute-done.13.refs_1_
  194.0 1.1 collective-permute-start.5
  195.1 4.5 %collective-permute-done.14.refs_2_ = s16[528,128]{1,0:T(8,128)(2,1)S(1)} collective-permute-done((s16[528,128]{1,0:T(8,128)(2,1)S(1)}, s16[528,128]{1,0:T(8,128)(2,1)S(1)}, u32[]{:S(2)}, u32[]{:S(2)}) %collective-permute-start.14) | collective-permute-done | bytes 135200 | tf_op jit(solution)/shard_map/ppermute | solution.py:239
  199.6 1.2 collective-permute-start.6
  200.8 4.3 %update.11.refs_4_ = f32[2048,1024]{1,0:T(8,128)} custom-call(s32[1]{0:T(128)} %bitcast.own, f32[1,1024]{1,0:T(1,128)} %add.195.vir_ref, f32[2048,128]{1,0:T(8,128)} %broadcast_in_dim.2.occ_ref, bf16[1024,1024]{1,0:T(8,128)(2,1)} %fusion.spread_ref, f32[2,256,1024]{2,1,0:T(8,128)} %get-tuple-element.59.ladder_ref, ...), custom_call_target="tpu_custom_call", output_to_operand_aliasing={{}: (9, {})} | custom-call | flops 1073741824 | bytes 2621440 | tf_op jit(solution)/shard_map/update/pallas_call | solution.py:173
  205.2 0.4 collective-permute-done.15.refs_3_
  205.5 3.8 %collective-permute-start.7 = (s16[528,128]{1,0:T(8,128)(2,1)S(1)}, s16[528,128]{1,0:T(8,128)(2,1)S(1)}, u32[]{:S(2)}, u32[]{:S(2)}) collective-permute-start(s16[528,128]{1,0:T(8,128)(2,1)S(1)} %copy-done.36), channel_id=1, source_target_pairs={{0,27},{1,26},{2,25},{3,24},{4,31},{5,30},{6,29},{7,28},{8,19},{9,... | collective-permute-start | bytes 405512 | tf_op jit(solution)/shard_map/ppermute | solution.py:239
  209.3 4.3 %update.12.refs_4_ = f32[2048,1024]{1,0:T(8,128)} custom-call(s32[1]{0:T(128)} %bitcast.own, f32[1,1024]{1,0:T(1,128)} %add.195.vir_ref, f32[2048,128]{1,0:T(8,128)} %broadcast_in_dim.2.occ_ref, bf16[1024,1024]{1,0:T(8,128)(2,1)} %fusion.spread_ref, f32[2,256,1024]{2,1,0:T(8,128)} %get-tuple-element.50.ladder_ref, ...), custom_call_target="tpu_custom_call", output_to_operand_aliasing={{}: (9, {})} | custom-call | flops 1073741824 | bytes 2621440 | tf_op jit(solution)/shard_map/update/pallas_call | solution.py:173
  213.8 5.1 %collective-permute-done.4.refs_0_ = s16[528,128]{1,0:T(8,128)(2,1)S(1)} collective-permute-done((s16[528,128]{1,0:T(8,128)(2,1)S(1)}, s16[528,128]{1,0:T(8,128)(2,1)S(1)}, u32[]{:S(2)}, u32[]{:S(2)}) %collective-permute-start.4) | collective-permute-done | bytes 135200 | tf_op jit(solution)/shard_map/ppermute | solution.py:239
  218.9 0.8 collective-permute-start.1
  219.6 14.6 %collective-permute-done.5.refs_1_ = s16[528,128]{1,0:T(8,128)(2,1)S(1)} collective-permute-done((s16[528,128]{1,0:T(8,128)(2,1)S(1)}, s16[528,128]{1,0:T(8,128)(2,1)S(1)}, u32[]{:S(2)}, u32[]{:S(2)}) %collective-permute-start.5) | collective-permute-done | bytes 135200 | tf_op jit(solution)/shard_map/ppermute | solution.py:239
  234.2 2.0 collective-permute-done.6.refs_2_
  236.2 1.7 collective-permute-start.3
  237.9 4.3 %update.13.refs_4_ = f32[2048,1024]{1,0:T(8,128)} custom-call(s32[1]{0:T(128)} %bitcast.own, f32[1,1024]{1,0:T(1,128)} %add.195.vir_ref, f32[2048,128]{1,0:T(8,128)} %broadcast_in_dim.2.occ_ref, bf16[1024,1024]{1,0:T(8,128)(2,1)} %fusion.spread_ref, f32[2,256,1024]{2,1,0:T(8,128)} %get-tuple-element.50.ladder_ref, ...), custom_call_target="tpu_custom_call", output_to_operand_aliasing={{}: (9, {})} | custom-call | flops 1073741824 | bytes 2621440 | tf_op jit(solution)/shard_map/update/pallas_call | solution.py:173
  242.2 0.6 copy-done.28
  242.9 4.3 %update.14.refs_4_ = f32[2048,1024]{1,0:T(8,128)} custom-call(s32[1]{0:T(128)} %bitcast.own, f32[1,1024]{1,0:T(1,128)} %add.195.vir_ref, f32[2048,128]{1,0:T(8,128)} %broadcast_in_dim.2.occ_ref, bf16[1024,1024]{1,0:T(8,128)(2,1)} %fusion.spread_ref, f32[2,256,1024]{2,1,0:T(8,128)} %get-tuple-element.41.ladder_ref, ...), custom_call_target="tpu_custom_call", output_to_operand_aliasing={{}: (9, {})} | custom-call | flops 1073741824 | bytes 2621440 | tf_op jit(solution)/shard_map/update/pallas_call | solution.py:173
  247.2 0.6 collective-permute-done.2.refs_2_
  247.8 3.7 %collective-permute-done.3.refs_3_ = s16[528,128]{1,0:T(8,128)(2,1)S(1)} collective-permute-done((s16[528,128]{1,0:T(8,128)(2,1)S(1)}, s16[528,128]{1,0:T(8,128)(2,1)S(1)}, u32[]{:S(2)}, u32[]{:S(2)}) %collective-permute-start.3) | collective-permute-done | bytes 135200 | tf_op jit(solution)/shard_map/ppermute | solution.py:239
  251.5 0.7 copy-done.30
  252.2 4.3 %update.15 = f32[2048,1024]{1,0:T(8,128)} custom-call(s32[1]{0:T(128)} %bitcast.own, f32[1,1024]{1,0:T(1,128)} %add.195.vir_ref, f32[2048,128]{1,0:T(8,128)} %broadcast_in_dim.2.occ_ref, bf16[1024,1024]{1,0:T(8,128)(2,1)} %fusion.spread_ref, f32[2,256,1024]{2,1,0:T(8,128)} %get-tuple-element.41.ladder_ref, ...), custom_call_target="tpu_custom_call", output_to_operand_aliasing={{}: (9, {})} | custom-call | flops 1073741824 | bytes 2621440 | tf_op jit(solution)/shard_map/update/pallas_call | solution.py:173
  (133 shorter events, 0.5 us)
Async XLA Ops:
  6.5 83.5 %all-gather.2.cloned.1.call-start = ((), (), s32[]{:S(2)}) async-start(), calls=%async_computation | async-start | bytes 9437184 | tf_op jit(solution)/shard_map/all_gather | solution.py:203
  101.4 8.5 %collective-permute-start.23 = (s16[528,128]{1,0:T(8,128)(2,1)}, s16[528,128]{1,0:T(8,128)(2,1)S(1)}, u32[]{:S(2)}, u32[]{:S(2)}) collective-permute-start(s16[528,128]{1,0:T(8,128)(2,1)} %get-tuple-element.69), channel_id=1, source_target_pairs={{0,12},{1,13},{2,14},{3,15},{4,8},{5,9},{6,10},{7,11},{8,4},{9,5},... | collective-permute-start | bytes 405512 | tf_op jit(solution)/shard_map/ppermute | solution.py:239
  104.7 18.5 %collective-permute-start.24 = (s16[528,128]{1,0:T(8,128)(2,1)}, s16[528,128]{1,0:T(8,128)(2,1)S(1)}, u32[]{:S(2)}, u32[]{:S(2)}) collective-permute-start(s16[528,128]{1,0:T(8,128)(2,1)} %get-tuple-element.70), channel_id=1, source_target_pairs={{0,13},{1,12},{2,15},{3,14},{4,9},{5,8},{6,11},{7,10},{8,5},{9,4},... | collective-permute-start | bytes 405512 | tf_op jit(solution)/shard_map/ppermute | solution.py:239
  105.7 19.2 %collective-permute-start.25 = (s16[528,128]{1,0:T(8,128)(2,1)}, s16[528,128]{1,0:T(8,128)(2,1)S(1)}, u32[]{:S(2)}, u32[]{:S(2)}) collective-permute-start(s16[528,128]{1,0:T(8,128)(2,1)} %get-tuple-element.71), channel_id=1, source_target_pairs={{0,14},{1,15},{2,12},{3,13},{4,10},{5,11},{6,8},{7,9},{8,6},{9,7},... | collective-permute-start | bytes 405512 | tf_op jit(solution)/shard_map/ppermute | solution.py:239
  108.3 17.1 %collective-permute-start.26 = (s16[528,128]{1,0:T(8,128)(2,1)}, s16[528,128]{1,0:T(8,128)(2,1)S(1)}, u32[]{:S(2)}, u32[]{:S(2)}) collective-permute-start(s16[528,128]{1,0:T(8,128)(2,1)} %get-tuple-element.72), channel_id=1, source_target_pairs={{0,15},{1,14},{2,13},{3,12},{4,11},{5,10},{6,9},{7,8},{8,7},{9,6},... | collective-permute-start | bytes 405512 | tf_op jit(solution)/shard_map/ppermute | solution.py:239
  108.4 17.9 %collective-permute-start.27 = (s16[528,128]{1,0:T(8,128)(2,1)}, s16[528,128]{1,0:T(8,128)(2,1)S(1)}, u32[]{:S(2)}, u32[]{:S(2)}) collective-permute-start(s16[528,128]{1,0:T(8,128)(2,1)} %get-tuple-element.73), channel_id=1, source_target_pairs={{0,8},{1,9},{2,10},{3,11},{4,12},{5,13},{6,14},{7,15},{8,0},{9,1},... | collective-permute-start | bytes 405512 | tf_op jit(solution)/shard_map/ppermute | solution.py:239
  109.9 13.3 %copy-start = (s16[528,128]{1,0:T(8,128)(2,1)}, s16[528,128]{1,0:T(8,128)(2,1)S(1)}, u32[]{:S(2)}) copy-start(s16[528,128]{1,0:T(8,128)(2,1)S(1)} %collective-permute-done.23.refs_0_) | copy-start | bytes 405508
  109.9 13.4 %copy-start.51 = (s16[528,128]{1,0:T(8,128)(2,1)S(1)}, s16[528,128]{1,0:T(8,128)(2,1)}, u32[]{:S(2)}) copy-start(s16[528,128]{1,0:T(8,128)(2,1)} %get-tuple-element.75) | copy-start | bytes 405508
  109.9 15.0 %copy-start.50 = (s16[528,128]{1,0:T(8,128)(2,1)S(1)}, s16[528,128]{1,0:T(8,128)(2,1)}, u32[]{:S(2)}) copy-start(s16[528,128]{1,0:T(8,128)(2,1)} %get-tuple-element.76) | copy-start | bytes 405508
  109.9 17.6 %collective-permute-start.28 = (s16[528,128]{1,0:T(8,128)(2,1)}, s16[528,128]{1,0:T(8,128)(2,1)S(1)}, u32[]{:S(2)}, u32[]{:S(2)}) collective-permute-start(s16[528,128]{1,0:T(8,128)(2,1)} %get-tuple-element.74), channel_id=1, source_target_pairs={{0,9},{1,8},{2,11},{3,10},{4,13},{5,12},{6,15},{7,14},{8,1},{9,0},... | collective-permute-start | bytes 405512 | tf_op jit(solution)/shard_map/ppermute | solution.py:239
  123.2 17.3 %copy-start.1 = (s16[528,128]{1,0:T(8,128)(2,1)}, s16[528,128]{1,0:T(8,128)(2,1)S(1)}, u32[]{:S(2)}) copy-start(s16[528,128]{1,0:T(8,128)(2,1)S(1)} %collective-permute-done.24.refs_1_) | copy-start | bytes 405508
  123.3 17.3 %collective-permute-start.29 = (s16[528,128]{1,0:T(8,128)(2,1)S(1)}, s16[528,128]{1,0:T(8,128)(2,1)S(1)}, u32[]{:S(2)}, u32[]{:S(2)}) collective-permute-start(s16[528,128]{1,0:T(8,128)(2,1)S(1)} %copy-done.51), channel_id=1, source_target_pairs={{0,10},{1,11},{2,8},{3,9},{4,14},{5,15},{6,12},{7,13},{8,2},{9,3},... | collective-permute-start | bytes 405512 | tf_op jit(solution)/shard_map/ppermute | solution.py:239
  124.9 15.6 %copy-start.3 = (s16[528,128]{1,0:T(8,128)(2,1)}, s16[528,128]{1,0:T(8,128)(2,1)S(1)}, u32[]{:S(2)}) copy-start(s16[528,128]{1,0:T(8,128)(2,1)S(1)} %collective-permute-done.25.refs_2_) | copy-start | bytes 405508
  124.9 16.0 %collective-permute-start.30 = (s16[528,128]{1,0:T(8,128)(2,1)S(1)}, s16[528,128]{1,0:T(8,128)(2,1)S(1)}, u32[]{:S(2)}, u32[]{:S(2)}) collective-permute-start(s16[528,128]{1,0:T(8,128)(2,1)S(1)} %copy-done.50), channel_id=1, source_target_pairs={{0,11},{1,10},{2,9},{3,8},{4,15},{5,14},{6,13},{7,12},{8,3},{9,2},... | collective-permute-start | bytes 405512 | tf_op jit(solution)/shard_map/ppermute | solution.py:239
  125.4 15.1 %copy-start.4 = (s16[528,128]{1,0:T(8,128)(2,1)}, s16[528,128]{1,0:T(8,128)(2,1)S(1)}, u32[]{:S(2)}) copy-start(s16[528,128]{1,0:T(8,128)(2,1)S(1)} %collective-permute-done.26.refs_3_) | copy-start | bytes 405508
  125.4 16.7 %collective-permute-start.16 = (s16[528,128]{1,0:T(8,128)(2,1)}, s16[528,128]{1,0:T(8,128)(2,1)S(1)}, u32[]{:S(2)}, u32[]{:S(2)}) collective-permute-start(s16[528,128]{1,0:T(8,128)(2,1)} %get-tuple-element.60), channel_id=1, source_target_pairs={{0,4},{1,5},{2,6},{3,7},{4,0},{5,1},{6,2},{7,3},{8,12},{9,13},{10,... | collective-permute-start | bytes 405512 | tf_op jit(solution)/shard_map/ppermute | solution.py:239
  126.3 14.2 %copy-start.11 = (s16[528,128]{1,0:T(8,128)(2,1)}, s16[528,128]{1,0:T(8,128)(2,1)S(1)}, u32[]{:S(2)}) copy-start(s16[528,128]{1,0:T(8,128)(2,1)S(1)} %collective-permute-done.27.refs_0_) | copy-start | bytes 405508
  126.3 17.1 %collective-permute-start.17 = (s16[528,128]{1,0:T(8,128)(2,1)}, s16[528,128]{1,0:T(8,128)(2,1)S(1)}, u32[]{:S(2)}, u32[]{:S(2)}) collective-permute-start(s16[528,128]{1,0:T(8,128)(2,1)} %get-tuple-element.61), channel_id=1, source_target_pairs={{0,5},{1,4},{2,7},{3,6},{4,1},{5,0},{6,3},{7,2},{8,13},{9,12},{10,... | collective-permute-start | bytes 405512 | tf_op jit(solution)/shard_map/ppermute | solution.py:239
  127.5 13.1 %copy-start.12 = (s16[528,128]{1,0:T(8,128)(2,1)}, s16[528,128]{1,0:T(8,128)(2,1)S(1)}, u32[]{:S(2)}) copy-start(s16[528,128]{1,0:T(8,128)(2,1)S(1)} %collective-permute-done.28.refs_1_) | copy-start | bytes 405508
  127.5 13.1 %copy-start.49 = (s16[528,128]{1,0:T(8,128)(2,1)S(1)}, s16[528,128]{1,0:T(8,128)(2,1)}, u32[]{:S(2)}) copy-start(s16[528,128]{1,0:T(8,128)(2,1)} %get-tuple-element.63) | copy-start | bytes 405508
  127.5 13.4 %copy-start.47 = (s16[528,128]{1,0:T(8,128)(2,1)S(1)}, s16[528,128]{1,0:T(8,128)(2,1)}, u32[]{:S(2)}) copy-start(s16[528,128]{1,0:T(8,128)(2,1)} %get-tuple-element.65) | copy-start | bytes 405508
  127.5 14.7 %copy-start.45 = (s16[528,128]{1,0:T(8,128)(2,1)S(1)}, s16[528,128]{1,0:T(8,128)(2,1)}, u32[]{:S(2)}) copy-start(s16[528,128]{1,0:T(8,128)(2,1)} %get-tuple-element.66) | copy-start | bytes 405508
  127.5 15.9 %copy-start.43 = (s16[528,128]{1,0:T(8,128)(2,1)S(1)}, s16[528,128]{1,0:T(8,128)(2,1)}, u32[]{:S(2)}) copy-start(s16[528,128]{1,0:T(8,128)(2,1)} %get-tuple-element.67) | copy-start | bytes 405508
  127.5 16.3 %collective-permute-start.18 = (s16[528,128]{1,0:T(8,128)(2,1)}, s16[528,128]{1,0:T(8,128)(2,1)S(1)}, u32[]{:S(2)}, u32[]{:S(2)}) collective-permute-start(s16[528,128]{1,0:T(8,128)(2,1)} %get-tuple-element.62), channel_id=1, source_target_pairs={{0,6},{1,7},{2,4},{3,5},{4,2},{5,3},{6,0},{7,1},{8,14},{9,15},{10,... | collective-permute-start | bytes 405512 | tf_op jit(solution)/shard_map/ppermute | solution.py:239
  140.6 16.4 %copy-start.13 = (s16[528,128]{1,0:T(8,128)(2,1)}, s16[528,128]{1,0:T(8,128)(2,1)S(1)}, u32[]{:S(2)}) copy-start(s16[528,128]{1,0:T(8,128)(2,1)S(1)} %collective-permute-done.29.refs_2_) | copy-start | bytes 405508
  140.6 16.5 %collective-permute-start.19 = (s16[528,128]{1,0:T(8,128)(2,1)S(1)}, s16[528,128]{1,0:T(8,128)(2,1)S(1)}, u32[]{:S(2)}, u32[]{:S(2)}) collective-permute-start(s16[528,128]{1,0:T(8,128)(2,1)S(1)} %copy-done.49), channel_id=1, source_target_pairs={{0,7},{1,6},{2,5},{3,4},{4,3},{5,2},{6,1},{7,0},{8,15},{9,14},{10,... | collective-permute-start | bytes 405512 | tf_op jit(solution)/shard_map/ppermute | solution.py:239
  140.9 16.1 %copy-start.15 = (s16[528,128]{1,0:T(8,128)(2,1)}, s16[528,128]{1,0:T(8,128)(2,1)S(1)}, u32[]{:S(2)}) copy-start(s16[528,128]{1,0:T(8,128)(2,1)S(1)} %collective-permute-done.30.refs_3_) | copy-start | bytes 405508
  140.9 23.6 %collective-permute-start.20 = (s16[528,128]{1,0:T(8,128)(2,1)S(1)}, s16[528,128]{1,0:T(8,128)(2,1)S(1)}, u32[]{:S(2)}, u32[]{:S(2)}) collective-permute-start(s16[528,128]{1,0:T(8,128)(2,1)S(1)} %copy-done.47), channel_id=1, source_target_pairs={{0,1},{1,0},{2,3},{3,2},{4,5},{5,4},{6,7},{7,6},{8,9},{9,8},{10,11... | collective-permute-start | bytes 405512 | tf_op jit(solution)/shard_map/ppermute | solution.py:239
  142.1 14.9 %copy-start.2 = (s16[528,128]{1,0:T(8,128)(2,1)}, s16[528,128]{1,0:T(8,128)(2,1)S(1)}, u32[]{:S(2)}) copy-start(s16[528,128]{1,0:T(8,128)(2,1)S(1)} %collective-permute-done.16.refs_0_) | copy-start | bytes 405508
  142.2 25.3 %collective-permute-start.21 = (s16[528,128]{1,0:T(8,128)(2,1)S(1)}, s16[528,128]{1,0:T(8,128)(2,1)S(1)}, u32[]{:S(2)}, u32[]{:S(2)}) collective-permute-start(s16[528,128]{1,0:T(8,128)(2,1)S(1)} %copy-done.45), channel_id=1, source_target_pairs={{0,2},{1,3},{2,0},{3,1},{4,6},{5,7},{6,4},{7,5},{8,10},{9,11},{10,... | collective-permute-start | bytes 405512 | tf_op jit(solution)/shard_map/ppermute | solution.py:239
  143.4 13.6 %copy-start.5 = (s16[528,128]{1,0:T(8,128)(2,1)}, s16[528,128]{1,0:T(8,128)(2,1)S(1)}, u32[]{:S(2)}) copy-start(s16[528,128]{1,0:T(8,128)(2,1)S(1)} %collective-permute-done.17.refs_1_) | copy-start | bytes 405508
  143.4 25.7 %collective-permute-start.22 = (s16[528,128]{1,0:T(8,128)(2,1)S(1)}, s16[528,128]{1,0:T(8,128)(2,1)S(1)}, u32[]{:S(2)}, u32[]{:S(2)}) collective-permute-start(s16[528,128]{1,0:T(8,128)(2,1)S(1)} %copy-done.43), channel_id=1, source_target_pairs={{0,3},{1,2},{2,1},{3,0},{4,7},{5,6},{6,5},{7,4},{8,11},{9,10},{10,... | collective-permute-start | bytes 405512 | tf_op jit(solution)/shard_map/ppermute | solution.py:239
  143.8 13.3 %copy-start.7 = (s16[528,128]{1,0:T(8,128)(2,1)}, s16[528,128]{1,0:T(8,128)(2,1)S(1)}, u32[]{:S(2)}) copy-start(s16[528,128]{1,0:T(8,128)(2,1)S(1)} %collective-permute-done.18.refs_2_) | copy-start | bytes 405508
  143.8 13.3 %copy-start.48 = (s16[528,128]{1,0:T(8,128)(2,1)S(1)}, s16[528,128]{1,0:T(8,128)(2,1)}, u32[]{:S(2)}) copy-start(s16[528,128]{1,0:T(8,128)(2,1)} %get-tuple-element.52) | copy-start | bytes 405508
  143.8 26.2 %collective-permute-start.8 = (s16[528,128]{1,0:T(8,128)(2,1)}, s16[528,128]{1,0:T(8,128)(2,1)S(1)}, u32[]{:S(2)}, u32[]{:S(2)}) collective-permute-start(s16[528,128]{1,0:T(8,128)(2,1)} %get-tuple-element.51), channel_id=1, source_target_pairs={{0,20},{1,21},{2,22},{3,23},{4,16},{5,17},{6,18},{7,19},{8,28},{9,... | collective-permute-start | bytes 405512 | tf_op jit(solution)/shard_map/ppermute | solution.py:239
  157.1 12.0 %copy-start.41 = (s16[528,128]{1,0:T(8,128)(2,1)S(1)}, s16[528,128]{1,0:T(8,128)(2,1)}, u32[]{:S(2)}) copy-start(s16[528,128]{1,0:T(8,128)(2,1)} %get-tuple-element.56) | copy-start | bytes 405508
  157.1 12.9 %copy-start.39 = (s16[528,128]{1,0:T(8,128)(2,1)S(1)}, s16[528,128]{1,0:T(8,128)(2,1)}, u32[]{:S(2)}) copy-start(s16[528,128]{1,0:T(8,128)(2,1)} %get-tuple-element.57) | copy-start | bytes 405508
  157.1 18.8 %copy-start.8 = (s16[528,128]{1,0:T(8,128)(2,1)}, s16[528,128]{1,0:T(8,128)(2,1)S(1)}, u32[]{:S(2)}) copy-start(s16[528,128]{1,0:T(8,128)(2,1)S(1)} %collective-permute-done.19.refs_3_) | copy-start | bytes 405508
  157.1 18.8 %collective-permute-start.9 = (s16[528,128]{1,0:T(8,128)(2,1)S(1)}, s16[528,128]{1,0:T(8,128)(2,1)S(1)}, u32[]{:S(2)}, u32[]{:S(2)}) collective-permute-start(s16[528,128]{1,0:T(8,128)(2,1)S(1)} %copy-done.48), channel_id=1, source_target_pairs={{0,21},{1,20},{2,23},{3,22},{4,17},{5,16},{6,19},{7,18},{8,29},{9,... | collective-permute-start | bytes 405512 | tf_op jit(solution)/shard_map/ppermute | solution.py:239
  164.5 11.4 %copy-start.14 = (s16[528,128]{1,0:T(8,128)(2,1)}, s16[528,128]{1,0:T(8,128)(2,1)S(1)}, u32[]{:S(2)}) copy-start(s16[528,128]{1,0:T(8,128)(2,1)S(1)} %collective-permute-done.20.refs_1_) | copy-start | bytes 405508
  164.5 20.8 %collective-permute-start.10 = (s16[528,128]{1,0:T(8,128)(2,1)S(1)}, s16[528,128]{1,0:T(8,128)(2,1)S(1)}, u32[]{:S(2)}, u32[]{:S(2)}) collective-permute-start(s16[528,128]{1,0:T(8,128)(2,1)S(1)} %copy-done.46), channel_id=1, source_target_pairs={{0,22},{1,23},{2,20},{3,21},{4,18},{5,19},{6,16},{7,17},{8,30},{9,... | collective-permute-start | bytes 405512 | tf_op jit(solution)/shard_map/ppermute | solution.py:239
  167.5 22.1 %collective-permute-start.12 = (s16[528,128]{1,0:T(8,128)(2,1)S(1)}, s16[528,128]{1,0:T(8,128)(2,1)S(1)}, u32[]{:S(2)}, u32[]{:S(2)}) collective-permute-start(s16[528,128]{1,0:T(8,128)(2,1)S(1)} %copy-done.44), channel_id=1, source_target_pairs={{0,16},{1,17},{2,18},{3,19},{4,20},{5,21},{6,22},{7,23},{8,24},{9,... | collective-permute-start | bytes 405512 | tf_op jit(solution)/shard_map/ppermute | solution.py:239
  169.1 24.9 %collective-permute-start.13 = (s16[528,128]{1,0:T(8,128)(2,1)S(1)}, s16[528,128]{1,0:T(8,128)(2,1)S(1)}, u32[]{:S(2)}, u32[]{:S(2)}) collective-permute-start(s16[528,128]{1,0:T(8,128)(2,1)S(1)} %copy-done.41), channel_id=1, source_target_pairs={{0,17},{1,16},{2,19},{3,18},{4,21},{5,20},{6,23},{7,22},{8,25},{9,... | collective-permute-start | bytes 405512 | tf_op jit(solution)/shard_map/ppermute | solution.py:239
  170.0 29.6 %collective-permute-start.14 = (s16[528,128]{1,0:T(8,128)(2,1)S(1)}, s16[528,128]{1,0:T(8,128)(2,1)S(1)}, u32[]{:S(2)}, u32[]{:S(2)}) collective-permute-start(s16[528,128]{1,0:T(8,128)(2,1)S(1)} %copy-done.39), channel_id=1, source_target_pairs={{0,18},{1,19},{2,16},{3,17},{4,22},{5,23},{6,20},{7,21},{8,26},{9,... | collective-permute-start | bytes 405512 | tf_op jit(solution)/shard_map/ppermute | solution.py:239
  176.0 29.6 %collective-permute-start.15 = (s16[528,128]{1,0:T(8,128)(2,1)S(1)}, s16[528,128]{1,0:T(8,128)(2,1)S(1)}, u32[]{:S(2)}, u32[]{:S(2)}) collective-permute-start(s16[528,128]{1,0:T(8,128)(2,1)S(1)} %copy-done.37), channel_id=1, source_target_pairs={{0,19},{1,18},{2,17},{3,16},{4,23},{5,22},{6,21},{7,20},{8,27},{9,... | collective-permute-start | bytes 405512 | tf_op jit(solution)/shard_map/ppermute | solution.py:239
  178.6 10.9 %copy-start.42 = (s16[528,128]{1,0:T(8,128)(2,1)S(1)}, s16[528,128]{1,0:T(8,128)(2,1)}, u32[]{:S(2)}) copy-start(s16[528,128]{1,0:T(8,128)(2,1)} %get-tuple-element.46) | copy-start | bytes 405508
  178.6 15.3 %copy-start.40 = (s16[528,128]{1,0:T(8,128)(2,1)S(1)}, s16[528,128]{1,0:T(8,128)(2,1)}, u32[]{:S(2)}) copy-start(s16[528,128]{1,0:T(8,128)(2,1)} %get-tuple-element.47) | copy-start | bytes 405508
  178.6 21.0 %copy-start.38 = (s16[528,128]{1,0:T(8,128)(2,1)S(1)}, s16[528,128]{1,0:T(8,128)(2,1)}, u32[]{:S(2)}) copy-start(s16[528,128]{1,0:T(8,128)(2,1)} %get-tuple-element.48) | copy-start | bytes 405508
  185.3 19.9 %copy-start.10 = (s16[528,128]{1,0:T(8,128)(2,1)}, s16[528,128]{1,0:T(8,128)(2,1)S(1)}, u32[]{:S(2)}) copy-start(s16[528,128]{1,0:T(8,128)(2,1)S(1)} %collective-permute-done.10.refs_2_) | copy-start | bytes 405508
  185.3 28.4 %collective-permute-start.11 = (s16[528,128]{1,0:T(8,128)(2,1)S(1)}, s16[528,128]{1,0:T(8,128)(2,1)S(1)}, u32[]{:S(2)}, u32[]{:S(2)}) collective-permute-start(s16[528,128]{1,0:T(8,128)(2,1)S(1)} %copy-done.35), channel_id=1, source_target_pairs={{0,23},{1,22},{2,21},{3,20},{4,19},{5,18},{6,17},{7,16},{8,31},{9,... | collective-permute-start | bytes 405512 | tf_op jit(solution)/shard_map/ppermute | solution.py:239
  189.6 15.6 %copy-start.18 = (s16[528,128]{1,0:T(8,128)(2,1)}, s16[528,128]{1,0:T(8,128)(2,1)S(1)}, u32[]{:S(2)}) copy-start(s16[528,128]{1,0:T(8,128)(2,1)S(1)} %collective-permute-done.12.refs_0_) | copy-start | bytes 405508
  189.6 29.3 %collective-permute-start.4 = (s16[528,128]{1,0:T(8,128)(2,1)S(1)}, s16[528,128]{1,0:T(8,128)(2,1)S(1)}, u32[]{:S(2)}, u32[]{:S(2)}) collective-permute-start(s16[528,128]{1,0:T(8,128)(2,1)S(1)} %copy-done.42), channel_id=1, source_target_pairs={{0,24},{1,25},{2,26},{3,27},{4,28},{5,29},{6,30},{7,31},{8,16},{9,... | collective-permute-start | bytes 405512 | tf_op jit(solution)/shard_map/ppermute | solution.py:239
  194.0 11.2 %copy-start.21 = (s16[528,128]{1,0:T(8,128)(2,1)}, s16[528,128]{1,0:T(8,128)(2,1)S(1)}, u32[]{:S(2)}) copy-start(s16[528,128]{1,0:T(8,128)(2,1)S(1)} %collective-permute-done.13.refs_1_) | copy-start | bytes 405508
  194.0 40.2 %collective-permute-start.5 = (s16[528,128]{1,0:T(8,128)(2,1)S(1)}, s16[528,128]{1,0:T(8,128)(2,1)S(1)}, u32[]{:S(2)}, u32[]{:S(2)}) collective-permute-start(s16[528,128]{1,0:T(8,128)(2,1)S(1)} %copy-done.40), channel_id=1, source_target_pairs={{0,25},{1,24},{2,27},{3,26},{4,29},{5,28},{6,31},{7,30},{8,17},{9,... | collective-permute-start | bytes 405512 | tf_op jit(solution)/shard_map/ppermute | solution.py:239
  199.6 36.6 %collective-permute-start.6 = (s16[528,128]{1,0:T(8,128)(2,1)S(1)}, s16[528,128]{1,0:T(8,128)(2,1)S(1)}, u32[]{:S(2)}, u32[]{:S(2)}) collective-permute-start(s16[528,128]{1,0:T(8,128)(2,1)S(1)} %copy-done.38), channel_id=1, source_target_pairs={{0,26},{1,27},{2,24},{3,25},{4,30},{5,31},{6,28},{7,29},{8,18},{9,... | collective-permute-start | bytes 405512 | tf_op jit(solution)/shard_map/ppermute | solution.py:239
  205.5 36.7 %collective-permute-start.7 = (s16[528,128]{1,0:T(8,128)(2,1)S(1)}, s16[528,128]{1,0:T(8,128)(2,1)S(1)}, u32[]{:S(2)}, u32[]{:S(2)}) collective-permute-start(s16[528,128]{1,0:T(8,128)(2,1)S(1)} %copy-done.36), channel_id=1, source_target_pairs={{0,27},{1,26},{2,25},{3,24},{4,31},{5,30},{6,29},{7,28},{8,19},{9,... | collective-permute-start | bytes 405512 | tf_op jit(solution)/shard_map/ppermute | solution.py:239
  209.3 24.9 %copy-start.32 = (s16[528,128]{1,0:T(8,128)(2,1)S(1)}, s16[528,128]{1,0:T(8,128)(2,1)}, u32[]{:S(2)}) copy-start(s16[528,128]{1,0:T(8,128)(2,1)} %get-tuple-element.44) | copy-start | bytes 405508
  209.3 26.9 %copy-start.31 = (s16[528,128]{1,0:T(8,128)(2,1)S(1)}, s16[528,128]{1,0:T(8,128)(2,1)}, u32[]{:S(2)}) copy-start(s16[528,128]{1,0:T(8,128)(2,1)} %get-tuple-element.45) | copy-start | bytes 405508
  213.7 24.2 %copy-start.19 = (s16[528,128]{1,0:T(8,128)(2,1)}, s16[528,128]{1,0:T(8,128)(2,1)S(1)}, u32[]{:S(2)}) copy-start(s16[528,128]{1,0:T(8,128)(2,1)S(1)} %collective-permute-done.11.refs_3_) | copy-start | bytes 405508
  213.7 33.5 %collective-permute-start = (s16[528,128]{1,0:T(8,128)(2,1)S(1)}, s16[528,128]{1,0:T(8,128)(2,1)S(1)}, u32[]{:S(2)}, u32[]{:S(2)}) collective-permute-start(s16[528,128]{1,0:T(8,128)(2,1)S(1)} %copy-done.34), channel_id=1, source_target_pairs={{0,28},{1,29},{2,30},{3,31},{4,24},{5,25},{6,26},{7,27},{8,20},{9,... | collective-permute-start | bytes 405512 | tf_op jit(solution)/shard_map/ppermute | solution.py:239
  218.8 23.3 %copy-start.20 = (s16[528,128]{1,0:T(8,128)(2,1)}, s16[528,128]{1,0:T(8,128)(2,1)S(1)}, u32[]{:S(2)}) copy-start(s16[528,128]{1,0:T(8,128)(2,1)S(1)} %collective-permute-done.4.refs_0_) | copy-start | bytes 405508
  218.9 28.3 %collective-permute-start.1 = (s16[528,128]{1,0:T(8,128)(2,1)S(1)}, s16[528,128]{1,0:T(8,128)(2,1)S(1)}, u32[]{:S(2)}, u32[]{:S(2)}) collective-permute-start(s16[528,128]{1,0:T(8,128)(2,1)S(1)} %copy-done.33), channel_id=1, source_target_pairs={{0,29},{1,28},{2,31},{3,30},{4,25},{5,24},{6,27},{7,26},{8,21},{9,... | collective-permute-start | bytes 405512 | tf_op jit(solution)/shard_map/ppermute | solution.py:239
  234.2 13.6 %collective-permute-start.2 = (s16[528,128]{1,0:T(8,128)(2,1)S(1)}, s16[528,128]{1,0:T(8,128)(2,1)S(1)}, u32[]{:S(2)}, u32[]{:S(2)}) collective-permute-start(s16[528,128]{1,0:T(8,128)(2,1)S(1)} %copy-done.32), channel_id=1, source_target_pairs={{0,30},{1,31},{2,28},{3,29},{4,26},{5,27},{6,24},{7,25},{8,22},{9,... | collective-permute-start | bytes 405512 | tf_op jit(solution)/shard_map/ppermute | solution.py:239
  236.2 15.3 %collective-permute-start.3 = (s16[528,128]{1,0:T(8,128)(2,1)S(1)}, s16[528,128]{1,0:T(8,128)(2,1)S(1)}, u32[]{:S(2)}, u32[]{:S(2)}) collective-permute-start(s16[528,128]{1,0:T(8,128)(2,1)S(1)} %copy-done.31), channel_id=1, source_target_pairs={{0,31},{1,30},{2,29},{3,28},{4,27},{5,26},{6,25},{7,24},{8,23},{9,... | collective-permute-start | bytes 405512 | tf_op jit(solution)/shard_map/ppermute | solution.py:239
  (20 other events, 115.5 us)
Sparse Core Ops, SparseCore 0:
  9.0 80.9 all-gather.1

commit v4 on v1

v4 whole, which is shorter than its diff:
```python
import functools

import jax
import jax.numpy as jnp
from jax import lax
from jax.experimental import pallas as pl
from jax.experimental.pallas import tpu as pltpu
from jax.sharding import PartitionSpec as P

VT = 32
NVT = 2
W = 64
ORBITALS_IN_GRP = 16
PAIR_SQ = ORBITALS_IN_GRP * ORBITALS_IN_GRP
CORES = 2
CODE_ROWS = 16
TOP = 32700.0
STEPS = 8.0
VMEM_LIMIT = 56 * 1024 * 1024


def one_hot_of(target, amount):
    return (target[:, None] == jnp.arange(amount)[None, :]).astype(jnp.bfloat16)


def split(values):
    high = values.astype(jnp.bfloat16)
    return high, (values - high.astype(jnp.float32)).astype(jnp.bfloat16)


def dot(left, right):
    return jnp.dot(left, right, preferred_element_type=jnp.float32)


def scale_of(code):
    return jnp.exp2(code * (1.0 / STEPS))


def screen_kernel(int_mask, slab_ref, *screened_refs):
    slab_rows, slab_cols = slab_ref.shape
    chunk = slab_cols // len(screened_refs)
    row_label = lax.axis_index("occ") * slab_rows // W // VT * NVT
    col_label = lax.axis_index("vir") * slab_cols // W // VT * NVT
    right = lax.broadcasted_iota(jnp.int32, (VT, chunk), 1) % W >= VT
    keep = []
    for d_tile in range(NVT):
        label = row_label + d_tile
        kept = jnp.where(right, int_mask[label, col_label + 1], int_mask[label, col_label])
        keep.append(kept.astype(jnp.float32).astype(jnp.bfloat16))
    for c, screened_ref in enumerate(screened_refs):
        for at in range(0, slab_rows, VT):
            screened_ref[at : at + VT, :] = (
                slab_ref[at : at + VT, c * chunk : (c + 1) * chunk] * keep[at // VT % NVT]
            )


def screen_call(chunks, int_mask, integrals):
    slab_rows, slab_cols = integrals.shape
    vmem = pl.BlockSpec(memory_space=pltpu.VMEM)
    return pl.pallas_call(
        screen_kernel,
        in_specs=[pl.BlockSpec(memory_space=pltpu.SMEM), vmem],
        out_specs=[vmem] * chunks,
        out_shape=[jax.ShapeDtypeStruct((slab_rows, slab_cols // chunks), integrals.dtype)] * chunks,
        name="screen",
    )(int_mask, integrals)


def line_gather(part, tile_total):
    chips = tile_total // CORES
    partner = lambda array: lax.ppermute(array, "occ", [(t, t ^ 1) for t in range(tile_total)])
    pieces = [(0, 0, False, part), (0, 0, True, partner(part))]
    travel = {1: part, -1: part}
    for step in range(1, chips):
        for sign in (1, -1):
            pairs = []
            for t in range(tile_total):
                chip = t // CORES
                if 0 <= chip + sign * step < chips:
                    pairs.append((t + sign * CORES, t))
            travel[sign] = lax.ppermute(travel[sign], "occ", pairs)
        for sign in (1, -1):
            holders = [t for t in range(tile_total) if 0 <= t // CORES + sign * step < chips]
            across = lax.ppermute(travel[sign], "occ", [(t, t ^ 1) for t in holders])
            pieces.append((sign, step, False, travel[sign]))
            pieces.append((sign, step, True, across))
    return pieces, travel


def fill_slab(layout, slab_rows, refs, slab_scr, sems):
    tile = lax.axis_index("occ")
    chips = lax.axis_size("occ") // CORES
    chip, core = tile // CORES, tile % CORES

    def each(act):
        for n, (sign, step, other) in enumerate(layout):
            at_chip = chip + sign * step

            @pl.when((at_chip >= 0) & (at_chip < chips))
            def _():
                place = at_chip * CORES + (1 - core if other else core)
                at = pl.ds(pl.multiple_of(place * slab_rows, slab_rows), slab_rows)
                act(pltpu.make_async_copy(refs[n], slab_scr.at[at, :], sems.at[n]))

    each(lambda copy: copy.start())
    each(lambda copy: copy.wait())


def ladder_kernel(vir_count, layout, amp_mask, numbers, rows_ref, swap_ref, perm_ref, *refs):
    pieces, (ladder_ref, packed_ref) = refs[: len(layout)], refs[len(layout) : len(layout) + 2]
    tile = pl.program_id(0)
    cols = perm_ref.shape[1]
    if len(layout) > 1:
        slab_ref, sems = refs[len(layout) + 2 :]

        @pl.when(tile == 0)
        def _():
            fill_slab(layout, pieces[0].shape[0], pieces, slab_ref, sems)
    else:
        slab_ref = pieces[0]

    lane = lax.broadcasted_iota(jnp.int32, (1, W * W), 1)
    low = lane < W * VT
    left = lane % W < VT
    keep = jnp.where(
        low,
        jnp.where(left, amp_mask[tile, 0], amp_mask[tile, 1]),
        jnp.where(left, amp_mask[tile, 2], amp_mask[tile, 3]),
    )
    screened = rows_ref[...] * keep.astype(jnp.float32).astype(jnp.bfloat16)
    ladder = dot(screened, slab_ref[...])
    pair = lax.broadcasted_iota(jnp.int32, (PAIR_SQ, 1), 0)
    own_number = numbers[lax.axis_index("occ")]
    nonzero = (pair // ORBITALS_IN_GRP < own_number) & (pair % ORBITALS_IN_GRP < numbers[tile])
    ladder = jnp.where(nonzero, ladder, 0.0)
    ladder_ref[...] = ladder
    high, low_part = split(ladder)
    mirror = dot(dot(swap_ref[...], high).astype(jnp.bfloat16), perm_ref[...]) + dot(
        dot(swap_ref[...], low_part).astype(jnp.bfloat16), perm_ref[...]
    )
    most = jnp.maximum(jnp.max(jnp.abs(mirror), axis=0, keepdims=True), 1e-30)
    code = jnp.ceil(jnp.log2(most) * STEPS)
    coded = jnp.round(mirror * (TOP / scale_of(code))).astype(jnp.int32).astype(jnp.int16)
    code_rows = jnp.broadcast_to(code.astype(jnp.int32), (CODE_ROWS, cols)).astype(jnp.int16)
    block = cols // vir_count
    for v in range(vir_count):
        packed_ref[0, v, :PAIR_SQ] = coded[:, v * block : (v + 1) * block]
        packed_ref[0, v, PAIR_SQ:] = code_rows[:, v * block : (v + 1) * block]


def ladder_call(tile_total, vir_count, layout, amp_mask, numbers, amplitudes, swap, perm, slab_parts):
    cols = perm.shape[1]
    block = cols // vir_count
    smem = pl.BlockSpec(memory_space=pltpu.SMEM)
    whole = lambda tile: (0, 0)
    rows = tile_total * PAIR_SQ
    if len(layout) > 1:
        slab_specs = [pl.BlockSpec(memory_space=pl.ANY)] * len(layout)
        scratch = [pltpu.VMEM((W * W, cols), jnp.bfloat16), pltpu.SemaphoreType.DMA((len(layout),))]
    else:
        slab_specs = [pl.BlockSpec((W * W, cols), whole)]
        scratch = []
    return pl.pallas_call(
        functools.partial(ladder_kernel, vir_count, layout),
        grid=(tile_total,),
        in_specs=[
            smem,
            smem,
            pl.BlockSpec((PAIR_SQ, W * W), lambda tile: (tile, 0)),
            pl.BlockSpec(swap.shape, whole),
            pl.BlockSpec(perm.shape, whole),
        ]
        + slab_specs,
        out_specs=[
            pl.BlockSpec((PAIR_SQ, cols), lambda tile: (tile, 0)),
            pl.BlockSpec((1, vir_count, PAIR_SQ + CODE_ROWS, block), lambda tile: (tile, 0, 0, 0)),
        ],
        out_shape=[
            jax.ShapeDtypeStruct((rows, cols), jnp.float32),
            jax.ShapeDtypeStruct((tile_total, vir_count, PAIR_SQ + CODE_ROWS, block), jnp.int16),
        ],
        scratch_shapes=scratch,
        compiler_params=pltpu.CompilerParams(vmem_limit_bytes=VMEM_LIMIT),
        cost_estimate=pl.CostEstimate(
            flops=2 * rows * cols * (W * W + 2 * PAIR_SQ + 2 * cols),
            bytes_accessed=rows * (W * W * 2 + cols * 6) + W * W * cols * 2,
            transcendentals=0,
        ),
        name="ladder",
    )(amp_mask, numbers, amplitudes, swap, perm, *slab_parts)


def mirror_of(vir_count, arrived_ref, spread_ref):
    highs, lows = [], []
    for v in range(vir_count):
        code = arrived_ref[0, v, PAIR_SQ:].astype(jnp.int32).astype(jnp.float32)[:1]
        values = arrived_ref[0, v, :PAIR_SQ].astype(jnp.int32).astype(jnp.float32)
        high, low = split(values * (scale_of(code) * (1.0 / TOP)))
        highs.append(high)
        lows.append(low)
    return dot(jnp.concatenate(highs, axis=1), spread_ref[...]) + dot(jnp.concatenate(lows, axis=1), spread_ref[...])


def add_kernel(vir_count, spread_ref, arrived_ref, *refs):
    ladders, total_ref = refs[:-1], refs[-1]
    mirror = mirror_of(vir_count, arrived_ref, spread_ref)
    cols = ladders[0].shape[1]
    for c, ladder_ref in enumerate(ladders):
        at = slice(c * cols, (c + 1) * cols)
        total_ref[:, at] = ladder_ref[...] + mirror[:, at]


def update_kernel(vir_count, spread_ref, arrived_ref, vir_ref, occ_ref, *refs):
    totals, update_ref = refs[:-1], refs[-1]
    mirror = mirror_of(vir_count, arrived_ref, spread_ref)
    cols = totals[0].shape[1]
    for c, total_ref in enumerate(totals):
        at = slice(c * cols, (c + 1) * cols)
        denominator = vir_ref[:, at] - occ_ref[:, :1]
        update_ref[:, at] = (total_ref[...] + mirror[:, at]) / denominator


def mirror_call(kernel, name, tile_total, spread, arrived, energies, totals):
    slab_cols = spread.shape[1]
    rows = tile_total * PAIR_SQ
    by_tile = lambda tile: (tile, 0)
    energy_specs = [pl.BlockSpec((1, slab_cols), lambda tile: (0, 0)), pl.BlockSpec((PAIR_SQ, 128), by_tile)]
    return pl.pallas_call(
        functools.partial(kernel, arrived.shape[1]),
        grid=(tile_total,),
        in_specs=[
            pl.BlockSpec(spread.shape, lambda tile: (0, 0)),
            pl.BlockSpec((1,) + arrived.shape[1:], lambda tile: (tile, 0, 0, 0)),
        ]
        + energy_specs[: len(energies)]
        + [pl.BlockSpec((PAIR_SQ, total.shape[1]), by_tile) for total in totals],
        out_specs=pl.BlockSpec((PAIR_SQ, slab_cols), by_tile),
        out_shape=jax.ShapeDtypeStruct((rows, slab_cols), jnp.float32),
        compiler_params=pltpu.CompilerParams(vmem_limit_bytes=VMEM_LIMIT),
        cost_estimate=pl.CostEstimate(
            flops=4 * rows * spread.shape[0] * slab_cols, bytes_accessed=rows * slab_cols * 9, transcendentals=0
        ),
        name=name,
    )(spread, arrived, *energies, *totals)


def body(amplitudes, amp_mask, integrals, int_mask, group_orbital_numbers, occ_energy, vir_energy):
    tile_total = lax.axis_size("occ")
    vir_count = lax.axis_size("vir")
    row_tile = lax.axis_index("occ")
    vir_place = lax.axis_index("vir")
    vir_span = W // vir_count
    slab_cols = vir_span * W
    chunks = 2 if vir_span >= 16 else 1
    chunk_cols = slab_cols // chunks
    chunk_span = vir_span // chunks
    block = chunk_cols // vir_count

    screened = screen_call(chunks, int_mask, integrals)
    pieces, last = line_gather(screened[0], tile_total)
    slabs = [([piece[:3] for piece in pieces], [piece[3] for piece in pieces])]
    if chunks > 1:
        later, _, _ = lax.optimization_barrier((screened[1], last[1], last[-1]))
        slabs.append(([(0, 0, False)], [lax.all_gather(later, "occ", axis=0, tiled=True)]))

    pair = jnp.arange(PAIR_SQ)
    swap = one_hot_of(pair % ORBITALS_IN_GRP * ORBITALS_IN_GRP + pair // ORBITALS_IN_GRP, PAIR_SQ)
    col = jnp.arange(chunk_cols)
    a, b = col // W, col % W
    perm = one_hot_of(b // vir_span * block + b % vir_span * chunk_span + a, chunk_cols)
    place = jnp.arange(chunk_cols)
    sender, here, there = place // block, place % block // chunk_span, place % chunk_span
    to_column = here * W + sender * vir_span + there

    occ_table = occ_energy.reshape(tile_total, ORBITALS_IN_GRP)
    own_energy = lax.dynamic_slice_in_dim(occ_table, row_tile, 1, 0)[0]
    occ_sum = jnp.broadcast_to(
        (own_energy[None, :, None] + occ_table[:, None, :]).reshape(-1, 1), (tile_total * PAIR_SQ, 128)
    )
    vir_own = lax.dynamic_slice_in_dim(vir_energy, vir_place * vir_span, vir_span, 0)
    vir_sum = (vir_own[:, None] + vir_energy[None, :]).reshape(1, -1)

    ladders, arrived = [], []
    for layout, slab_parts in slabs:
        ladder, packed = ladder_call(
            tile_total, vir_count, layout, amp_mask[0], group_orbital_numbers, amplitudes, swap, perm, slab_parts
        )
        rows = PAIR_SQ + CODE_ROWS
        moved = lax.all_to_all(
            packed.reshape(tile_total * vir_count, rows, block), ("occ", "vir"), split_axis=0, concat_axis=0, tiled=True
        )
        ladders.append(ladder)
        arrived.append(moved.reshape(tile_total, vir_count, rows, block))
    spreads = [one_hot_of(to_column + c * chunk_span, slab_cols) for c in range(chunks)]
    totals = ladders
    for c in range(chunks - 1):
        totals = [mirror_call(add_kernel, "add", tile_total, spreads[c], arrived[c], [], totals)]
    return mirror_call(
        update_kernel, "update", tile_total, spreads[-1], arrived[-1], [vir_sum, occ_sum], totals
    )


def solution(mesh):
    in_specs = (P("occ", None), P("occ", None, None), P("occ", "vir"), P(), P(), P(), P())
    out_specs = P("occ", "vir")
    return jax.shard_map(body, mesh=mesh, in_specs=in_specs, out_specs=out_specs, check_vma=False)
```

time: 233 us -> 229 us (0.983)
  waiting for transfers between devices: 143 us -> 105 us
  starting transfers between devices: 7.88 us -> 31.4 us
  Pallas kernels: 57.7 us -> 67 us
    all_gather x2 -> x1, waiting for transfers between devices: 93.5 us -> 8.57 us  [body(): lax.all_gather(later, 'occ', axis=0, tiled=True)]
    ppermute x0 -> x13, waiting for transfers between devices: none -> 35.2 us  [the longest x6 35.2 us: line_gather(): travel[sign] = lax.ppermute(travel[sign], 'occ', pairs)]
    ppermute x0 -> x13, starting transfers between devices: none -> 19.7 us  [the longest x6 10.8 us: line_gather(): travel[sign] = lax.ppermute(travel[sign], 'occ', pairs)]
    all_to_all x2, waiting for transfers between devices: 48.7 us -> 60.7 us  [body(): lax.all_to_all(packed.reshape(tile_total * vir_count, rows, block), ('occ...]
    pallas_call x3 -> x5, Pallas kernels: 57.7 us -> 67 us  [the longest x2 40.6 us: ladder_call(): pl.pallas_call(functools.partial(ladder_kernel, vir_count, layout), grid=...]
    all_to_all x2, starting transfers between devices: 7.84 us -> 11.7 us  [body(): lax.all_to_all(packed.reshape(tile_total * vir_count, rows, block), ('occ...]
    unnamed x6 -> x28, local copies, waits for them, and re-layouts: 0.01 us -> 3.4 us
  transfers between devices with their start and end apart: 4 -> 16, of which waited for: 3 -> 6; matrix products, arithmetic and copies ran while one was open for 3% -> 3% of each run, Pallas kernels for 18% -> 23%
where the time goes in v4:
time: 229 us; the launch traced here: 228 us
  waiting for transfers between devices  105 us (46%)
  Pallas kernels  67 us (29%)
  starting transfers between devices  31.4 us (14%)
  between operations  13.7 us (6%)
  local copies, waits for them, and re-layouts  6.98 us (3%)
  other arithmetic  4.32 us (2%)
    all_to_all x2, waiting for transfers between devices, body(): lax.all_to_all(packed.reshape(tile_total * vir_count, rows, block), ('occ...  60.7 us
    pallas_call x2, Pallas kernels, ladder_call(): pl.pallas_call(functools.partial(ladder_kernel, vir_count, layout), grid=...  40.6 us
    ppermute x6, waiting for transfers between devices, line_gather(): travel[sign] = lax.ppermute(travel[sign], 'occ', pairs)  35.2 us
    pallas_call x2, Pallas kernels, mirror_call(): pl.pallas_call(functools.partial(kernel, arrived.shape[1]), grid=(tile_to...  24.1 us
    all_to_all x2, starting transfers between devices, body(): lax.all_to_all(packed.reshape(tile_total * vir_count, rows, block), ('occ...  11.7 us
    ppermute x6, starting transfers between devices, line_gather(): travel[sign] = lax.ppermute(travel[sign], 'occ', pairs)  10.8 us
    ppermute x6, starting transfers between devices, line_gather(): across = lax.ppermute(travel[sign], 'occ', [(t, t ^ 1) for t in holders])  8.8 us
    all_gather x1, waiting for transfers between devices, body(): lax.all_gather(later, 'occ', axis=0, tiled=True)  8.57 us
  transfers between devices with their start and end apart: 16, of which 6 were waited for; matrix products, arithmetic and copies ran while one was open for 3% of the time, Pallas kernels for 23%

profile of v4, /device:TPU:0, one launch (start us, length us, event | category | flops | bytes accessed | tf_op | source)
XLA Modules:
  0.0 228.0 jit_solution(6396976663542770532)
XLA Ops:
  6.5 0.0 all-gather.2.cloned.1.call-start
  6.5 2.3 screen.1
  8.8 1.3 collective-permute-start
  10.1 5.6 %collective-permute-start.3 = (bf16[512,512]{1,0:T(8,128)(2,1)}, bf16[512,512]{1,0:T(8,128)(2,1)S(1)}, u32[]{:S(2)}, u32[]{:S(2)}) collective-permute-start(bf16[512,512]{1,0:T(8,128)(2,1)} %get-tuple-element.13.refs_0_), channel_id=1, source_target_pairs={{0,8},{4,12},{8,16},{12,20},{16,24},{20,28},{1,9},{5,13},{9,17},{1... | collective-permute-start | bytes 1572872 | tf_op jit(solution)/shard_map/ppermute | solution.py:81
  15.7 10.2 %collective-permute-done.refs_2_ = bf16[512,512]{1,0:T(8,128)(2,1)S(1)} collective-permute-done((bf16[512,512]{1,0:T(8,128)(2,1)}, bf16[512,512]{1,0:T(8,128)(2,1)S(1)}, u32[]{:S(2)}, u32[]{:S(2)}) %collective-permute-start) | collective-permute-done | bytes 524320 | tf_op jit(solution)/shard_map/ppermute | solution.py:81
  25.9 1.3 collective-permute-start.1
  27.1 0.0 collective-permute-done.3.refs_4_
  27.1 0.0 copy-start.4
  27.2 0.7 collective-permute-start.4
  27.9 13.0 %collective-permute-done.1.refs_6_ = bf16[512,512]{1,0:T(8,128)(2,1)S(1)} collective-permute-done((bf16[512,512]{1,0:T(8,128)(2,1)S(1)}, bf16[512,512]{1,0:T(8,128)(2,1)S(1)}, u32[]{:S(2)}, u32[]{:S(2)}) %collective-permute-start.1) | collective-permute-done | bytes 524320 | tf_op jit(solution)/shard_map/ppermute | solution.py:81
  40.8 1.3 collective-permute-start.2
  42.1 0.0 collective-permute-done.4.refs_8_
  42.2 0.7 collective-permute-start.5
  42.9 12.1 %collective-permute-done.2.refs_10_ = bf16[512,512]{1,0:T(8,128)(2,1)S(1)} collective-permute-done((bf16[512,512]{1,0:T(8,128)(2,1)S(1)}, bf16[512,512]{1,0:T(8,128)(2,1)S(1)}, u32[]{:S(2)}, u32[]{:S(2)}) %collective-permute-start.2) | collective-permute-done | bytes 524320 | tf_op jit(solution)/shard_map/ppermute | solution.py:81
  54.9 0.0 collective-permute-done.5.refs_12_
  54.9 0.0 all-gather.2.cloned.1.call-update
  54.9 0.1 collective-permute-start.6
  55.0 2.4 %collective-permute-start.7 = (bf16[512,512]{1,0:T(8,128)(2,1)S(1)}, bf16[512,512]{1,0:T(8,128)(2,1)}, u32[]{:S(2)}, u32[]{:S(2)}) collective-permute-start(bf16[512,512]{1,0:T(8,128)(2,1)S(1)} %collective-permute-done.refs_2_), channel_id=1, source_target_pairs={{0,4},{4,0},{8,12},{12,8},{16,20},{20,16},{1,5},{5,1},{9,13},{13,9... | collective-permute-start | bytes 1572872 | tf_op jit(solution)/shard_map/ppermute | solution.py:84
  57.4 1.3 copy.8.amp_mask
  58.8 0.7 collective-permute-start.8
  59.5 0.7 collective-permute-start.10
  60.2 1.9 collective-permute-start.9
  62.1 0.0 collective-permute-done.6.refs_1_
  62.1 2.4 %collective-permute-start.11 = (bf16[512,512]{1,0:T(8,128)(2,1)S(1)}, bf16[512,512]{1,0:T(8,128)(2,1)S(1)}, u32[]{:S(2)}, u32[]{:S(2)}) collective-permute-start(bf16[512,512]{1,0:T(8,128)(2,1)S(1)} %collective-permute-done.2.refs_10_), channel_id=1, source_target_pairs={{0,4},{4,0},{1,5},{5,1},{2,6},{6,2},{3,7},{7,3}} | collective-permute-start | bytes 1572872 | tf_op jit(solution)/shard_map/ppermute | solution.py:84
  64.5 0.0 collective-permute-done.7.refs_3_
  64.5 0.7 collective-permute-start.12
  65.3 0.8 fusion.3.swap_ref
  66.0 0.9 fusion.2.perm_ref
  67.0 0.0 collective-permute-done.8.refs_5_
  67.0 0.0 collective-permute-done.10.refs_9_
  67.0 0.0 copy-start.10
  67.0 0.0 collective-permute-done.9.refs_7_
  67.0 0.0 collective-permute-done.11.refs_11_
  67.0 0.0 collective-permute-done.12.refs_13_
  67.0 0.0 copy-done.3
  67.0 0.0 copy-done.4
  67.1 0.0 copy-done.5
  67.1 0.0 copy-done.6
  67.1 0.0 copy-done.7
  67.1 0.0 copy-done.8
  67.1 0.7 copy-done.9
  67.8 0.2 copy-done.10
  68.0 0.2 copy-done.11
  68.1 0.1 copy-done.12
  68.3 0.8 copy-done.13
  69.1 20.9 %ladder.3 = (f32[2048,512]{1,0:T(8,128)}, s16[8,4,272,128]{3,2,1,0:T(8,128)(2,1)}) custom-call(s32[8,4]{1,0:T(8,128)} %copy.8.amp_mask, s32[8]{0:T(128)} %numbers.3, bf16[2048,4096]{1,0:T(8,128)(2,1)} %rows_ref.3, bf16[256,256]{1,0:T(8,128)(2,1)} %fusion.3.swap_ref, bf16[512,512]{1,0:T(8,128)(2,1)} %fusion.2.perm_ref, ...), custom_call_target="tpu_custom_call" | custom-call | flops 11811160064 | bytes 27262976 | tf_op jit(solution)/shard_map/ladder/pallas_call | solution.py:163
  90.0 7.7 %all-to-all-start.1 = ((s16[32,272,128]{2,1,0:T(8,128)(2,1)}), s16[32,272,128]{2,1,0:T(8,128)(2,1)S(1)}, u32[]{:S(2)}, u32[]{:S(2)}) async-start(s16[32,272,128]{2,1,0:T(8,128)(2,1)} %bitcast.9), calls=%async_computation.1 | async-start | bytes 4456448 | tf_op jit(solution)/shard_map/all_to_all | solution.py:289
  97.8 8.6 %all-gather.2.cloned.1.call-done.refs_0_ = bf16[4096,512]{1,0:T(8,128)(2,1)} async-done(((bf16[512,512]{1,0:T(8,128)(2,1)}), bf16[4096,512]{1,0:T(8,128)(2,1)}) %all-gather.2.cloned.1.call-update) | async-done | bytes 4194320 | tf_op jit(solution)/shard_map/all_gather | solution.py:264
  106.3 19.7 %ladder.2 = (f32[2048,512]{1,0:T(8,128)}, s16[8,4,272,128]{3,2,1,0:T(8,128)(2,1)}) custom-call(s32[8,4]{1,0:T(8,128)} %copy.8.amp_mask, s32[8]{0:T(128)} %numbers.3, bf16[2048,4096]{1,0:T(8,128)(2,1)} %rows_ref.3, bf16[256,256]{1,0:T(8,128)(2,1)} %fusion.3.swap_ref, bf16[512,512]{1,0:T(8,128)(2,1)} %fusion.2.perm_ref, ...), custom_call_target="tpu_custom_call" | custom-call | flops 11811160064 | bytes 27262976 | tf_op jit(solution)/shard_map/ladder/pallas_call | solution.py:163
  126.0 24.6 %all-to-all-done.1 = s16[32,272,128]{2,1,0:T(8,128)(2,1)S(1)} async-done(((s16[32,272,128]{2,1,0:T(8,128)(2,1)}), s16[32,272,128]{2,1,0:T(8,128)(2,1)S(1)}, u32[]{:S(2)}, u32[]{:S(2)}) %all-to-all-start.1) | async-done | bytes 2228256 | tf_op jit(solution)/shard_map/all_to_all | solution.py:289
  150.7 1.4 copy-done
  152.1 4.0 %all-to-all-start = ((s16[32,272,128]{2,1,0:T(8,128)(2,1)}), s16[32,272,128]{2,1,0:T(8,128)(2,1)}, u32[]{:S(2)}, u32[]{:S(2)}) async-start(s16[32,272,128]{2,1,0:T(8,128)(2,1)} %bitcast.8), calls=%async_computation | async-start | bytes 4456448 | tf_op jit(solution)/shard_map/all_to_all | solution.py:289
  156.1 0.1 reshape.179
  156.2 0.1 broadcast_add_fusion
  156.2 0.1 add.222
  156.3 0.1 dynamic_slice.6
  156.4 0.1 broadcast_add_fusion.1
  156.5 0.7 add.216.vir_ref
  157.2 1.2 fusion.1.spread_ref
  158.4 1.2 fusion.spread_ref
  159.6 11.9 %add.286.refs_0_ = f32[2048,1024]{1,0:T(8,128)} custom-call(bf16[512,1024]{1,0:T(8,128)(2,1)} %fusion.1.spread_ref, s16[8,4,272,128]{3,2,1,0:T(8,128)(2,1)} %bitcast.7, f32[2048,512]{1,0:T(8,128)} %get-tuple-element.17.refs_0_, f32[2048,512]{1,0:T(8,128)} %get-tuple-element.18.refs_1_), custom_call_target="tpu_custom_call" | custom-call | flops 4294967296 | bytes 18874368 | tf_op jit(solution)/shard_map/add/pallas_call | solution.py:228
  171.5 36.1 %all-to-all-done = s16[32,272,128]{2,1,0:T(8,128)(2,1)} async-done(((s16[32,272,128]{2,1,0:T(8,128)(2,1)}), s16[32,272,128]{2,1,0:T(8,128)(2,1)}, u32[]{:S(2)}, u32[]{:S(2)}) %all-to-all-start) | async-done | bytes 2228256 | tf_op jit(solution)/shard_map/all_to_all | solution.py:289
  207.6 1.3 broadcast_in_dim.2.occ_ref
  208.9 12.3 %update.1 = f32[2048,1024]{1,0:T(8,128)} custom-call(bf16[512,1024]{1,0:T(8,128)(2,1)} %fusion.spread_ref, s16[8,4,272,128]{3,2,1,0:T(8,128)(2,1)} %bitcast.2.arrived_ref, f32[1,1024]{1,0:T(1,128)} %add.216.vir_ref, f32[2048,128]{1,0:T(8,128)} %broadcast_in_dim.2.occ_ref, f32[2048,1024]{1,0:T(8,128)} %add.286.refs_0_), custom_call_target="tpu_custom_call" | custom-call | flops 4294967296 | bytes 18874368 | tf_op jit(solution)/shard_map/update/pallas_call | solution.py:228
  (19 shorter events, 0.1 us)
Async XLA Ops:
  6.5 99.8 %all-gather.2.cloned.1.call-start = ((), (), s32[]{:S(2)}) async-start(), calls=%async_computation.2 | async-start | bytes 4718592 | tf_op jit(solution)/shard_map/all_gather | solution.py:264
  8.8 17.0 %collective-permute-start = (bf16[512,512]{1,0:T(8,128)(2,1)}, bf16[512,512]{1,0:T(8,128)(2,1)S(1)}, u32[]{:S(2)}, u32[]{:S(2)}) collective-permute-start(bf16[512,512]{1,0:T(8,128)(2,1)} %get-tuple-element.13.refs_0_), channel_id=1, source_target_pairs={{8,0},{12,4},{16,8},{20,12},{24,16},{28,20},{9,1},{13,5},{17,9},{2... | collective-permute-start | bytes 1572872 | tf_op jit(solution)/shard_map/ppermute | solution.py:81
  10.1 17.1 %collective-permute-start.3 = (bf16[512,512]{1,0:T(8,128)(2,1)}, bf16[512,512]{1,0:T(8,128)(2,1)S(1)}, u32[]{:S(2)}, u32[]{:S(2)}) collective-permute-start(bf16[512,512]{1,0:T(8,128)(2,1)} %get-tuple-element.13.refs_0_), channel_id=1, source_target_pairs={{0,8},{4,12},{8,16},{12,20},{16,24},{20,28},{1,9},{5,13},{9,17},{1... | collective-permute-start | bytes 1572872 | tf_op jit(solution)/shard_map/ppermute | solution.py:81
  25.8 41.2 %copy-start.3 = (bf16[512,512]{1,0:T(8,128)(2,1)}, bf16[512,512]{1,0:T(8,128)(2,1)S(1)}, u32[]{:S(2)}) copy-start(bf16[512,512]{1,0:T(8,128)(2,1)S(1)} %collective-permute-done.refs_2_) | copy-start | bytes 1572868
  25.9 15.0 %collective-permute-start.1 = (bf16[512,512]{1,0:T(8,128)(2,1)S(1)}, bf16[512,512]{1,0:T(8,128)(2,1)S(1)}, u32[]{:S(2)}, u32[]{:S(2)}) collective-permute-start(bf16[512,512]{1,0:T(8,128)(2,1)S(1)} %collective-permute-done.refs_2_), channel_id=1, source_target_pairs={{8,0},{12,4},{16,8},{20,12},{9,1},{13,5},{17,9},{21,13},{10,2},{14... | collective-permute-start | bytes 1572872 | tf_op jit(solution)/shard_map/ppermute | solution.py:81
  27.1 39.9 %copy-start.4 = (bf16[512,512]{1,0:T(8,128)(2,1)}, bf16[512,512]{1,0:T(8,128)(2,1)S(1)}, u32[]{:S(2)}) copy-start(bf16[512,512]{1,0:T(8,128)(2,1)S(1)} %collective-permute-done.3.refs_4_) | copy-start | bytes 1572868
  27.2 15.0 %collective-permute-start.4 = (bf16[512,512]{1,0:T(8,128)(2,1)S(1)}, bf16[512,512]{1,0:T(8,128)(2,1)S(1)}, u32[]{:S(2)}, u32[]{:S(2)}) collective-permute-start(bf16[512,512]{1,0:T(8,128)(2,1)S(1)} %collective-permute-done.3.refs_4_), channel_id=1, source_target_pairs={{8,16},{12,20},{16,24},{20,28},{9,17},{13,21},{17,25},{21,29},{10,... | collective-permute-start | bytes 1572872 | tf_op jit(solution)/shard_map/ppermute | solution.py:81
  40.8 26.2 %copy-start.5 = (bf16[512,512]{1,0:T(8,128)(2,1)}, bf16[512,512]{1,0:T(8,128)(2,1)S(1)}, u32[]{:S(2)}) copy-start(bf16[512,512]{1,0:T(8,128)(2,1)S(1)} %collective-permute-done.1.refs_6_) | copy-start | bytes 1572868
  40.8 14.1 %collective-permute-start.2 = (bf16[512,512]{1,0:T(8,128)(2,1)S(1)}, bf16[512,512]{1,0:T(8,128)(2,1)S(1)}, u32[]{:S(2)}, u32[]{:S(2)}) collective-permute-start(bf16[512,512]{1,0:T(8,128)(2,1)S(1)} %collective-permute-done.1.refs_6_), channel_id=1, source_target_pairs={{8,0},{12,4},{9,1},{13,5},{10,2},{14,6},{11,3},{15,7}} | collective-permute-start | bytes 1572872 | tf_op jit(solution)/shard_map/ppermute | solution.py:81
  42.1 24.9 %copy-start.6 = (bf16[512,512]{1,0:T(8,128)(2,1)}, bf16[512,512]{1,0:T(8,128)(2,1)S(1)}, u32[]{:S(2)}) copy-start(bf16[512,512]{1,0:T(8,128)(2,1)S(1)} %collective-permute-done.4.refs_8_) | copy-start | bytes 1572868
  42.2 12.8 %collective-permute-start.5 = (bf16[512,512]{1,0:T(8,128)(2,1)S(1)}, bf16[512,512]{1,0:T(8,128)(2,1)S(1)}, u32[]{:S(2)}, u32[]{:S(2)}) collective-permute-start(bf16[512,512]{1,0:T(8,128)(2,1)S(1)} %collective-permute-done.4.refs_8_), channel_id=1, source_target_pairs={{16,24},{20,28},{17,25},{21,29},{18,26},{22,30},{19,27},{23,31}} | collective-permute-start | bytes 1572872 | tf_op jit(solution)/shard_map/ppermute | solution.py:81
  54.9 12.2 %copy-start.7 = (bf16[512,512]{1,0:T(8,128)(2,1)}, bf16[512,512]{1,0:T(8,128)(2,1)S(1)}, u32[]{:S(2)}) copy-start(bf16[512,512]{1,0:T(8,128)(2,1)S(1)} %collective-permute-done.2.refs_10_) | copy-start | bytes 1572868
  54.9 12.2 %copy-start.8 = (bf16[512,512]{1,0:T(8,128)(2,1)}, bf16[512,512]{1,0:T(8,128)(2,1)S(1)}, u32[]{:S(2)}) copy-start(bf16[512,512]{1,0:T(8,128)(2,1)S(1)} %collective-permute-done.5.refs_12_) | copy-start | bytes 1572868
  54.9 7.2 %collective-permute-start.6 = (bf16[512,512]{1,0:T(8,128)(2,1)}, bf16[512,512]{1,0:T(8,128)(2,1)}, u32[]{:S(2)}, u32[]{:S(2)}) collective-permute-start(bf16[512,512]{1,0:T(8,128)(2,1)} %get-tuple-element.13.refs_0_), channel_id=1, source_target_pairs={{0,4},{4,0},{8,12},{12,8},{16,20},{20,16},{24,28},{28,24},{1,5},{5... | collective-permute-start | bytes 1572872 | tf_op jit(solution)/shard_map/ppermute | solution.py:71
  55.0 9.5 %collective-permute-start.7 = (bf16[512,512]{1,0:T(8,128)(2,1)S(1)}, bf16[512,512]{1,0:T(8,128)(2,1)}, u32[]{:S(2)}, u32[]{:S(2)}) collective-permute-start(bf16[512,512]{1,0:T(8,128)(2,1)S(1)} %collective-permute-done.refs_2_), channel_id=1, source_target_pairs={{0,4},{4,0},{8,12},{12,8},{16,20},{20,16},{1,5},{5,1},{9,13},{13,9... | collective-permute-start | bytes 1572872 | tf_op jit(solution)/shard_map/ppermute | solution.py:84
  58.8 8.2 %collective-permute-start.8 = (bf16[512,512]{1,0:T(8,128)(2,1)S(1)}, bf16[512,512]{1,0:T(8,128)(2,1)S(1)}, u32[]{:S(2)}, u32[]{:S(2)}) collective-permute-start(bf16[512,512]{1,0:T(8,128)(2,1)S(1)} %collective-permute-done.3.refs_4_), channel_id=1, source_target_pairs={{8,12},{12,8},{16,20},{20,16},{24,28},{28,24},{9,13},{13,9},{17,21... | collective-permute-start | bytes 1572872 | tf_op jit(solution)/shard_map/ppermute | solution.py:84
  59.5 7.5 %collective-permute-start.10 = (bf16[512,512]{1,0:T(8,128)(2,1)S(1)}, bf16[512,512]{1,0:T(8,128)(2,1)S(1)}, u32[]{:S(2)}, u32[]{:S(2)}) collective-permute-start(bf16[512,512]{1,0:T(8,128)(2,1)S(1)} %collective-permute-done.4.refs_8_), channel_id=1, source_target_pairs={{16,20},{20,16},{24,28},{28,24},{17,21},{21,17},{25,29},{29,25},{1... | collective-permute-start | bytes 1572872 | tf_op jit(solution)/shard_map/ppermute | solution.py:84
  60.2 6.8 %collective-permute-start.9 = (bf16[512,512]{1,0:T(8,128)(2,1)S(1)}, bf16[512,512]{1,0:T(8,128)(2,1)S(1)}, u32[]{:S(2)}, u32[]{:S(2)}) collective-permute-start(bf16[512,512]{1,0:T(8,128)(2,1)S(1)} %collective-permute-done.1.refs_6_), channel_id=1, source_target_pairs={{0,4},{4,0},{8,12},{12,8},{1,5},{5,1},{9,13},{13,9},{2,6},{6,2},{1... | collective-permute-start | bytes 1572872 | tf_op jit(solution)/shard_map/ppermute | solution.py:84
  62.1 4.9 %collective-permute-start.11 = (bf16[512,512]{1,0:T(8,128)(2,1)S(1)}, bf16[512,512]{1,0:T(8,128)(2,1)S(1)}, u32[]{:S(2)}, u32[]{:S(2)}) collective-permute-start(bf16[512,512]{1,0:T(8,128)(2,1)S(1)} %collective-permute-done.2.refs_10_), channel_id=1, source_target_pairs={{0,4},{4,0},{1,5},{5,1},{2,6},{6,2},{3,7},{7,3}} | collective-permute-start | bytes 1572872 | tf_op jit(solution)/shard_map/ppermute | solution.py:84
  64.5 2.5 %collective-permute-start.12 = (bf16[512,512]{1,0:T(8,128)(2,1)S(1)}, bf16[512,512]{1,0:T(8,128)(2,1)S(1)}, u32[]{:S(2)}, u32[]{:S(2)}) collective-permute-start(bf16[512,512]{1,0:T(8,128)(2,1)S(1)} %collective-permute-done.5.refs_12_), channel_id=1, source_target_pairs={{24,28},{28,24},{25,29},{29,25},{26,30},{30,26},{27,31},{31,27}} | collective-permute-start | bytes 1572872 | tf_op jit(solution)/shard_map/ppermute | solution.py:84
  67.0 0.8 copy-start.9
  67.0 1.0 copy-start.10
  67.0 1.1 copy-start.11
  67.0 1.3 copy-start.12
  68.3 0.8 copy-start.13
  90.0 60.6 %all-to-all-start.1 = ((s16[32,272,128]{2,1,0:T(8,128)(2,1)}), s16[32,272,128]{2,1,0:T(8,128)(2,1)S(1)}, u32[]{:S(2)}, u32[]{:S(2)}) async-start(s16[32,272,128]{2,1,0:T(8,128)(2,1)} %bitcast.9), calls=%async_computation.1 | async-start | bytes 4456448 | tf_op jit(solution)/shard_map/all_to_all | solution.py:289
  150.7 1.4 copy-start
  150.7 5.4 %copy-start.1 = (f32[128]{0:T(128)S(1)}, f32[128]{0:T(128)}, u32[]{:S(2)}) copy-start(f32[128]{0:T(128)} %param.12) | copy-start | bytes 1540
  150.7 5.7 %copy-start.2 = (f32[64]{0:T(128)S(1)}, f32[64]{0:T(128)}, u32[]{:S(2)}) copy-start(f32[64]{0:T(128)} %param.13) | copy-start | bytes 772
  152.1 55.5 %all-to-all-start = ((s16[32,272,128]{2,1,0:T(8,128)(2,1)}), s16[32,272,128]{2,1,0:T(8,128)(2,1)}, u32[]{:S(2)}, u32[]{:S(2)}) async-start(s16[32,272,128]{2,1,0:T(8,128)(2,1)} %bitcast.8), calls=%async_computation | async-start | bytes 4456448 | tf_op jit(solution)/shard_map/all_to_all | solution.py:289
Sparse Core Ops, SparseCore 0:
  55.1 51.2 all-gather.1

commit v5 on v4

--- a/solution.py
+++ b/solution.py
@@ -69,8 +69,11 @@
 def line_gather(part, tile_total):
     chips = tile_total // CORES
     partner = lambda array: lax.ppermute(array, "occ", [(t, t ^ 1) for t in range(tile_total)])
-    pieces = [(0, 0, False, part), (0, 0, True, partner(part))]
+    across = partner(part)
+    pieces = [(0, 0, False, part), (0, 0, True, across)]
     travel = {1: part, -1: part}
+    crossed = [across]
+    reached = []
     for step in range(1, chips):
         for sign in (1, -1):
             pairs = []
@@ -79,12 +82,17 @@
                 if 0 <= chip + sign * step < chips:
                     pairs.append((t + sign * CORES, t))
             travel[sign] = lax.ppermute(travel[sign], "occ", pairs)
+        reached.append(tuple(travel.values()))
+        latest = []
         for sign in (1, -1):
             holders = [t for t in range(tile_total) if 0 <= t // CORES + sign * step < chips]
             across = lax.ppermute(travel[sign], "occ", [(t, t ^ 1) for t in holders])
             pieces.append((sign, step, False, travel[sign]))
             pieces.append((sign, step, True, across))
-    return pieces, travel
+            latest.append(across)
+        travel[1], travel[-1], *_ = lax.optimization_barrier((travel[1], travel[-1], *crossed))
+        crossed = latest
+    return pieces, reached
 
 
 def fill_slab(layout, slab_rows, refs, slab_scr, sems):
@@ -106,7 +114,7 @@
     each(lambda copy: copy.wait())
 
 
-def ladder_kernel(vir_count, layout, amp_mask, numbers, rows_ref, swap_ref, perm_ref, *refs):
+def ladder_kernel(vir_count, layout, amp_mask, numbers, rows_ref, perm_ref, *refs):
     pieces, (ladder_ref, packed_ref) = refs[: len(layout)], refs[len(layout) : len(layout) + 2]
     tile = pl.program_id(0)
     cols = perm_ref.shape[1]
@@ -134,10 +142,9 @@
     nonzero = (pair // ORBITALS_IN_GRP < own_number) & (pair % ORBITALS_IN_GRP < numbers[tile])
     ladder = jnp.where(nonzero, ladder, 0.0)
     ladder_ref[...] = ladder
-    high, low_part = split(ladder)
-    mirror = dot(dot(swap_ref[...], high).astype(jnp.bfloat16), perm_ref[...]) + dot(
-        dot(swap_ref[...], low_part).astype(jnp.bfloat16), perm_ref[...]
-    )
+    by_place = ladder.reshape(ORBITALS_IN_GRP, ORBITALS_IN_GRP, cols)
+    high, low_part = split(jnp.swapaxes(by_place, 0, 1).reshape(PAIR_SQ, cols))
+    mirror = dot(high, perm_ref[...]) + dot(low_part, perm_ref[...])
     most = jnp.maximum(jnp.max(jnp.abs(mirror), axis=0, keepdims=True), 1e-30)
     code = jnp.ceil(jnp.log2(most) * STEPS)
     coded = jnp.round(mirror * (TOP / scale_of(code))).astype(jnp.int32).astype(jnp.int16)
@@ -148,7 +155,7 @@
         packed_ref[0, v, PAIR_SQ:] = code_rows[:, v * block : (v + 1) * block]
 
 
-def ladder_call(tile_total, vir_count, layout, amp_mask, numbers, amplitudes, swap, perm, slab_parts):
+def ladder_call(tile_total, vir_count, layout, amp_mask, numbers, amplitudes, perm, slab_parts):
     cols = perm.shape[1]
     block = cols // vir_count
     smem = pl.BlockSpec(memory_space=pltpu.SMEM)
@@ -167,7 +174,6 @@
             smem,
             smem,
             pl.BlockSpec((PAIR_SQ, W * W), lambda tile: (tile, 0)),
-            pl.BlockSpec(swap.shape, whole),
             pl.BlockSpec(perm.shape, whole),
         ]
         + slab_specs,
@@ -182,15 +188,15 @@
         scratch_shapes=scratch,
         compiler_params=pltpu.CompilerParams(vmem_limit_bytes=VMEM_LIMIT),
         cost_estimate=pl.CostEstimate(
-            flops=2 * rows * cols * (W * W + 2 * PAIR_SQ + 2 * cols),
+            flops=2 * rows * cols * (W * W + 2 * cols),
             bytes_accessed=rows * (W * W * 2 + cols * 6) + W * W * cols * 2,
             transcendentals=0,
         ),
         name="ladder",
-    )(amp_mask, numbers, amplitudes, swap, perm, *slab_parts)
-
-
-def mirror_of(vir_count, arrived_ref, spread_ref):
+    )(amp_mask, numbers, amplitudes, perm, *slab_parts)
+
+
+def decoded(vir_count, arrived_ref):
     highs, lows = [], []
     for v in range(vir_count):
         code = arrived_ref[0, v, PAIR_SQ:].astype(jnp.int32).astype(jnp.float32)[:1]
@@ -198,35 +204,40 @@
         high, low = split(values * (scale_of(code) * (1.0 / TOP)))
         highs.append(high)
         lows.append(low)
-    return dot(jnp.concatenate(highs, axis=1), spread_ref[...]) + dot(jnp.concatenate(lows, axis=1), spread_ref[...])
-
-
-def add_kernel(vir_count, spread_ref, arrived_ref, *refs):
-    ladders, total_ref = refs[:-1], refs[-1]
-    mirror = mirror_of(vir_count, arrived_ref, spread_ref)
-    cols = ladders[0].shape[1]
-    for c, ladder_ref in enumerate(ladders):
-        at = slice(c * cols, (c + 1) * cols)
-        total_ref[:, at] = ladder_ref[...] + mirror[:, at]
-
-
-def update_kernel(vir_count, spread_ref, arrived_ref, vir_ref, occ_ref, *refs):
-    totals, update_ref = refs[:-1], refs[-1]
-    mirror = mirror_of(vir_count, arrived_ref, spread_ref)
-    cols = totals[0].shape[1]
-    for c, total_ref in enumerate(totals):
-        at = slice(c * cols, (c + 1) * cols)
-        denominator = vir_ref[:, at] - occ_ref[:, :1]
-        update_ref[:, at] = (total_ref[...] + mirror[:, at]) / denominator
-
-
-def mirror_call(kernel, name, tile_total, spread, arrived, energies, totals):
-    slab_cols = spread.shape[1]
+    return highs, lows
+
+
+def mirror_halves(vir_count, halves, spread_ref, arrived_ref, totals):
+    parts = decoded(vir_count, arrived_ref)
+    lanes = parts[0][0].shape[1] // halves
+    cols = spread_ref.shape[1]
+    for h in range(halves):
+        high, low = [
+            jnp.concatenate([block[:, h * lanes : (h + 1) * lanes] for block in blocks], axis=1) for blocks in parts
+        ]
+        mirror = dot(high, spread_ref[...]) + dot(low, spread_ref[...])
+        at = slice(h * cols, (h + 1) * cols)
+        total = totals[h][...] if len(totals) == halves else totals[0][:, at]
+        yield at, total + mirror
+
+
+def add_kernel(vir_count, halves, spread_ref, arrived_ref, *refs):
+    for at, total in mirror_halves(vir_count, halves, spread_ref, arrived_ref, refs[:-1]):
+        refs[-1][:, at] = total
+
+
+def update_kernel(vir_count, halves, spread_ref, arrived_ref, vir_ref, occ_ref, *refs):
+    for at, total in mirror_halves(vir_count, halves, spread_ref, arrived_ref, refs[:-1]):
+        refs[-1][:, at] = total / (vir_ref[:, at] - occ_ref[:, :1])
+
+
+def mirror_call(kernel, name, tile_total, halves, spread, arrived, energies, totals):
+    slab_cols = spread.shape[1] * halves
     rows = tile_total * PAIR_SQ
     by_tile = lambda tile: (tile, 0)
     energy_specs = [pl.BlockSpec((1, slab_cols), lambda tile: (0, 0)), pl.BlockSpec((PAIR_SQ, 128), by_tile)]
     return pl.pallas_call(
-        functools.partial(kernel, arrived.shape[1]),
+        functools.partial(kernel, arrived.shape[1], halves),
         grid=(tile_total,),
         in_specs=[
             pl.BlockSpec(spread.shape, lambda tile: (0, 0)),
@@ -257,19 +268,19 @@
     block = chunk_cols // vir_count
 
     screened = screen_call(chunks, int_mask, integrals)
-    pieces, last = line_gather(screened[0], tile_total)
+    pieces, reached = line_gather(screened[0], tile_total)
     slabs = [([piece[:3] for piece in pieces], [piece[3] for piece in pieces])]
     if chunks > 1:
-        later, _, _ = lax.optimization_barrier((screened[1], last[1], last[-1]))
+        later, *_ = lax.optimization_barrier((screened[1], *reached[-2]) if len(reached) > 1 else (screened[1],))
         slabs.append(([(0, 0, False)], [lax.all_gather(later, "occ", axis=0, tiled=True)]))
 
-    pair = jnp.arange(PAIR_SQ)
-    swap = one_hot_of(pair % ORBITALS_IN_GRP * ORBITALS_IN_GRP + pair // ORBITALS_IN_GRP, PAIR_SQ)
     col = jnp.arange(chunk_cols)
     a, b = col // W, col % W
     perm = one_hot_of(b // vir_span * block + b % vir_span * chunk_span + a, chunk_cols)
-    place = jnp.arange(chunk_cols)
-    sender, here, there = place // block, place % block // chunk_span, place % chunk_span
+    halves = chunks
+    lanes = block // halves
+    place = jnp.arange(vir_count * lanes)
+    sender, here, there = place // lanes, place % lanes // chunk_span, place % chunk_span
     to_column = here * W + sender * vir_span + there
 
     occ_table = occ_energy.reshape(tile_total, ORBITALS_IN_GRP)
@@ -283,7 +294,7 @@
     ladders, arrived = [], []
     for layout, slab_parts in slabs:
         ladder, packed = ladder_call(
-            tile_total, vir_count, layout, amp_mask[0], group_orbital_numbers, amplitudes, swap, perm, slab_parts
+            tile_total, vir_count, layout, amp_mask[0], group_orbital_numbers, amplitudes, perm, slab_parts
         )
         rows = PAIR_SQ + CODE_ROWS
         moved = lax.all_to_all(
@@ -291,12 +302,12 @@
         )
         ladders.append(ladder)
         arrived.append(moved.reshape(tile_total, vir_count, rows, block))
-    spreads = [one_hot_of(to_column + c * chunk_span, slab_cols) for c in range(chunks)]
+    spreads = [one_hot_of(to_column + c * chunk_span, slab_cols // halves) for c in range(chunks)]
     totals = ladders
     for c in range(chunks - 1):
-        totals = [mirror_call(add_kernel, "add", tile_total, spreads[c], arrived[c], [], totals)]
+        totals = [mirror_call(add_kernel, "add", tile_total, halves, spreads[c], arrived[c], [], totals)]
     return mirror_call(
-        update_kernel, "update", tile_total, spreads[-1], arrived[-1], [vir_sum, occ_sum], totals
+        update_kernel, "update", tile_total, halves, spreads[-1], arrived[-1], [vir_sum, occ_sum], totals
     )
 
 

time: 229 us -> 252 us (1.10)
  waiting for transfers between devices: 105 us -> 136 us
  Pallas kernels: 67 us -> 62.8 us
  local copies, waits for them, and re-layouts: 6.98 us -> 3.66 us
    ppermute x6, waiting for transfers between devices: 35.2 us -> 63.9 us  [line_gather(): travel[sign] = lax.ppermute(travel[sign], 'occ', pairs)]
    all_to_all x2, waiting for transfers between devices: 60.7 us -> 70.6 us  [body(): lax.all_to_all(packed.reshape(tile_total * vir_count, rows, block), ('occ...]
    all_gather x1, waiting for transfers between devices: 8.57 us -> 0.02 us  [body(): lax.all_gather(later, 'occ', axis=0, tiled=True)]
    unnamed x28 -> x20, local copies, waits for them, and re-layouts: 3.4 us -> 0.04 us
    pallas_call x2, Pallas kernels: 40.6 us -> 37.8 us  [ladder_call(): pl.pallas_call(functools.partial(ladder_kernel, vir_count, layout), grid=...]
  transfers between devices with their start and end apart: 16 -> 16, of which waited for: 6 -> 7; matrix products, arithmetic and copies ran while one was open for 3% -> 2% of each run, Pallas kernels for 23% -> 20%
where the time goes in v5:
time: 252 us; the launch traced here: 251 us
  waiting for transfers between devices  136 us (54%)
  Pallas kernels  62.8 us (25%)
  starting transfers between devices  32.4 us (13%)
  between operations  13.6 us (5%)
  local copies, waits for them, and re-layouts  3.66 us (1%)
  other arithmetic  2.77 us (1%)
    all_to_all x2, waiting for transfers between devices, body(): lax.all_to_all(packed.reshape(tile_total * vir_count, rows, block), ('occ...  70.6 us
    ppermute x6, waiting for transfers between devices, line_gather(): travel[sign] = lax.ppermute(travel[sign], 'occ', pairs)  63.9 us
    pallas_call x2, Pallas kernels, ladder_call(): pl.pallas_call(functools.partial(ladder_kernel, vir_count, layout), grid=...  37.8 us
    pallas_call x2, Pallas kernels, mirror_call(): pl.pallas_call(functools.partial(kernel, arrived.shape[1], halves), grid=...  22.7 us
    ppermute x6, starting transfers between devices, line_gather(): travel[sign] = lax.ppermute(travel[sign], 'occ', pairs)  11.6 us
    all_to_all x2, starting transfers between devices, body(): lax.all_to_all(packed.reshape(tile_total * vir_count, rows, block), ('occ...  11.2 us
    ppermute x6, starting transfers between devices, line_gather(): across = lax.ppermute(travel[sign], 'occ', [(t, t ^ 1) for t in holders])  9.47 us
  transfers between devices with their start and end apart: 16, of which 7 were waited for; matrix products, arithmetic and copies ran while one was open for 2% of the time, Pallas kernels for 20%

profile of v5, /device:TPU:0, one launch (start us, length us, event | category | flops | bytes accessed | tf_op | source)
XLA Modules:
  0.0 251.0 jit_solution(9861160749432929620)
XLA Ops:
  6.5 0.0 all-gather.2.cloned.1.call-start
  6.5 2.3 screen.1
  8.8 1.3 collective-permute-start
  10.1 5.6 %collective-permute-start.1 = (bf16[512,512]{1,0:T(8,128)(2,1)}, bf16[512,512]{1,0:T(8,128)(2,1)S(1)}, u32[]{:S(2)}, u32[]{:S(2)}) collective-permute-start(bf16[512,512]{1,0:T(8,128)(2,1)} %get-tuple-element.17.refs_0_), channel_id=1, source_target_pairs={{0,8},{4,12},{8,16},{12,20},{16,24},{20,28},{1,9},{5,13},{9,17},{1... | collective-permute-start | bytes 1572872 | tf_op jit(solution)/shard_map/ppermute | solution.py:84
  15.7 0.1 collective-permute-start.2
  15.8 10.1 %collective-permute-done.refs_2_ = bf16[512,512]{1,0:T(8,128)(2,1)S(1)} collective-permute-done((bf16[512,512]{1,0:T(8,128)(2,1)}, bf16[512,512]{1,0:T(8,128)(2,1)S(1)}, u32[]{:S(2)}, u32[]{:S(2)}) %collective-permute-start) | collective-permute-done | bytes 524320 | tf_op jit(solution)/shard_map/ppermute | solution.py:84
  25.9 0.0 copy-start.3
  25.9 1.3 collective-permute-done.1.refs_4_
  27.2 0.0 copy-start.4
  27.2 0.0 collective-permute-done.2.refs_1_
  27.2 0.0 copy-start.5
  27.2 1.3 collective-permute-start.3
  28.4 0.7 collective-permute-start.4
  29.1 13.3 %collective-permute-done.3.refs_6_ = bf16[512,512]{1,0:T(8,128)(2,1)S(1)} collective-permute-done((bf16[512,512]{1,0:T(8,128)(2,1)S(1)}, bf16[512,512]{1,0:T(8,128)(2,1)S(1)}, u32[]{:S(2)}, u32[]{:S(2)}) %collective-permute-start.3) | collective-permute-done | bytes 524320 | tf_op jit(solution)/shard_map/ppermute | solution.py:84
  42.5 0.0 copy-start.6
  42.5 0.0 collective-permute-done.4.refs_8_
  42.5 0.0 copy-start.7
  42.5 0.0 all-gather.2.cloned.1.call-update
  42.5 1.9 collective-permute-start.5
  44.4 0.7 collective-permute-start.6
  45.1 1.2 collective-permute-done.5.refs_3_
  46.3 0.0 collective-permute-done.6.refs_5_
  46.3 1.3 collective-permute-start.9
  47.6 1.5 collective-permute-start.11
  49.1 2.0 collective-permute-start.7
  51.2 1.5 collective-permute-start.8
  52.6 39.2 %collective-permute-done.9.refs_10_ = bf16[512,512]{1,0:T(8,128)(2,1)} collective-permute-done((bf16[512,512]{1,0:T(8,128)(2,1)S(1)}, bf16[512,512]{1,0:T(8,128)(2,1)}, u32[]{:S(2)}, u32[]{:S(2)}) %collective-permute-start.9) | collective-permute-done | bytes 524320 | tf_op jit(solution)/shard_map/ppermute | solution.py:84
  91.8 1.9 collective-permute-start.10
  93.8 0.0 collective-permute-done.11.refs_12_
  93.8 0.0 copy-done.9
  93.8 1.5 collective-permute-start.12
  95.3 1.3 copy.8.amp_mask
  96.6 0.9 fusion.perm_ref
  97.5 0.0 collective-permute-done.7.refs_7_
  97.6 0.0 collective-permute-done.8.refs_9_
  97.6 0.0 collective-permute-done.10.refs_11_
  97.6 0.0 collective-permute-done.12.refs_13_
  97.6 0.0 copy-done.3
  97.6 0.0 copy-done.4
  97.6 0.0 copy-done.5
  97.6 0.0 copy-done.6
  97.6 0.0 copy-done.7
  97.6 0.0 copy-done.8
  97.6 19.5 %ladder.3 = (f32[2048,512]{1,0:T(8,128)}, s16[8,4,272,128]{3,2,1,0:T(8,128)(2,1)}) custom-call(s32[8,4]{1,0:T(8,128)} %copy.8.amp_mask, s32[8]{0:T(128)} %numbers.3, bf16[2048,4096]{1,0:T(8,128)(2,1)} %rows_ref.3, bf16[512,512]{1,0:T(8,128)(2,1)} %fusion.perm_ref, bf16[512,512]{1,0:T(8,128)(2,1)} %get-tuple-element.17.refs_0_, bf16[512,512]{1,0:T(8,128)(2,1)} %copy-done.5, ...), custom_call_target="tpu_custom_call" | custom-call | flops 10737418240 | bytes 27262976 | tf_op jit(solution)/shard_map/ladder/pallas_call | solution.py:170
  117.2 6.7 %all-to-all-start.1 = ((s16[32,272,128]{2,1,0:T(8,128)(2,1)}), s16[32,272,128]{2,1,0:T(8,128)(2,1)S(1)}, u32[]{:S(2)}, u32[]{:S(2)}) async-start(s16[32,272,128]{2,1,0:T(8,128)(2,1)} %bitcast.9), calls=%async_computation.1 | async-start | bytes 4456448 | tf_op jit(solution)/shard_map/all_to_all | solution.py:300
  123.8 0.0 all-gather.2.cloned.1.call-done.refs_0_
  123.9 18.3 %ladder.2 = (f32[2048,512]{1,0:T(8,128)}, s16[8,4,272,128]{3,2,1,0:T(8,128)(2,1)}) custom-call(s32[8,4]{1,0:T(8,128)} %copy.8.amp_mask, s32[8]{0:T(128)} %numbers.3, bf16[2048,4096]{1,0:T(8,128)(2,1)} %rows_ref.3, bf16[512,512]{1,0:T(8,128)(2,1)} %fusion.perm_ref, bf16[4096,512]{1,0:T(8,128)(2,1)} %all-gather.2.cloned.1.call-done.refs_0_), custom_call_target="tpu_custom_call" | custom-call | flops 10737418240 | bytes 27262976 | tf_op jit(solution)/shard_map/ladder/pallas_call | solution.py:170
  142.2 33.2 %all-to-all-done.1 = s16[32,272,128]{2,1,0:T(8,128)(2,1)S(1)} async-done(((s16[32,272,128]{2,1,0:T(8,128)(2,1)}), s16[32,272,128]{2,1,0:T(8,128)(2,1)S(1)}, u32[]{:S(2)}, u32[]{:S(2)}) %all-to-all-start.1) | async-done | bytes 2228256 | tf_op jit(solution)/shard_map/all_to_all | solution.py:300
  175.3 4.5 %all-to-all-start = ((s16[32,272,128]{2,1,0:T(8,128)(2,1)}), s16[32,272,128]{2,1,0:T(8,128)(2,1)}, u32[]{:S(2)}, u32[]{:S(2)}) async-start(s16[32,272,128]{2,1,0:T(8,128)(2,1)} %bitcast.8), calls=%async_computation | async-start | bytes 4456448 | tf_op jit(solution)/shard_map/all_to_all | solution.py:300
  179.9 0.0 copy-done.1
  179.9 0.1 reshape.158
  180.0 0.1 broadcast_add_fusion
  180.1 0.1 add.197
  180.2 0.0 copy-done.2
  180.2 0.1 dynamic_slice.6
  180.2 0.1 broadcast_add_fusion.1
  180.3 0.7 add.191.vir_ref
  181.0 0.8 fusion.2.spread_ref
  181.8 0.8 fusion.1.spread_ref
  182.6 0.0 copy-done
  182.6 11.3 %add.241.refs_0_ = f32[2048,1024]{1,0:T(8,128)} custom-call(bf16[256,512]{1,0:T(8,128)(2,1)} %fusion.2.spread_ref, s16[8,4,272,128]{3,2,1,0:T(8,128)(2,1)} %bitcast.7, f32[2048,512]{1,0:T(8,128)} %get-tuple-element.25.refs_0_, f32[2048,512]{1,0:T(8,128)} %get-tuple-element.26.refs_1_), custom_call_target="tpu_custom_call" | custom-call | flops 2147483648 | bytes 18874368 | tf_op jit(solution)/shard_map/add/pallas_call | solution.py:239
  193.9 37.5 %all-to-all-done = s16[32,272,128]{2,1,0:T(8,128)(2,1)} async-done(((s16[32,272,128]{2,1,0:T(8,128)(2,1)}), s16[32,272,128]{2,1,0:T(8,128)(2,1)}, u32[]{:S(2)}, u32[]{:S(2)}) %all-to-all-start) | async-done | bytes 2228256 | tf_op jit(solution)/shard_map/all_to_all | solution.py:300
  231.4 1.4 broadcast_in_dim.2.occ_ref
  232.8 11.4 %update.1 = f32[2048,1024]{1,0:T(8,128)} custom-call(bf16[256,512]{1,0:T(8,128)(2,1)} %fusion.1.spread_ref, s16[8,4,272,128]{3,2,1,0:T(8,128)(2,1)} %bitcast.2.arrived_ref, f32[1,1024]{1,0:T(1,128)} %add.191.vir_ref, f32[2048,128]{1,0:T(8,128)} %broadcast_in_dim.2.occ_ref, f32[2048,1024]{1,0:T(8,128)} %add.241.refs_0_), custom_call_target="tpu_custom_call" | custom-call | flops 2147483648 | bytes 18874368 | tf_op jit(solution)/shard_map/update/pallas_call | solution.py:239
  (9 shorter events, 0.0 us)
Async XLA Ops:
  6.5 117.3 %all-gather.2.cloned.1.call-start = ((), (), s32[]{:S(2)}) async-start(), calls=%async_computation.2 | async-start | bytes 4718592 | tf_op jit(solution)/shard_map/all_gather | solution.py:275
  8.8 17.0 %collective-permute-start = (bf16[512,512]{1,0:T(8,128)(2,1)}, bf16[512,512]{1,0:T(8,128)(2,1)S(1)}, u32[]{:S(2)}, u32[]{:S(2)}) collective-permute-start(bf16[512,512]{1,0:T(8,128)(2,1)} %get-tuple-element.17.refs_0_), channel_id=1, source_target_pairs={{8,0},{12,4},{16,8},{20,12},{24,16},{28,20},{9,1},{13,5},{17,9},{2... | collective-permute-start | bytes 1572872 | tf_op jit(solution)/shard_map/ppermute | solution.py:84
  10.1 17.0 %collective-permute-start.1 = (bf16[512,512]{1,0:T(8,128)(2,1)}, bf16[512,512]{1,0:T(8,128)(2,1)S(1)}, u32[]{:S(2)}, u32[]{:S(2)}) collective-permute-start(bf16[512,512]{1,0:T(8,128)(2,1)} %get-tuple-element.17.refs_0_), channel_id=1, source_target_pairs={{0,8},{4,12},{8,16},{12,20},{16,24},{20,28},{1,9},{5,13},{9,17},{1... | collective-permute-start | bytes 1572872 | tf_op jit(solution)/shard_map/ppermute | solution.py:84
  15.7 11.5 %collective-permute-start.2 = (bf16[512,512]{1,0:T(8,128)(2,1)}, bf16[512,512]{1,0:T(8,128)(2,1)S(1)}, u32[]{:S(2)}, u32[]{:S(2)}) collective-permute-start(bf16[512,512]{1,0:T(8,128)(2,1)} %get-tuple-element.17.refs_0_), channel_id=1, source_target_pairs={{0,4},{4,0},{8,12},{12,8},{16,20},{20,16},{24,28},{28,24},{1,5},{5... | collective-permute-start | bytes 1572872 | tf_op jit(solution)/shard_map/ppermute | solution.py:71
  25.9 71.7 %copy-start.3 = (bf16[512,512]{1,0:T(8,128)(2,1)}, bf16[512,512]{1,0:T(8,128)(2,1)S(1)}, u32[]{:S(2)}) copy-start(bf16[512,512]{1,0:T(8,128)(2,1)S(1)} %collective-permute-done.refs_2_) | copy-start | bytes 1572868
  27.2 70.4 %copy-start.4 = (bf16[512,512]{1,0:T(8,128)(2,1)}, bf16[512,512]{1,0:T(8,128)(2,1)S(1)}, u32[]{:S(2)}) copy-start(bf16[512,512]{1,0:T(8,128)(2,1)S(1)} %collective-permute-done.1.refs_4_) | copy-start | bytes 1572868
  27.2 70.4 %copy-start.5 = (bf16[512,512]{1,0:T(8,128)(2,1)}, bf16[512,512]{1,0:T(8,128)(2,1)S(1)}, u32[]{:S(2)}) copy-start(bf16[512,512]{1,0:T(8,128)(2,1)S(1)} %collective-permute-done.2.refs_1_) | copy-start | bytes 1572868
  27.2 15.3 %collective-permute-start.3 = (bf16[512,512]{1,0:T(8,128)(2,1)S(1)}, bf16[512,512]{1,0:T(8,128)(2,1)S(1)}, u32[]{:S(2)}, u32[]{:S(2)}) collective-permute-start(bf16[512,512]{1,0:T(8,128)(2,1)S(1)} %collective-permute-done.refs_2_), channel_id=1, source_target_pairs={{8,0},{12,4},{16,8},{20,12},{9,1},{13,5},{17,9},{21,13},{10,2},{14... | collective-permute-start | bytes 1572872 | tf_op jit(solution)/shard_map/ppermute | solution.py:84
  28.4 14.0 %collective-permute-start.4 = (bf16[512,512]{1,0:T(8,128)(2,1)S(1)}, bf16[512,512]{1,0:T(8,128)(2,1)S(1)}, u32[]{:S(2)}, u32[]{:S(2)}) collective-permute-start(bf16[512,512]{1,0:T(8,128)(2,1)S(1)} %collective-permute-done.1.refs_4_), channel_id=1, source_target_pairs={{8,16},{12,20},{16,24},{20,28},{9,17},{13,21},{17,25},{21,29},{10,... | collective-permute-start | bytes 1572872 | tf_op jit(solution)/shard_map/ppermute | solution.py:84
  42.5 55.1 %copy-start.6 = (bf16[512,512]{1,0:T(8,128)(2,1)}, bf16[512,512]{1,0:T(8,128)(2,1)S(1)}, u32[]{:S(2)}) copy-start(bf16[512,512]{1,0:T(8,128)(2,1)S(1)} %collective-permute-done.3.refs_6_) | copy-start | bytes 1572868
  42.5 55.1 %copy-start.7 = (bf16[512,512]{1,0:T(8,128)(2,1)}, bf16[512,512]{1,0:T(8,128)(2,1)S(1)}, u32[]{:S(2)}) copy-start(bf16[512,512]{1,0:T(8,128)(2,1)S(1)} %collective-permute-done.4.refs_8_) | copy-start | bytes 1572868
  42.5 3.8 %collective-permute-start.5 = (bf16[512,512]{1,0:T(8,128)(2,1)S(1)}, bf16[512,512]{1,0:T(8,128)(2,1)S(1)}, u32[]{:S(2)}, u32[]{:S(2)}) collective-permute-start(bf16[512,512]{1,0:T(8,128)(2,1)S(1)} %collective-permute-done.refs_2_), channel_id=1, source_target_pairs={{0,4},{4,0},{8,12},{12,8},{16,20},{20,16},{1,5},{5,1},{9,13},{13,9... | collective-permute-start | bytes 1572872 | tf_op jit(solution)/shard_map/ppermute | solution.py:89
  44.4 1.9 collective-permute-start.6
  46.3 51.3 %copy-start.8 = (bf16[512,512]{1,0:T(8,128)(2,1)}, bf16[512,512]{1,0:T(8,128)(2,1)S(1)}, u32[]{:S(2)}) copy-start(bf16[512,512]{1,0:T(8,128)(2,1)S(1)} %collective-permute-done.5.refs_3_) | copy-start | bytes 1572868
  46.3 47.5 %copy-start.9 = (bf16[512,512]{1,0:T(8,128)(2,1)}, bf16[512,512]{1,0:T(8,128)(2,1)S(1)}, u32[]{:S(2)}) copy-start(bf16[512,512]{1,0:T(8,128)(2,1)S(1)} %collective-permute-done.6.refs_5_) | copy-start | bytes 1572868
  46.3 45.5 %collective-permute-start.9 = (bf16[512,512]{1,0:T(8,128)(2,1)S(1)}, bf16[512,512]{1,0:T(8,128)(2,1)}, u32[]{:S(2)}, u32[]{:S(2)}) collective-permute-start(bf16[512,512]{1,0:T(8,128)(2,1)S(1)} %collective-permute-done.3.refs_6_), channel_id=1, source_target_pairs={{8,0},{12,4},{9,1},{13,5},{10,2},{14,6},{11,3},{15,7}} | collective-permute-start | bytes 1572872 | tf_op jit(solution)/shard_map/ppermute | solution.py:84
  47.6 46.1 %collective-permute-start.11 = (bf16[512,512]{1,0:T(8,128)(2,1)S(1)}, bf16[512,512]{1,0:T(8,128)(2,1)}, u32[]{:S(2)}, u32[]{:S(2)}) collective-permute-start(bf16[512,512]{1,0:T(8,128)(2,1)S(1)} %collective-permute-done.4.refs_8_), channel_id=1, source_target_pairs={{16,24},{20,28},{17,25},{21,29},{18,26},{22,30},{19,27},{23,31}} | collective-permute-start | bytes 1572872 | tf_op jit(solution)/shard_map/ppermute | solution.py:84
  49.1 48.4 %collective-permute-start.7 = (bf16[512,512]{1,0:T(8,128)(2,1)S(1)}, bf16[512,512]{1,0:T(8,128)(2,1)}, u32[]{:S(2)}, u32[]{:S(2)}) collective-permute-start(bf16[512,512]{1,0:T(8,128)(2,1)S(1)} %collective-permute-done.3.refs_6_), channel_id=1, source_target_pairs={{0,4},{4,0},{8,12},{12,8},{1,5},{5,1},{9,13},{13,9},{2,6},{6,2},{1... | collective-permute-start | bytes 1572872 | tf_op jit(solution)/shard_map/ppermute | solution.py:89
  51.2 46.4 %collective-permute-start.8 = (bf16[512,512]{1,0:T(8,128)(2,1)S(1)}, bf16[512,512]{1,0:T(8,128)(2,1)}, u32[]{:S(2)}, u32[]{:S(2)}) collective-permute-start(bf16[512,512]{1,0:T(8,128)(2,1)S(1)} %collective-permute-done.4.refs_8_), channel_id=1, source_target_pairs={{16,20},{20,16},{24,28},{28,24},{17,21},{21,17},{25,29},{29,25},{1... | collective-permute-start | bytes 1572872 | tf_op jit(solution)/shard_map/ppermute | solution.py:89
  91.8 5.7 %collective-permute-start.10 = (bf16[512,512]{1,0:T(8,128)(2,1)}, bf16[512,512]{1,0:T(8,128)(2,1)}, u32[]{:S(2)}, u32[]{:S(2)}) collective-permute-start(bf16[512,512]{1,0:T(8,128)(2,1)} %collective-permute-done.9.refs_10_), channel_id=1, source_target_pairs={{0,4},{4,0},{1,5},{5,1},{2,6},{6,2},{3,7},{7,3}} | collective-permute-start | bytes 1572872 | tf_op jit(solution)/shard_map/ppermute | solution.py:89
  93.8 3.8 %collective-permute-start.12 = (bf16[512,512]{1,0:T(8,128)(2,1)}, bf16[512,512]{1,0:T(8,128)(2,1)}, u32[]{:S(2)}, u32[]{:S(2)}) collective-permute-start(bf16[512,512]{1,0:T(8,128)(2,1)} %collective-permute-done.11.refs_12_), channel_id=1, source_target_pairs={{24,28},{28,24},{25,29},{29,25},{26,30},{30,26},{27,31},{31,27}} | collective-permute-start | bytes 1572872 | tf_op jit(solution)/shard_map/ppermute | solution.py:89
  117.2 58.2 %all-to-all-start.1 = ((s16[32,272,128]{2,1,0:T(8,128)(2,1)}), s16[32,272,128]{2,1,0:T(8,128)(2,1)S(1)}, u32[]{:S(2)}, u32[]{:S(2)}) async-start(s16[32,272,128]{2,1,0:T(8,128)(2,1)} %bitcast.9), calls=%async_computation.1 | async-start | bytes 4456448 | tf_op jit(solution)/shard_map/all_to_all | solution.py:300
  142.2 37.7 %copy-start.1 = (f32[128]{0:T(128)S(1)}, f32[128]{0:T(128)}, u32[]{:S(2)}) copy-start(f32[128]{0:T(128)} %param.12) | copy-start | bytes 1540
  142.2 38.0 %copy-start.2 = (f32[64]{0:T(128)S(1)}, f32[64]{0:T(128)}, u32[]{:S(2)}) copy-start(f32[64]{0:T(128)} %param.13) | copy-start | bytes 772
  175.3 7.3 %copy-start = (s16[32,272,128]{2,1,0:T(8,128)(2,1)}, s16[32,272,128]{2,1,0:T(8,128)(2,1)S(1)}, u32[]{:S(2)}) copy-start(s16[32,272,128]{2,1,0:T(8,128)(2,1)S(1)} %all-to-all-done.1) | copy-start | bytes 6684676
  175.3 56.0 %all-to-all-start = ((s16[32,272,128]{2,1,0:T(8,128)(2,1)}), s16[32,272,128]{2,1,0:T(8,128)(2,1)}, u32[]{:S(2)}, u32[]{:S(2)}) async-start(s16[32,272,128]{2,1,0:T(8,128)(2,1)} %bitcast.8), calls=%async_computation | async-start | bytes 4456448 | tf_op jit(solution)/shard_map/all_to_all | solution.py:300
Sparse Core Ops, SparseCore 0:
  42.6 57.6 all-gather.1

commit v6 on v4

v6 whole, which is shorter than its diff:
```python
import functools

import jax
import jax.numpy as jnp
from jax import lax
from jax.experimental import pallas as pl
from jax.experimental.pallas import tpu as pltpu
from jax.sharding import PartitionSpec as P

VT = 32
NVT = 2
W = 64
ORBITALS_IN_GRP = 16
PAIR_SQ = ORBITALS_IN_GRP * ORBITALS_IN_GRP
CORES = 2
CODE_ROWS = 16
TOP = 32700.0
STEPS = 8.0
VMEM_LIMIT = 56 * 1024 * 1024


def one_hot_of(target, amount):
    return (target[:, None] == jnp.arange(amount)[None, :]).astype(jnp.bfloat16)


def split(values):
    high = values.astype(jnp.bfloat16)
    return high, (values - high.astype(jnp.float32)).astype(jnp.bfloat16)


def dot(left, right):
    return jnp.dot(left, right, preferred_element_type=jnp.float32)


def scale_of(code):
    return jnp.exp2(code * (1.0 / STEPS))


def screen_kernel(chunk, part, int_mask, slab_ref, screened_ref):
    slab_rows, slab_cols = slab_ref.shape
    cols = screened_ref.shape[1]
    span = slab_cols // W
    row_label = lax.axis_index("occ") * slab_rows // W // VT * NVT
    col_label = lax.axis_index("vir") * slab_cols // W // VT * NVT
    natural = lax.broadcasted_iota(jnp.int32, (slab_cols, 1), 0)
    a, b = natural // W, natural % W
    target = b // span * (part * span) + (a // part * part + b % part) * part + a % part
    target = jnp.where(b % span // part == chunk, target, -1)
    place = lax.broadcasted_iota(jnp.int32, (slab_cols, cols), 1)
    moved = dot(slab_ref[...], (place == target).astype(jnp.float32).astype(jnp.bfloat16)).astype(jnp.bfloat16)
    to = lax.broadcasted_iota(jnp.int32, (VT, cols), 1)
    owner, of_part = to // (part * span), to // part % part
    right = owner * span + chunk * part + of_part >= VT
    for d_tile in range(NVT):
        label = row_label + d_tile
        kept = jnp.where(right, int_mask[label, col_label + 1], int_mask[label, col_label])
        kept = kept.astype(jnp.float32).astype(jnp.bfloat16)
        for at in range(d_tile * VT, slab_rows, NVT * VT):
            screened_ref[at : at + VT, :] = moved[at : at + VT, :] * kept


def screen_call(chunk, chunks, int_mask, integrals):
    slab_rows, slab_cols = integrals.shape
    vmem = pl.BlockSpec(memory_space=pltpu.VMEM)
    return pl.pallas_call(
        functools.partial(screen_kernel, chunk, slab_cols // W // chunks),
        in_specs=[pl.BlockSpec(memory_space=pltpu.SMEM), vmem],
        out_specs=vmem,
        out_shape=jax.ShapeDtypeStruct((slab_rows, slab_cols // chunks), integrals.dtype),
        compiler_params=pltpu.CompilerParams(vmem_limit_bytes=VMEM_LIMIT),
        name="screen",
    )(int_mask, integrals)


def line_step(travel, step, tile_total):
    chips = tile_total // CORES
    arrived = {}
    for sign in (1, -1):
        pairs = [(t + sign * CORES, t) for t in range(tile_total) if 0 <= t // CORES + sign * step < chips]
        arrived[sign] = lax.ppermute(travel[sign], "occ", pairs)
    return arrived


def across(travel, step, tile_total):
    chips = tile_total // CORES
    pieces = []
    for sign in (1, -1) if step else (1,):
        pairs = [(t, t ^ 1) for t in range(tile_total) if 0 <= t // CORES + sign * step < chips]
        pieces.append((sign, step, False, travel[sign]))
        pieces.append((sign, step, True, lax.ppermute(travel[sign], "occ", pairs)))
    return pieces


def fill_slab(layout, refs, slab_scr, sems):
    tile = lax.axis_index("occ")
    chips = lax.axis_size("occ") // CORES
    chip, core = tile // CORES, tile % CORES
    slab_rows = refs[0].shape[0]

    def each(act):
        for n, (sign, step, other) in enumerate(layout):
            at_chip = chip + sign * step

            @pl.when((at_chip >= 0) & (at_chip < chips))
            def _():
                place = at_chip * CORES + (1 - core if other else core)
                at = pl.ds(pl.multiple_of(place * slab_rows, slab_rows), slab_rows)
                act(pltpu.make_async_copy(refs[n], slab_scr.at[at, :], sems.at[n]))

    each(lambda copy: copy.start())
    each(lambda copy: copy.wait())


def ladder_kernel(first, vir_count, chunks, layout, amp_mask, numbers, rows_ref, *refs):
    pieces, refs = refs[: len(layout)], refs[len(layout) :]
    if first:
        refs = refs[2:]
    ladder_ref, packed_ref, refs = refs[0], refs[1], refs[2:]
    tile = pl.program_id(0) + first
    if len(layout) > 1:
        slab_ref, sems = refs

        @pl.when(pl.program_id(0) == 0)
        def _():
            fill_slab(layout, pieces, slab_ref, sems)
    else:
        slab_ref = pieces[0]
    cols = slab_ref.shape[1]
    lane = lax.broadcasted_iota(jnp.int32, (1, W * W), 1)
    low = lane < W * VT
    left = lane % W < VT
    keep = jnp.where(
        low,
        jnp.where(left, amp_mask[tile, 0], amp_mask[tile, 1]),
        jnp.where(left, amp_mask[tile, 2], amp_mask[tile, 3]),
    )
    screened = rows_ref[...] * keep.astype(jnp.float32).astype(jnp.bfloat16)
    ladder = dot(screened, slab_ref[...])
    pair = lax.broadcasted_iota(jnp.int32, (PAIR_SQ, 1), 0)
    own_number = numbers[lax.axis_index("occ")]
    nonzero = (pair // ORBITALS_IN_GRP < own_number) & (pair % ORBITALS_IN_GRP < numbers[tile])
    ladder = jnp.where(nonzero, ladder, 0.0)
    block = cols // vir_count
    lanes = block // chunks
    for h in range(chunks):
        ladder_ref[h] = jnp.concatenate(
            [ladder[:, v * block + h * lanes : v * block + (h + 1) * lanes] for v in range(vir_count)], axis=1
        )
    by_place = ladder.reshape(ORBITALS_IN_GRP, ORBITALS_IN_GRP, cols)
    mirror = jnp.swapaxes(by_place, 0, 1).reshape(PAIR_SQ, cols)
    most = jnp.maximum(jnp.max(jnp.abs(ladder), axis=0, keepdims=True), 1e-30)
    code = jnp.ceil(jnp.log2(most) * STEPS)
    coded = jnp.round(mirror * (TOP / scale_of(code))).astype(jnp.int32).astype(jnp.int16)
    code_rows = jnp.broadcast_to(code.astype(jnp.int32), (CODE_ROWS, cols)).astype(jnp.int16)
    for v in range(vir_count):
        packed_ref[0, v, :PAIR_SQ] = coded[:, v * block : (v + 1) * block]
        packed_ref[0, v, PAIR_SQ:] = code_rows[:, v * block : (v + 1) * block]


def ladder_call(tiles, tile_total, vir_count, chunks, layout, amp_mask, numbers, amplitudes, slab_parts, earlier):
    first, last = tiles
    cols = slab_parts[0].shape[1]
    block = cols // vir_count
    smem = pl.BlockSpec(memory_space=pltpu.SMEM)
    somewhere = pl.BlockSpec(memory_space=pl.ANY)
    rows = (last - first) * PAIR_SQ
    if len(layout) > 1:
        slab_specs = [somewhere] * len(layout)
        scratch = [pltpu.VMEM((W * W, cols), jnp.bfloat16), pltpu.SemaphoreType.DMA((len(layout),))]
    else:
        slab_specs = [pl.BlockSpec((W * W, cols), lambda tile: (0, 0))]
        scratch = []
    args = [amp_mask, numbers, amplitudes, *slab_parts]
    aliases = {len(args): 0, len(args) + 1: 1} if first else {}
    return pl.pallas_call(
        functools.partial(ladder_kernel, first, vir_count, chunks, layout),
        grid=(last - first,),
        in_specs=[smem, smem, pl.BlockSpec((PAIR_SQ, W * W), lambda tile: (tile + first, 0))]
        + slab_specs
        + [somewhere] * len(aliases),
        out_specs=[
            pl.BlockSpec((chunks, PAIR_SQ, cols // chunks), lambda tile: (0, tile + first, 0)),
            pl.BlockSpec((1, vir_count, PAIR_SQ + CODE_ROWS, block), lambda tile: (tile + first, 0, 0, 0)),
        ],
        out_shape=[
            jax.ShapeDtypeStruct((chunks, tile_total * PAIR_SQ, cols // chunks), jnp.float32),
            jax.ShapeDtypeStruct((tile_total, vir_count, PAIR_SQ + CODE_ROWS, block), jnp.int16),
        ],
        scratch_shapes=scratch,
        input_output_aliases=aliases,
        compiler_params=pltpu.CompilerParams(vmem_limit_bytes=VMEM_LIMIT),
        cost_estimate=pl.CostEstimate(
            flops=2 * rows * cols * W * W,
            bytes_accessed=rows * (W * W * 2 + cols * 6) + W * W * cols * 2,
            transcendentals=0,
        ),
        name="ladder",
    )(*args, *(earlier if first else []))


def update_kernel(chunks, vir_count, arrived_ref, spread_ref, vir_ref, occ_ref, *refs):
    ladders, update_ref = refs[:chunks], refs[-1]
    highs, lows = [], []

    def take(values):
        high, low = split(values)
        highs.append(high)
        lows.append(low)

    for v in range(vir_count):
        code = arrived_ref[0, v, PAIR_SQ:].astype(jnp.int32).astype(jnp.float32)[:1]
        values = arrived_ref[0, v, :PAIR_SQ].astype(jnp.int32).astype(jnp.float32)
        take(values * (scale_of(code) * (1.0 / TOP)))
    for ladder_ref in ladders:
        take(ladder_ref[0])
    total = dot(jnp.concatenate(highs, axis=1), spread_ref[...]) + dot(jnp.concatenate(lows, axis=1), spread_ref[...])
    update_ref[...] = total / (vir_ref[...] - occ_ref[:, :1])


def update_call(chunk, tile_total, arrived, spread, vir_sum, occ_sum, ladders, earlier):
    chunks = len(ladders)
    cols = spread.shape[1]
    rows = tile_total * PAIR_SQ
    args = [arrived, spread, vir_sum, occ_sum, *ladders]
    in_specs = [
        pl.BlockSpec((1,) + arrived.shape[1:], lambda tile: (tile, 0, 0, 0)),
        pl.BlockSpec(spread.shape, lambda tile: (0, 0)),
        pl.BlockSpec((1, cols), lambda tile: (0, chunk)),
        pl.BlockSpec((PAIR_SQ, 128), lambda tile: (tile, 0)),
    ] + [pl.BlockSpec((1, PAIR_SQ, ladder.shape[2]), lambda tile: (chunk, tile, 0)) for ladder in ladders]
    aliases = {}
    if earlier is not None:
        aliases = {len(args): 0}
        args.append(earlier)
        in_specs.append(pl.BlockSpec(memory_space=pl.ANY))
    return pl.pallas_call(
        functools.partial(update_kernel, chunks, arrived.shape[1]),
        grid=(tile_total,),
        in_specs=in_specs,
        out_specs=pl.BlockSpec((PAIR_SQ, cols), lambda tile: (tile, chunk)),
        out_shape=jax.ShapeDtypeStruct((rows, chunks * cols), jnp.float32),
        input_output_aliases=aliases,
        compiler_params=pltpu.CompilerParams(vmem_limit_bytes=VMEM_LIMIT),
        cost_estimate=pl.CostEstimate(
            flops=4 * rows * spread.shape[0] * cols, bytes_accessed=rows * cols * 10, transcendentals=0
        ),
        name="update",
    )(*args)


def body(amplitudes, amp_mask, integrals, int_mask, group_orbital_numbers, occ_energy, vir_energy):
    tile_total = lax.axis_size("occ")
    vir_count = lax.axis_size("vir")
    row_tile = lax.axis_index("occ")
    vir_place = lax.axis_index("vir")
    span = W // vir_count
    slab_cols = span * W
    chunks = 2 if span >= 16 else 1
    part = span // chunks
    block = part * span
    rows = PAIR_SQ + CODE_ROWS
    barrier = lax.optimization_barrier

    def ladder_of(tiles, layout, slab_parts, earlier=None):
        return ladder_call(
            tiles, tile_total, vir_count, chunks, layout, amp_mask[0], group_orbital_numbers, amplitudes,
            slab_parts, earlier,
        )

    def exchanged(packed):
        moved = lax.all_to_all(
            packed.reshape(tile_total * vir_count, rows, block), ("occ", "vir"), split_axis=0, concat_axis=0, tiled=True
        )
        return moved.reshape(tile_total, vir_count, rows, block)

    if chunks > 1:
        ring_part = screen_call(1, chunks, int_mask, integrals)
        ring_part, integrals = barrier((ring_part, integrals))
        travel = {1: ring_part, -1: ring_part}
        pieces = across(travel, 0, tile_total)
        steps = tile_total // CORES - 1
        for step in range(1, steps):
            travel = line_step(travel, step, tile_total)
            pieces += across(travel, step, tile_total)
    slab = lax.all_gather(screen_call(0, chunks, int_mask, integrals), "occ", axis=0, tiled=True)
    whole = [(0, 0, False)]
    half = tile_total // 2
    results = list(ladder_of((0, half), whole, [slab]))
    if chunks > 1 and steps > 0:
        travel[1], travel[-1], results[1] = barrier((travel[1], travel[-1], results[1]))
        travel = line_step(travel, steps, tile_total)
        pieces += across(travel, steps, tile_total)
    results = [ladder_of((half, tile_total), whole, [slab], results)]
    arrived = [exchanged(results[0][1])]
    if chunks > 1:
        results.append(ladder_of((0, tile_total), [piece[:3] for piece in pieces], [piece[3] for piece in pieces]))
        arrived.append(exchanged(results[1][1]))
    ladders = [result[0] for result in results]

    place = jnp.arange(vir_count * block)
    owner, there_part = place // block, place // (part * part) % chunks
    here, there = place // part % part, place % part
    mirror_to = here * W + owner * span + there_part * part + there
    place = jnp.arange(vir_count * part * part)
    owner, b, a = place // (part * part), place // part % part, place % part
    direct_to = [a * W + owner * span + c * part + b for c in range(chunks)]
    spread = one_hot_of(jnp.concatenate([mirror_to, *direct_to]), part * W)

    occ_table = occ_energy.reshape(tile_total, ORBITALS_IN_GRP)
    own_energy = lax.dynamic_slice_in_dim(occ_table, row_tile, 1, 0)[0]
    occ_sum = jnp.broadcast_to(
        (own_energy[None, :, None] + occ_table[:, None, :]).reshape(-1, 1), (tile_total * PAIR_SQ, 128)
    )
    vir_own = lax.dynamic_slice_in_dim(vir_energy, vir_place * span, span, 0)
    vir_sum = (vir_own[:, None] + vir_energy[None, :]).reshape(1, -1)
    update = None
    for chunk in range(chunks):
        update = update_call(chunk, tile_total, arrived[chunk], spread, vir_sum, occ_sum, ladders, update)
    return update


def solution(mesh):
    in_specs = (P("occ", None), P("occ", None, None), P("occ", "vir"), P(), P(), P(), P())
    out_specs = P("occ", "vir")
    return jax.shard_map(body, mesh=mesh, in_specs=in_specs, out_specs=out_specs, check_vma=False)
```

time: 229 us -> 248 us (1.083)
  waiting for transfers between devices: 105 us -> 134 us
  starting transfers between devices: 31.4 us -> 26.9 us
  other arithmetic: 4.32 us -> 1.41 us
    ppermute x13, waiting for transfers between devices: 35.2 us -> 71.1 us  [the longest x6 70 us: line_step(): arrived[sign] = lax.ppermute(travel[sign], 'occ', pairs)]
    all_to_all x2, waiting for transfers between devices: 60.7 us -> 37.4 us  [exchanged(): lax.all_to_all(packed.reshape(tile_total * vir_count, rows, block), ('occ...]
    all_gather x1, waiting for transfers between devices: 8.57 us -> 24.9 us  [body(): lax.all_gather(screen_call(0, chunks, int_mask, integrals), 'occ', axis=0...]
    all_to_all x2, starting transfers between devices: 11.7 us -> 8.07 us  [exchanged(): lax.all_to_all(packed.reshape(tile_total * vir_count, rows, block), ('occ...]
    convert_element_type x4 -> x1, other arithmetic: 4.13 us -> 1.23 us  [one_hot_of(): return (target[:, None] == jnp.arange(amount)[None, :]).astype(jnp.bfloat16)]
    pallas_call x5 -> x7, Pallas kernels: 67 us -> 65.5 us  [the longest x3 39 us: ladder_call(): pl.pallas_call(functools.partial(ladder_kernel, first, vir_count, chunks,...]
  transfers between devices with their start and end apart: 16 -> 16, of which waited for: 6 -> 6; matrix products, arithmetic and copies ran while one was open for 3% -> 2% of each run, Pallas kernels for 23% -> 16%
where the time goes in v6:
time: 248 us; the launch traced here: 246 us
  waiting for transfers between devices  134 us (54%)
  Pallas kernels  65.5 us (26%)
  starting transfers between devices  26.9 us (11%)
  between operations  13.8 us (6%)
  local copies, waits for them, and re-layouts  5.21 us (2%)
    ppermute x6, waiting for transfers between devices, line_step(): arrived[sign] = lax.ppermute(travel[sign], 'occ', pairs)  70 us
    pallas_call x3, Pallas kernels, ladder_call(): pl.pallas_call(functools.partial(ladder_kernel, first, vir_count, chunks,...  39 us
    all_to_all x2, waiting for transfers between devices, exchanged(): lax.all_to_all(packed.reshape(tile_total * vir_count, rows, block), ('occ...  37.4 us
    all_gather x1, waiting for transfers between devices, body(): lax.all_gather(screen_call(0, chunks, int_mask, integrals), 'occ', axis=0...  24.9 us
    pallas_call x2, Pallas kernels, update_call(): pl.pallas_call(functools.partial(update_kernel, chunks, arrived.shape[1])...  20.7 us
    ppermute x6, starting transfers between devices, line_step(): arrived[sign] = lax.ppermute(travel[sign], 'occ', pairs)  10.2 us
    ppermute x7, starting transfers between devices, across(): pieces.append((sign, step, True, lax.ppermute(travel[sign], 'occ', pairs)))  8.62 us
    all_to_all x2, starting transfers between devices, exchanged(): lax.all_to_all(packed.reshape(tile_total * vir_count, rows, block), ('occ...  8.07 us
  transfers between devices with their start and end apart: 16, of which 6 were waited for; matrix products, arithmetic and copies ran while one was open for 2% of the time, Pallas kernels for 16%

profile of v6, /device:TPU:0, one launch (start us, length us, event | category | flops | bytes accessed | tf_op | source)
XLA Modules:
  0.0 246.3 jit_solution(8690781772220035657)
XLA Ops:
  6.5 0.0 all-gather.2.cloned.1.call-start
  6.5 2.9 %screen.2.refs_0_ = bf16[512,512]{1,0:T(8,128)(2,1)} custom-call(s32[4,4]{1,0:T(4,128)} %int_mask.3, bf16[512,1024]{1,0:T(8,128)(2,1)} %slab_ref.2), custom_call_target="tpu_custom_call" | custom-call | tf_op jit(solution)/shard_map/screen/pallas_call | solution.py:65
  9.4 2.9 %screen.3 = bf16[512,512]{1,0:T(8,128)(2,1)} custom-call(s32[4,4]{1,0:T(4,128)} %int_mask.3, bf16[512,1024]{1,0:T(8,128)(2,1)} %slab_ref.2), custom_call_target="tpu_custom_call" | custom-call | tf_op jit(solution)/shard_map/screen/pallas_call | solution.py:65
  12.3 0.0 all-gather.2.cloned.1.call-update
  12.3 5.0 %collective-permute-start.3 = (bf16[512,512]{1,0:T(8,128)(2,1)}, bf16[512,512]{1,0:T(8,128)(2,1)S(1)}, u32[]{:S(2)}, u32[]{:S(2)}) collective-permute-start(bf16[512,512]{1,0:T(8,128)(2,1)} %screen.2.refs_0_), channel_id=1, source_target_pairs={{0,8},{4,12},{8,16},{12,20},{16,24},{20,28},{1,9},{5,13},{9,17},{1... | collective-permute-start | bytes 1572872 | tf_op jit(solution)/shard_map/ppermute | solution.py:80
  17.3 1.3 collective-permute-start.1
  18.6 16.4 %collective-permute-done.3.refs_4_ = bf16[512,512]{1,0:T(8,128)(2,1)S(1)} collective-permute-done((bf16[512,512]{1,0:T(8,128)(2,1)}, bf16[512,512]{1,0:T(8,128)(2,1)S(1)}, u32[]{:S(2)}, u32[]{:S(2)}) %collective-permute-start.3) | collective-permute-done | bytes 524320 | tf_op jit(solution)/shard_map/ppermute | solution.py:80
  35.0 0.7 collective-permute-start.7
  35.7 14.0 %collective-permute-done.1.refs_2_ = bf16[512,512]{1,0:T(8,128)(2,1)S(1)} collective-permute-done((bf16[512,512]{1,0:T(8,128)(2,1)}, bf16[512,512]{1,0:T(8,128)(2,1)S(1)}, u32[]{:S(2)}, u32[]{:S(2)}) %collective-permute-start.1) | collective-permute-done | bytes 524320 | tf_op jit(solution)/shard_map/ppermute | solution.py:80
  49.7 1.3 collective-permute-start.5
  51.0 1.3 copy.12.amp_mask
  52.3 24.9 %all-gather.2.cloned.1.call-done.refs_0_ = bf16[4096,512]{1,0:T(8,128)(2,1)} async-done(((bf16[512,512]{1,0:T(8,128)(2,1)}), bf16[4096,512]{1,0:T(8,128)(2,1)}) %all-gather.2.cloned.1.call-update) | async-done | bytes 4194320 | tf_op jit(solution)/shard_map/all_gather | solution.py:285
  77.2 10.2 %ladder.3 = (f32[2,2048,256]{2,1,0:T(8,128)}, s16[8,4,272,128]{3,2,1,0:T(8,128)(2,1)}) custom-call(s32[8,4]{1,0:T(8,128)} %copy.12.amp_mask, s32[8]{0:T(128)} %numbers.5, bf16[2048,4096]{1,0:T(8,128)(2,1)} %rows_ref.5, bf16[4096,512]{1,0:T(8,128)(2,1)} %all-gather.2.cloned.1.call-done.refs_0_), custom_call_target="tpu_custom_call" | custom-call | flops 4294967296 | bytes 15728640 | tf_op jit(solution)/shard_map/ladder/pallas_call | solution.py:175
  87.4 0.0 copy-done.5
  87.4 0.0 collective-permute-done.7.refs_8_
  87.4 0.0 copy-start.6
  87.4 0.0 collective-permute-done.5.refs_6_
  87.4 0.0 copy-start.7
  87.5 10.5 %ladder.5 = (f32[2,2048,256]{2,1,0:T(8,128)}, s16[8,4,272,128]{3,2,1,0:T(8,128)(2,1)}) custom-call(s32[8,4]{1,0:T(8,128)} %copy.12.amp_mask, s32[8]{0:T(128)} %numbers.5, bf16[2048,4096]{1,0:T(8,128)(2,1)} %rows_ref.5, bf16[4096,512]{1,0:T(8,128)(2,1)} %all-gather.2.cloned.1.call-done.refs_0_, ...), custom_call_target="tpu_custom_call", output_to_operand_aliasing={{0}: (4, {}), {1}: (5, {})} | custom-call | flops 4294967296 | bytes 15728640 | tf_op jit(solution)/shard_map/ladder/pallas_call | solution.py:175
  98.0 0.0 copy-done.6
  98.0 0.0 copy-done.7
  98.0 0.0 copy-start.1
  98.0 3.5 %all-to-all-start.1 = ((s16[32,272,128]{2,1,0:T(8,128)(2,1)}), s16[32,272,128]{2,1,0:T(8,128)(2,1)S(1)}, u32[]{:S(2)}, u32[]{:S(2)}) async-start(s16[32,272,128]{2,1,0:T(8,128)(2,1)} %bitcast.7), calls=%async_computation.1 | async-start | bytes 4456448 | tf_op jit(solution)/shard_map/all_to_all | solution.py:271
  101.5 0.0 copy-done.1
  101.5 0.3 collective-permute-start
  101.8 0.7 collective-permute-start.4
  102.5 1.3 collective-permute-start.9
  103.8 0.7 collective-permute-start.11
  104.5 2.2 collective-permute-start.2
  106.7 0.0 collective-permute-done.refs_1_
  106.7 0.7 collective-permute-start.8
  107.4 0.0 collective-permute-done.4.refs_5_
  107.4 0.0 copy-start.9
  107.4 2.2 collective-permute-start.6
  109.6 39.6 %collective-permute-done.9.refs_10_ = bf16[512,512]{1,0:T(8,128)(2,1)S(1)} collective-permute-done((bf16[512,512]{1,0:T(8,128)(2,1)}, bf16[512,512]{1,0:T(8,128)(2,1)S(1)}, u32[]{:S(2)}, u32[]{:S(2)}) %collective-permute-start.9) | collective-permute-done | bytes 524320 | tf_op jit(solution)/shard_map/ppermute | solution.py:80
  149.2 1.9 collective-permute-start.10
  151.2 0.0 collective-permute-done.11.refs_12_
  151.2 0.7 collective-permute-start.12
  151.9 0.0 collective-permute-done.2.refs_3_
  151.9 0.0 copy-start.12
  151.9 0.0 collective-permute-done.8.refs_9_
  151.9 0.0 collective-permute-done.6.refs_7_
  151.9 1.1 collective-permute-done.10.refs_11_
  153.0 0.0 collective-permute-done.12.refs_13_
  153.0 0.0 copy-done.8
  153.1 0.7 copy-done.15
  153.8 0.8 copy-done.16
  154.7 18.3 %ladder.4 = (f32[2,2048,256]{2,1,0:T(8,128)}, s16[8,4,272,128]{3,2,1,0:T(8,128)(2,1)}) custom-call(s32[8,4]{1,0:T(8,128)} %copy.12.amp_mask, s32[8]{0:T(128)} %numbers.5, bf16[2048,4096]{1,0:T(8,128)(2,1)} %rows_ref.5, bf16[512,512]{1,0:T(8,128)(2,1)} %screen.2.refs_0_, bf16[512,512]{1,0:T(8,128)(2,1)} %copy-done.8, bf16[512,512]{1,0:T(8,128)(2,1)} %copy-done.5, ...), custom_call_target="tpu_custom_call" | custom-call | flops 8589934592 | bytes 27262976 | tf_op jit(solution)/shard_map/ladder/pallas_call | solution.py:175
  173.0 0.0 copy-start.2
  173.0 0.0 copy-start.3
  173.0 0.0 all-to-all-done.1
  173.0 4.6 %all-to-all-start = ((s16[32,272,128]{2,1,0:T(8,128)(2,1)}), s16[32,272,128]{2,1,0:T(8,128)(2,1)}, u32[]{:S(2)}, u32[]{:S(2)}) async-start(s16[32,272,128]{2,1,0:T(8,128)(2,1)} %bitcast.9), calls=%async_computation | async-start | bytes 4456448 | tf_op jit(solution)/shard_map/all_to_all | solution.py:271
  177.6 0.1 reshape.60
  177.7 0.0 copy-done.3
  177.7 0.1 dynamic_slice.6
  177.8 0.1 broadcast_add_fusion.1
  177.8 0.7 add.125.vir_ref
  178.5 0.1 broadcast_add_fusion
  178.6 0.1 add.131
  178.7 1.2 fusion.spread_ref
  179.9 1.3 broadcast_in_dim.2.occ_ref
  181.3 10.4 %update.2.refs_2_ = f32[2048,1024]{1,0:T(8,128)} custom-call(s16[8,4,272,128]{3,2,1,0:T(8,128)(2,1)} %bitcast.8, bf16[1024,512]{1,0:T(8,128)(2,1)} %fusion.spread_ref, f32[1,1024]{1,0:T(1,128)} %add.125.vir_ref, f32[2048,128]{1,0:T(8,128)} %broadcast_in_dim.2.occ_ref, f32[2,2048,256]{2,1,0:T(8,128)} %get-tuple-element.24.refs_0_, ...), custom_call_target="tpu_custom_call" | custom-call | flops 4294967296 | bytes 10485760 | tf_op jit(solution)/shard_map/update/pallas_call | solution.py:236
  191.7 37.4 %all-to-all-done = s16[32,272,128]{2,1,0:T(8,128)(2,1)} async-done(((s16[32,272,128]{2,1,0:T(8,128)(2,1)}), s16[32,272,128]{2,1,0:T(8,128)(2,1)}, u32[]{:S(2)}, u32[]{:S(2)}) %all-to-all-start) | async-done | bytes 2228256 | tf_op jit(solution)/shard_map/all_to_all | solution.py:271
  229.1 10.4 %update.3 = f32[2048,1024]{1,0:T(8,128)} custom-call(s16[8,4,272,128]{3,2,1,0:T(8,128)(2,1)} %bitcast.2.arrived_ref, bf16[1024,512]{1,0:T(8,128)(2,1)} %fusion.spread_ref, f32[1,1024]{1,0:T(1,128)} %add.125.vir_ref, f32[2048,128]{1,0:T(8,128)} %broadcast_in_dim.2.occ_ref, f32[2,2048,256]{2,1,0:T(8,128)} %get-tuple-element.24.refs_0_, ...), custom_call_target="tpu_custom_call", output_to_operand_aliasing={{}: (6, {})} | custom-call | flops 4294967296 | bytes 10485760 | tf_op jit(solution)/shard_map/update/pallas_call | solution.py:236
  (23 shorter events, 0.1 us)
Async XLA Ops:
  6.5 70.7 %all-gather.2.cloned.1.call-start = ((), (), s32[]{:S(2)}) async-start(), calls=%async_computation.2 | async-start | bytes 4718592 | tf_op jit(solution)/shard_map/all_gather | solution.py:285
  12.3 22.7 %collective-permute-start.3 = (bf16[512,512]{1,0:T(8,128)(2,1)}, bf16[512,512]{1,0:T(8,128)(2,1)S(1)}, u32[]{:S(2)}, u32[]{:S(2)}) collective-permute-start(bf16[512,512]{1,0:T(8,128)(2,1)} %screen.2.refs_0_), channel_id=1, source_target_pairs={{0,8},{4,12},{8,16},{12,20},{16,24},{20,28},{1,9},{5,13},{9,17},{1... | collective-permute-start | bytes 1572872 | tf_op jit(solution)/shard_map/ppermute | solution.py:80
  17.3 32.4 %collective-permute-start.1 = (bf16[512,512]{1,0:T(8,128)(2,1)}, bf16[512,512]{1,0:T(8,128)(2,1)S(1)}, u32[]{:S(2)}, u32[]{:S(2)}) collective-permute-start(bf16[512,512]{1,0:T(8,128)(2,1)} %screen.2.refs_0_), channel_id=1, source_target_pairs={{8,0},{12,4},{16,8},{20,12},{24,16},{28,20},{9,1},{13,5},{17,9},{2... | collective-permute-start | bytes 1572872 | tf_op jit(solution)/shard_map/ppermute | solution.py:80
  35.0 66.9 %copy-start.4 = (bf16[512,512]{1,0:T(8,128)(2,1)}, bf16[512,512]{1,0:T(8,128)(2,1)S(1)}, u32[]{:S(2)}) copy-start(bf16[512,512]{1,0:T(8,128)(2,1)S(1)} %collective-permute-done.3.refs_4_) | copy-start | bytes 1572868
  35.0 52.4 %collective-permute-start.7 = (bf16[512,512]{1,0:T(8,128)(2,1)S(1)}, bf16[512,512]{1,0:T(8,128)(2,1)S(1)}, u32[]{:S(2)}, u32[]{:S(2)}) collective-permute-start(bf16[512,512]{1,0:T(8,128)(2,1)S(1)} %collective-permute-done.3.refs_4_), channel_id=1, source_target_pairs={{8,16},{12,20},{16,24},{20,28},{9,17},{13,21},{17,25},{21,29},{10,... | collective-permute-start | bytes 1572872 | tf_op jit(solution)/shard_map/ppermute | solution.py:80
  49.7 37.8 %copy-start.5 = (bf16[512,512]{1,0:T(8,128)(2,1)}, bf16[512,512]{1,0:T(8,128)(2,1)S(1)}, u32[]{:S(2)}) copy-start(bf16[512,512]{1,0:T(8,128)(2,1)S(1)} %collective-permute-done.1.refs_2_) | copy-start | bytes 1572868
  49.7 37.8 %collective-permute-start.5 = (bf16[512,512]{1,0:T(8,128)(2,1)S(1)}, bf16[512,512]{1,0:T(8,128)(2,1)S(1)}, u32[]{:S(2)}, u32[]{:S(2)}) collective-permute-start(bf16[512,512]{1,0:T(8,128)(2,1)S(1)} %collective-permute-done.1.refs_2_), channel_id=1, source_target_pairs={{8,0},{12,4},{16,8},{20,12},{9,1},{13,5},{17,9},{21,13},{10,2},{14... | collective-permute-start | bytes 1572872 | tf_op jit(solution)/shard_map/ppermute | solution.py:80
  87.4 10.6 %copy-start.6 = (bf16[512,512]{1,0:T(8,128)(2,1)}, bf16[512,512]{1,0:T(8,128)(2,1)S(1)}, u32[]{:S(2)}) copy-start(bf16[512,512]{1,0:T(8,128)(2,1)S(1)} %collective-permute-done.7.refs_8_) | copy-start | bytes 1572868
  87.4 10.5 %copy-start.7 = (bf16[512,512]{1,0:T(8,128)(2,1)}, bf16[512,512]{1,0:T(8,128)(2,1)S(1)}, u32[]{:S(2)}) copy-start(bf16[512,512]{1,0:T(8,128)(2,1)S(1)} %collective-permute-done.5.refs_6_) | copy-start | bytes 1572868
  98.0 3.5 %copy-start.1 = (bf16[512,512]{1,0:T(8,128)(2,1)S(1)}, bf16[512,512]{1,0:T(8,128)(2,1)}, u32[]{:S(2)}) copy-start(bf16[512,512]{1,0:T(8,128)(2,1)} %screen.2.refs_0_) | copy-start | bytes 1572868
  98.0 75.0 %all-to-all-start.1 = ((s16[32,272,128]{2,1,0:T(8,128)(2,1)}), s16[32,272,128]{2,1,0:T(8,128)(2,1)S(1)}, u32[]{:S(2)}, u32[]{:S(2)}) async-start(s16[32,272,128]{2,1,0:T(8,128)(2,1)} %bitcast.7), calls=%async_computation.1 | async-start | bytes 4456448 | tf_op jit(solution)/shard_map/all_to_all | solution.py:271
  101.5 5.2 %collective-permute-start = (bf16[512,512]{1,0:T(8,128)(2,1)S(1)}, bf16[512,512]{1,0:T(8,128)(2,1)S(1)}, u32[]{:S(2)}, u32[]{:S(2)}) collective-permute-start(bf16[512,512]{1,0:T(8,128)(2,1)S(1)} %copy-done.1), channel_id=1, source_target_pairs={{0,4},{4,0},{8,12},{12,8},{16,20},{20,16},{24,28},{28,24},{1,5},{5... | collective-permute-start | bytes 1572872 | tf_op jit(solution)/shard_map/ppermute | solution.py:90
  101.8 5.6 %collective-permute-start.4 = (bf16[512,512]{1,0:T(8,128)(2,1)S(1)}, bf16[512,512]{1,0:T(8,128)(2,1)S(1)}, u32[]{:S(2)}, u32[]{:S(2)}) collective-permute-start(bf16[512,512]{1,0:T(8,128)(2,1)S(1)} %collective-permute-done.3.refs_4_), channel_id=1, source_target_pairs={{8,12},{12,8},{16,20},{20,16},{24,28},{28,24},{9,13},{13,9},{17,21... | collective-permute-start | bytes 1572872 | tf_op jit(solution)/shard_map/ppermute | solution.py:90
  102.5 46.7 %collective-permute-start.9 = (bf16[512,512]{1,0:T(8,128)(2,1)}, bf16[512,512]{1,0:T(8,128)(2,1)S(1)}, u32[]{:S(2)}, u32[]{:S(2)}) collective-permute-start(bf16[512,512]{1,0:T(8,128)(2,1)} %copy-done.7), channel_id=1, source_target_pairs={{8,0},{12,4},{9,1},{13,5},{10,2},{14,6},{11,3},{15,7}} | collective-permute-start | bytes 1572872 | tf_op jit(solution)/shard_map/ppermute | solution.py:80
  103.8 47.3 %collective-permute-start.11 = (bf16[512,512]{1,0:T(8,128)(2,1)}, bf16[512,512]{1,0:T(8,128)(2,1)S(1)}, u32[]{:S(2)}, u32[]{:S(2)}) collective-permute-start(bf16[512,512]{1,0:T(8,128)(2,1)} %copy-done.6), channel_id=1, source_target_pairs={{16,24},{20,28},{17,25},{21,29},{18,26},{22,30},{19,27},{23,31}} | collective-permute-start | bytes 1572872 | tf_op jit(solution)/shard_map/ppermute | solution.py:80
  104.5 47.4 %collective-permute-start.2 = (bf16[512,512]{1,0:T(8,128)(2,1)}, bf16[512,512]{1,0:T(8,128)(2,1)S(1)}, u32[]{:S(2)}, u32[]{:S(2)}) collective-permute-start(bf16[512,512]{1,0:T(8,128)(2,1)} %copy-done.5), channel_id=1, source_target_pairs={{0,4},{4,0},{8,12},{12,8},{16,20},{20,16},{1,5},{5,1},{9,13},{13,9... | collective-permute-start | bytes 1572872 | tf_op jit(solution)/shard_map/ppermute | solution.py:90
  106.7 46.3 %copy-start.8 = (bf16[512,512]{1,0:T(8,128)(2,1)}, bf16[512,512]{1,0:T(8,128)(2,1)S(1)}, u32[]{:S(2)}) copy-start(bf16[512,512]{1,0:T(8,128)(2,1)S(1)} %collective-permute-done.refs_1_) | copy-start | bytes 1572868
  106.7 45.2 %collective-permute-start.8 = (bf16[512,512]{1,0:T(8,128)(2,1)}, bf16[512,512]{1,0:T(8,128)(2,1)S(1)}, u32[]{:S(2)}, u32[]{:S(2)}) collective-permute-start(bf16[512,512]{1,0:T(8,128)(2,1)} %copy-done.6), channel_id=1, source_target_pairs={{16,20},{20,16},{24,28},{28,24},{17,21},{21,17},{25,29},{29,25},{1... | collective-permute-start | bytes 1572872 | tf_op jit(solution)/shard_map/ppermute | solution.py:90
  107.4 45.6 %copy-start.9 = (bf16[512,512]{1,0:T(8,128)(2,1)}, bf16[512,512]{1,0:T(8,128)(2,1)S(1)}, u32[]{:S(2)}) copy-start(bf16[512,512]{1,0:T(8,128)(2,1)S(1)} %collective-permute-done.4.refs_5_) | copy-start | bytes 1572868
  107.4 44.5 %collective-permute-start.6 = (bf16[512,512]{1,0:T(8,128)(2,1)}, bf16[512,512]{1,0:T(8,128)(2,1)S(1)}, u32[]{:S(2)}, u32[]{:S(2)}) collective-permute-start(bf16[512,512]{1,0:T(8,128)(2,1)} %copy-done.7), channel_id=1, source_target_pairs={{0,4},{4,0},{8,12},{12,8},{1,5},{5,1},{9,13},{13,9},{2,6},{6,2},{1... | collective-permute-start | bytes 1572872 | tf_op jit(solution)/shard_map/ppermute | solution.py:90
  149.2 3.8 %copy-start.10 = (bf16[512,512]{1,0:T(8,128)(2,1)}, bf16[512,512]{1,0:T(8,128)(2,1)S(1)}, u32[]{:S(2)}) copy-start(bf16[512,512]{1,0:T(8,128)(2,1)S(1)} %collective-permute-done.9.refs_10_) | copy-start | bytes 1572868
  149.2 3.8 %collective-permute-start.10 = (bf16[512,512]{1,0:T(8,128)(2,1)S(1)}, bf16[512,512]{1,0:T(8,128)(2,1)S(1)}, u32[]{:S(2)}, u32[]{:S(2)}) collective-permute-start(bf16[512,512]{1,0:T(8,128)(2,1)S(1)} %collective-permute-done.9.refs_10_), channel_id=1, source_target_pairs={{0,4},{4,0},{1,5},{5,1},{2,6},{6,2},{3,7},{7,3}} | collective-permute-start | bytes 1572872 | tf_op jit(solution)/shard_map/ppermute | solution.py:90
  151.2 1.9 copy-start.11
  151.2 1.9 collective-permute-start.12
  151.9 1.2 copy-start.12
  151.9 1.2 copy-start.13
  151.9 1.2 copy-start.14
  153.0 0.8 copy-start.15
  153.8 0.8 copy-start.16
  173.0 4.6 %copy-start.2 = (f32[128]{0:T(128)S(1)}, f32[128]{0:T(128)}, u32[]{:S(2)}) copy-start(f32[128]{0:T(128)} %param.12) | copy-start | bytes 1540
  173.0 4.7 %copy-start.3 = (f32[64]{0:T(128)S(1)}, f32[64]{0:T(128)}, u32[]{:S(2)}) copy-start(f32[64]{0:T(128)} %param.13) | copy-start | bytes 772
  173.0 8.3 %copy-start = (s16[32,272,128]{2,1,0:T(8,128)(2,1)}, s16[32,272,128]{2,1,0:T(8,128)(2,1)S(1)}, u32[]{:S(2)}) copy-start(s16[32,272,128]{2,1,0:T(8,128)(2,1)S(1)} %all-to-all-done.1) | copy-start | bytes 6684676
  173.0 56.1 %all-to-all-start = ((s16[32,272,128]{2,1,0:T(8,128)(2,1)}), s16[32,272,128]{2,1,0:T(8,128)(2,1)}, u32[]{:S(2)}, u32[]{:S(2)}) async-start(s16[32,272,128]{2,1,0:T(8,128)(2,1)} %bitcast.9), calls=%async_computation | async-start | bytes 4456448 | tf_op jit(solution)/shard_map/all_to_all | solution.py:271
Sparse Core Ops, SparseCore 0:
  12.4 64.7 all-gather.1

commit v7 on v6

v7 whole, which is shorter than its diff:
```python
import functools

import jax
import jax.numpy as jnp
from jax import lax
from jax.experimental import pallas as pl
from jax.experimental.pallas import tpu as pltpu
from jax.sharding import PartitionSpec as P

VT = 32
NVT = 2
W = 64
ORBITALS_IN_GRP = 16
PAIR_SQ = ORBITALS_IN_GRP * ORBITALS_IN_GRP
CORES = 2
CODE_ROWS = 16
AT_ONCE = 2
TOP = 32700.0
STEPS = 8.0
VMEM_LIMIT = 56 * 1024 * 1024


def one_hot_of(target, amount):
    return (target[:, None] == jnp.arange(amount)[None, :]).astype(jnp.bfloat16)


def split(values):
    high = values.astype(jnp.bfloat16)
    return high, (values - high.astype(jnp.float32)).astype(jnp.bfloat16)


def dot(left, right):
    return jnp.dot(left, right, preferred_element_type=jnp.float32)


def scale_of(code):
    return jnp.exp2(code * (1.0 / STEPS))


def screen_kernel(chunk, part, int_mask, slab_ref, screened_ref):
    slab_rows, slab_cols = slab_ref.shape
    cols = screened_ref.shape[1]
    span = slab_cols // W
    row_label = lax.axis_index("occ") * slab_rows // W // VT * NVT
    col_label = lax.axis_index("vir") * slab_cols // W // VT * NVT
    natural = lax.broadcasted_iota(jnp.int32, (slab_cols, 1), 0)
    a, b = natural // W, natural % W
    target = b // span * (part * span) + (a // part * part + b % part) * part + a % part
    target = jnp.where(b % span // part == chunk, target, -1)
    place = lax.broadcasted_iota(jnp.int32, (slab_cols, cols), 1)
    moved = dot(slab_ref[...], (place == target).astype(jnp.float32).astype(jnp.bfloat16)).astype(jnp.bfloat16)
    to = lax.broadcasted_iota(jnp.int32, (VT, cols), 1)
    owner, of_part = to // (part * span), to // part % part
    right = owner * span + chunk * part + of_part >= VT
    for d_tile in range(NVT):
        label = row_label + d_tile
        kept = jnp.where(right, int_mask[label, col_label + 1], int_mask[label, col_label])
        kept = kept.astype(jnp.float32).astype(jnp.bfloat16)
        for at in range(d_tile * VT, slab_rows, NVT * VT):
            screened_ref[at : at + VT, :] = moved[at : at + VT, :] * kept


def screen_call(chunk, chunks, int_mask, integrals):
    slab_rows, slab_cols = integrals.shape
    vmem = pl.BlockSpec(memory_space=pltpu.VMEM)
    return pl.pallas_call(
        functools.partial(screen_kernel, chunk, slab_cols // W // chunks),
        in_specs=[pl.BlockSpec(memory_space=pltpu.SMEM), vmem],
        out_specs=vmem,
        out_shape=jax.ShapeDtypeStruct((slab_rows, slab_cols // chunks), integrals.dtype),
        compiler_params=pltpu.CompilerParams(vmem_limit_bytes=VMEM_LIMIT),
        name="screen",
    )(int_mask, integrals)


def line_step(travel, step, tile_total):
    chips = tile_total // CORES
    arrived = {}
    for sign in (1, -1):
        pairs = [(t + sign * CORES, t) for t in range(tile_total) if 0 <= t // CORES + sign * step < chips]
        arrived[sign] = lax.ppermute(travel[sign], "occ", pairs)
    return arrived


def across(travel, step, tile_total):
    chips = tile_total // CORES
    pieces = []
    for sign in (1, -1) if step else (1,):
        pairs = [(t, t ^ 1) for t in range(tile_total) if 0 <= t // CORES + sign * step < chips]
        pieces.append((sign, step, False, travel[sign]))
        pieces.append((sign, step, True, lax.ppermute(travel[sign], "occ", pairs)))
    return pieces


def fill_slab(layout, refs, slab_scr, sems):
    tile = lax.axis_index("occ")
    chips = lax.axis_size("occ") // CORES
    chip, core = tile // CORES, tile % CORES
    slab_rows = refs[0].shape[0]

    def each(act):
        for n, (sign, step, other) in enumerate(layout):
            at_chip = chip + sign * step

            @pl.when((at_chip >= 0) & (at_chip < chips))
            def _():
                place = at_chip * CORES + (1 - core if other else core)
                at = pl.ds(pl.multiple_of(place * slab_rows, slab_rows), slab_rows)
                act(pltpu.make_async_copy(refs[n], slab_scr.at[at, :], sems.at[n]))

    each(lambda copy: copy.start())
    each(lambda copy: copy.wait())


def ladder_kernel(tile_total, vir_count, chunks, layout, amp_mask, numbers, rows_ref, *refs):
    pieces, refs = refs[: len(layout)], refs[len(layout) :]
    ladder_ref, packed_ref, product, refs = refs[0], refs[1], refs[2], refs[3:]
    step = pl.program_id(0)
    if len(layout) > 1:
        slab_ref, sems = refs

        @pl.when(step == 0)
        def _():
            fill_slab(layout, pieces, slab_ref, sems)
    else:
        slab_ref = pieces[0]
    cols = slab_ref.shape[1]

    tile = jnp.maximum(step - 1, 0)
    pair = lax.broadcasted_iota(jnp.int32, (PAIR_SQ, 1), 0)
    own_number = numbers[lax.axis_index("occ")]
    nonzero = (pair // ORBITALS_IN_GRP < own_number) & (pair % ORBITALS_IN_GRP < numbers[tile])
    ladder = jnp.where(nonzero, product[...], 0.0)
    block = cols // vir_count
    lanes = block // chunks
    for h in range(chunks):
        ladder_ref[h] = jnp.concatenate(
            [ladder[:, v * block + h * lanes : v * block + (h + 1) * lanes] for v in range(vir_count)], axis=1
        )
    by_place = ladder.reshape(ORBITALS_IN_GRP, ORBITALS_IN_GRP, cols)
    mirror = jnp.swapaxes(by_place, 0, 1).reshape(PAIR_SQ, cols)
    most = jnp.maximum(jnp.max(jnp.abs(ladder), axis=0, keepdims=True), 1e-30)
    code = jnp.ceil(jnp.log2(most) * STEPS)
    coded = jnp.round(mirror * (TOP / scale_of(code))).astype(jnp.int32).astype(jnp.int16)
    code_rows = jnp.broadcast_to(code.astype(jnp.int32), (CODE_ROWS, cols)).astype(jnp.int16)
    for v in range(vir_count):
        packed_ref[0, v, :PAIR_SQ] = coded[:, v * block : (v + 1) * block]
        packed_ref[0, v, PAIR_SQ:] = code_rows[:, v * block : (v + 1) * block]

    tile = jnp.minimum(step, tile_total - 1)
    lane = lax.broadcasted_iota(jnp.int32, (1, W * W), 1)
    low = lane < W * VT
    left = lane % W < VT
    keep = jnp.where(
        low,
        jnp.where(left, amp_mask[tile, 0], amp_mask[tile, 1]),
        jnp.where(left, amp_mask[tile, 2], amp_mask[tile, 3]),
    )
    screened = rows_ref[...] * keep.astype(jnp.float32).astype(jnp.bfloat16)
    product[...] = dot(screened, slab_ref[...])


def ladder_call(tile_total, vir_count, chunks, layout, amp_mask, numbers, amplitudes, slab_parts):
    cols = slab_parts[0].shape[1]
    block = cols // vir_count
    smem = pl.BlockSpec(memory_space=pltpu.SMEM)
    rows = tile_total * PAIR_SQ
    scratch = [pltpu.VMEM((PAIR_SQ, cols), jnp.float32)]
    if len(layout) > 1:
        slab_specs = [pl.BlockSpec(memory_space=pl.ANY)] * len(layout)
        scratch += [pltpu.VMEM((W * W, cols), jnp.bfloat16), pltpu.SemaphoreType.DMA((len(layout),))]
    else:
        slab_specs = [pl.BlockSpec((W * W, cols), lambda step: (0, 0))]
    return pl.pallas_call(
        functools.partial(ladder_kernel, tile_total, vir_count, chunks, layout),
        grid=(tile_total + 1,),
        in_specs=[smem, smem, pl.BlockSpec((PAIR_SQ, W * W), lambda step: (jnp.minimum(step, tile_total - 1), 0))]
        + slab_specs,
        out_specs=[
            pl.BlockSpec((chunks, PAIR_SQ, cols // chunks), lambda step: (0, jnp.maximum(step - 1, 0), 0)),
            pl.BlockSpec(
                (1, vir_count, PAIR_SQ + CODE_ROWS, block), lambda step: (jnp.maximum(step - 1, 0), 0, 0, 0)
            ),
        ],
        out_shape=[
            jax.ShapeDtypeStruct((chunks, rows, cols // chunks), jnp.float32),
            jax.ShapeDtypeStruct((tile_total, vir_count, PAIR_SQ + CODE_ROWS, block), jnp.int16),
        ],
        scratch_shapes=scratch,
        compiler_params=pltpu.CompilerParams(vmem_limit_bytes=VMEM_LIMIT),
        cost_estimate=pl.CostEstimate(
            flops=2 * rows * cols * W * W,
            bytes_accessed=rows * (W * W * 2 + cols * 6) + W * W * cols * 2,
            transcendentals=0,
        ),
        name="ladder",
    )(amp_mask, numbers, amplitudes, *slab_parts)


def moved_columns(values, spread_ref):
    both = dot(jnp.concatenate(split(values), axis=0), spread_ref[...])
    return both[: values.shape[0]] + both[values.shape[0] :]


def direct_kernel(spread_ref, *refs):
    refs[-1][...] = moved_columns(jnp.concatenate([ref[0] for ref in refs[:-1]], axis=1), spread_ref)


def direct_call(chunk, spread, ladders):
    rows = ladders[0].shape[1]
    step_rows = AT_ONCE * PAIR_SQ
    return pl.pallas_call(
        direct_kernel,
        grid=(rows // step_rows,),
        in_specs=[pl.BlockSpec(spread.shape, lambda step: (0, 0))]
        + [pl.BlockSpec((1, step_rows, ladder.shape[2]), lambda step: (chunk, step, 0)) for ladder in ladders],
        out_specs=pl.BlockSpec((step_rows, spread.shape[1]), lambda step: (step, 0)),
        out_shape=jax.ShapeDtypeStruct((rows, spread.shape[1]), jnp.float32),
        compiler_params=pltpu.CompilerParams(vmem_limit_bytes=VMEM_LIMIT),
        cost_estimate=pl.CostEstimate(
            flops=4 * rows * spread.size, bytes_accessed=rows * spread.shape[1] * 8, transcendentals=0
        ),
        name="direct",
    )(spread, *ladders)


def update_kernel(vir_count, arrived_ref, spread_ref, vir_ref, occ_ref, direct_ref, *refs):
    tiles = []
    for n in range(AT_ONCE):
        blocks = []
        for v in range(vir_count):
            code = arrived_ref[n, v, PAIR_SQ:].astype(jnp.int32).astype(jnp.float32)[:1]
            values = arrived_ref[n, v, :PAIR_SQ].astype(jnp.int32).astype(jnp.float32)
            blocks.append(values * (scale_of(code) * (1.0 / TOP)))
        tiles.append(jnp.concatenate(blocks, axis=1))
    mirror = moved_columns(jnp.concatenate(tiles, axis=0), spread_ref)
    refs[-1][...] = (direct_ref[...] + mirror) / (vir_ref[...] - occ_ref[:, :1])


def update_call(chunk, chunks, arrived, spread, vir_sum, occ_sum, direct, earlier):
    cols = spread.shape[1]
    rows = direct.shape[0]
    step_rows = AT_ONCE * PAIR_SQ
    args = [arrived, spread, vir_sum, occ_sum, direct]
    in_specs = [
        pl.BlockSpec((AT_ONCE,) + arrived.shape[1:], lambda step: (step, 0, 0, 0)),
        pl.BlockSpec(spread.shape, lambda step: (0, 0)),
        pl.BlockSpec((1, cols), lambda step: (0, chunk)),
        pl.BlockSpec((step_rows, 128), lambda step: (step, 0)),
        pl.BlockSpec((step_rows, cols), lambda step: (step, 0)),
    ]
    aliases = {}
    if earlier is not None:
        aliases = {len(args): 0}
        args.append(earlier)
        in_specs.append(pl.BlockSpec(memory_space=pl.ANY))
    return pl.pallas_call(
        functools.partial(update_kernel, arrived.shape[1]),
        grid=(rows // step_rows,),
        in_specs=in_specs,
        out_specs=pl.BlockSpec((step_rows, cols), lambda step: (step, chunk)),
        out_shape=jax.ShapeDtypeStruct((rows, chunks * cols), jnp.float32),
        input_output_aliases=aliases,
        compiler_params=pltpu.CompilerParams(vmem_limit_bytes=VMEM_LIMIT),
        cost_estimate=pl.CostEstimate(
            flops=4 * rows * spread.size, bytes_accessed=rows * cols * 10, transcendentals=0
        ),
        name="update",
    )(*args)


def body(amplitudes, amp_mask, integrals, int_mask, group_orbital_numbers, occ_energy, vir_energy):
    tile_total = lax.axis_size("occ")
    vir_count = lax.axis_size("vir")
    row_tile = lax.axis_index("occ")
    vir_place = lax.axis_index("vir")
    span = W // vir_count
    slab_cols = span * W
    chunks = 2 if span >= 16 else 1
    part = span // chunks
    block = part * span
    rows = PAIR_SQ + CODE_ROWS
    barrier = lax.optimization_barrier

    def ladder_of(layout, slab_parts):
        return ladder_call(
            tile_total, vir_count, chunks, layout, amp_mask[0], group_orbital_numbers, amplitudes, slab_parts
        )

    def exchanged(packed):
        moved = lax.all_to_all(
            packed.reshape(tile_total * vir_count, rows, block), ("occ", "vir"), split_axis=0, concat_axis=0, tiled=True
        )
        return moved.reshape(tile_total, vir_count, rows, block)

    slabs = []
    if chunks > 1:
        ring_part, integrals = barrier((screen_call(0, chunks, int_mask, integrals), integrals))
    last = screen_call(chunks - 1, chunks, int_mask, integrals)
    if chunks > 1:
        travel = {1: ring_part, -1: ring_part}
        reached = ()
        pieces = across(travel, 0, tile_total)
        crossed = [piece[3] for piece in pieces] + [last]
        for step in range(1, tile_total // CORES):
            travel = line_step(travel, step, tile_total)
            reached = travel[1], travel[-1]
            exchange = across(travel, step, tile_total)
            pieces += exchange
            travel[1], travel[-1], *_ = barrier((*reached, *crossed))
            crossed = [piece[3] for piece in exchange]
        last, *_ = barrier((last, *reached))
        slabs.append(([piece[:3] for piece in pieces], [piece[3] for piece in pieces]))
    slabs.append(([(0, 0, False)], [lax.all_gather(last, "occ", axis=0, tiled=True)]))
    ladders, arrived = [], []
    for layout, slab_parts in slabs:
        ladder, packed = ladder_of(layout, slab_parts)
        ladders.append(ladder)
        arrived.append(exchanged(packed))

    place = jnp.arange(vir_count * block)
    owner, there_part = place // block, place // (part * part) % chunks
    here, there = place // part % part, place % part
    mirror_spread = one_hot_of(here * W + owner * span + there_part * part + there, part * W)
    place = jnp.arange(vir_count * part * part)
    owner, b, a = place // (part * part), place // part % part, place % part
    direct_spread = one_hot_of(
        jnp.concatenate([a * W + owner * span + c * part + b for c in range(chunks)]), part * W
    )

    occ_table = occ_energy.reshape(tile_total, ORBITALS_IN_GRP)
    own_energy = lax.dynamic_slice_in_dim(occ_table, row_tile, 1, 0)[0]
    occ_sum = jnp.broadcast_to(
        (own_energy[None, :, None] + occ_table[:, None, :]).reshape(-1, 1), (tile_total * PAIR_SQ, 128)
    )
    vir_own = lax.dynamic_slice_in_dim(vir_energy, vir_place * span, span, 0)
    vir_sum = (vir_own[:, None] + vir_energy[None, :]).reshape(1, -1)
    update = None
    for chunk in range(chunks):
        direct = direct_call(chunk, direct_spread, ladders)
        update = update_call(chunk, chunks, arrived[chunk], mirror_spread, vir_sum, occ_sum, direct, update)
    return update


def solution(mesh):
    in_specs = (P("occ", None), P("occ", None, None), P("occ", "vir"), P(), P(), P(), P())
    out_specs = P("occ", "vir")
    return jax.shard_map(body, mesh=mesh, in_specs=in_specs, out_specs=out_specs, check_vma=False)
```

time: 248 us -> 231 us (0.931)
  waiting for transfers between devices: 134 us -> 109 us
  starting transfers between devices: 26.9 us -> 31.6 us
  Pallas kernels: 65.5 us -> 68.8 us
    ppermute x6, waiting for transfers between devices: 70 us -> 38.8 us  [line_step(): arrived[sign] = lax.ppermute(travel[sign], 'occ', pairs)]
    all_to_all x2, waiting for transfers between devices: 37.4 us -> 44.2 us  [exchanged(): lax.all_to_all(packed.reshape(tile_total * vir_count, rows, block), ('occ...]
    pallas_call x5 -> x6, Pallas kernels: 59.7 us -> 63.1 us  [the longest x2 36.3 us: ladder_call(): pl.pallas_call(functools.partial(ladder_kernel, tile_total, vir_count, ch...]
    all_to_all x2, starting transfers between devices: 8.07 us -> 10.7 us  [exchanged(): lax.all_to_all(packed.reshape(tile_total * vir_count, rows, block), ('occ...]
  transfers between devices with their start and end apart: 16 -> 16, of which waited for: 6 -> 7; matrix products, arithmetic and copies ran while one was open for 2% -> 2% of each run, Pallas kernels for 16% -> 26%
where the time goes in v7:
time: 231 us; the launch traced here: 230 us
  waiting for transfers between devices  109 us (47%)
  Pallas kernels  68.8 us (30%)
  starting transfers between devices  31.6 us (14%)
  between operations  13.6 us (6%)
  local copies, waits for them, and re-layouts  4.4 us (2%)
    all_to_all x2, waiting for transfers between devices, exchanged(): lax.all_to_all(packed.reshape(tile_total * vir_count, rows, block), ('occ...  44.2 us
    ppermute x6, waiting for transfers between devices, line_step(): arrived[sign] = lax.ppermute(travel[sign], 'occ', pairs)  38.8 us
    pallas_call x2, Pallas kernels, ladder_call(): pl.pallas_call(functools.partial(ladder_kernel, tile_total, vir_count, ch...  36.3 us
    all_gather x1, waiting for transfers between devices, body(): lax.all_gather(last, 'occ', axis=0, tiled=True)  26.4 us
    pallas_call x2, Pallas kernels, update_call(): pl.pallas_call(functools.partial(update_kernel, arrived.shape[1]), grid=(...  14.2 us
    pallas_call x2, Pallas kernels, direct_call(): pl.pallas_call(direct_kernel, grid=(rows // step_rows,), in_specs=[pl.Blo...  12.5 us
    all_to_all x2, starting transfers between devices, exchanged(): lax.all_to_all(packed.reshape(tile_total * vir_count, rows, block), ('occ...  10.7 us
    ppermute x6, starting transfers between devices, line_step(): arrived[sign] = lax.ppermute(travel[sign], 'occ', pairs)  10.5 us
  transfers between devices with their start and end apart: 16, of which 7 were waited for; matrix products, arithmetic and copies ran while one was open for 2% of the time, Pallas kernels for 26%

profile of v7, /device:TPU:0, one launch (start us, length us, event | category | flops | bytes accessed | tf_op | source)
XLA Modules:
  0.0 229.9 jit_solution(9346721768423509295)
XLA Ops:
  6.5 0.0 all-gather.2.cloned.1.call-start
  6.5 2.8 %screen.2.refs_0_ = bf16[512,512]{1,0:T(8,128)(2,1)} custom-call(s32[4,4]{1,0:T(4,128)} %int_mask.3, bf16[512,1024]{1,0:T(8,128)(2,1)} %slab_ref.2), custom_call_target="tpu_custom_call" | custom-call | tf_op jit(solution)/shard_map/screen/pallas_call | solution.py:66
  9.4 0.5 collective-permute-start.2
  9.8 4.5 %collective-permute-start.1 = (bf16[512,512]{1,0:T(8,128)(2,1)}, bf16[512,512]{1,0:T(8,128)(2,1)S(1)}, u32[]{:S(2)}, u32[]{:S(2)}) collective-permute-start(bf16[512,512]{1,0:T(8,128)(2,1)} %screen.2.refs_0_), channel_id=1, source_target_pairs={{0,8},{4,12},{8,16},{12,20},{16,24},{20,28},{1,9},{5,13},{9,17},{1... | collective-permute-start | bytes 1572872 | tf_op jit(solution)/shard_map/ppermute | solution.py:81
  14.3 1.3 collective-permute-start
  15.6 2.9 %screen.3 = bf16[512,512]{1,0:T(8,128)(2,1)} custom-call(s32[4,4]{1,0:T(4,128)} %int_mask.3, bf16[512,1024]{1,0:T(8,128)(2,1)} %slab_ref.2), custom_call_target="tpu_custom_call" | custom-call | tf_op jit(solution)/shard_map/screen/pallas_call | solution.py:66
  18.5 0.0 collective-permute-done.2.refs_1_
  18.5 7.9 %collective-permute-done.1.refs_4_ = bf16[512,512]{1,0:T(8,128)(2,1)S(1)} collective-permute-done((bf16[512,512]{1,0:T(8,128)(2,1)}, bf16[512,512]{1,0:T(8,128)(2,1)S(1)}, u32[]{:S(2)}, u32[]{:S(2)}) %collective-permute-start.1) | collective-permute-done | bytes 524320 | tf_op jit(solution)/shard_map/ppermute | solution.py:81
  26.5 4.0 %collective-permute-done.refs_2_ = bf16[512,512]{1,0:T(8,128)(2,1)S(1)} collective-permute-done((bf16[512,512]{1,0:T(8,128)(2,1)}, bf16[512,512]{1,0:T(8,128)(2,1)S(1)}, u32[]{:S(2)}, u32[]{:S(2)}) %collective-permute-start) | collective-permute-done | bytes 524320 | tf_op jit(solution)/shard_map/ppermute | solution.py:81
  30.5 1.3 collective-permute-start.3
  31.8 0.7 collective-permute-start.6
  32.5 0.7 collective-permute-start.4
  33.2 1.9 collective-permute-start.5
  35.1 0.0 collective-permute-done.6.refs_5_
  35.1 0.0 copy-start.7
  35.1 10.5 %collective-permute-done.3.refs_6_ = bf16[512,512]{1,0:T(8,128)(2,1)S(1)} collective-permute-done((bf16[512,512]{1,0:T(8,128)(2,1)S(1)}, bf16[512,512]{1,0:T(8,128)(2,1)S(1)}, u32[]{:S(2)}, u32[]{:S(2)}) %collective-permute-start.3) | collective-permute-done | bytes 524320 | tf_op jit(solution)/shard_map/ppermute | solution.py:81
  45.6 0.0 collective-permute-done.4.refs_8_
  45.6 0.0 collective-permute-done.5.refs_3_
  45.6 0.0 copy-start.9
  45.6 1.3 collective-permute-start.7
  46.9 1.5 collective-permute-start.8
  48.4 16.3 %collective-permute-done.7.refs_10_ = bf16[512,512]{1,0:T(8,128)(2,1)S(1)} collective-permute-done((bf16[512,512]{1,0:T(8,128)(2,1)S(1)}, bf16[512,512]{1,0:T(8,128)(2,1)S(1)}, u32[]{:S(2)}, u32[]{:S(2)}) %collective-permute-start.7) | collective-permute-done | bytes 524320 | tf_op jit(solution)/shard_map/ppermute | solution.py:81
  64.8 0.0 copy-done.9
  64.8 0.8 copy-done.10
  65.6 0.0 collective-permute-done.8.refs_12_
  65.6 0.0 all-gather.2.cloned.1.call-update
  65.6 1.9 collective-permute-start.9
  67.5 1.5 collective-permute-start.10
  69.0 2.4 %collective-permute-start.11 = (bf16[512,512]{1,0:T(8,128)(2,1)}, bf16[512,512]{1,0:T(8,128)(2,1)}, u32[]{:S(2)}, u32[]{:S(2)}) collective-permute-start(bf16[512,512]{1,0:T(8,128)(2,1)} %copy-done.10), channel_id=1, source_target_pairs={{0,4},{4,0},{1,5},{5,1},{2,6},{6,2},{3,7},{7,3}} | collective-permute-start | bytes 1572872 | tf_op jit(solution)/shard_map/ppermute | solution.py:91
  71.4 1.5 collective-permute-start.12
  72.9 1.3 copy.9.amp_mask
  74.2 0.0 collective-permute-done.9.refs_7_
  74.2 0.0 collective-permute-done.10.refs_9_
  74.2 0.0 collective-permute-done.11.refs_11_
  74.2 0.0 collective-permute-done.12.refs_13_
  74.2 0.0 copy-done.3
  74.3 0.0 copy-done.4
  74.3 0.0 copy-done.5
  74.3 0.0 copy-done.7
  74.3 0.0 copy-done.6
  74.3 0.0 copy-done.8
  74.3 18.9 %ladder.3 = (f32[2,2048,256]{2,1,0:T(8,128)}, s16[8,4,272,128]{3,2,1,0:T(8,128)(2,1)}) custom-call(s32[8,4]{1,0:T(8,128)} %copy.9.amp_mask, s32[8]{0:T(128)} %numbers.3, bf16[2048,4096]{1,0:T(8,128)(2,1)} %rows_ref.3, bf16[512,512]{1,0:T(8,128)(2,1)} %screen.2.refs_0_, bf16[512,512]{1,0:T(8,128)(2,1)} %copy-done.3, bf16[512,512]{1,0:T(8,128)(2,1)} %copy-done.5, ...), custom_call_target="tpu_custom_call" | custom-call | flops 8589934592 | bytes 27262976 | tf_op jit(solution)/shard_map/ladder/pallas_call | solution.py:174
  93.2 7.1 %all-to-all-start.1 = ((s16[32,272,128]{2,1,0:T(8,128)(2,1)}), s16[32,272,128]{2,1,0:T(8,128)(2,1)S(1)}, u32[]{:S(2)}, u32[]{:S(2)}) async-start(s16[32,272,128]{2,1,0:T(8,128)(2,1)} %bitcast.9), calls=%async_computation.1 | async-start | bytes 4456448 | tf_op jit(solution)/shard_map/all_to_all | solution.py:291
  100.3 26.4 %all-gather.2.cloned.1.call-done.refs_0_ = bf16[4096,512]{1,0:T(8,128)(2,1)} async-done(((bf16[512,512]{1,0:T(8,128)(2,1)}), bf16[4096,512]{1,0:T(8,128)(2,1)}) %all-gather.2.cloned.1.call-update) | async-done | bytes 4194320 | tf_op jit(solution)/shard_map/all_gather | solution.py:314
  126.8 17.4 %ladder.2 = (f32[2,2048,256]{2,1,0:T(8,128)}, s16[8,4,272,128]{3,2,1,0:T(8,128)(2,1)}) custom-call(s32[8,4]{1,0:T(8,128)} %copy.9.amp_mask, s32[8]{0:T(128)} %numbers.3, bf16[2048,4096]{1,0:T(8,128)(2,1)} %rows_ref.3, bf16[4096,512]{1,0:T(8,128)(2,1)} %all-gather.2.cloned.1.call-done.refs_0_), custom_call_target="tpu_custom_call" | custom-call | flops 8589934592 | bytes 27262976 | tf_op jit(solution)/shard_map/ladder/pallas_call | solution.py:174
  144.2 16.7 %all-to-all-done.1 = s16[32,272,128]{2,1,0:T(8,128)(2,1)S(1)} async-done(((s16[32,272,128]{2,1,0:T(8,128)(2,1)}), s16[32,272,128]{2,1,0:T(8,128)(2,1)S(1)}, u32[]{:S(2)}, u32[]{:S(2)}) %all-to-all-start.1) | async-done | bytes 2228256 | tf_op jit(solution)/shard_map/all_to_all | solution.py:291
  160.9 3.6 %all-to-all-start = ((s16[32,272,128]{2,1,0:T(8,128)(2,1)}), s16[32,272,128]{2,1,0:T(8,128)(2,1)}, u32[]{:S(2)}, u32[]{:S(2)}) async-start(s16[32,272,128]{2,1,0:T(8,128)(2,1)} %bitcast.8), calls=%async_computation | async-start | bytes 4456448 | tf_op jit(solution)/shard_map/all_to_all | solution.py:291
  164.5 0.0 copy-done.1
  164.5 0.1 reshape.124
  164.6 0.0 copy-done.2
  164.6 0.1 dynamic_slice.6
  164.7 0.1 broadcast_add_fusion.1
  164.7 0.7 add.167.vir_ref
  165.4 0.1 broadcast_add_fusion
  165.5 0.1 add.173
  165.6 0.9 fusion.1.spread_ref
  166.6 0.9 fusion.spread_ref
  167.5 6.1 %direct.3.direct_ref = f32[2048,512]{1,0:T(8,128)} custom-call(bf16[512,512]{1,0:T(8,128)(2,1)} %fusion.1.spread_ref, f32[2,2048,256]{2,1,0:T(8,128)} %get-tuple-element.24.refs_0_, f32[2,2048,256]{2,1,0:T(8,128)} %get-tuple-element.25.refs_1_), custom_call_target="tpu_custom_call" | custom-call | flops 2147483648 | bytes 8388608 | tf_op jit(solution)/shard_map/direct/pallas_call | solution.py:212
  173.6 0.0 copy-done
  173.6 6.4 %direct.2.direct_ref = f32[2048,512]{1,0:T(8,128)} custom-call(bf16[512,512]{1,0:T(8,128)(2,1)} %fusion.1.spread_ref, f32[2,2048,256]{2,1,0:T(8,128)} %get-tuple-element.24.refs_0_, f32[2,2048,256]{2,1,0:T(8,128)} %get-tuple-element.25.refs_1_), custom_call_target="tpu_custom_call" | custom-call | flops 2147483648 | bytes 8388608 | tf_op jit(solution)/shard_map/direct/pallas_call | solution.py:212
  180.0 1.3 broadcast_in_dim.2.occ_ref
  181.3 7.1 %update.2.refs_0_ = f32[2048,1024]{1,0:T(8,128)} custom-call(s16[8,4,272,128]{3,2,1,0:T(8,128)(2,1)} %bitcast.7, bf16[512,512]{1,0:T(8,128)(2,1)} %fusion.spread_ref, f32[1,1024]{1,0:T(1,128)} %add.167.vir_ref, f32[2048,128]{1,0:T(8,128)} %broadcast_in_dim.2.occ_ref, f32[2048,512]{1,0:T(8,128)} %direct.3.direct_ref), custom_call_target="tpu_custom_call" | custom-call | flops 2147483648 | bytes 10485760 | tf_op jit(solution)/shard_map/update/pallas_call | solution.py:257
  188.5 27.5 %all-to-all-done = s16[32,272,128]{2,1,0:T(8,128)(2,1)} async-done(((s16[32,272,128]{2,1,0:T(8,128)(2,1)}), s16[32,272,128]{2,1,0:T(8,128)(2,1)}, u32[]{:S(2)}, u32[]{:S(2)}) %all-to-all-start) | async-done | bytes 2228256 | tf_op jit(solution)/shard_map/all_to_all | solution.py:291
  216.0 7.1 %update.3 = f32[2048,1024]{1,0:T(8,128)} custom-call(s16[8,4,272,128]{3,2,1,0:T(8,128)(2,1)} %bitcast.2.arrived_ref, bf16[512,512]{1,0:T(8,128)(2,1)} %fusion.spread_ref, f32[1,1024]{1,0:T(1,128)} %add.167.vir_ref, f32[2048,128]{1,0:T(8,128)} %broadcast_in_dim.2.occ_ref, f32[2048,512]{1,0:T(8,128)} %direct.2.direct_ref, ...), custom_call_target="tpu_custom_call", output_to_operand_aliasing={{}: (5, {})} | custom-call | flops 2147483648 | bytes 10485760 | tf_op jit(solution)/shard_map/update/pallas_call | solution.py:257
  (13 shorter events, 0.0 us)
Async XLA Ops:
  6.5 120.2 %all-gather.2.cloned.1.call-start = ((), (), s32[]{:S(2)}) async-start(), calls=%async_computation.2 | async-start | bytes 4718592 | tf_op jit(solution)/shard_map/all_gather | solution.py:314
  9.4 9.1 %collective-permute-start.2 = (bf16[512,512]{1,0:T(8,128)(2,1)}, bf16[512,512]{1,0:T(8,128)(2,1)S(1)}, u32[]{:S(2)}, u32[]{:S(2)}) collective-permute-start(bf16[512,512]{1,0:T(8,128)(2,1)} %screen.2.refs_0_), channel_id=1, source_target_pairs={{0,4},{4,0},{8,12},{12,8},{16,20},{20,16},{24,28},{28,24},{1,5},{5... | collective-permute-start | bytes 1572872 | tf_op jit(solution)/shard_map/ppermute | solution.py:91
  9.8 16.6 %collective-permute-start.1 = (bf16[512,512]{1,0:T(8,128)(2,1)}, bf16[512,512]{1,0:T(8,128)(2,1)S(1)}, u32[]{:S(2)}, u32[]{:S(2)}) collective-permute-start(bf16[512,512]{1,0:T(8,128)(2,1)} %screen.2.refs_0_), channel_id=1, source_target_pairs={{0,8},{4,12},{8,16},{12,20},{16,24},{20,28},{1,9},{5,13},{9,17},{1... | collective-permute-start | bytes 1572872 | tf_op jit(solution)/shard_map/ppermute | solution.py:81
  14.3 16.2 %collective-permute-start = (bf16[512,512]{1,0:T(8,128)(2,1)}, bf16[512,512]{1,0:T(8,128)(2,1)S(1)}, u32[]{:S(2)}, u32[]{:S(2)}) collective-permute-start(bf16[512,512]{1,0:T(8,128)(2,1)} %screen.2.refs_0_), channel_id=1, source_target_pairs={{8,0},{12,4},{16,8},{20,12},{24,16},{28,20},{9,1},{13,5},{17,9},{2... | collective-permute-start | bytes 1572872 | tf_op jit(solution)/shard_map/ppermute | solution.py:81
  18.5 55.7 %copy-start.3 = (bf16[512,512]{1,0:T(8,128)(2,1)}, bf16[512,512]{1,0:T(8,128)(2,1)S(1)}, u32[]{:S(2)}) copy-start(bf16[512,512]{1,0:T(8,128)(2,1)S(1)} %collective-permute-done.2.refs_1_) | copy-start | bytes 1572868
  26.5 47.8 %copy-start.4 = (bf16[512,512]{1,0:T(8,128)(2,1)}, bf16[512,512]{1,0:T(8,128)(2,1)S(1)}, u32[]{:S(2)}) copy-start(bf16[512,512]{1,0:T(8,128)(2,1)S(1)} %collective-permute-done.1.refs_4_) | copy-start | bytes 1572868
  30.5 43.8 %copy-start.5 = (bf16[512,512]{1,0:T(8,128)(2,1)}, bf16[512,512]{1,0:T(8,128)(2,1)S(1)}, u32[]{:S(2)}) copy-start(bf16[512,512]{1,0:T(8,128)(2,1)S(1)} %collective-permute-done.refs_2_) | copy-start | bytes 1572868
  30.5 15.1 %collective-permute-start.3 = (bf16[512,512]{1,0:T(8,128)(2,1)S(1)}, bf16[512,512]{1,0:T(8,128)(2,1)S(1)}, u32[]{:S(2)}, u32[]{:S(2)}) collective-permute-start(bf16[512,512]{1,0:T(8,128)(2,1)S(1)} %collective-permute-done.refs_2_), channel_id=1, source_target_pairs={{8,0},{12,4},{16,8},{20,12},{9,1},{13,5},{17,9},{21,13},{10,2},{14... | collective-permute-start | bytes 1572872 | tf_op jit(solution)/shard_map/ppermute | solution.py:81
  31.8 3.3 %collective-permute-start.6 = (bf16[512,512]{1,0:T(8,128)(2,1)S(1)}, bf16[512,512]{1,0:T(8,128)(2,1)S(1)}, u32[]{:S(2)}, u32[]{:S(2)}) collective-permute-start(bf16[512,512]{1,0:T(8,128)(2,1)S(1)} %collective-permute-done.1.refs_4_), channel_id=1, source_target_pairs={{8,12},{12,8},{16,20},{20,16},{24,28},{28,24},{9,13},{13,9},{17,21... | collective-permute-start | bytes 1572872 | tf_op jit(solution)/shard_map/ppermute | solution.py:91
  32.5 13.1 %collective-permute-start.4 = (bf16[512,512]{1,0:T(8,128)(2,1)S(1)}, bf16[512,512]{1,0:T(8,128)(2,1)S(1)}, u32[]{:S(2)}, u32[]{:S(2)}) collective-permute-start(bf16[512,512]{1,0:T(8,128)(2,1)S(1)} %collective-permute-done.1.refs_4_), channel_id=1, source_target_pairs={{8,16},{12,20},{16,24},{20,28},{9,17},{13,21},{17,25},{21,29},{10,... | collective-permute-start | bytes 1572872 | tf_op jit(solution)/shard_map/ppermute | solution.py:81
  33.2 12.4 %collective-permute-start.5 = (bf16[512,512]{1,0:T(8,128)(2,1)S(1)}, bf16[512,512]{1,0:T(8,128)(2,1)S(1)}, u32[]{:S(2)}, u32[]{:S(2)}) collective-permute-start(bf16[512,512]{1,0:T(8,128)(2,1)S(1)} %collective-permute-done.refs_2_), channel_id=1, source_target_pairs={{0,4},{4,0},{8,12},{12,8},{16,20},{20,16},{1,5},{5,1},{9,13},{13,9... | collective-permute-start | bytes 1572872 | tf_op jit(solution)/shard_map/ppermute | solution.py:91
  35.1 39.1 %copy-start.7 = (bf16[512,512]{1,0:T(8,128)(2,1)}, bf16[512,512]{1,0:T(8,128)(2,1)S(1)}, u32[]{:S(2)}) copy-start(bf16[512,512]{1,0:T(8,128)(2,1)S(1)} %collective-permute-done.6.refs_5_) | copy-start | bytes 1572868
  45.6 28.7 %copy-start.6 = (bf16[512,512]{1,0:T(8,128)(2,1)}, bf16[512,512]{1,0:T(8,128)(2,1)S(1)}, u32[]{:S(2)}) copy-start(bf16[512,512]{1,0:T(8,128)(2,1)S(1)} %collective-permute-done.3.refs_6_) | copy-start | bytes 1572868
  45.6 28.7 %copy-start.8 = (bf16[512,512]{1,0:T(8,128)(2,1)}, bf16[512,512]{1,0:T(8,128)(2,1)S(1)}, u32[]{:S(2)}) copy-start(bf16[512,512]{1,0:T(8,128)(2,1)S(1)} %collective-permute-done.4.refs_8_) | copy-start | bytes 1572868
  45.6 19.1 %copy-start.9 = (bf16[512,512]{1,0:T(8,128)(2,1)}, bf16[512,512]{1,0:T(8,128)(2,1)S(1)}, u32[]{:S(2)}) copy-start(bf16[512,512]{1,0:T(8,128)(2,1)S(1)} %collective-permute-done.5.refs_3_) | copy-start | bytes 1572868
  45.6 19.1 %collective-permute-start.7 = (bf16[512,512]{1,0:T(8,128)(2,1)S(1)}, bf16[512,512]{1,0:T(8,128)(2,1)S(1)}, u32[]{:S(2)}, u32[]{:S(2)}) collective-permute-start(bf16[512,512]{1,0:T(8,128)(2,1)S(1)} %collective-permute-done.3.refs_6_), channel_id=1, source_target_pairs={{8,0},{12,4},{9,1},{13,5},{10,2},{14,6},{11,3},{15,7}} | collective-permute-start | bytes 1572872 | tf_op jit(solution)/shard_map/ppermute | solution.py:81
  46.9 18.6 %collective-permute-start.8 = (bf16[512,512]{1,0:T(8,128)(2,1)S(1)}, bf16[512,512]{1,0:T(8,128)(2,1)}, u32[]{:S(2)}, u32[]{:S(2)}) collective-permute-start(bf16[512,512]{1,0:T(8,128)(2,1)S(1)} %collective-permute-done.4.refs_8_), channel_id=1, source_target_pairs={{16,24},{20,28},{17,25},{21,29},{18,26},{22,30},{19,27},{23,31}} | collective-permute-start | bytes 1572872 | tf_op jit(solution)/shard_map/ppermute | solution.py:81
  64.8 0.8 copy-start.10
  65.6 8.6 %collective-permute-start.9 = (bf16[512,512]{1,0:T(8,128)(2,1)S(1)}, bf16[512,512]{1,0:T(8,128)(2,1)}, u32[]{:S(2)}, u32[]{:S(2)}) collective-permute-start(bf16[512,512]{1,0:T(8,128)(2,1)S(1)} %collective-permute-done.3.refs_6_), channel_id=1, source_target_pairs={{0,4},{4,0},{8,12},{12,8},{1,5},{5,1},{9,13},{13,9},{2,6},{6,2},{1... | collective-permute-start | bytes 1572872 | tf_op jit(solution)/shard_map/ppermute | solution.py:91
  67.5 6.7 %collective-permute-start.10 = (bf16[512,512]{1,0:T(8,128)(2,1)S(1)}, bf16[512,512]{1,0:T(8,128)(2,1)}, u32[]{:S(2)}, u32[]{:S(2)}) collective-permute-start(bf16[512,512]{1,0:T(8,128)(2,1)S(1)} %collective-permute-done.4.refs_8_), channel_id=1, source_target_pairs={{16,20},{20,16},{24,28},{28,24},{17,21},{21,17},{25,29},{29,25},{1... | collective-permute-start | bytes 1572872 | tf_op jit(solution)/shard_map/ppermute | solution.py:91
  69.0 5.2 %collective-permute-start.11 = (bf16[512,512]{1,0:T(8,128)(2,1)}, bf16[512,512]{1,0:T(8,128)(2,1)}, u32[]{:S(2)}, u32[]{:S(2)}) collective-permute-start(bf16[512,512]{1,0:T(8,128)(2,1)} %copy-done.10), channel_id=1, source_target_pairs={{0,4},{4,0},{1,5},{5,1},{2,6},{6,2},{3,7},{7,3}} | collective-permute-start | bytes 1572872 | tf_op jit(solution)/shard_map/ppermute | solution.py:91
  71.4 2.8 %collective-permute-start.12 = (bf16[512,512]{1,0:T(8,128)(2,1)}, bf16[512,512]{1,0:T(8,128)(2,1)}, u32[]{:S(2)}, u32[]{:S(2)}) collective-permute-start(bf16[512,512]{1,0:T(8,128)(2,1)} %collective-permute-done.8.refs_12_), channel_id=1, source_target_pairs={{24,28},{28,24},{25,29},{29,25},{26,30},{30,26},{27,31},{31,27}} | collective-permute-start | bytes 1572872 | tf_op jit(solution)/shard_map/ppermute | solution.py:91
  93.2 67.7 %all-to-all-start.1 = ((s16[32,272,128]{2,1,0:T(8,128)(2,1)}), s16[32,272,128]{2,1,0:T(8,128)(2,1)S(1)}, u32[]{:S(2)}, u32[]{:S(2)}) async-start(s16[32,272,128]{2,1,0:T(8,128)(2,1)} %bitcast.9), calls=%async_computation.1 | async-start | bytes 4456448 | tf_op jit(solution)/shard_map/all_to_all | solution.py:291
  144.2 20.3 %copy-start.1 = (f32[128]{0:T(128)S(1)}, f32[128]{0:T(128)}, u32[]{:S(2)}) copy-start(f32[128]{0:T(128)} %param.12) | copy-start | bytes 1540
  144.2 20.4 %copy-start.2 = (f32[64]{0:T(128)S(1)}, f32[64]{0:T(128)}, u32[]{:S(2)}) copy-start(f32[64]{0:T(128)} %param.13) | copy-start | bytes 772
  160.9 12.8 %copy-start = (s16[32,272,128]{2,1,0:T(8,128)(2,1)}, s16[32,272,128]{2,1,0:T(8,128)(2,1)S(1)}, u32[]{:S(2)}) copy-start(s16[32,272,128]{2,1,0:T(8,128)(2,1)S(1)} %all-to-all-done.1) | copy-start | bytes 6684676
  160.9 55.1 %all-to-all-start = ((s16[32,272,128]{2,1,0:T(8,128)(2,1)}), s16[32,272,128]{2,1,0:T(8,128)(2,1)}, u32[]{:S(2)}, u32[]{:S(2)}) async-start(s16[32,272,128]{2,1,0:T(8,128)(2,1)} %bitcast.8), calls=%async_computation | async-start | bytes 4456448 | tf_op jit(solution)/shard_map/all_to_all | solution.py:291
Sparse Core Ops, SparseCore 0:
  65.7 61.0 all-gather.1

commit v8 on v7

--- a/solution.py
+++ b/solution.py
@@ -12,9 +12,9 @@
 W = 64
 ORBITALS_IN_GRP = 16
 PAIR_SQ = ORBITALS_IN_GRP * ORBITALS_IN_GRP
-CORES = 2
 CODE_ROWS = 16
 AT_ONCE = 2
+SLAB_BITS = 14.0
 TOP = 32700.0
 STEPS = 8.0
 VMEM_LIMIT = 56 * 1024 * 1024
@@ -37,93 +37,85 @@
     return jnp.exp2(code * (1.0 / STEPS))
 
 
-def screen_kernel(chunk, part, int_mask, slab_ref, screened_ref):
+def screen_kernel(part, int_mask, slab_ref, coded_ref, *later_refs):
     slab_rows, slab_cols = slab_ref.shape
-    cols = screened_ref.shape[1]
+    cols = coded_ref.shape[1]
     span = slab_cols // W
     row_label = lax.axis_index("occ") * slab_rows // W // VT * NVT
     col_label = lax.axis_index("vir") * slab_cols // W // VT * NVT
     natural = lax.broadcasted_iota(jnp.int32, (slab_cols, 1), 0)
     a, b = natural // W, natural % W
     target = b // span * (part * span) + (a // part * part + b % part) * part + a % part
-    target = jnp.where(b % span // part == chunk, target, -1)
     place = lax.broadcasted_iota(jnp.int32, (slab_cols, cols), 1)
-    moved = dot(slab_ref[...], (place == target).astype(jnp.float32).astype(jnp.bfloat16)).astype(jnp.bfloat16)
-    to = lax.broadcasted_iota(jnp.int32, (VT, cols), 1)
-    owner, of_part = to // (part * span), to // part % part
-    right = owner * span + chunk * part + of_part >= VT
-    for d_tile in range(NVT):
-        label = row_label + d_tile
-        kept = jnp.where(right, int_mask[label, col_label + 1], int_mask[label, col_label])
-        kept = kept.astype(jnp.float32).astype(jnp.bfloat16)
-        for at in range(d_tile * VT, slab_rows, NVT * VT):
-            screened_ref[at : at + VT, :] = moved[at : at + VT, :] * kept
-
-
-def screen_call(chunk, chunks, int_mask, integrals):
+    to = lax.broadcasted_iota(jnp.int32, (1, cols), 1)
+    second = lax.broadcasted_iota(jnp.int32, (slab_rows, 1), 0) % W >= VT
+    for chunk in range(1 + len(later_refs)):
+        right = to // (part * span) * span + chunk * part + to // part % part >= VT
+        kept = [
+            jnp.where(right, int_mask[label, col_label + 1], int_mask[label, col_label])
+            for label in (row_label, row_label + 1)
+        ]
+        ones = place == jnp.where(b % span // part == chunk, target, -1)
+        moved = dot(slab_ref[...], ones.astype(jnp.float32).astype(jnp.bfloat16))
+        moved = jnp.where(jnp.where(second, kept[1], kept[0]) > 0, moved, 0.0)
+        if chunk:
+            later_refs[chunk - 1][...] = moved.astype(jnp.bfloat16)
+        else:
+            most = jnp.maximum(jnp.max(jnp.abs(moved), axis=0, keepdims=True), 1e-30)
+            code = jnp.floor(jnp.log2(most)) + 1.0
+            coded = jnp.round(moved * jnp.exp2(SLAB_BITS - code)).astype(jnp.int32)
+            coded_ref[:slab_rows, :] = coded.astype(jnp.int16)
+            coded_ref[slab_rows:, :] = jnp.broadcast_to(code.astype(jnp.int32), (CODE_ROWS, cols)).astype(jnp.int16)
+
+
+def screen_call(chunks, int_mask, integrals):
     slab_rows, slab_cols = integrals.shape
+    cols = slab_cols // chunks
     vmem = pl.BlockSpec(memory_space=pltpu.VMEM)
     return pl.pallas_call(
-        functools.partial(screen_kernel, chunk, slab_cols // W // chunks),
+        functools.partial(screen_kernel, slab_cols // W // chunks),
         in_specs=[pl.BlockSpec(memory_space=pltpu.SMEM), vmem],
-        out_specs=vmem,
-        out_shape=jax.ShapeDtypeStruct((slab_rows, slab_cols // chunks), integrals.dtype),
+        out_specs=[vmem] * chunks,
+        out_shape=[jax.ShapeDtypeStruct((slab_rows + CODE_ROWS, cols), jnp.int16)]
+        + [jax.ShapeDtypeStruct((slab_rows, cols), integrals.dtype)] * (chunks - 1),
         compiler_params=pltpu.CompilerParams(vmem_limit_bytes=VMEM_LIMIT),
         name="screen",
     )(int_mask, integrals)
 
 
-def line_step(travel, step, tile_total):
-    chips = tile_total // CORES
-    arrived = {}
-    for sign in (1, -1):
-        pairs = [(t + sign * CORES, t) for t in range(tile_total) if 0 <= t // CORES + sign * step < chips]
-        arrived[sign] = lax.ppermute(travel[sign], "occ", pairs)
-    return arrived
-
-
-def across(travel, step, tile_total):
-    chips = tile_total // CORES
-    pieces = []
-    for sign in (1, -1) if step else (1,):
-        pairs = [(t, t ^ 1) for t in range(tile_total) if 0 <= t // CORES + sign * step < chips]
-        pieces.append((sign, step, False, travel[sign]))
-        pieces.append((sign, step, True, lax.ppermute(travel[sign], "occ", pairs)))
-    return pieces
-
-
-def fill_slab(layout, refs, slab_scr, sems):
-    tile = lax.axis_index("occ")
-    chips = lax.axis_size("occ") // CORES
-    chip, core = tile // CORES, tile % CORES
-    slab_rows = refs[0].shape[0]
-
-    def each(act):
-        for n, (sign, step, other) in enumerate(layout):
-            at_chip = chip + sign * step
-
-            @pl.when((at_chip >= 0) & (at_chip < chips))
-            def _():
-                place = at_chip * CORES + (1 - core if other else core)
-                at = pl.ds(pl.multiple_of(place * slab_rows, slab_rows), slab_rows)
-                act(pltpu.make_async_copy(refs[n], slab_scr.at[at, :], sems.at[n]))
-
-    each(lambda copy: copy.start())
-    each(lambda copy: copy.wait())
-
-
-def ladder_kernel(tile_total, vir_count, chunks, layout, amp_mask, numbers, rows_ref, *refs):
-    pieces, refs = refs[: len(layout)], refs[len(layout) :]
-    ladder_ref, packed_ref, product, refs = refs[0], refs[1], refs[2], refs[3:]
+def decode_slab(tile_total, coded_ref, stage, slab_scr, sems):
+    slab_rows = slab_scr.shape[0] // tile_total
+    coded_rows = slab_rows + CODE_ROWS
+
+    def copy_of(tile):
+        at = pl.ds(pl.multiple_of(tile * coded_rows, CODE_ROWS), coded_rows)
+        return pltpu.make_async_copy(coded_ref.at[at, :], stage.at[at, :], sems.at[tile])
+
+    for tile in range(tile_total):
+        copy_of(tile).start()
+
+    def decode(tile, carry):
+        copy_of(tile).wait()
+        at = pl.multiple_of(tile * coded_rows, CODE_ROWS)
+        code = stage[pl.ds(pl.multiple_of(at + slab_rows, CODE_ROWS), CODE_ROWS), :]
+        values = stage[pl.ds(at, slab_rows), :].astype(jnp.int32).astype(jnp.float32)
+        scale = jnp.exp2(code.astype(jnp.int32).astype(jnp.float32)[:1] - SLAB_BITS)
+        to = pl.ds(pl.multiple_of(tile * slab_rows, slab_rows), slab_rows)
+        slab_scr[to, :] = (values * scale).astype(jnp.bfloat16)
+        return carry
+
+    lax.fori_loop(0, tile_total, decode, 0)
+
+
+def ladder_kernel(tile_total, vir_count, chunks, amp_mask, numbers, rows_ref, slab_ref, *refs):
+    ladder_ref, packed_ref, product = refs[:3]
     step = pl.program_id(0)
-    if len(layout) > 1:
-        slab_ref, sems = refs
+    if len(refs) > 3:
+        coded_ref, (stage, slab_ref, sems) = slab_ref, refs[3:]
 
         @pl.when(step == 0)
         def _():
-            fill_slab(layout, pieces, slab_ref, sems)
-    else:
-        slab_ref = pieces[0]
+            decode_slab(tile_total, coded_ref, stage, slab_ref, sems)
     cols = slab_ref.shape[1]
 
     tile = jnp.maximum(step - 1, 0)
@@ -160,22 +152,29 @@
     product[...] = dot(screened, slab_ref[...])
 
 
-def ladder_call(tile_total, vir_count, chunks, layout, amp_mask, numbers, amplitudes, slab_parts):
-    cols = slab_parts[0].shape[1]
+def ladder_call(tile_total, vir_count, chunks, amp_mask, numbers, amplitudes, slab):
+    cols = slab.shape[1]
     block = cols // vir_count
     smem = pl.BlockSpec(memory_space=pltpu.SMEM)
     rows = tile_total * PAIR_SQ
     scratch = [pltpu.VMEM((PAIR_SQ, cols), jnp.float32)]
-    if len(layout) > 1:
-        slab_specs = [pl.BlockSpec(memory_space=pl.ANY)] * len(layout)
-        scratch += [pltpu.VMEM((W * W, cols), jnp.bfloat16), pltpu.SemaphoreType.DMA((len(layout),))]
-    else:
-        slab_specs = [pl.BlockSpec((W * W, cols), lambda step: (0, 0))]
+    slab_spec = pl.BlockSpec((W * W, cols), lambda step: (0, 0))
+    if slab.dtype == jnp.int16:
+        slab_spec = pl.BlockSpec(memory_space=pl.ANY)
+        scratch += [
+            pltpu.VMEM(slab.shape, slab.dtype),
+            pltpu.VMEM((W * W, cols), jnp.bfloat16),
+            pltpu.SemaphoreType.DMA((tile_total,)),
+        ]
     return pl.pallas_call(
-        functools.partial(ladder_kernel, tile_total, vir_count, chunks, layout),
+        functools.partial(ladder_kernel, tile_total, vir_count, chunks),
         grid=(tile_total + 1,),
-        in_specs=[smem, smem, pl.BlockSpec((PAIR_SQ, W * W), lambda step: (jnp.minimum(step, tile_total - 1), 0))]
-        + slab_specs,
+        in_specs=[
+            smem,
+            smem,
+            pl.BlockSpec((PAIR_SQ, W * W), lambda step: (jnp.minimum(step, tile_total - 1), 0)),
+            slab_spec,
+        ],
         out_specs=[
             pl.BlockSpec((chunks, PAIR_SQ, cols // chunks), lambda step: (0, jnp.maximum(step - 1, 0), 0)),
             pl.BlockSpec(
@@ -194,7 +193,7 @@
             transcendentals=0,
         ),
         name="ladder",
-    )(amp_mask, numbers, amplitudes, *slab_parts)
+    )(amp_mask, numbers, amplitudes, slab)
 
 
 def moved_columns(values, spread_ref):
@@ -280,12 +279,6 @@
     part = span // chunks
     block = part * span
     rows = PAIR_SQ + CODE_ROWS
-    barrier = lax.optimization_barrier
-
-    def ladder_of(layout, slab_parts):
-        return ladder_call(
-            tile_total, vir_count, chunks, layout, amp_mask[0], group_orbital_numbers, amplitudes, slab_parts
-        )
 
     def exchanged(packed):
         moved = lax.all_to_all(
@@ -293,28 +286,16 @@
         )
         return moved.reshape(tile_total, vir_count, rows, block)
 
-    slabs = []
-    if chunks > 1:
-        ring_part, integrals = barrier((screen_call(0, chunks, int_mask, integrals), integrals))
-    last = screen_call(chunks - 1, chunks, int_mask, integrals)
-    if chunks > 1:
-        travel = {1: ring_part, -1: ring_part}
-        reached = ()
-        pieces = across(travel, 0, tile_total)
-        crossed = [piece[3] for piece in pieces] + [last]
-        for step in range(1, tile_total // CORES):
-            travel = line_step(travel, step, tile_total)
-            reached = travel[1], travel[-1]
-            exchange = across(travel, step, tile_total)
-            pieces += exchange
-            travel[1], travel[-1], *_ = barrier((*reached, *crossed))
-            crossed = [piece[3] for piece in exchange]
-        last, *_ = barrier((last, *reached))
-        slabs.append(([piece[:3] for piece in pieces], [piece[3] for piece in pieces]))
-    slabs.append(([(0, 0, False)], [lax.all_gather(last, "occ", axis=0, tiled=True)]))
+    coded, *later = screen_call(chunks, int_mask, integrals)
+    slabs = [lax.all_gather(coded, "occ", axis=0, tiled=True)]
+    for part_later in later:
+        part_later, _ = lax.optimization_barrier((part_later, slabs[-1]))
+        slabs.append(lax.all_gather(part_later, "occ", axis=0, tiled=True))
     ladders, arrived = [], []
-    for layout, slab_parts in slabs:
-        ladder, packed = ladder_of(layout, slab_parts)
+    for slab in slabs:
+        ladder, packed = ladder_call(
+            tile_total, vir_count, chunks, amp_mask[0], group_orbital_numbers, amplitudes, slab
+        )
         ladders.append(ladder)
         arrived.append(exchanged(packed))
 

time: 231 us -> 218 us (0.944)
  blocking collectives: 0 us -> 42.6 us
  waiting for transfers between devices: 109 us -> 79.1 us
  starting transfers between devices: 31.6 us -> 9.59 us
    all_gather x0 -> x1, blocking collectives: none -> 42.6 us  [body(): slabs = [lax.all_gather(coded, 'occ', axis=0, tiled=True)]]
    ppermute x13 -> x0, waiting for transfers between devices: 38.8 us -> none  [the longest x6 38.8 us: line_step(): arrived[sign] = lax.ppermute(travel[sign], 'occ', pairs)]
    all_gather x1, waiting for transfers between devices: 26.4 us -> 47.9 us  [body(): slabs.append(lax.all_gather(part_later, 'occ', axis=0, tiled=True))]
    ppermute x13 -> x0, starting transfers between devices: 20.9 us -> none  [the longest x6 10.5 us: line_step(): arrived[sign] = lax.ppermute(travel[sign], 'occ', pairs)]
    all_to_all x2, waiting for transfers between devices: 44.2 us -> 31.2 us  [exchanged(): lax.all_to_all(packed.reshape(tile_total * vir_count, rows, block), ('occ...]
    pallas_call x2 -> x1, Pallas kernels: 5.71 us -> 3.67 us  [screen_call(): pl.pallas_call(functools.partial(screen_kernel, slab_cols // W // chunks)...]
  transfers between devices with their start and end apart: 16 -> 3, of which waited for: 7 -> 3; matrix products, arithmetic and copies ran while one was open for 2% -> 2% of each run, Pallas kernels for 26% -> 26%
where the time goes in v8:
time: 218 us; the launch traced here: 217 us
  waiting for transfers between devices  79.1 us (36%)
  Pallas kernels  66.9 us (31%)
  blocking collectives  42.6 us (20%)
  between operations  13.5 us (6%)
  starting transfers between devices  9.59 us (4%)
  local copies, waits for them, and re-layouts  2.92 us (1%)
    all_gather x1, waiting for transfers between devices, body(): slabs.append(lax.all_gather(part_later, 'occ', axis=0, tiled=True))  47.9 us
    all_gather x1, blocking collectives, body(): slabs = [lax.all_gather(coded, 'occ', axis=0, tiled=True)]  42.6 us
    pallas_call x2, Pallas kernels, ladder_call(): pl.pallas_call(functools.partial(ladder_kernel, tile_total, vir_count, ch...  36.5 us
    all_to_all x2, waiting for transfers between devices, exchanged(): lax.all_to_all(packed.reshape(tile_total * vir_count, rows, block), ('occ...  31.2 us
    pallas_call x2, Pallas kernels, update_call(): pl.pallas_call(functools.partial(update_kernel, arrived.shape[1]), grid=(...  14.2 us
    pallas_call x2, Pallas kernels, direct_call(): pl.pallas_call(direct_kernel, grid=(rows // step_rows,), in_specs=[pl.Blo...  12.5 us
    all_to_all x2, starting transfers between devices, exchanged(): lax.all_to_all(packed.reshape(tile_total * vir_count, rows, block), ('occ...  9.59 us
  transfers between devices with their start and end apart: 3, of which 3 were waited for; matrix products, arithmetic and copies ran while one was open for 2% of the time, Pallas kernels for 26%

profile of v8, /device:TPU:0, one launch (start us, length us, event | category | flops | bytes accessed | tf_op | source)
XLA Modules:
  0.0 216.7 jit_solution(10173965045044130143)
XLA Ops:
  6.5 0.0 copy-start.1
  6.5 0.0 all-gather.3.cloned.1.call-start
  6.5 3.7 %screen.1 = (s16[528,512]{1,0:T(8,128)(2,1)}, bf16[512,512]{1,0:T(8,128)(2,1)}) custom-call(s32[4,4]{1,0:T(4,128)} %int_mask.1, bf16[512,1024]{1,0:T(8,128)(2,1)} %slab_ref.1), custom_call_target="tpu_custom_call" | custom-call | tf_op jit(solution)/shard_map/screen/pallas_call | solution.py:75
  10.2 42.6 %all-gather.4.slab_ref = s16[4224,512]{1,0:T(8,128)(2,1)} all-gather(s16[528,512]{1,0:T(8,128)(2,1)} %get-tuple-element.13), channel_id=1, replica_groups=mesh['occ'=8,'vir'=4] {'occ'}, dimensions={0}, use_global_device_ids=true | all-gather | bytes 4866048 | tf_op jit(solution)/shard_map/all_gather | solution.py:290
  52.8 0.0 all-gather.3.cloned.1.call-update
  52.8 0.0 copy-done.1
  52.8 0.7 copy.9.amp_mask
  53.5 19.0 %ladder.3 = (f32[2,2048,256]{2,1,0:T(8,128)}, s16[8,4,272,128]{3,2,1,0:T(8,128)(2,1)}) custom-call(s32[8,4]{1,0:T(8,128)} %copy.9.amp_mask, s32[8]{0:T(128)} %numbers.3, bf16[2048,4096]{1,0:T(8,128)(2,1)} %rows_ref.3, s16[4224,512]{1,0:T(8,128)(2,1)} %all-gather.4.slab_ref), custom_call_target="tpu_custom_call" | custom-call | flops 8589934592 | bytes 27262976 | tf_op jit(solution)/shard_map/ladder/pallas_call | solution.py:169
  72.5 6.0 %all-to-all-start.1 = ((s16[32,272,128]{2,1,0:T(8,128)(2,1)}), s16[32,272,128]{2,1,0:T(8,128)(2,1)S(1)}, u32[]{:S(2)}, u32[]{:S(2)}) async-start(s16[32,272,128]{2,1,0:T(8,128)(2,1)} %bitcast.9), calls=%async_computation.1 | async-start | bytes 4456448 | tf_op jit(solution)/shard_map/all_to_all | solution.py:284
  78.5 47.9 %all-gather.3.cloned.1.call-done.slab_ref = bf16[4096,512]{1,0:T(8,128)(2,1)} async-done(((bf16[512,512]{1,0:T(8,128)(2,1)}), bf16[4096,512]{1,0:T(8,128)(2,1)}) %all-gather.3.cloned.1.call-update) | async-done | bytes 4194320 | tf_op jit(solution)/shard_map/all_gather | solution.py:293
  126.4 17.4 %ladder.2 = (f32[2,2048,256]{2,1,0:T(8,128)}, s16[8,4,272,128]{3,2,1,0:T(8,128)(2,1)}) custom-call(s32[8,4]{1,0:T(8,128)} %copy.9.amp_mask, s32[8]{0:T(128)} %numbers.3, bf16[2048,4096]{1,0:T(8,128)(2,1)} %rows_ref.3, bf16[4096,512]{1,0:T(8,128)(2,1)} %all-gather.3.cloned.1.call-done.slab_ref), custom_call_target="tpu_custom_call" | custom-call | flops 8589934592 | bytes 27262976 | tf_op jit(solution)/shard_map/ladder/pallas_call | solution.py:169
  143.8 0.0 copy-start.2
  143.8 0.0 copy-start.3
  143.8 3.8 %all-to-all-done.1 = s16[32,272,128]{2,1,0:T(8,128)(2,1)S(1)} async-done(((s16[32,272,128]{2,1,0:T(8,128)(2,1)}), s16[32,272,128]{2,1,0:T(8,128)(2,1)S(1)}, u32[]{:S(2)}, u32[]{:S(2)}) %all-to-all-start.1) | async-done | bytes 2228256 | tf_op jit(solution)/shard_map/all_to_all | solution.py:284
  147.6 0.0 copy-start
  147.6 3.6 %all-to-all-start = ((s16[32,272,128]{2,1,0:T(8,128)(2,1)}), s16[32,272,128]{2,1,0:T(8,128)(2,1)}, u32[]{:S(2)}, u32[]{:S(2)}) async-start(s16[32,272,128]{2,1,0:T(8,128)(2,1)} %bitcast.8), calls=%async_computation | async-start | bytes 4456448 | tf_op jit(solution)/shard_map/all_to_all | solution.py:284
  151.2 0.0 copy-done.2
  151.2 0.1 reshape.124
  151.3 0.0 copy-done.3
  151.3 0.1 dynamic_slice.6
  151.4 0.1 broadcast_add_fusion.1
  151.5 0.7 add.167.vir_ref
  152.1 0.1 broadcast_add_fusion
  152.2 0.1 add.173
  152.3 0.9 fusion.1.spread_ref
  153.3 1.0 fusion.spread_ref
  154.3 6.1 %direct.3.direct_ref = f32[2048,512]{1,0:T(8,128)} custom-call(bf16[512,512]{1,0:T(8,128)(2,1)} %fusion.1.spread_ref, f32[2,2048,256]{2,1,0:T(8,128)} %get-tuple-element.16.refs_0_, f32[2,2048,256]{2,1,0:T(8,128)} %get-tuple-element.17.refs_1_), custom_call_target="tpu_custom_call" | custom-call | flops 2147483648 | bytes 8388608 | tf_op jit(solution)/shard_map/direct/pallas_call | solution.py:211
  160.4 0.0 copy-done
  160.4 6.4 %direct.2.direct_ref = f32[2048,512]{1,0:T(8,128)} custom-call(bf16[512,512]{1,0:T(8,128)(2,1)} %fusion.1.spread_ref, f32[2,2048,256]{2,1,0:T(8,128)} %get-tuple-element.16.refs_0_, f32[2,2048,256]{2,1,0:T(8,128)} %get-tuple-element.17.refs_1_), custom_call_target="tpu_custom_call" | custom-call | flops 2147483648 | bytes 8388608 | tf_op jit(solution)/shard_map/direct/pallas_call | solution.py:211
  166.8 1.3 broadcast_in_dim.2.occ_ref
  168.1 7.1 %update.2.refs_0_ = f32[2048,1024]{1,0:T(8,128)} custom-call(s16[8,4,272,128]{3,2,1,0:T(8,128)(2,1)} %bitcast.7, bf16[512,512]{1,0:T(8,128)(2,1)} %fusion.spread_ref, f32[1,1024]{1,0:T(1,128)} %add.167.vir_ref, f32[2048,128]{1,0:T(8,128)} %broadcast_in_dim.2.occ_ref, f32[2048,512]{1,0:T(8,128)} %direct.3.direct_ref), custom_call_target="tpu_custom_call" | custom-call | flops 2147483648 | bytes 10485760 | tf_op jit(solution)/shard_map/update/pallas_call | solution.py:256
  175.2 27.5 %all-to-all-done = s16[32,272,128]{2,1,0:T(8,128)(2,1)} async-done(((s16[32,272,128]{2,1,0:T(8,128)(2,1)}), s16[32,272,128]{2,1,0:T(8,128)(2,1)}, u32[]{:S(2)}, u32[]{:S(2)}) %all-to-all-start) | async-done | bytes 2228256 | tf_op jit(solution)/shard_map/all_to_all | solution.py:284
  202.7 7.1 %update.3 = f32[2048,1024]{1,0:T(8,128)} custom-call(s16[8,4,272,128]{3,2,1,0:T(8,128)(2,1)} %bitcast.2.arrived_ref, bf16[512,512]{1,0:T(8,128)(2,1)} %fusion.spread_ref, f32[1,1024]{1,0:T(1,128)} %add.167.vir_ref, f32[2048,128]{1,0:T(8,128)} %broadcast_in_dim.2.occ_ref, f32[2048,512]{1,0:T(8,128)} %direct.2.direct_ref, ...), custom_call_target="tpu_custom_call", output_to_operand_aliasing={{}: (5, {})} | custom-call | flops 2147483648 | bytes 10485760 | tf_op jit(solution)/shard_map/update/pallas_call | solution.py:256
  (4 shorter events, 0.0 us)
Async XLA Ops:
  6.5 46.3 %copy-start.1 = (s32[1,8,4]{1,2,0:T(4,128)S(1)}, s32[1,8,4]{1,2,0:T(4,128)}, u32[]{:S(2)}) copy-start(s32[1,8,4]{1,2,0:T(4,128)} %param.8) | copy-start | bytes 388
  6.5 119.9 %all-gather.3.cloned.1.call-start = ((), (), s32[]{:S(2)}) async-start(), calls=%async_computation.2 | async-start | bytes 4718592 | tf_op jit(solution)/shard_map/all_gather | solution.py:293
  72.5 75.1 %all-to-all-start.1 = ((s16[32,272,128]{2,1,0:T(8,128)(2,1)}), s16[32,272,128]{2,1,0:T(8,128)(2,1)S(1)}, u32[]{:S(2)}, u32[]{:S(2)}) async-start(s16[32,272,128]{2,1,0:T(8,128)(2,1)} %bitcast.9), calls=%async_computation.1 | async-start | bytes 4456448 | tf_op jit(solution)/shard_map/all_to_all | solution.py:284
  143.8 7.4 %copy-start.2 = (f32[128]{0:T(128)S(1)}, f32[128]{0:T(128)}, u32[]{:S(2)}) copy-start(f32[128]{0:T(128)} %param.12) | copy-start | bytes 1540
  143.8 7.5 %copy-start.3 = (f32[64]{0:T(128)S(1)}, f32[64]{0:T(128)}, u32[]{:S(2)}) copy-start(f32[64]{0:T(128)} %param.13) | copy-start | bytes 772
  147.6 12.8 %copy-start = (s16[32,272,128]{2,1,0:T(8,128)(2,1)}, s16[32,272,128]{2,1,0:T(8,128)(2,1)S(1)}, u32[]{:S(2)}) copy-start(s16[32,272,128]{2,1,0:T(8,128)(2,1)S(1)} %all-to-all-done.1) | copy-start | bytes 6684676
  147.6 55.1 %all-to-all-start = ((s16[32,272,128]{2,1,0:T(8,128)(2,1)}), s16[32,272,128]{2,1,0:T(8,128)(2,1)}, u32[]{:S(2)}, u32[]{:S(2)}) async-start(s16[32,272,128]{2,1,0:T(8,128)(2,1)} %bitcast.8), calls=%async_computation | async-start | bytes 4456448 | tf_op jit(solution)/shard_map/all_to_all | solution.py:284
Sparse Core Ops, SparseCore 0:
  52.9 73.4 all-gather.2

commit v9 on v8

--- a/solution.py
+++ b/solution.py
@@ -13,6 +13,7 @@
 ORBITALS_IN_GRP = 16
 PAIR_SQ = ORBITALS_IN_GRP * ORBITALS_IN_GRP
 CODE_ROWS = 16
+EXCHANGE_CODE_ROWS = 8
 AT_ONCE = 2
 SLAB_BITS = 14.0
 TOP = 32700.0
@@ -134,7 +135,7 @@
     most = jnp.maximum(jnp.max(jnp.abs(ladder), axis=0, keepdims=True), 1e-30)
     code = jnp.ceil(jnp.log2(most) * STEPS)
     coded = jnp.round(mirror * (TOP / scale_of(code))).astype(jnp.int32).astype(jnp.int16)
-    code_rows = jnp.broadcast_to(code.astype(jnp.int32), (CODE_ROWS, cols)).astype(jnp.int16)
+    code_rows = jnp.broadcast_to(code.astype(jnp.int32), (EXCHANGE_CODE_ROWS, cols)).astype(jnp.int16)
     for v in range(vir_count):
         packed_ref[0, v, :PAIR_SQ] = coded[:, v * block : (v + 1) * block]
         packed_ref[0, v, PAIR_SQ:] = code_rows[:, v * block : (v + 1) * block]
@@ -178,12 +179,12 @@
         out_specs=[
             pl.BlockSpec((chunks, PAIR_SQ, cols // chunks), lambda step: (0, jnp.maximum(step - 1, 0), 0)),
             pl.BlockSpec(
-                (1, vir_count, PAIR_SQ + CODE_ROWS, block), lambda step: (jnp.maximum(step - 1, 0), 0, 0, 0)
+                (1, vir_count, PAIR_SQ + EXCHANGE_CODE_ROWS, block), lambda step: (jnp.maximum(step - 1, 0), 0, 0, 0)
             ),
         ],
         out_shape=[
             jax.ShapeDtypeStruct((chunks, rows, cols // chunks), jnp.float32),
-            jax.ShapeDtypeStruct((tile_total, vir_count, PAIR_SQ + CODE_ROWS, block), jnp.int16),
+            jax.ShapeDtypeStruct((tile_total, vir_count, PAIR_SQ + EXCHANGE_CODE_ROWS, block), jnp.int16),
         ],
         scratch_shapes=scratch,
         compiler_params=pltpu.CompilerParams(vmem_limit_bytes=VMEM_LIMIT),
@@ -278,7 +279,7 @@
     chunks = 2 if span >= 16 else 1
     part = span // chunks
     block = part * span
-    rows = PAIR_SQ + CODE_ROWS
+    rows = PAIR_SQ + EXCHANGE_CODE_ROWS
 
     def exchanged(packed):
         moved = lax.all_to_all(
@@ -296,6 +297,7 @@
         ladder, packed = ladder_call(
             tile_total, vir_count, chunks, amp_mask[0], group_orbital_numbers, amplitudes, slab
         )
+        packed, _ = lax.optimization_barrier((packed, slabs[-1]))
         ladders.append(ladder)
         arrived.append(exchanged(packed))
 

time: 218 us -> 225 us (1.032)
  waiting for transfers between devices: 79.1 us -> 87.7 us
    all_to_all x2, waiting for transfers between devices: 31.2 us -> 58.7 us  [exchanged(): lax.all_to_all(packed.reshape(tile_total * vir_count, rows, block), ('occ...]
    all_gather x1, waiting for transfers between devices: 47.9 us -> 29 us  [body(): slabs.append(lax.all_gather(part_later, 'occ', axis=0, tiled=True))]
  transfers between devices with their start and end apart: 3 -> 3, of which waited for: 3 -> 3; matrix products, arithmetic and copies ran while one was open for 2% -> 2% of each run, Pallas kernels for 26% -> 25%
where the time goes in v9:
time: 225 us; the launch traced here: 224 us
  waiting for transfers between devices  87.7 us (39%)
  Pallas kernels  66.9 us (30%)
  blocking collectives  42.6 us (19%)
  between operations  13.5 us (6%)
  starting transfers between devices  7.82 us (3%)
  local copies, waits for them, and re-layouts  2.92 us (1%)
    all_to_all x2, waiting for transfers between devices, exchanged(): lax.all_to_all(packed.reshape(tile_total * vir_count, rows, block), ('occ...  58.7 us
    all_gather x1, blocking collectives, body(): slabs = [lax.all_gather(coded, 'occ', axis=0, tiled=True)]  42.6 us
    pallas_call x2, Pallas kernels, ladder_call(): pl.pallas_call(functools.partial(ladder_kernel, tile_total, vir_count, ch...  36.5 us
    all_gather x1, waiting for transfers between devices, body(): slabs.append(lax.all_gather(part_later, 'occ', axis=0, tiled=True))  29 us
    pallas_call x2, Pallas kernels, update_call(): pl.pallas_call(functools.partial(update_kernel, arrived.shape[1]), grid=(...  14.2 us
    pallas_call x2, Pallas kernels, direct_call(): pl.pallas_call(direct_kernel, grid=(rows // step_rows,), in_specs=[pl.Blo...  12.5 us
    all_to_all x2, starting transfers between devices, exchanged(): lax.all_to_all(packed.reshape(tile_total * vir_count, rows, block), ('occ...  7.82 us
  transfers between devices with their start and end apart: 3, of which 3 were waited for; matrix products, arithmetic and copies ran while one was open for 2% of the time, Pallas kernels for 25%

profile of v9, /device:TPU:0, one launch (start us, length us, event | category | flops | bytes accessed | tf_op | source)
XLA Modules:
  0.0 223.6 jit_solution(557274733656674908)
XLA Ops:
  6.5 0.0 copy-start.1
  6.5 0.0 all-gather.3.cloned.1.call-start
  6.5 3.7 %screen.1 = (s16[528,512]{1,0:T(8,128)(2,1)}, bf16[512,512]{1,0:T(8,128)(2,1)}) custom-call(s32[4,4]{1,0:T(4,128)} %int_mask.1, bf16[512,1024]{1,0:T(8,128)(2,1)} %slab_ref.1), custom_call_target="tpu_custom_call" | custom-call | tf_op jit(solution)/shard_map/screen/pallas_call | solution.py:76
  10.2 42.6 %all-gather.4.slab_ref = s16[4224,512]{1,0:T(8,128)(2,1)} all-gather(s16[528,512]{1,0:T(8,128)(2,1)} %get-tuple-element.15), channel_id=1, replica_groups=mesh['occ'=8,'vir'=4] {'occ'}, dimensions={0}, use_global_device_ids=true | all-gather | bytes 4866048 | tf_op jit(solution)/shard_map/all_gather | solution.py:291
  52.8 0.0 all-gather.3.cloned.1.call-update
  52.8 0.0 copy-done.1
  52.8 0.7 copy.9.amp_mask
  53.5 19.1 %ladder.3 = (f32[2,2048,256]{2,1,0:T(8,128)}, s16[8,4,264,128]{3,2,1,0:T(8,128)(2,1)}) custom-call(s32[8,4]{1,0:T(8,128)} %copy.9.amp_mask, s32[8]{0:T(128)} %numbers.3, bf16[2048,4096]{1,0:T(8,128)(2,1)} %rows_ref.3, s16[4224,512]{1,0:T(8,128)(2,1)} %all-gather.4.slab_ref), custom_call_target="tpu_custom_call" | custom-call | flops 8589934592 | bytes 27262976 | tf_op jit(solution)/shard_map/ladder/pallas_call | solution.py:170
  72.6 29.0 %all-gather.3.cloned.1.call-done.slab_ref = bf16[4096,512]{1,0:T(8,128)(2,1)} async-done(((bf16[512,512]{1,0:T(8,128)(2,1)}), bf16[4096,512]{1,0:T(8,128)(2,1)}) %all-gather.3.cloned.1.call-update) | async-done | bytes 4194320 | tf_op jit(solution)/shard_map/all_gather | solution.py:294
  101.5 3.3 %all-to-all-start.1 = ((s16[32,264,128]{2,1,0:T(8,128)(2,1)}), s16[32,264,128]{2,1,0:T(8,128)(2,1)S(1)}, u32[]{:S(2)}, u32[]{:S(2)}) async-start(s16[32,264,128]{2,1,0:T(8,128)(2,1)} %bitcast.9), calls=%async_computation.1 | async-start | bytes 4325376 | tf_op jit(solution)/shard_map/all_to_all | solution.py:285
  104.9 17.5 %ladder.2 = (f32[2,2048,256]{2,1,0:T(8,128)}, s16[8,4,264,128]{3,2,1,0:T(8,128)(2,1)}) custom-call(s32[8,4]{1,0:T(8,128)} %copy.9.amp_mask, s32[8]{0:T(128)} %numbers.3, bf16[2048,4096]{1,0:T(8,128)(2,1)} %rows_ref.3, bf16[4096,512]{1,0:T(8,128)(2,1)} %all-gather.3.cloned.1.call-done.slab_ref), custom_call_target="tpu_custom_call" | custom-call | flops 8589934592 | bytes 27262976 | tf_op jit(solution)/shard_map/ladder/pallas_call | solution.py:170
  122.3 0.0 copy-start.2
  122.3 0.0 copy-start.3
  122.4 32.6 %all-to-all-done.1 = s16[32,264,128]{2,1,0:T(8,128)(2,1)S(1)} async-done(((s16[32,264,128]{2,1,0:T(8,128)(2,1)}), s16[32,264,128]{2,1,0:T(8,128)(2,1)S(1)}, u32[]{:S(2)}, u32[]{:S(2)}) %all-to-all-start.1) | async-done | bytes 2162720 | tf_op jit(solution)/shard_map/all_to_all | solution.py:285
  155.0 0.0 copy-start
  155.0 4.5 %all-to-all-start = ((s16[32,264,128]{2,1,0:T(8,128)(2,1)}), s16[32,264,128]{2,1,0:T(8,128)(2,1)}, u32[]{:S(2)}, u32[]{:S(2)}) async-start(s16[32,264,128]{2,1,0:T(8,128)(2,1)} %bitcast.8), calls=%async_computation | async-start | bytes 4325376 | tf_op jit(solution)/shard_map/all_to_all | solution.py:285
  159.5 0.0 copy-done.2
  159.5 0.1 reshape.124
  159.6 0.0 copy-done.3
  159.6 0.1 dynamic_slice.6
  159.7 0.1 broadcast_add_fusion.1
  159.7 0.7 add.167.vir_ref
  160.4 0.1 broadcast_add_fusion
  160.5 0.1 add.173
  160.6 0.9 fusion.1.spread_ref
  161.6 1.0 fusion.spread_ref
  162.6 6.1 %direct.3.direct_ref = f32[2048,512]{1,0:T(8,128)} custom-call(bf16[512,512]{1,0:T(8,128)(2,1)} %fusion.1.spread_ref, f32[2,2048,256]{2,1,0:T(8,128)} %get-tuple-element.19.refs_0_, f32[2,2048,256]{2,1,0:T(8,128)} %get-tuple-element.20.refs_1_), custom_call_target="tpu_custom_call" | custom-call | flops 2147483648 | bytes 8388608 | tf_op jit(solution)/shard_map/direct/pallas_call | solution.py:212
  168.7 0.0 copy-done
  168.7 6.4 %direct.2.direct_ref = f32[2048,512]{1,0:T(8,128)} custom-call(bf16[512,512]{1,0:T(8,128)(2,1)} %fusion.1.spread_ref, f32[2,2048,256]{2,1,0:T(8,128)} %get-tuple-element.19.refs_0_, f32[2,2048,256]{2,1,0:T(8,128)} %get-tuple-element.20.refs_1_), custom_call_target="tpu_custom_call" | custom-call | flops 2147483648 | bytes 8388608 | tf_op jit(solution)/shard_map/direct/pallas_call | solution.py:212
  175.1 1.3 broadcast_in_dim.2.occ_ref
  176.4 7.1 %update.2.refs_0_ = f32[2048,1024]{1,0:T(8,128)} custom-call(s16[8,4,264,128]{3,2,1,0:T(8,128)(2,1)} %bitcast.7, bf16[512,512]{1,0:T(8,128)(2,1)} %fusion.spread_ref, f32[1,1024]{1,0:T(1,128)} %add.167.vir_ref, f32[2048,128]{1,0:T(8,128)} %broadcast_in_dim.2.occ_ref, f32[2048,512]{1,0:T(8,128)} %direct.3.direct_ref), custom_call_target="tpu_custom_call" | custom-call | flops 2147483648 | bytes 10485760 | tf_op jit(solution)/shard_map/update/pallas_call | solution.py:257
  183.5 26.1 %all-to-all-done = s16[32,264,128]{2,1,0:T(8,128)(2,1)} async-done(((s16[32,264,128]{2,1,0:T(8,128)(2,1)}), s16[32,264,128]{2,1,0:T(8,128)(2,1)}, u32[]{:S(2)}, u32[]{:S(2)}) %all-to-all-start) | async-done | bytes 2162720 | tf_op jit(solution)/shard_map/all_to_all | solution.py:285
  209.6 7.1 %update.3 = f32[2048,1024]{1,0:T(8,128)} custom-call(s16[8,4,264,128]{3,2,1,0:T(8,128)(2,1)} %bitcast.2.arrived_ref, bf16[512,512]{1,0:T(8,128)(2,1)} %fusion.spread_ref, f32[1,1024]{1,0:T(1,128)} %add.167.vir_ref, f32[2048,128]{1,0:T(8,128)} %broadcast_in_dim.2.occ_ref, f32[2048,512]{1,0:T(8,128)} %direct.2.direct_ref, ...), custom_call_target="tpu_custom_call", output_to_operand_aliasing={{}: (5, {})} | custom-call | flops 2147483648 | bytes 10485760 | tf_op jit(solution)/shard_map/update/pallas_call | solution.py:257
  (4 shorter events, 0.0 us)
Async XLA Ops:
  6.5 46.3 %copy-start.1 = (s32[1,8,4]{1,2,0:T(4,128)S(1)}, s32[1,8,4]{1,2,0:T(4,128)}, u32[]{:S(2)}) copy-start(s32[1,8,4]{1,2,0:T(4,128)} %param.8) | copy-start | bytes 388
  6.5 95.0 %all-gather.3.cloned.1.call-start = ((), (), s32[]{:S(2)}) async-start(), calls=%async_computation.2 | async-start | bytes 4718592 | tf_op jit(solution)/shard_map/all_gather | solution.py:294
  101.5 53.4 %all-to-all-start.1 = ((s16[32,264,128]{2,1,0:T(8,128)(2,1)}), s16[32,264,128]{2,1,0:T(8,128)(2,1)S(1)}, u32[]{:S(2)}, u32[]{:S(2)}) async-start(s16[32,264,128]{2,1,0:T(8,128)(2,1)} %bitcast.9), calls=%async_computation.1 | async-start | bytes 4325376 | tf_op jit(solution)/shard_map/all_to_all | solution.py:285
  122.3 37.2 %copy-start.2 = (f32[128]{0:T(128)S(1)}, f32[128]{0:T(128)}, u32[]{:S(2)}) copy-start(f32[128]{0:T(128)} %param.12) | copy-start | bytes 1540
  122.3 37.2 %copy-start.3 = (f32[64]{0:T(128)S(1)}, f32[64]{0:T(128)}, u32[]{:S(2)}) copy-start(f32[64]{0:T(128)} %param.13) | copy-start | bytes 772
  155.0 13.7 %copy-start = (s16[32,264,128]{2,1,0:T(8,128)(2,1)}, s16[32,264,128]{2,1,0:T(8,128)(2,1)S(1)}, u32[]{:S(2)}) copy-start(s16[32,264,128]{2,1,0:T(8,128)(2,1)S(1)} %all-to-all-done.1) | copy-start | bytes 6488068
  155.0 54.6 %all-to-all-start = ((s16[32,264,128]{2,1,0:T(8,128)(2,1)}), s16[32,264,128]{2,1,0:T(8,128)(2,1)}, u32[]{:S(2)}, u32[]{:S(2)}) async-start(s16[32,264,128]{2,1,0:T(8,128)(2,1)} %bitcast.8), calls=%async_computation | async-start | bytes 4325376 | tf_op jit(solution)/shard_map/all_to_all | solution.py:285
Sparse Core Ops, SparseCore 0:
  52.9 48.5 all-gather.2

commit v10 on v9

--- a/solution.py
+++ b/solution.py
@@ -14,6 +14,7 @@
 PAIR_SQ = ORBITALS_IN_GRP * ORBITALS_IN_GRP
 CODE_ROWS = 16
 EXCHANGE_CODE_ROWS = 8
+CODED_PARTS = 2
 AT_ONCE = 2
 SLAB_BITS = 14.0
 TOP = 32700.0
@@ -38,9 +39,11 @@
     return jnp.exp2(code * (1.0 / STEPS))
 
 
-def screen_kernel(part, int_mask, slab_ref, coded_ref, *later_refs):
+def screen_kernel(part, int_mask, slab_ref, *refs):
+    coded_refs, later_refs = refs[:CODED_PARTS], refs[CODED_PARTS:]
     slab_rows, slab_cols = slab_ref.shape
-    cols = coded_ref.shape[1]
+    coded_cols = coded_refs[0].shape[1]
+    cols = coded_cols * CODED_PARTS
     span = slab_cols // W
     row_label = lax.axis_index("occ") * slab_rows // W // VT * NVT
     col_label = lax.axis_index("vir") * slab_cols // W // VT * NVT
@@ -64,9 +67,12 @@
         else:
             most = jnp.maximum(jnp.max(jnp.abs(moved), axis=0, keepdims=True), 1e-30)
             code = jnp.floor(jnp.log2(most)) + 1.0
-            coded = jnp.round(moved * jnp.exp2(SLAB_BITS - code)).astype(jnp.int32)
-            coded_ref[:slab_rows, :] = coded.astype(jnp.int16)
-            coded_ref[slab_rows:, :] = jnp.broadcast_to(code.astype(jnp.int32), (CODE_ROWS, cols)).astype(jnp.int16)
+            coded = jnp.round(moved * jnp.exp2(SLAB_BITS - code)).astype(jnp.int32).astype(jnp.int16)
+            code_rows = jnp.broadcast_to(code.astype(jnp.int32), (CODE_ROWS, cols)).astype(jnp.int16)
+            for n, coded_ref in enumerate(coded_refs):
+                at = slice(n * coded_cols, (n + 1) * coded_cols)
+                coded_ref[:slab_rows, :] = coded[:, at]
+                coded_ref[slab_rows:, :] = code_rows[:, at]
 
 
 def screen_call(chunks, int_mask, integrals):
@@ -76,47 +82,51 @@
     return pl.pallas_call(
         functools.partial(screen_kernel, slab_cols // W // chunks),
         in_specs=[pl.BlockSpec(memory_space=pltpu.SMEM), vmem],
-        out_specs=[vmem] * chunks,
-        out_shape=[jax.ShapeDtypeStruct((slab_rows + CODE_ROWS, cols), jnp.int16)]
+        out_specs=[vmem] * (CODED_PARTS + chunks - 1),
+        out_shape=[jax.ShapeDtypeStruct((slab_rows + CODE_ROWS, cols // CODED_PARTS), jnp.int16)] * CODED_PARTS
         + [jax.ShapeDtypeStruct((slab_rows, cols), integrals.dtype)] * (chunks - 1),
         compiler_params=pltpu.CompilerParams(vmem_limit_bytes=VMEM_LIMIT),
         name="screen",
     )(int_mask, integrals)
 
 
-def decode_slab(tile_total, coded_ref, stage, slab_scr, sems):
+def decode_slab(tile_total, coded_refs, stage, slab_scr, sems):
     slab_rows = slab_scr.shape[0] // tile_total
-    coded_rows = slab_rows + CODE_ROWS
-
-    def copy_of(tile):
+    coded_rows, cols = slab_rows + CODE_ROWS, coded_refs[0].shape[1]
+
+    def copy_of(part, tile):
         at = pl.ds(pl.multiple_of(tile * coded_rows, CODE_ROWS), coded_rows)
-        return pltpu.make_async_copy(coded_ref.at[at, :], stage.at[at, :], sems.at[tile])
+        return pltpu.make_async_copy(coded_refs[part].at[at, :], stage.at[part, at, :], sems.at[part, tile])
 
     for tile in range(tile_total):
-        copy_of(tile).start()
+        for part in range(CODED_PARTS):
+            copy_of(part, tile).start()
 
     def decode(tile, carry):
-        copy_of(tile).wait()
         at = pl.multiple_of(tile * coded_rows, CODE_ROWS)
-        code = stage[pl.ds(pl.multiple_of(at + slab_rows, CODE_ROWS), CODE_ROWS), :]
-        values = stage[pl.ds(at, slab_rows), :].astype(jnp.int32).astype(jnp.float32)
-        scale = jnp.exp2(code.astype(jnp.int32).astype(jnp.float32)[:1] - SLAB_BITS)
         to = pl.ds(pl.multiple_of(tile * slab_rows, slab_rows), slab_rows)
-        slab_scr[to, :] = (values * scale).astype(jnp.bfloat16)
+        for part in range(CODED_PARTS):
+            copy_of(part, tile).wait()
+            code = stage[part, pl.ds(pl.multiple_of(at + slab_rows, CODE_ROWS), CODE_ROWS), :]
+            values = stage[part, pl.ds(at, slab_rows), :].astype(jnp.int32).astype(jnp.float32)
+            scale = jnp.exp2(code.astype(jnp.int32).astype(jnp.float32)[:1] - SLAB_BITS)
+            slab_scr[to, part * cols : (part + 1) * cols] = (values * scale).astype(jnp.bfloat16)
         return carry
 
     lax.fori_loop(0, tile_total, decode, 0)
 
 
-def ladder_kernel(tile_total, vir_count, chunks, amp_mask, numbers, rows_ref, slab_ref, *refs):
+def ladder_kernel(tile_total, vir_count, chunks, coded, amp_mask, numbers, rows_ref, *refs):
+    slab_refs, refs = (refs[:CODED_PARTS], refs[CODED_PARTS:]) if coded else (refs[:1], refs[1:])
     ladder_ref, packed_ref, product = refs[:3]
     step = pl.program_id(0)
-    if len(refs) > 3:
-        coded_ref, (stage, slab_ref, sems) = slab_ref, refs[3:]
+    slab_ref = slab_refs[0]
+    if coded:
+        stage, slab_ref, sems = refs[3:]
 
         @pl.when(step == 0)
         def _():
-            decode_slab(tile_total, coded_ref, stage, slab_ref, sems)
+            decode_slab(tile_total, slab_refs, stage, slab_ref, sems)
     cols = slab_ref.shape[1]
 
     tile = jnp.maximum(step - 1, 0)
@@ -154,27 +164,28 @@
 
 
 def ladder_call(tile_total, vir_count, chunks, amp_mask, numbers, amplitudes, slab):
-    cols = slab.shape[1]
+    coded = len(slab) > 1
+    cols = sum(part.shape[1] for part in slab)
     block = cols // vir_count
     smem = pl.BlockSpec(memory_space=pltpu.SMEM)
     rows = tile_total * PAIR_SQ
     scratch = [pltpu.VMEM((PAIR_SQ, cols), jnp.float32)]
-    slab_spec = pl.BlockSpec((W * W, cols), lambda step: (0, 0))
-    if slab.dtype == jnp.int16:
-        slab_spec = pl.BlockSpec(memory_space=pl.ANY)
+    slab_specs = [pl.BlockSpec((W * W, cols), lambda step: (0, 0))]
+    if coded:
+        slab_specs = [pl.BlockSpec(memory_space=pl.ANY)] * CODED_PARTS
         scratch += [
-            pltpu.VMEM(slab.shape, slab.dtype),
+            pltpu.VMEM((CODED_PARTS,) + slab[0].shape, slab[0].dtype),
             pltpu.VMEM((W * W, cols), jnp.bfloat16),
-            pltpu.SemaphoreType.DMA((tile_total,)),
+            pltpu.SemaphoreType.DMA((CODED_PARTS, tile_total)),
         ]
     return pl.pallas_call(
-        functools.partial(ladder_kernel, tile_total, vir_count, chunks),
+        functools.partial(ladder_kernel, tile_total, vir_count, chunks, coded),
         grid=(tile_total + 1,),
         in_specs=[
             smem,
             smem,
             pl.BlockSpec((PAIR_SQ, W * W), lambda step: (jnp.minimum(step, tile_total - 1), 0)),
-            slab_spec,
+            *slab_specs,
         ],
         out_specs=[
             pl.BlockSpec((chunks, PAIR_SQ, cols // chunks), lambda step: (0, jnp.maximum(step - 1, 0), 0)),
@@ -194,7 +205,7 @@
             transcendentals=0,
         ),
         name="ladder",
-    )(amp_mask, numbers, amplitudes, slab)
+    )(amp_mask, numbers, amplitudes, *slab)
 
 
 def moved_columns(values, spread_ref):
@@ -277,8 +288,8 @@
     span = W // vir_count
     slab_cols = span * W
     chunks = 2 if span >= 16 else 1
-    part = span // chunks
-    block = part * span
+    width = span // chunks
+    block = width * span
     rows = PAIR_SQ + EXCHANGE_CODE_ROWS
 
     def exchanged(packed):
@@ -287,28 +298,30 @@
         )
         return moved.reshape(tile_total, vir_count, rows, block)
 
-    coded, *later = screen_call(chunks, int_mask, integrals)
-    slabs = [lax.all_gather(coded, "occ", axis=0, tiled=True)]
-    for part_later in later:
-        part_later, _ = lax.optimization_barrier((part_later, slabs[-1]))
-        slabs.append(lax.all_gather(part_later, "occ", axis=0, tiled=True))
+    parts = screen_call(chunks, int_mask, integrals)
+    coded, later = parts[:CODED_PARTS], parts[CODED_PARTS:]
+    first = lax.all_gather(coded[0], "occ", axis=0, tiled=True)
+    *coded, first = lax.optimization_barrier((*coded[1:], first))
+    slabs = [[first] + [lax.all_gather(part, "occ", axis=0, tiled=True) for part in coded]]
+    for part in later:
+        part, _ = lax.optimization_barrier((part, first))
+        slabs.append([lax.all_gather(part, "occ", axis=0, tiled=True)])
     ladders, arrived = [], []
     for slab in slabs:
         ladder, packed = ladder_call(
             tile_total, vir_count, chunks, amp_mask[0], group_orbital_numbers, amplitudes, slab
         )
-        packed, _ = lax.optimization_barrier((packed, slabs[-1]))
         ladders.append(ladder)
         arrived.append(exchanged(packed))
 
     place = jnp.arange(vir_count * block)
-    owner, there_part = place // block, place // (part * part) % chunks
-    here, there = place // part % part, place % part
-    mirror_spread = one_hot_of(here * W + owner * span + there_part * part + there, part * W)
-    place = jnp.arange(vir_count * part * part)
-    owner, b, a = place // (part * part), place // part % part, place % part
+    owner, there_part = place // block, place // (width * width) % chunks
+    here, there = place // width % width, place % width
+    mirror_spread = one_hot_of(here * W + owner * span + there_part * width + there, width * W)
+    place = jnp.arange(vir_count * width * width)
+    owner, b, a = place // (width * width), place // width % width, place % width
     direct_spread = one_hot_of(
-        jnp.concatenate([a * W + owner * span + c * part + b for c in range(chunks)]), part * W
+        jnp.concatenate([a * W + owner * span + c * width + b for c in range(chunks)]), width * W
     )
 
     occ_table = occ_energy.reshape(tile_total, ORBITALS_IN_GRP)

time: 225 us -> 220 us (0.978)
  waiting for transfers between devices: 87.7 us -> 58.9 us
  blocking collectives: 42.6 us -> 62 us
  starting transfers between devices: 7.82 us -> 12.3 us
    all_gather x1, waiting for transfers between devices: 29 us -> 0.02 us  [body(): slabs.append([lax.all_gather(part, 'occ', axis=0, tiled=True)])]
    all_gather x1 -> x2, blocking collectives: 42.6 us -> 62 us  [the longest x1 35.6 us: body(): lax.all_gather(part, 'occ', axis=0, tiled=True)]
    all_to_all x2, starting transfers between devices: 7.82 us -> 12.3 us  [exchanged(): lax.all_to_all(packed.reshape(tile_total * vir_count, rows, block), ('occ...]
  transfers between devices with their start and end apart: 3 -> 3, of which waited for: 3 -> 2; matrix products, arithmetic and copies ran while one was open for 2% -> 3% of each run, Pallas kernels for 25% -> 26%
where the time goes in v10:
time: 220 us; the launch traced here: 219 us
  Pallas kernels  66.6 us (30%)
  blocking collectives  62 us (28%)
  waiting for transfers between devices  58.9 us (27%)
  between operations  13.5 us (6%)
  starting transfers between devices  12.3 us (6%)
  local copies, waits for them, and re-layouts  3.58 us (2%)
    all_to_all x2, waiting for transfers between devices, exchanged(): lax.all_to_all(packed.reshape(tile_total * vir_count, rows, block), ('occ...  58.8 us
    pallas_call x2, Pallas kernels, ladder_call(): pl.pallas_call(functools.partial(ladder_kernel, tile_total, vir_count, ch...  36.3 us
    all_gather x1, blocking collectives, body(): lax.all_gather(part, 'occ', axis=0, tiled=True)  35.6 us
    all_gather x1, blocking collectives, body(): first = lax.all_gather(coded[0], 'occ', axis=0, tiled=True)  26.4 us
    pallas_call x2, Pallas kernels, update_call(): pl.pallas_call(functools.partial(update_kernel, arrived.shape[1]), grid=(...  14.2 us
    pallas_call x2, Pallas kernels, direct_call(): pl.pallas_call(direct_kernel, grid=(rows // step_rows,), in_specs=[pl.Blo...  12.5 us
    all_to_all x2, starting transfers between devices, exchanged(): lax.all_to_all(packed.reshape(tile_total * vir_count, rows, block), ('occ...  12.3 us
  transfers between devices with their start and end apart: 3, of which 2 were waited for; matrix products, arithmetic and copies ran while one was open for 3% of the time, Pallas kernels for 26%

profile of v10, /device:TPU:0, one launch (start us, length us, event | category | flops | bytes accessed | tf_op | source)
XLA Modules:
  0.0 218.9 jit_solution(4908106667861711692)
XLA Ops:
  6.5 0.0 all-gather.4.cloned.1.call-start
  6.5 3.7 %screen.1 = (s16[528,256]{1,0:T(8,128)(2,1)}, s16[528,256]{1,0:T(8,128)(2,1)}, bf16[512,512]{1,0:T(8,128)(2,1)}) custom-call(s32[4,4]{1,0:T(4,128)} %int_mask.1, bf16[512,1024]{1,0:T(8,128)(2,1)} %slab_ref.1), custom_call_target="tpu_custom_call" | custom-call | tf_op jit(solution)/shard_map/screen/pallas_call | solution.py:82
  10.2 26.4 %all-gather.5.refs_0_ = s16[4224,256]{1,0:T(8,128)(2,1)} all-gather(s16[528,256]{1,0:T(8,128)(2,1)} %get-tuple-element.17), channel_id=1, replica_groups=mesh['occ'=8,'vir'=4] {'occ'}, dimensions={0}, use_global_device_ids=true | all-gather | bytes 2433024 | tf_op jit(solution)/shard_map/all_gather | solution.py:303
  36.6 0.0 all-gather.4.cloned.1.call-update
  36.7 1.4 copy.9.amp_mask
  38.0 35.6 %all-gather.6.refs_1_ = s16[4224,256]{1,0:T(8,128)(2,1)} all-gather(s16[528,256]{1,0:T(8,128)(2,1)} %get-tuple-element.21), channel_id=1, replica_groups=mesh['occ'=8,'vir'=4] {'occ'}, dimensions={0}, use_global_device_ids=true | all-gather | bytes 2433024 | tf_op jit(solution)/shard_map/all_gather | solution.py:305
  73.6 18.8 %ladder.3 = (f32[2,2048,256]{2,1,0:T(8,128)}, s16[8,4,264,128]{3,2,1,0:T(8,128)(2,1)}) custom-call(s32[8,4]{1,0:T(8,128)} %copy.9.amp_mask, s32[8]{0:T(128)} %numbers.3, bf16[2048,4096]{1,0:T(8,128)(2,1)} %rows_ref.3, s16[4224,256]{1,0:T(8,128)(2,1)} %all-gather.5.refs_0_, s16[4224,256]{1,0:T(8,128)(2,1)} %all-gather.6.refs_1_), custom_call_target="tpu_custom_call" | custom-call | flops 8589934592 | bytes 27262976 | tf_op jit(solution)/shard_map/ladder/pallas_call | solution.py:181
  92.5 7.8 %all-to-all-start.1 = ((s16[32,264,128]{2,1,0:T(8,128)(2,1)}), s16[32,264,128]{2,1,0:T(8,128)(2,1)S(1)}, u32[]{:S(2)}, u32[]{:S(2)}) async-start(s16[32,264,128]{2,1,0:T(8,128)(2,1)} %bitcast.9), calls=%async_computation.1 | async-start | bytes 4325376 | tf_op jit(solution)/shard_map/all_to_all | solution.py:296
  100.3 0.0 all-gather.4.cloned.1.call-done.refs_0_
  100.3 17.5 %ladder.2 = (f32[2,2048,256]{2,1,0:T(8,128)}, s16[8,4,264,128]{3,2,1,0:T(8,128)(2,1)}) custom-call(s32[8,4]{1,0:T(8,128)} %copy.9.amp_mask, s32[8]{0:T(128)} %numbers.3, bf16[2048,4096]{1,0:T(8,128)(2,1)} %rows_ref.3, bf16[4096,512]{1,0:T(8,128)(2,1)} %all-gather.4.cloned.1.call-done.refs_0_), custom_call_target="tpu_custom_call" | custom-call | flops 8589934592 | bytes 27262976 | tf_op jit(solution)/shard_map/ladder/pallas_call | solution.py:181
  117.7 0.0 copy-start.1
  117.8 0.0 copy-start.2
  117.8 32.6 %all-to-all-done.1 = s16[32,264,128]{2,1,0:T(8,128)(2,1)S(1)} async-done(((s16[32,264,128]{2,1,0:T(8,128)(2,1)}), s16[32,264,128]{2,1,0:T(8,128)(2,1)S(1)}, u32[]{:S(2)}, u32[]{:S(2)}) %all-to-all-start.1) | async-done | bytes 2162720 | tf_op jit(solution)/shard_map/all_to_all | solution.py:296
  150.4 0.0 copy-start
  150.4 4.5 %all-to-all-start = ((s16[32,264,128]{2,1,0:T(8,128)(2,1)}), s16[32,264,128]{2,1,0:T(8,128)(2,1)}, u32[]{:S(2)}, u32[]{:S(2)}) async-start(s16[32,264,128]{2,1,0:T(8,128)(2,1)} %bitcast.8), calls=%async_computation | async-start | bytes 4325376 | tf_op jit(solution)/shard_map/all_to_all | solution.py:296
  154.9 0.0 copy-done.1
  154.9 0.1 reshape.124
  155.0 0.0 copy-done.2
  155.0 0.1 dynamic_slice.6
  155.1 0.1 broadcast_add_fusion.1
  155.1 0.7 add.167.vir_ref
  155.8 0.1 broadcast_add_fusion
  155.9 0.1 add.173
  156.0 0.9 fusion.1.spread_ref
  157.0 1.0 fusion.spread_ref
  157.9 6.1 %direct.3.direct_ref = f32[2048,512]{1,0:T(8,128)} custom-call(bf16[512,512]{1,0:T(8,128)(2,1)} %fusion.1.spread_ref, f32[2,2048,256]{2,1,0:T(8,128)} %get-tuple-element.22.refs_0_, f32[2,2048,256]{2,1,0:T(8,128)} %get-tuple-element.23.refs_1_), custom_call_target="tpu_custom_call" | custom-call | flops 2147483648 | bytes 8388608 | tf_op jit(solution)/shard_map/direct/pallas_call | solution.py:223
  164.0 0.0 copy-done
  164.0 6.3 %direct.2.direct_ref = f32[2048,512]{1,0:T(8,128)} custom-call(bf16[512,512]{1,0:T(8,128)(2,1)} %fusion.1.spread_ref, f32[2,2048,256]{2,1,0:T(8,128)} %get-tuple-element.22.refs_0_, f32[2,2048,256]{2,1,0:T(8,128)} %get-tuple-element.23.refs_1_), custom_call_target="tpu_custom_call" | custom-call | flops 2147483648 | bytes 8388608 | tf_op jit(solution)/shard_map/direct/pallas_call | solution.py:223
  170.4 1.3 broadcast_in_dim.2.occ_ref
  171.7 7.1 %update.2.refs_0_ = f32[2048,1024]{1,0:T(8,128)} custom-call(s16[8,4,264,128]{3,2,1,0:T(8,128)(2,1)} %bitcast.7, bf16[512,512]{1,0:T(8,128)(2,1)} %fusion.spread_ref, f32[1,1024]{1,0:T(1,128)} %add.167.vir_ref, f32[2048,128]{1,0:T(8,128)} %broadcast_in_dim.2.occ_ref, f32[2048,512]{1,0:T(8,128)} %direct.3.direct_ref), custom_call_target="tpu_custom_call" | custom-call | flops 2147483648 | bytes 10485760 | tf_op jit(solution)/shard_map/update/pallas_call | solution.py:268
  178.8 26.2 %all-to-all-done = s16[32,264,128]{2,1,0:T(8,128)(2,1)} async-done(((s16[32,264,128]{2,1,0:T(8,128)(2,1)}), s16[32,264,128]{2,1,0:T(8,128)(2,1)}, u32[]{:S(2)}, u32[]{:S(2)}) %all-to-all-start) | async-done | bytes 2162720 | tf_op jit(solution)/shard_map/all_to_all | solution.py:296
  205.0 7.1 %update.3 = f32[2048,1024]{1,0:T(8,128)} custom-call(s16[8,4,264,128]{3,2,1,0:T(8,128)(2,1)} %bitcast.2.arrived_ref, bf16[512,512]{1,0:T(8,128)(2,1)} %fusion.spread_ref, f32[1,1024]{1,0:T(1,128)} %add.167.vir_ref, f32[2048,128]{1,0:T(8,128)} %broadcast_in_dim.2.occ_ref, f32[2048,512]{1,0:T(8,128)} %direct.2.direct_ref, ...), custom_call_target="tpu_custom_call", output_to_operand_aliasing={{}: (5, {})} | custom-call | flops 2147483648 | bytes 10485760 | tf_op jit(solution)/shard_map/update/pallas_call | solution.py:268
  (4 shorter events, 0.0 us)
Async XLA Ops:
  6.5 93.7 %all-gather.4.cloned.1.call-start = ((), (), s32[]{:S(2)}) async-start(), calls=%async_computation.2 | async-start | bytes 4718592 | tf_op jit(solution)/shard_map/all_gather | solution.py:308
  92.5 57.9 %all-to-all-start.1 = ((s16[32,264,128]{2,1,0:T(8,128)(2,1)}), s16[32,264,128]{2,1,0:T(8,128)(2,1)S(1)}, u32[]{:S(2)}, u32[]{:S(2)}) async-start(s16[32,264,128]{2,1,0:T(8,128)(2,1)} %bitcast.9), calls=%async_computation.1 | async-start | bytes 4325376 | tf_op jit(solution)/shard_map/all_to_all | solution.py:296
  117.7 37.1 %copy-start.1 = (f32[128]{0:T(128)S(1)}, f32[128]{0:T(128)}, u32[]{:S(2)}) copy-start(f32[128]{0:T(128)} %param.12) | copy-start | bytes 1540
  117.8 37.2 %copy-start.2 = (f32[64]{0:T(128)S(1)}, f32[64]{0:T(128)}, u32[]{:S(2)}) copy-start(f32[64]{0:T(128)} %param.13) | copy-start | bytes 772
  150.4 13.7 %copy-start = (s16[32,264,128]{2,1,0:T(8,128)(2,1)}, s16[32,264,128]{2,1,0:T(8,128)(2,1)S(1)}, u32[]{:S(2)}) copy-start(s16[32,264,128]{2,1,0:T(8,128)(2,1)S(1)} %all-to-all-done.1) | copy-start | bytes 6488068
  150.4 54.6 %all-to-all-start = ((s16[32,264,128]{2,1,0:T(8,128)(2,1)}), s16[32,264,128]{2,1,0:T(8,128)(2,1)}, u32[]{:S(2)}, u32[]{:S(2)}) async-start(s16[32,264,128]{2,1,0:T(8,128)(2,1)} %bitcast.8), calls=%async_computation | async-start | bytes 4325376 | tf_op jit(solution)/shard_map/all_to_all | solution.py:296
Sparse Core Ops, SparseCore 0:
  36.8 58.8 all-gather.3

commit v11 on v10

--- a/solution.py
+++ b/solution.py
@@ -14,7 +14,8 @@
 PAIR_SQ = ORBITALS_IN_GRP * ORBITALS_IN_GRP
 CODE_ROWS = 16
 EXCHANGE_CODE_ROWS = 8
-CODED_PARTS = 2
+CODED_PARTS = 1
+PIECES = 4
 AT_ONCE = 2
 SLAB_BITS = 14.0
 TOP = 32700.0
@@ -116,7 +117,8 @@
     lax.fori_loop(0, tile_total, decode, 0)
 
 
-def ladder_kernel(tile_total, vir_count, chunks, coded, amp_mask, numbers, rows_ref, *refs):
+def ladder_kernel(tile_total, vir_count, chunks, coded, amp_mask, numbers, *refs):
+    rows_refs, refs = refs[:PIECES], refs[PIECES:]
     slab_refs, refs = (refs[:CODED_PARTS], refs[CODED_PARTS:]) if coded else (refs[:1], refs[1:])
     ladder_ref, packed_ref, product = refs[:3]
     step = pl.program_id(0)
@@ -159,12 +161,13 @@
         jnp.where(left, amp_mask[tile, 0], amp_mask[tile, 1]),
         jnp.where(left, amp_mask[tile, 2], amp_mask[tile, 3]),
     )
-    screened = rows_ref[...] * keep.astype(jnp.float32).astype(jnp.bfloat16)
+    keep = keep.astype(jnp.float32).astype(jnp.bfloat16)
+    screened = jnp.concatenate([rows_ref[...] * keep for rows_ref in rows_refs], axis=0)
     product[...] = dot(screened, slab_ref[...])
 
 
 def ladder_call(tile_total, vir_count, chunks, amp_mask, numbers, amplitudes, slab):
-    coded = len(slab) > 1
+    coded = slab[0].dtype == jnp.int16
     cols = sum(part.shape[1] for part in slab)
     block = cols // vir_count
     smem = pl.BlockSpec(memory_space=pltpu.SMEM)
@@ -184,7 +187,13 @@
         in_specs=[
             smem,
             smem,
-            pl.BlockSpec((PAIR_SQ, W * W), lambda step: (jnp.minimum(step, tile_total - 1), 0)),
+            *[
+                pl.BlockSpec(
+                    (PAIR_SQ // PIECES, W * W),
+                    lambda step, n=n: (jnp.minimum(step, tile_total - 1) * PIECES + n, 0),
+                )
+                for n in range(PIECES)
+            ],
             *slab_specs,
         ],
         out_specs=[
@@ -205,7 +214,7 @@
             transcendentals=0,
         ),
         name="ladder",
-    )(amp_mask, numbers, amplitudes, *slab)
+    )(amp_mask, numbers, *[amplitudes] * PIECES, *slab)
 
 
 def moved_columns(values, spread_ref):
@@ -235,38 +244,45 @@
     )(spread, *ladders)
 
 
-def update_kernel(vir_count, arrived_ref, spread_ref, vir_ref, occ_ref, direct_ref, *refs):
+def update_kernel(vir_count, spread_ref, vir_ref, occ_ref, *refs):
+    arrived_refs, refs = refs[:vir_count], refs[vir_count:]
+    direct_refs = refs[:AT_ONCE]
     tiles = []
     for n in range(AT_ONCE):
         blocks = []
         for v in range(vir_count):
-            code = arrived_ref[n, v, PAIR_SQ:].astype(jnp.int32).astype(jnp.float32)[:1]
-            values = arrived_ref[n, v, :PAIR_SQ].astype(jnp.int32).astype(jnp.float32)
+            code = arrived_refs[v][n, 0, PAIR_SQ:].astype(jnp.int32).astype(jnp.float32)[:1]
+            values = arrived_refs[v][n, 0, :PAIR_SQ].astype(jnp.int32).astype(jnp.float32)
             blocks.append(values * (scale_of(code) * (1.0 / TOP)))
         tiles.append(jnp.concatenate(blocks, axis=1))
     mirror = moved_columns(jnp.concatenate(tiles, axis=0), spread_ref)
-    refs[-1][...] = (direct_ref[...] + mirror) / (vir_ref[...] - occ_ref[:, :1])
+    for n, direct_ref in enumerate(direct_refs):
+        at = slice(n * PAIR_SQ, (n + 1) * PAIR_SQ)
+        refs[-1][at, :] = (direct_ref[...] + mirror[at]) / (vir_ref[...] - occ_ref[at, :1])
 
 
 def update_call(chunk, chunks, arrived, spread, vir_sum, occ_sum, direct, earlier):
     cols = spread.shape[1]
     rows = direct.shape[0]
     step_rows = AT_ONCE * PAIR_SQ
-    args = [arrived, spread, vir_sum, occ_sum, direct]
+    vir_count = arrived.shape[1]
+    args = [spread, vir_sum, occ_sum] + [arrived] * vir_count + [direct] * AT_ONCE
     in_specs = [
-        pl.BlockSpec((AT_ONCE,) + arrived.shape[1:], lambda step: (step, 0, 0, 0)),
         pl.BlockSpec(spread.shape, lambda step: (0, 0)),
         pl.BlockSpec((1, cols), lambda step: (0, chunk)),
         pl.BlockSpec((step_rows, 128), lambda step: (step, 0)),
-        pl.BlockSpec((step_rows, cols), lambda step: (step, 0)),
     ]
+    in_specs += [
+        pl.BlockSpec((AT_ONCE, 1) + arrived.shape[2:], lambda step, v=v: (step, v, 0, 0)) for v in range(vir_count)
+    ]
+    in_specs += [pl.BlockSpec((PAIR_SQ, cols), lambda step, n=n: (step * AT_ONCE + n, 0)) for n in range(AT_ONCE)]
     aliases = {}
     if earlier is not None:
         aliases = {len(args): 0}
         args.append(earlier)
         in_specs.append(pl.BlockSpec(memory_space=pl.ANY))
     return pl.pallas_call(
-        functools.partial(update_kernel, arrived.shape[1]),
+        functools.partial(update_kernel, vir_count),
         grid=(rows // step_rows,),
         in_specs=in_specs,
         out_specs=pl.BlockSpec((step_rows, cols), lambda step: (step, chunk)),

time: 220 us -> 218 us (level)
  blocking collectives: 62 us -> 42.6 us
  waiting for transfers between devices: 58.9 us -> 76.8 us
  starting transfers between devices: 12.3 us -> 9.58 us
    all_gather x1, waiting for transfers between devices: 0.02 us -> 50.2 us  [body(): slabs.append([lax.all_gather(part, 'occ', axis=0, tiled=True)])]
    all_gather x1 -> x0, blocking collectives: 35.6 us -> none  [body(): lax.all_gather(part, 'occ', axis=0, tiled=True)]
    all_to_all x2, waiting for transfers between devices: 58.8 us -> 26.5 us  [exchanged(): lax.all_to_all(packed.reshape(tile_total * vir_count, rows, block), ('occ...]
    all_gather x1, blocking collectives: 26.4 us -> 42.6 us  [body(): first = lax.all_gather(coded[0], 'occ', axis=0, tiled=True)]
    unnamed x6 -> x10, local copies, waits for them, and re-layouts: 0.01 us -> 2.82 us
    all_to_all x2, starting transfers between devices: 12.3 us -> 9.58 us  [exchanged(): lax.all_to_all(packed.reshape(tile_total * vir_count, rows, block), ('occ...]
  transfers between devices with their start and end apart: 3 -> 3, of which waited for: 2 -> 3; matrix products, arithmetic and copies ran while one was open for 3% -> 2% of each run, Pallas kernels for 26% -> 26%
where the time goes in v11:
time: 218 us; the launch traced here: 217 us
  waiting for transfers between devices  76.8 us (35%)
  Pallas kernels  66.5 us (31%)
  blocking collectives  42.6 us (20%)
  between operations  13.5 us (6%)
  starting transfers between devices  9.58 us (4%)
  local copies, waits for them, and re-layouts  5.7 us (3%)
    all_gather x1, waiting for transfers between devices, body(): slabs.append([lax.all_gather(part, 'occ', axis=0, tiled=True)])  50.2 us
    all_gather x1, blocking collectives, body(): first = lax.all_gather(coded[0], 'occ', axis=0, tiled=True)  42.6 us
    pallas_call x2, Pallas kernels, ladder_call(): pl.pallas_call(functools.partial(ladder_kernel, tile_total, vir_count, ch...  36.1 us
    all_to_all x2, waiting for transfers between devices, exchanged(): lax.all_to_all(packed.reshape(tile_total * vir_count, rows, block), ('occ...  26.5 us
    pallas_call x2, Pallas kernels, update_call(): pl.pallas_call(functools.partial(update_kernel, vir_count), grid=(rows //...  14.3 us
    pallas_call x2, Pallas kernels, direct_call(): pl.pallas_call(direct_kernel, grid=(rows // step_rows,), in_specs=[pl.Blo...  12.4 us
    all_to_all x2, starting transfers between devices, exchanged(): lax.all_to_all(packed.reshape(tile_total * vir_count, rows, block), ('occ...  9.58 us
  transfers between devices with their start and end apart: 3, of which 3 were waited for; matrix products, arithmetic and copies ran while one was open for 2% of the time, Pallas kernels for 26%

profile of v11, /device:TPU:0, one launch (start us, length us, event | category | flops | bytes accessed | tf_op | source)
XLA Modules:
  0.0 216.6 jit_solution(2388871965982966678)
XLA Ops:
  6.5 0.0 copy-start.2
  6.5 0.0 all-gather.3.cloned.1.call-start
  6.5 3.7 %screen.1 = (s16[528,512]{1,0:T(8,128)(2,1)}, bf16[512,512]{1,0:T(8,128)(2,1)}) custom-call(s32[4,4]{1,0:T(4,128)} %int_mask.1, bf16[512,1024]{1,0:T(8,128)(2,1)} %slab_ref.1), custom_call_target="tpu_custom_call" | custom-call | tf_op jit(solution)/shard_map/screen/pallas_call | solution.py:83
  10.2 42.6 %all-gather.4.refs_4_ = s16[4224,512]{1,0:T(8,128)(2,1)} all-gather(s16[528,512]{1,0:T(8,128)(2,1)} %get-tuple-element.13), channel_id=1, replica_groups=mesh['occ'=8,'vir'=4] {'occ'}, dimensions={0}, use_global_device_ids=true | all-gather | bytes 4866048 | tf_op jit(solution)/shard_map/all_gather | solution.py:319
  52.8 0.0 all-gather.3.cloned.1.call-update
  52.8 0.0 copy-done.2
  52.8 0.7 copy.9.amp_mask
  53.5 18.7 %ladder.3 = (f32[2,2048,256]{2,1,0:T(8,128)}, s16[8,4,264,128]{3,2,1,0:T(8,128)(2,1)}) custom-call(s32[8,4]{1,0:T(8,128)} %copy.9.amp_mask, s32[8]{0:T(128)} %numbers.3, bf16[2048,4096]{1,0:T(8,128)(2,1)} %refs_3_.3, bf16[2048,4096]{1,0:T(8,128)(2,1)} %refs_3_.3, bf16[2048,4096]{1,0:T(8,128)(2,1)} %refs_3_.3, bf16[2048,4096]{1,0:T(8,128)(2,1)} %refs_3_.3, ...), custom_call_target="tpu_custom_call" | custom-call | flops 8589934592 | bytes 27262976 | tf_op jit(solution)/shard_map/ladder/pallas_call | solution.py:184
  72.2 6.0 %all-to-all-start.1 = ((s16[32,264,128]{2,1,0:T(8,128)(2,1)}), s16[32,264,128]{2,1,0:T(8,128)(2,1)S(1)}, u32[]{:S(2)}, u32[]{:S(2)}) async-start(s16[32,264,128]{2,1,0:T(8,128)(2,1)} %bitcast.16), calls=%async_computation.1 | async-start | bytes 4325376 | tf_op jit(solution)/shard_map/all_to_all | solution.py:312
  78.2 50.2 %all-gather.3.cloned.1.call-done.refs_4_ = bf16[4096,512]{1,0:T(8,128)(2,1)} async-done(((bf16[512,512]{1,0:T(8,128)(2,1)}), bf16[4096,512]{1,0:T(8,128)(2,1)}) %all-gather.3.cloned.1.call-update) | async-done | bytes 4194320 | tf_op jit(solution)/shard_map/all_gather | solution.py:324
  128.4 17.4 %ladder.2 = (f32[2,2048,256]{2,1,0:T(8,128)}, s16[8,4,264,128]{3,2,1,0:T(8,128)(2,1)}) custom-call(s32[8,4]{1,0:T(8,128)} %copy.9.amp_mask, s32[8]{0:T(128)} %numbers.3, bf16[2048,4096]{1,0:T(8,128)(2,1)} %refs_3_.3, bf16[2048,4096]{1,0:T(8,128)(2,1)} %refs_3_.3, bf16[2048,4096]{1,0:T(8,128)(2,1)} %refs_3_.3, bf16[2048,4096]{1,0:T(8,128)(2,1)} %refs_3_.3, ...), custom_call_target="tpu_custom_call" | custom-call | flops 8589934592 | bytes 27262976 | tf_op jit(solution)/shard_map/ladder/pallas_call | solution.py:184
  145.8 0.0 copy-start.3
  145.8 0.0 copy-start.4
  145.9 0.3 all-to-all-done.1
  146.2 0.0 copy-start.1
  146.2 1.4 copy-done.1
  147.6 3.5 %all-to-all-start = ((s16[32,264,128]{2,1,0:T(8,128)(2,1)}), s16[32,264,128]{2,1,0:T(8,128)(2,1)S(1)}, u32[]{:S(2)}, u32[]{:S(2)}) async-start(s16[32,264,128]{2,1,0:T(8,128)(2,1)} %bitcast.15), calls=%async_computation | async-start | bytes 4325376 | tf_op jit(solution)/shard_map/all_to_all | solution.py:312
  151.2 0.0 copy-done.3
  151.2 0.1 reshape.122
  151.3 0.0 copy-done.4
  151.3 0.1 dynamic_slice.6
  151.4 0.1 broadcast_add_fusion.1
  151.4 0.7 add.167.vir_ref
  152.1 0.1 broadcast_add_fusion
  152.2 0.1 add.173
  152.3 1.0 fusion.1.spread_ref
  153.3 0.9 fusion.spread_ref
  154.2 6.1 %direct.3.refs_4_.refs_5_ = f32[2048,512]{1,0:T(8,128)} custom-call(bf16[512,512]{1,0:T(8,128)(2,1)} %fusion.1.spread_ref, f32[2,2048,256]{2,1,0:T(8,128)} %get-tuple-element.16.refs_0_, f32[2,2048,256]{2,1,0:T(8,128)} %get-tuple-element.17.refs_1_), custom_call_target="tpu_custom_call" | custom-call | flops 2147483648 | bytes 8388608 | tf_op jit(solution)/shard_map/direct/pallas_call | solution.py:232
  160.3 6.3 %direct.2.refs_4_.refs_5_ = f32[2048,512]{1,0:T(8,128)} custom-call(bf16[512,512]{1,0:T(8,128)(2,1)} %fusion.1.spread_ref, f32[2,2048,256]{2,1,0:T(8,128)} %get-tuple-element.16.refs_0_, f32[2,2048,256]{2,1,0:T(8,128)} %get-tuple-element.17.refs_1_), custom_call_target="tpu_custom_call" | custom-call | flops 2147483648 | bytes 8388608 | tf_op jit(solution)/shard_map/direct/pallas_call | solution.py:232
  166.6 1.3 broadcast_in_dim.2.occ_ref
  167.9 7.2 %update.2.refs_6_ = f32[2048,1024]{1,0:T(8,128)} custom-call(bf16[512,512]{1,0:T(8,128)(2,1)} %fusion.spread_ref, f32[1,1024]{1,0:T(1,128)} %add.167.vir_ref, f32[2048,128]{1,0:T(8,128)} %broadcast_in_dim.2.occ_ref, s16[8,4,264,128]{3,2,1,0:T(8,128)(2,1)} %bitcast.11, s16[8,4,264,128]{3,2,1,0:T(8,128)(2,1)} %bitcast.12, s16[8,4,264,128]{3,2,1,0:T(8,128)(2,1)} %bitcast.13, ...), custom_call_target="tpu_custom_call" | custom-call | flops 2147483648 | bytes 10485760 | tf_op jit(solution)/shard_map/update/pallas_call | solution.py:284
  175.1 26.2 %all-to-all-done = s16[32,264,128]{2,1,0:T(8,128)(2,1)S(1)} async-done(((s16[32,264,128]{2,1,0:T(8,128)(2,1)}), s16[32,264,128]{2,1,0:T(8,128)(2,1)S(1)}, u32[]{:S(2)}, u32[]{:S(2)}) %all-to-all-start) | async-done | bytes 2162720 | tf_op jit(solution)/shard_map/all_to_all | solution.py:312
  201.3 0.0 copy-start
  201.3 1.4 copy-done
  202.7 7.1 %update.3 = f32[2048,1024]{1,0:T(8,128)} custom-call(bf16[512,512]{1,0:T(8,128)(2,1)} %fusion.spread_ref, f32[1,1024]{1,0:T(1,128)} %add.167.vir_ref, f32[2048,128]{1,0:T(8,128)} %broadcast_in_dim.2.occ_ref, s16[8,4,264,128]{3,2,1,0:T(8,128)(2,1)} %bitcast.7, s16[8,4,264,128]{3,2,1,0:T(8,128)(2,1)} %bitcast.8, ...), custom_call_target="tpu_custom_call", output_to_operand_aliasing={{}: (9, {})} | custom-call | flops 2147483648 | bytes 10485760 | tf_op jit(solution)/shard_map/update/pallas_call | solution.py:284
  (4 shorter events, 0.0 us)
Async XLA Ops:
  6.5 46.3 %copy-start.2 = (s32[1,8,4]{1,2,0:T(4,128)S(1)}, s32[1,8,4]{1,2,0:T(4,128)}, u32[]{:S(2)}) copy-start(s32[1,8,4]{1,2,0:T(4,128)} %param.8) | copy-start | bytes 388
  6.5 121.9 %all-gather.3.cloned.1.call-start = ((), (), s32[]{:S(2)}) async-start(), calls=%async_computation.2 | async-start | bytes 4718592 | tf_op jit(solution)/shard_map/all_gather | solution.py:324
  72.2 74.0 %all-to-all-start.1 = ((s16[32,264,128]{2,1,0:T(8,128)(2,1)}), s16[32,264,128]{2,1,0:T(8,128)(2,1)S(1)}, u32[]{:S(2)}, u32[]{:S(2)}) async-start(s16[32,264,128]{2,1,0:T(8,128)(2,1)} %bitcast.16), calls=%async_computation.1 | async-start | bytes 4325376 | tf_op jit(solution)/shard_map/all_to_all | solution.py:312
  145.8 5.3 %copy-start.3 = (f32[128]{0:T(128)S(1)}, f32[128]{0:T(128)}, u32[]{:S(2)}) copy-start(f32[128]{0:T(128)} %param.12) | copy-start | bytes 1540
  145.8 5.4 %copy-start.4 = (f32[64]{0:T(128)S(1)}, f32[64]{0:T(128)}, u32[]{:S(2)}) copy-start(f32[64]{0:T(128)} %param.13) | copy-start | bytes 772
  146.2 1.4 copy-start.1
  147.6 53.7 %all-to-all-start = ((s16[32,264,128]{2,1,0:T(8,128)(2,1)}), s16[32,264,128]{2,1,0:T(8,128)(2,1)S(1)}, u32[]{:S(2)}, u32[]{:S(2)}) async-start(s16[32,264,128]{2,1,0:T(8,128)(2,1)} %bitcast.15), calls=%async_computation | async-start | bytes 4325376 | tf_op jit(solution)/shard_map/all_to_all | solution.py:312
  201.3 1.4 copy-start
Sparse Core Ops, SparseCore 0:
  52.9 75.4 all-gather.2

commit v12 on v11

--- a/solution.py
+++ b/solution.py
@@ -15,7 +15,6 @@
 CODE_ROWS = 16
 EXCHANGE_CODE_ROWS = 8
 CODED_PARTS = 1
-PIECES = 4
 AT_ONCE = 2
 SLAB_BITS = 14.0
 TOP = 32700.0
@@ -117,8 +116,7 @@
     lax.fori_loop(0, tile_total, decode, 0)
 
 
-def ladder_kernel(tile_total, vir_count, chunks, coded, amp_mask, numbers, *refs):
-    rows_refs, refs = refs[:PIECES], refs[PIECES:]
+def ladder_kernel(tile_total, vir_count, chunks, tiles, dot_cols, coded, amp_mask, numbers, rows_ref, *refs):
     slab_refs, refs = (refs[:CODED_PARTS], refs[CODED_PARTS:]) if coded else (refs[:1], refs[1:])
     ladder_ref, packed_ref, product = refs[:3]
     step = pl.program_id(0)
@@ -130,49 +128,56 @@
         def _():
             decode_slab(tile_total, slab_refs, stage, slab_ref, sems)
     cols = slab_ref.shape[1]
-
-    tile = jnp.maximum(step - 1, 0)
+    block = cols // vir_count
+    lanes = block // chunks
+
     pair = lax.broadcasted_iota(jnp.int32, (PAIR_SQ, 1), 0)
     own_number = numbers[lax.axis_index("occ")]
-    nonzero = (pair // ORBITALS_IN_GRP < own_number) & (pair % ORBITALS_IN_GRP < numbers[tile])
-    ladder = jnp.where(nonzero, product[...], 0.0)
-    block = cols // vir_count
-    lanes = block // chunks
-    for h in range(chunks):
-        ladder_ref[h] = jnp.concatenate(
-            [ladder[:, v * block + h * lanes : v * block + (h + 1) * lanes] for v in range(vir_count)], axis=1
-        )
-    by_place = ladder.reshape(ORBITALS_IN_GRP, ORBITALS_IN_GRP, cols)
-    mirror = jnp.swapaxes(by_place, 0, 1).reshape(PAIR_SQ, cols)
-    most = jnp.maximum(jnp.max(jnp.abs(ladder), axis=0, keepdims=True), 1e-30)
-    code = jnp.ceil(jnp.log2(most) * STEPS)
-    coded = jnp.round(mirror * (TOP / scale_of(code))).astype(jnp.int32).astype(jnp.int16)
-    code_rows = jnp.broadcast_to(code.astype(jnp.int32), (EXCHANGE_CODE_ROWS, cols)).astype(jnp.int16)
-    for v in range(vir_count):
-        packed_ref[0, v, :PAIR_SQ] = coded[:, v * block : (v + 1) * block]
-        packed_ref[0, v, PAIR_SQ:] = code_rows[:, v * block : (v + 1) * block]
-
-    tile = jnp.minimum(step, tile_total - 1)
+    for n in range(tiles):
+        tile = jnp.maximum(step - 1, 0) * tiles + n
+        rows = slice(n * PAIR_SQ, (n + 1) * PAIR_SQ)
+        nonzero = (pair // ORBITALS_IN_GRP < own_number) & (pair % ORBITALS_IN_GRP < numbers[tile])
+        ladder = jnp.where(nonzero, product[rows, :], 0.0)
+        for h in range(chunks):
+            ladder_ref[h, rows, :] = jnp.concatenate(
+                [ladder[:, v * block + h * lanes : v * block + (h + 1) * lanes] for v in range(vir_count)], axis=1
+            )
+        by_place = ladder.reshape(ORBITALS_IN_GRP, ORBITALS_IN_GRP, cols)
+        mirror = jnp.swapaxes(by_place, 0, 1).reshape(PAIR_SQ, cols)
+        most = jnp.maximum(jnp.max(jnp.abs(ladder), axis=0, keepdims=True), 1e-30)
+        code = jnp.ceil(jnp.log2(most) * STEPS)
+        coded_rows = jnp.round(mirror * (TOP / scale_of(code))).astype(jnp.int32).astype(jnp.int16)
+        code_rows = jnp.broadcast_to(code.astype(jnp.int32), (EXCHANGE_CODE_ROWS, cols)).astype(jnp.int16)
+        for v in range(vir_count):
+            packed_ref[n, v, :PAIR_SQ] = coded_rows[:, v * block : (v + 1) * block]
+            packed_ref[n, v, PAIR_SQ:] = code_rows[:, v * block : (v + 1) * block]
+
     lane = lax.broadcasted_iota(jnp.int32, (1, W * W), 1)
     low = lane < W * VT
     left = lane % W < VT
-    keep = jnp.where(
-        low,
-        jnp.where(left, amp_mask[tile, 0], amp_mask[tile, 1]),
-        jnp.where(left, amp_mask[tile, 2], amp_mask[tile, 3]),
-    )
-    keep = keep.astype(jnp.float32).astype(jnp.bfloat16)
-    screened = jnp.concatenate([rows_ref[...] * keep for rows_ref in rows_refs], axis=0)
-    product[...] = dot(screened, slab_ref[...])
-
-
-def ladder_call(tile_total, vir_count, chunks, amp_mask, numbers, amplitudes, slab):
+    screened = []
+    for n in range(tiles):
+        tile = jnp.minimum(step * tiles + n, tile_total - 1)
+        keep = jnp.where(
+            low,
+            jnp.where(left, amp_mask[tile, 0], amp_mask[tile, 1]),
+            jnp.where(left, amp_mask[tile, 2], amp_mask[tile, 3]),
+        )
+        keep = keep.astype(jnp.float32).astype(jnp.bfloat16)
+        screened.append(rows_ref[n * PAIR_SQ : (n + 1) * PAIR_SQ, :] * keep)
+    screened = jnp.concatenate(screened, axis=0)
+    for at in range(0, cols, dot_cols):
+        product[:, at : at + dot_cols] = dot(screened, slab_ref[:, at : at + dot_cols])
+
+
+def ladder_call(tile_total, vir_count, chunks, tiles, dot_cols, amp_mask, numbers, amplitudes, slab):
     coded = slab[0].dtype == jnp.int16
     cols = sum(part.shape[1] for part in slab)
     block = cols // vir_count
     smem = pl.BlockSpec(memory_space=pltpu.SMEM)
     rows = tile_total * PAIR_SQ
-    scratch = [pltpu.VMEM((PAIR_SQ, cols), jnp.float32)]
+    steps = tile_total // tiles
+    scratch = [pltpu.VMEM((tiles * PAIR_SQ, cols), jnp.float32)]
     slab_specs = [pl.BlockSpec((W * W, cols), lambda step: (0, 0))]
     if coded:
         slab_specs = [pl.BlockSpec(memory_space=pl.ANY)] * CODED_PARTS
@@ -181,30 +186,24 @@
             pltpu.VMEM((W * W, cols), jnp.bfloat16),
             pltpu.SemaphoreType.DMA((CODED_PARTS, tile_total)),
         ]
+    before = lambda step: jnp.maximum(step - 1, 0)
+    packed_block = (vir_count, PAIR_SQ + EXCHANGE_CODE_ROWS, block)
     return pl.pallas_call(
-        functools.partial(ladder_kernel, tile_total, vir_count, chunks, coded),
-        grid=(tile_total + 1,),
+        functools.partial(ladder_kernel, tile_total, vir_count, chunks, tiles, min(dot_cols, cols), coded),
+        grid=(steps + 1,),
         in_specs=[
             smem,
             smem,
-            *[
-                pl.BlockSpec(
-                    (PAIR_SQ // PIECES, W * W),
-                    lambda step, n=n: (jnp.minimum(step, tile_total - 1) * PIECES + n, 0),
-                )
-                for n in range(PIECES)
-            ],
+            pl.BlockSpec((tiles * PAIR_SQ, W * W), lambda step: (jnp.minimum(step, steps - 1), 0)),
             *slab_specs,
         ],
         out_specs=[
-            pl.BlockSpec((chunks, PAIR_SQ, cols // chunks), lambda step: (0, jnp.maximum(step - 1, 0), 0)),
-            pl.BlockSpec(
-                (1, vir_count, PAIR_SQ + EXCHANGE_CODE_ROWS, block), lambda step: (jnp.maximum(step - 1, 0), 0, 0, 0)
-            ),
+            pl.BlockSpec((chunks, tiles * PAIR_SQ, cols // chunks), lambda step: (0, before(step), 0)),
+            pl.BlockSpec((tiles,) + packed_block, lambda step: (before(step), 0, 0, 0)),
         ],
         out_shape=[
             jax.ShapeDtypeStruct((chunks, rows, cols // chunks), jnp.float32),
-            jax.ShapeDtypeStruct((tile_total, vir_count, PAIR_SQ + EXCHANGE_CODE_ROWS, block), jnp.int16),
+            jax.ShapeDtypeStruct((tile_total,) + packed_block, jnp.int16),
         ],
         scratch_shapes=scratch,
         compiler_params=pltpu.CompilerParams(vmem_limit_bytes=VMEM_LIMIT),
@@ -214,7 +213,7 @@
             transcendentals=0,
         ),
         name="ladder",
-    )(amp_mask, numbers, *[amplitudes] * PIECES, *slab)
+    )(amp_mask, numbers, amplitudes, *slab)
 
 
 def moved_columns(values, spread_ref):
@@ -244,11 +243,11 @@
     )(spread, *ladders)
 
 
-def update_kernel(vir_count, spread_ref, vir_ref, occ_ref, *refs):
+def update_kernel(vir_count, at_once, spread_ref, vir_ref, occ_ref, *refs):
     arrived_refs, refs = refs[:vir_count], refs[vir_count:]
-    direct_refs = refs[:AT_ONCE]
+    direct_refs = refs[:at_once]
     tiles = []
-    for n in range(AT_ONCE):
+    for n in range(at_once):
         blocks = []
         for v in range(vir_count):
             code = arrived_refs[v][n, 0, PAIR_SQ:].astype(jnp.int32).astype(jnp.float32)[:1]
@@ -261,28 +260,28 @@
         refs[-1][at, :] = (direct_ref[...] + mirror[at]) / (vir_ref[...] - occ_ref[at, :1])
 
 
-def update_call(chunk, chunks, arrived, spread, vir_sum, occ_sum, direct, earlier):
+def update_call(chunk, chunks, at_once, arrived, spread, vir_sum, occ_sum, direct, earlier):
     cols = spread.shape[1]
     rows = direct.shape[0]
-    step_rows = AT_ONCE * PAIR_SQ
+    step_rows = at_once * PAIR_SQ
     vir_count = arrived.shape[1]
-    args = [spread, vir_sum, occ_sum] + [arrived] * vir_count + [direct] * AT_ONCE
+    args = [spread, vir_sum, occ_sum] + [arrived] * vir_count + [direct] * at_once
     in_specs = [
         pl.BlockSpec(spread.shape, lambda step: (0, 0)),
         pl.BlockSpec((1, cols), lambda step: (0, chunk)),
         pl.BlockSpec((step_rows, 128), lambda step: (step, 0)),
     ]
     in_specs += [
-        pl.BlockSpec((AT_ONCE, 1) + arrived.shape[2:], lambda step, v=v: (step, v, 0, 0)) for v in range(vir_count)
+        pl.BlockSpec((at_once, 1) + arrived.shape[2:], lambda step, v=v: (step, v, 0, 0)) for v in range(vir_count)
     ]
-    in_specs += [pl.BlockSpec((PAIR_SQ, cols), lambda step, n=n: (step * AT_ONCE + n, 0)) for n in range(AT_ONCE)]
+    in_specs += [pl.BlockSpec((PAIR_SQ, cols), lambda step, n=n: (step * at_once + n, 0)) for n in range(at_once)]
     aliases = {}
     if earlier is not None:
         aliases = {len(args): 0}
         args.append(earlier)
         in_specs.append(pl.BlockSpec(memory_space=pl.ANY))
     return pl.pallas_call(
-        functools.partial(update_kernel, vir_count),
+        functools.partial(update_kernel, vir_count, at_once),
         grid=(rows // step_rows,),
         in_specs=in_specs,
         out_specs=pl.BlockSpec((step_rows, cols), lambda step: (step, chunk)),
@@ -324,8 +323,9 @@
         slabs.append([lax.all_gather(part, "occ", axis=0, tiled=True)])
     ladders, arrived = [], []
     for slab in slabs:
+        tiles, dot_cols = (2, 512) if ladders else (1, 256)
         ladder, packed = ladder_call(
-            tile_total, vir_count, chunks, amp_mask[0], group_orbital_numbers, amplitudes, slab
+            tile_total, vir_count, chunks, tiles, dot_cols, amp_mask[0], group_orbital_numbers, amplitudes, slab
         )
         ladders.append(ladder)
         arrived.append(exchanged(packed))
@@ -350,7 +350,7 @@
     update = None
     for chunk in range(chunks):
         direct = direct_call(chunk, direct_spread, ladders)
-        update = update_call(chunk, chunks, arrived[chunk], mirror_spread, vir_sum, occ_sum, direct, update)
+        update = update_call(chunk, chunks, 4 if chunk else 1, arrived[chunk], mirror_spread, vir_sum, occ_sum, direct, update)
     return update
 
 

time: 218 us -> 214 us (0.982)
  local copies, waits for them, and re-layouts: 5.7 us -> 2.92 us
  waiting for transfers between devices: 76.8 us -> 74.3 us
    unnamed x10 -> x8, local copies, waits for them, and re-layouts: 2.82 us -> 0.01 us
    all_gather x1, waiting for transfers between devices: 50.2 us -> 47.6 us  [body(): slabs.append([lax.all_gather(part, 'occ', axis=0, tiled=True)])]
  transfers between devices with their start and end apart: 3 -> 3, of which waited for: 3 -> 3; matrix products, arithmetic and copies ran while one was open for 2% -> 2% of each run, Pallas kernels for 26% -> 27%
where the time goes in v12:
time: 214 us; the launch traced here: 213 us
  waiting for transfers between devices  74.3 us (35%)
  Pallas kernels  68.1 us (32%)
  blocking collectives  42.6 us (20%)
  between operations  13.5 us (6%)
  starting transfers between devices  9.59 us (4%)
  local copies, waits for them, and re-layouts  2.92 us (1%)
    all_gather x1, waiting for transfers between devices, body(): slabs.append([lax.all_gather(part, 'occ', axis=0, tiled=True)])  47.6 us
    all_gather x1, blocking collectives, body(): first = lax.all_gather(coded[0], 'occ', axis=0, tiled=True)  42.6 us
    pallas_call x2, Pallas kernels, ladder_call(): pl.pallas_call(functools.partial(ladder_kernel, tile_total, vir_count, ch...  36.6 us
    all_to_all x2, waiting for transfers between devices, exchanged(): lax.all_to_all(packed.reshape(tile_total * vir_count, rows, block), ('occ...  26.7 us
    pallas_call x2, Pallas kernels, update_call(): pl.pallas_call(functools.partial(update_kernel, vir_count, at_once), grid...  15.3 us
    pallas_call x2, Pallas kernels, direct_call(): pl.pallas_call(direct_kernel, grid=(rows // step_rows,), in_specs=[pl.Blo...  12.5 us
    all_to_all x2, starting transfers between devices, exchanged(): lax.all_to_all(packed.reshape(tile_total * vir_count, rows, block), ('occ...  9.59 us
  transfers between devices with their start and end apart: 3, of which 3 were waited for; matrix products, arithmetic and copies ran while one was open for 2% of the time, Pallas kernels for 27%

profile of v12, /device:TPU:0, one launch (start us, length us, event | category | flops | bytes accessed | tf_op | source)
XLA Modules:
  0.0 213.1 jit_solution(15866866836228869090)
XLA Ops:
  6.5 0.0 copy-start.1
  6.5 0.0 all-gather.3.cloned.1.call-start
  6.5 3.7 %screen.1 = (s16[528,512]{1,0:T(8,128)(2,1)}, bf16[512,512]{1,0:T(8,128)(2,1)}) custom-call(s32[4,4]{1,0:T(4,128)} %int_mask.1, bf16[512,1024]{1,0:T(8,128)(2,1)} %slab_ref.1), custom_call_target="tpu_custom_call" | custom-call | tf_op jit(solution)/shard_map/screen/pallas_call | solution.py:82
  10.2 42.6 %all-gather.4.refs_0_ = s16[4224,512]{1,0:T(8,128)(2,1)} all-gather(s16[528,512]{1,0:T(8,128)(2,1)} %get-tuple-element.13), channel_id=1, replica_groups=mesh['occ'=8,'vir'=4] {'occ'}, dimensions={0}, use_global_device_ids=true | all-gather | bytes 4866048 | tf_op jit(solution)/shard_map/all_gather | solution.py:318
  52.8 0.0 all-gather.3.cloned.1.call-update
  52.8 0.0 copy-done.1
  52.8 0.7 copy.9.amp_mask
  53.5 19.1 %ladder.3 = (f32[2,2048,256]{2,1,0:T(8,128)}, s16[8,4,264,128]{3,2,1,0:T(8,128)(2,1)}) custom-call(s32[8,4]{1,0:T(8,128)} %copy.9.amp_mask, s32[8]{0:T(128)} %numbers.3, bf16[2048,4096]{1,0:T(8,128)(2,1)} %rows_ref.3, s16[4224,512]{1,0:T(8,128)(2,1)} %all-gather.4.refs_0_), custom_call_target="tpu_custom_call" | custom-call | flops 8589934592 | bytes 27262976 | tf_op jit(solution)/shard_map/ladder/pallas_call | solution.py:191
  72.6 6.0 %all-to-all-start.1 = ((s16[32,264,128]{2,1,0:T(8,128)(2,1)}), s16[32,264,128]{2,1,0:T(8,128)(2,1)S(1)}, u32[]{:S(2)}, u32[]{:S(2)}) async-start(s16[32,264,128]{2,1,0:T(8,128)(2,1)} %bitcast.12), calls=%async_computation.1 | async-start | bytes 4325376 | tf_op jit(solution)/shard_map/all_to_all | solution.py:311
  78.6 47.6 %all-gather.3.cloned.1.call-done.refs_0_ = bf16[4096,512]{1,0:T(8,128)(2,1)} async-done(((bf16[512,512]{1,0:T(8,128)(2,1)}), bf16[4096,512]{1,0:T(8,128)(2,1)}) %all-gather.3.cloned.1.call-update) | async-done | bytes 4194320 | tf_op jit(solution)/shard_map/all_gather | solution.py:323
  126.2 17.5 %ladder.2 = (f32[2,2048,256]{2,1,0:T(8,128)}, s16[8,4,264,128]{3,2,1,0:T(8,128)(2,1)}) custom-call(s32[8,4]{1,0:T(8,128)} %copy.9.amp_mask, s32[8]{0:T(128)} %numbers.3, bf16[2048,4096]{1,0:T(8,128)(2,1)} %rows_ref.3, bf16[4096,512]{1,0:T(8,128)(2,1)} %all-gather.3.cloned.1.call-done.refs_0_), custom_call_target="tpu_custom_call" | custom-call | flops 8589934592 | bytes 27262976 | tf_op jit(solution)/shard_map/ladder/pallas_call | solution.py:191
  143.7 0.0 copy-start.2
  143.7 0.0 copy-start.3
  143.7 2.5 %all-to-all-done.1 = s16[32,264,128]{2,1,0:T(8,128)(2,1)S(1)} async-done(((s16[32,264,128]{2,1,0:T(8,128)(2,1)}), s16[32,264,128]{2,1,0:T(8,128)(2,1)S(1)}, u32[]{:S(2)}, u32[]{:S(2)}) %all-to-all-start.1) | async-done | bytes 2162720 | tf_op jit(solution)/shard_map/all_to_all | solution.py:311
  146.2 0.0 copy-start
  146.2 3.6 %all-to-all-start = ((s16[32,264,128]{2,1,0:T(8,128)(2,1)}), s16[32,264,128]{2,1,0:T(8,128)(2,1)}, u32[]{:S(2)}, u32[]{:S(2)}) async-start(s16[32,264,128]{2,1,0:T(8,128)(2,1)} %bitcast.11), calls=%async_computation | async-start | bytes 4325376 | tf_op jit(solution)/shard_map/all_to_all | solution.py:311
  149.8 0.0 copy-done.2
  149.8 0.1 reshape.122
  149.9 0.0 copy-done.3
  149.9 0.1 dynamic_slice.6
  150.0 0.1 broadcast_add_fusion.1
  150.0 0.7 add.167.vir_ref
  150.7 0.1 broadcast_add_fusion
  150.8 0.1 add.173
  150.9 0.9 fusion.1.spread_ref
  151.9 1.0 fusion.spread_ref
  152.9 6.1 %direct.3.refs_4_ = f32[2048,512]{1,0:T(8,128)} custom-call(bf16[512,512]{1,0:T(8,128)(2,1)} %fusion.1.spread_ref, f32[2,2048,256]{2,1,0:T(8,128)} %get-tuple-element.16.refs_0_, f32[2,2048,256]{2,1,0:T(8,128)} %get-tuple-element.17.refs_1_), custom_call_target="tpu_custom_call" | custom-call | flops 2147483648 | bytes 8388608 | tf_op jit(solution)/shard_map/direct/pallas_call | solution.py:231
  159.0 0.0 copy-done
  159.0 6.4 %direct.2.refs_4_.refs_5_.refs_6_.refs_7_ = f32[2048,512]{1,0:T(8,128)} custom-call(bf16[512,512]{1,0:T(8,128)(2,1)} %fusion.1.spread_ref, f32[2,2048,256]{2,1,0:T(8,128)} %get-tuple-element.16.refs_0_, f32[2,2048,256]{2,1,0:T(8,128)} %get-tuple-element.17.refs_1_), custom_call_target="tpu_custom_call" | custom-call | flops 2147483648 | bytes 8388608 | tf_op jit(solution)/shard_map/direct/pallas_call | solution.py:231
  165.4 1.3 broadcast_in_dim.2.occ_ref
  166.7 9.0 %update.2.refs_8_ = f32[2048,1024]{1,0:T(8,128)} custom-call(bf16[512,512]{1,0:T(8,128)(2,1)} %fusion.spread_ref, f32[1,1024]{1,0:T(1,128)} %add.167.vir_ref, f32[2048,128]{1,0:T(8,128)} %broadcast_in_dim.2.occ_ref, s16[8,4,264,128]{3,2,1,0:T(8,128)(2,1)} %bitcast.7, s16[8,4,264,128]{3,2,1,0:T(8,128)(2,1)} %bitcast.8, s16[8,4,264,128]{3,2,1,0:T(8,128)(2,1)} %bitcast.9, ...), custom_call_target="tpu_custom_call" | custom-call | flops 2147483648 | bytes 10485760 | tf_op jit(solution)/shard_map/update/pallas_call | solution.py:283
  175.7 24.2 %all-to-all-done = s16[32,264,128]{2,1,0:T(8,128)(2,1)} async-done(((s16[32,264,128]{2,1,0:T(8,128)(2,1)}), s16[32,264,128]{2,1,0:T(8,128)(2,1)}, u32[]{:S(2)}, u32[]{:S(2)}) %all-to-all-start) | async-done | bytes 2162720 | tf_op jit(solution)/shard_map/all_to_all | solution.py:311
  199.9 6.3 %update.3 = f32[2048,1024]{1,0:T(8,128)} custom-call(bf16[512,512]{1,0:T(8,128)(2,1)} %fusion.spread_ref, f32[1,1024]{1,0:T(1,128)} %add.167.vir_ref, f32[2048,128]{1,0:T(8,128)} %broadcast_in_dim.2.occ_ref, s16[8,4,264,128]{3,2,1,0:T(8,128)(2,1)} %bitcast.3.refs_0_.refs_1_.refs_2_.refs_3_, ...), custom_call_target="tpu_custom_call", output_to_operand_aliasing={{}: (11, {})} | custom-call | flops 2147483648 | bytes 10485760 | tf_op jit(solution)/shard_map/update/pallas_call | solution.py:283
  (4 shorter events, 0.0 us)
Async XLA Ops:
  6.5 46.3 %copy-start.1 = (s32[1,8,4]{1,2,0:T(4,128)S(1)}, s32[1,8,4]{1,2,0:T(4,128)}, u32[]{:S(2)}) copy-start(s32[1,8,4]{1,2,0:T(4,128)} %param.8) | copy-start | bytes 388
  6.5 119.6 %all-gather.3.cloned.1.call-start = ((), (), s32[]{:S(2)}) async-start(), calls=%async_computation.2 | async-start | bytes 4718592 | tf_op jit(solution)/shard_map/all_gather | solution.py:323
  72.6 73.6 %all-to-all-start.1 = ((s16[32,264,128]{2,1,0:T(8,128)(2,1)}), s16[32,264,128]{2,1,0:T(8,128)(2,1)S(1)}, u32[]{:S(2)}, u32[]{:S(2)}) async-start(s16[32,264,128]{2,1,0:T(8,128)(2,1)} %bitcast.12), calls=%async_computation.1 | async-start | bytes 4325376 | tf_op jit(solution)/shard_map/all_to_all | solution.py:311
  143.7 6.2 %copy-start.2 = (f32[128]{0:T(128)S(1)}, f32[128]{0:T(128)}, u32[]{:S(2)}) copy-start(f32[128]{0:T(128)} %param.12) | copy-start | bytes 1540
  143.7 6.2 %copy-start.3 = (f32[64]{0:T(128)S(1)}, f32[64]{0:T(128)}, u32[]{:S(2)}) copy-start(f32[64]{0:T(128)} %param.13) | copy-start | bytes 772
  146.2 12.8 %copy-start = (s16[32,264,128]{2,1,0:T(8,128)(2,1)}, s16[32,264,128]{2,1,0:T(8,128)(2,1)S(1)}, u32[]{:S(2)}) copy-start(s16[32,264,128]{2,1,0:T(8,128)(2,1)S(1)} %all-to-all-done.1) | copy-start | bytes 6488068
  146.2 53.7 %all-to-all-start = ((s16[32,264,128]{2,1,0:T(8,128)(2,1)}), s16[32,264,128]{2,1,0:T(8,128)(2,1)}, u32[]{:S(2)}, u32[]{:S(2)}) async-start(s16[32,264,128]{2,1,0:T(8,128)(2,1)} %bitcast.11), calls=%async_computation | async-start | bytes 4325376 | tf_op jit(solution)/shard_map/all_to_all | solution.py:311
Sparse Core Ops, SparseCore 0:
  52.9 73.1 all-gather.2

commit v13 on v12

--- a/solution.py
+++ b/solution.py
@@ -15,11 +15,12 @@
 CODE_ROWS = 16
 EXCHANGE_CODE_ROWS = 8
 CODED_PARTS = 1
-AT_ONCE = 2
+AT_ONCE = 4
 SLAB_BITS = 14.0
 TOP = 32700.0
 STEPS = 8.0
 VMEM_LIMIT = 56 * 1024 * 1024
+LADDER_VMEM_LIMIT = 30 * 1024 * 1024
 
 
 def one_hot_of(target, amount):
@@ -116,20 +117,42 @@
     lax.fori_loop(0, tile_total, decode, 0)
 
 
-def ladder_kernel(tile_total, vir_count, chunks, tiles, dot_cols, coded, amp_mask, numbers, rows_ref, *refs):
+def ladder_kernel(tile_total, vir_count, chunks, tiles, dot_cols, coded, amp_mask, numbers, all_rows_ref, *refs):
     slab_refs, refs = (refs[:CODED_PARTS], refs[CODED_PARTS:]) if coded else (refs[:1], refs[1:])
-    ladder_ref, packed_ref, product = refs[:3]
+    ladder_ref, packed_ref, product, rows_scr, rows_sems = refs[:5]
     step = pl.program_id(0)
     slab_ref = slab_refs[0]
     if coded:
-        stage, slab_ref, sems = refs[3:]
+        stage, slab_ref, sems = refs[5:]
+    steps = tile_total // tiles
+
+    def rows_copy(at_step):
+        at = pl.ds(pl.multiple_of(at_step * (tiles * PAIR_SQ), PAIR_SQ), tiles * PAIR_SQ)
+        slot = lax.rem(at_step, 2)
+        return pltpu.make_async_copy(all_rows_ref.at[at, :], rows_scr.at[slot], rows_sems.at[slot])
+
+    @pl.when(step == 0)
+    def _():
+        rows_copy(0).start()
+
+    @pl.when(step + 1 < steps)
+    def _():
+        rows_copy(step + 1).start()
+
+    if coded:
 
         @pl.when(step == 0)
         def _():
             decode_slab(tile_total, slab_refs, stage, slab_ref, sems)
+
+    @pl.when(step < steps)
+    def _():
+        rows_copy(step).wait()
+
     cols = slab_ref.shape[1]
     block = cols // vir_count
     lanes = block // chunks
+    rows_ref = rows_scr.at[lax.rem(jnp.minimum(step, steps - 1), 2)]
 
     pair = lax.broadcasted_iota(jnp.int32, (PAIR_SQ, 1), 0)
     own_number = numbers[lax.axis_index("occ")]
@@ -177,7 +200,11 @@
     smem = pl.BlockSpec(memory_space=pltpu.SMEM)
     rows = tile_total * PAIR_SQ
     steps = tile_total // tiles
-    scratch = [pltpu.VMEM((tiles * PAIR_SQ, cols), jnp.float32)]
+    scratch = [
+        pltpu.VMEM((tiles * PAIR_SQ, cols), jnp.float32),
+        pltpu.VMEM((2, tiles * PAIR_SQ, W * W), jnp.bfloat16),
+        pltpu.SemaphoreType.DMA((2,)),
+    ]
     slab_specs = [pl.BlockSpec((W * W, cols), lambda step: (0, 0))]
     if coded:
         slab_specs = [pl.BlockSpec(memory_space=pl.ANY)] * CODED_PARTS
@@ -194,7 +221,7 @@
         in_specs=[
             smem,
             smem,
-            pl.BlockSpec((tiles * PAIR_SQ, W * W), lambda step: (jnp.minimum(step, steps - 1), 0)),
+            pl.BlockSpec(memory_space=pl.ANY),
             *slab_specs,
         ],
         out_specs=[
@@ -206,7 +233,7 @@
             jax.ShapeDtypeStruct((tile_total,) + packed_block, jnp.int16),
         ],
         scratch_shapes=scratch,
-        compiler_params=pltpu.CompilerParams(vmem_limit_bytes=VMEM_LIMIT),
+        compiler_params=pltpu.CompilerParams(vmem_limit_bytes=LADDER_VMEM_LIMIT),
         cost_estimate=pl.CostEstimate(
             flops=2 * rows * cols * W * W,
             bytes_accessed=rows * (W * W * 2 + cols * 6) + W * W * cols * 2,
@@ -323,7 +350,7 @@
         slabs.append([lax.all_gather(part, "occ", axis=0, tiled=True)])
     ladders, arrived = [], []
     for slab in slabs:
-        tiles, dot_cols = (2, 512) if ladders else (1, 256)
+        tiles, dot_cols = (1, 512)
         ladder, packed = ladder_call(
             tile_total, vir_count, chunks, tiles, dot_cols, amp_mask[0], group_orbital_numbers, amplitudes, slab
         )
@@ -350,7 +377,7 @@
     update = None
     for chunk in range(chunks):
         direct = direct_call(chunk, direct_spread, ladders)
-        update = update_call(chunk, chunks, 4 if chunk else 1, arrived[chunk], mirror_spread, vir_sum, occ_sum, direct, update)
+        update = update_call(chunk, chunks, 4, arrived[chunk], mirror_spread, vir_sum, occ_sum, direct, update)
     return update
 
 

time: 214 us -> 215 us (level)
  Pallas kernels: 68.1 us -> 59.8 us
  local copies, waits for them, and re-layouts: 2.92 us -> 10.7 us
    unnamed x8 -> x18, local copies, waits for them, and re-layouts: 0.01 us -> 8.42 us
    all_to_all x2, waiting for transfers between devices: 26.7 us -> 31 us  [exchanged(): lax.all_to_all(packed.reshape(tile_total * vir_count, rows, block), ('occ...]
    pallas_call x2, Pallas kernels: 36.6 us -> 32.5 us  [ladder_call(): pl.pallas_call(functools.partial(ladder_kernel, tile_total, vir_count, ch...]
    all_gather x1, waiting for transfers between devices: 47.6 us -> 43.7 us  [body(): slabs.append([lax.all_gather(part, 'occ', axis=0, tiled=True)])]
    pallas_call x2, Pallas kernels: 15.3 us -> 12.6 us  [update_call(): pl.pallas_call(functools.partial(update_kernel, vir_count, at_once), grid...]
  transfers between devices with their start and end apart: 3 -> 3, of which waited for: 3 -> 3; matrix products, arithmetic and copies ran while one was open for 2% -> 2% of each run, Pallas kernels for 27% -> 23%
where the time goes in v13:
time: 215 us; the launch traced here: 214 us
  waiting for transfers between devices  74.8 us (35%)
  Pallas kernels  59.8 us (28%)
  blocking collectives  42.6 us (20%)
  between operations  13.5 us (6%)
  local copies, waits for them, and re-layouts  10.7 us (5%)
  starting transfers between devices  10.3 us (5%)
    all_gather x1, waiting for transfers between devices, body(): slabs.append([lax.all_gather(part, 'occ', axis=0, tiled=True)])  43.7 us
    all_gather x1, blocking collectives, body(): first = lax.all_gather(coded[0], 'occ', axis=0, tiled=True)  42.6 us
    pallas_call x2, Pallas kernels, ladder_call(): pl.pallas_call(functools.partial(ladder_kernel, tile_total, vir_count, ch...  32.5 us
    all_to_all x2, waiting for transfers between devices, exchanged(): lax.all_to_all(packed.reshape(tile_total * vir_count, rows, block), ('occ...  31 us
    pallas_call x2, Pallas kernels, update_call(): pl.pallas_call(functools.partial(update_kernel, vir_count, at_once), grid...  12.6 us
    pallas_call x2, Pallas kernels, direct_call(): pl.pallas_call(direct_kernel, grid=(rows // step_rows,), in_specs=[pl.Blo...  11 us
    all_to_all x2, starting transfers between devices, exchanged(): lax.all_to_all(packed.reshape(tile_total * vir_count, rows, block), ('occ...  10.3 us
    unnamed x18, local copies, waits for them, and re-layouts  8.42 us
  transfers between devices with their start and end apart: 3, of which 3 were waited for; matrix products, arithmetic and copies ran while one was open for 2% of the time, Pallas kernels for 23%

profile of v13, /device:TPU:0, one launch (start us, length us, event | category | flops | bytes accessed | tf_op | source)
XLA Modules:
  0.0 213.8 jit_solution(9414683014374644156)
XLA Ops:
  6.5 0.0 copy-start.6
  6.5 0.0 copy-start.4
  6.5 0.0 all-gather.3.cloned.1.call-start
  6.5 3.7 %screen.1 = (s16[528,512]{1,0:T(8,128)(2,1)}, bf16[512,512]{1,0:T(8,128)(2,1)}) custom-call(s32[4,4]{1,0:T(4,128)} %int_mask.1, bf16[512,1024]{1,0:T(8,128)(2,1)} %slab_ref.1), custom_call_target="tpu_custom_call" | custom-call | tf_op jit(solution)/shard_map/screen/pallas_call | solution.py:83
  10.2 42.6 %all-gather.4.refs_0_ = s16[4224,512]{1,0:T(8,128)(2,1)} all-gather(s16[528,512]{1,0:T(8,128)(2,1)} %get-tuple-element.13), channel_id=1, replica_groups=mesh['occ'=8,'vir'=4] {'occ'}, dimensions={0}, use_global_device_ids=true | all-gather | bytes 4866048 | tf_op jit(solution)/shard_map/all_gather | solution.py:345
  52.8 0.0 all-gather.3.cloned.1.call-update
  52.9 0.0 copy-done.6
  52.9 0.1 copy.9.amp_mask
  52.9 0.0 copy-done.4
  52.9 0.0 copy-start.2
  53.0 2.2 %copy-done.2 = s16[4224,512]{1,0:T(8,128)(2,1)S(1)} copy-done((s16[4224,512]{1,0:T(8,128)(2,1)S(1)}, s16[4224,512]{1,0:T(8,128)(2,1)}, u32[]{:S(2)}) %copy-start.2) | copy-done | bytes 4325400
  55.2 16.4 %ladder.3 = (f32[2,2048,256]{2,1,0:T(8,128)S(1)}, s16[8,4,264,128]{3,2,1,0:T(8,128)(2,1)}) custom-call(s32[8,4]{1,0:T(8,128)S(1)} %copy.9.amp_mask, s32[8]{0:T(128)S(1)} %copy-done.4, bf16[2048,4096]{1,0:T(8,128)(2,1)} %all_rows_ref.3, s16[4224,512]{1,0:T(8,128)(2,1)S(1)} %copy-done.2), custom_call_target="tpu_custom_call" | custom-call | flops 8589934592 | bytes 27262976 | tf_op jit(solution)/shard_map/ladder/pallas_call | solution.py:218
  71.6 0.0 copy-start
  71.6 2.0 copy-done
  73.6 6.1 %all-to-all-start.1 = ((s16[32,264,128]{2,1,0:T(8,128)(2,1)}), s16[32,264,128]{2,1,0:T(8,128)(2,1)S(1)}, u32[]{:S(2)}, u32[]{:S(2)}) async-start(s16[32,264,128]{2,1,0:T(8,128)(2,1)} %bitcast.4), calls=%async_computation.1 | async-start | bytes 4325376 | tf_op jit(solution)/shard_map/all_to_all | solution.py:338
  79.7 43.7 %all-gather.3.cloned.1.call-done.refs_0_ = bf16[4096,512]{1,0:T(8,128)(2,1)} async-done(((bf16[512,512]{1,0:T(8,128)(2,1)}), bf16[4096,512]{1,0:T(8,128)(2,1)}) %all-gather.3.cloned.1.call-update) | async-done | bytes 4194320 | tf_op jit(solution)/shard_map/all_gather | solution.py:350
  123.4 0.0 copy-start.3
  123.4 2.2 %copy-done.3 = bf16[4096,512]{1,0:T(8,128)(2,1)S(1)} copy-done((bf16[4096,512]{1,0:T(8,128)(2,1)S(1)}, bf16[4096,512]{1,0:T(8,128)(2,1)}, u32[]{:S(2)}) %copy-start.3) | copy-done | bytes 4194328
  125.6 16.1 %ladder.2 = (f32[2,2048,256]{2,1,0:T(8,128)S(1)}, s16[8,4,264,128]{3,2,1,0:T(8,128)(2,1)}) custom-call(s32[8,4]{1,0:T(8,128)S(1)} %copy.9.amp_mask, s32[8]{0:T(128)S(1)} %copy-done.4, bf16[2048,4096]{1,0:T(8,128)(2,1)} %all_rows_ref.3, bf16[4096,512]{1,0:T(8,128)(2,1)S(1)} %copy-done.3), custom_call_target="tpu_custom_call" | custom-call | flops 8589934592 | bytes 27262976 | tf_op jit(solution)/shard_map/ladder/pallas_call | solution.py:218
  141.7 0.0 copy-start.1
  141.7 2.0 copy-done.1
  143.7 0.0 copy-start.7
  143.7 0.0 copy-start.8
  143.7 2.6 %all-to-all-done.1 = s16[32,264,128]{2,1,0:T(8,128)(2,1)S(1)} async-done(((s16[32,264,128]{2,1,0:T(8,128)(2,1)}), s16[32,264,128]{2,1,0:T(8,128)(2,1)S(1)}, u32[]{:S(2)}, u32[]{:S(2)}) %all-to-all-start.1) | async-done | bytes 2162720 | tf_op jit(solution)/shard_map/all_to_all | solution.py:338
  146.3 0.0 copy-start.5
  146.3 4.2 %all-to-all-start = ((s16[32,264,128]{2,1,0:T(8,128)(2,1)}), s16[32,264,128]{2,1,0:T(8,128)(2,1)}, u32[]{:S(2)}, u32[]{:S(2)}) async-start(s16[32,264,128]{2,1,0:T(8,128)(2,1)} %bitcast.2), calls=%async_computation | async-start | bytes 4325376 | tf_op jit(solution)/shard_map/all_to_all | solution.py:338
  150.5 0.0 copy-done.7
  150.5 0.1 reshape.122
  150.6 0.0 copy-done.8
  150.6 0.1 dynamic_slice.6
  150.6 0.1 broadcast_add_fusion.1
  150.7 0.7 add.167.vir_ref
  151.4 0.1 broadcast_add_fusion
  151.5 0.1 add.173
  151.6 0.9 fusion.1.spread_ref
  152.5 1.0 fusion.spread_ref
  153.5 5.5 %direct.3.refs_4_.refs_5_.refs_6_.refs_7_ = f32[2048,512]{1,0:T(8,128)} custom-call(bf16[512,512]{1,0:T(8,128)(2,1)} %fusion.1.spread_ref, f32[2,2048,256]{2,1,0:T(8,128)} %copy-done, f32[2,2048,256]{2,1,0:T(8,128)} %copy-done.1), custom_call_target="tpu_custom_call" | custom-call | flops 2147483648 | bytes 8388608 | tf_op jit(solution)/shard_map/direct/pallas_call | solution.py:258
  159.0 0.0 copy-done.5
  159.0 5.5 %direct.2.refs_4_.refs_5_.refs_6_.refs_7_ = f32[2048,512]{1,0:T(8,128)} custom-call(bf16[512,512]{1,0:T(8,128)(2,1)} %fusion.1.spread_ref, f32[2,2048,256]{2,1,0:T(8,128)} %copy-done, f32[2,2048,256]{2,1,0:T(8,128)} %copy-done.1), custom_call_target="tpu_custom_call" | custom-call | flops 2147483648 | bytes 8388608 | tf_op jit(solution)/shard_map/direct/pallas_call | solution.py:258
  164.5 1.3 broadcast_in_dim.2.occ_ref
  165.8 6.3 %update.2.refs_8_ = f32[2048,1024]{1,0:T(8,128)} custom-call(bf16[512,512]{1,0:T(8,128)(2,1)} %fusion.spread_ref, f32[1,1024]{1,0:T(1,128)} %add.167.vir_ref, f32[2048,128]{1,0:T(8,128)} %broadcast_in_dim.2.occ_ref, s16[8,4,264,128]{3,2,1,0:T(8,128)(2,1)} %bitcast.7, s16[8,4,264,128]{3,2,1,0:T(8,128)(2,1)} %bitcast.8, s16[8,4,264,128]{3,2,1,0:T(8,128)(2,1)} %bitcast.9, ...), custom_call_target="tpu_custom_call" | custom-call | flops 2147483648 | bytes 10485760 | tf_op jit(solution)/shard_map/update/pallas_call | solution.py:310
  172.1 28.5 %all-to-all-done = s16[32,264,128]{2,1,0:T(8,128)(2,1)} async-done(((s16[32,264,128]{2,1,0:T(8,128)(2,1)}), s16[32,264,128]{2,1,0:T(8,128)(2,1)}, u32[]{:S(2)}, u32[]{:S(2)}) %all-to-all-start) | async-done | bytes 2162720 | tf_op jit(solution)/shard_map/all_to_all | solution.py:338
  200.6 6.3 %update.3 = f32[2048,1024]{1,0:T(8,128)} custom-call(bf16[512,512]{1,0:T(8,128)(2,1)} %fusion.spread_ref, f32[1,1024]{1,0:T(1,128)} %add.167.vir_ref, f32[2048,128]{1,0:T(8,128)} %broadcast_in_dim.2.occ_ref, s16[8,4,264,128]{3,2,1,0:T(8,128)(2,1)} %bitcast.3.refs_0_.refs_1_.refs_2_.refs_3_, ...), custom_call_target="tpu_custom_call", output_to_operand_aliasing={{}: (11, {})} | custom-call | flops 2147483648 | bytes 10485760 | tf_op jit(solution)/shard_map/update/pallas_call | solution.py:310
  (4 shorter events, 0.0 us)
Async XLA Ops:
  6.5 46.3 %copy-start.6 = (s32[1,8,4]{1,2,0:T(4,128)S(1)}, s32[1,8,4]{1,2,0:T(4,128)}, u32[]{:S(2)}) copy-start(s32[1,8,4]{1,2,0:T(4,128)} %param.8) | copy-start | bytes 388
  6.5 46.4 %copy-start.4 = (s32[8]{0:T(128)S(1)}, s32[8]{0:T(128)}, u32[]{:S(2)}) copy-start(s32[8]{0:T(128)} %numbers.3) | copy-start | bytes 100
  6.5 116.8 %all-gather.3.cloned.1.call-start = ((), (), s32[]{:S(2)}) async-start(), calls=%async_computation.2 | async-start | bytes 4718592 | tf_op jit(solution)/shard_map/all_gather | solution.py:350
  52.9 2.2 %copy-start.2 = (s16[4224,512]{1,0:T(8,128)(2,1)S(1)}, s16[4224,512]{1,0:T(8,128)(2,1)}, u32[]{:S(2)}) copy-start(s16[4224,512]{1,0:T(8,128)(2,1)} %all-gather.4.refs_0_) | copy-start | bytes 12976132
  71.6 2.0 copy-start
  73.6 72.7 %all-to-all-start.1 = ((s16[32,264,128]{2,1,0:T(8,128)(2,1)}), s16[32,264,128]{2,1,0:T(8,128)(2,1)S(1)}, u32[]{:S(2)}, u32[]{:S(2)}) async-start(s16[32,264,128]{2,1,0:T(8,128)(2,1)} %bitcast.4), calls=%async_computation.1 | async-start | bytes 4325376 | tf_op jit(solution)/shard_map/all_to_all | solution.py:338
  123.4 2.2 %copy-start.3 = (bf16[4096,512]{1,0:T(8,128)(2,1)S(1)}, bf16[4096,512]{1,0:T(8,128)(2,1)}, u32[]{:S(2)}) copy-start(bf16[4096,512]{1,0:T(8,128)(2,1)} %all-gather.3.cloned.1.call-done.refs_0_) | copy-start | bytes 12582916
  141.7 2.0 copy-start.1
  143.7 6.8 %copy-start.7 = (f32[128]{0:T(128)S(1)}, f32[128]{0:T(128)}, u32[]{:S(2)}) copy-start(f32[128]{0:T(128)} %param.12) | copy-start | bytes 1540
  143.7 6.9 %copy-start.8 = (f32[64]{0:T(128)S(1)}, f32[64]{0:T(128)}, u32[]{:S(2)}) copy-start(f32[64]{0:T(128)} %param.13) | copy-start | bytes 772
  146.3 12.8 %copy-start.5 = (s16[32,264,128]{2,1,0:T(8,128)(2,1)}, s16[32,264,128]{2,1,0:T(8,128)(2,1)S(1)}, u32[]{:S(2)}) copy-start(s16[32,264,128]{2,1,0:T(8,128)(2,1)S(1)} %all-to-all-done.1) | copy-start | bytes 6488068
  146.3 54.3 %all-to-all-start = ((s16[32,264,128]{2,1,0:T(8,128)(2,1)}), s16[32,264,128]{2,1,0:T(8,128)(2,1)}, u32[]{:S(2)}, u32[]{:S(2)}) async-start(s16[32,264,128]{2,1,0:T(8,128)(2,1)} %bitcast.2), calls=%async_computation | async-start | bytes 4325376 | tf_op jit(solution)/shard_map/all_to_all | solution.py:338
Sparse Core Ops, SparseCore 0:
  53.0 70.3 all-gather.2

commit v14 on v12

--- a/solution.py
+++ b/solution.py
@@ -14,8 +14,7 @@
 PAIR_SQ = ORBITALS_IN_GRP * ORBITALS_IN_GRP
 CODE_ROWS = 16
 EXCHANGE_CODE_ROWS = 8
-CODED_PARTS = 1
-AT_ONCE = 2
+AT_ONCE = 4
 SLAB_BITS = 14.0
 TOP = 32700.0
 STEPS = 8.0
@@ -39,11 +38,9 @@
     return jnp.exp2(code * (1.0 / STEPS))
 
 
-def screen_kernel(part, int_mask, slab_ref, *refs):
-    coded_refs, later_refs = refs[:CODED_PARTS], refs[CODED_PARTS:]
+def screen_kernel(part, int_mask, slab_ref, coded_ref, *later_refs):
     slab_rows, slab_cols = slab_ref.shape
-    coded_cols = coded_refs[0].shape[1]
-    cols = coded_cols * CODED_PARTS
+    cols = coded_ref.shape[1]
     span = slab_cols // W
     row_label = lax.axis_index("occ") * slab_rows // W // VT * NVT
     col_label = lax.axis_index("vir") * slab_cols // W // VT * NVT
@@ -69,10 +66,8 @@
             code = jnp.floor(jnp.log2(most)) + 1.0
             coded = jnp.round(moved * jnp.exp2(SLAB_BITS - code)).astype(jnp.int32).astype(jnp.int16)
             code_rows = jnp.broadcast_to(code.astype(jnp.int32), (CODE_ROWS, cols)).astype(jnp.int16)
-            for n, coded_ref in enumerate(coded_refs):
-                at = slice(n * coded_cols, (n + 1) * coded_cols)
-                coded_ref[:slab_rows, :] = coded[:, at]
-                coded_ref[slab_rows:, :] = code_rows[:, at]
+            coded_ref[:slab_rows, :] = coded
+            coded_ref[slab_rows:, :] = code_rows
 
 
 def screen_call(chunks, int_mask, integrals):
@@ -82,64 +77,42 @@
     return pl.pallas_call(
         functools.partial(screen_kernel, slab_cols // W // chunks),
         in_specs=[pl.BlockSpec(memory_space=pltpu.SMEM), vmem],
-        out_specs=[vmem] * (CODED_PARTS + chunks - 1),
-        out_shape=[jax.ShapeDtypeStruct((slab_rows + CODE_ROWS, cols // CODED_PARTS), jnp.int16)] * CODED_PARTS
+        out_specs=[vmem] * chunks,
+        out_shape=[jax.ShapeDtypeStruct((slab_rows + CODE_ROWS, cols), jnp.int16)]
         + [jax.ShapeDtypeStruct((slab_rows, cols), integrals.dtype)] * (chunks - 1),
         compiler_params=pltpu.CompilerParams(vmem_limit_bytes=VMEM_LIMIT),
         name="screen",
     )(int_mask, integrals)
 
 
-def decode_slab(tile_total, coded_refs, stage, slab_scr, sems):
+def ladder_kernel(tile_total, vir_count, chunks, coded, amp_mask, numbers, rows_ref, gathered_ref, *refs):
+    ladder_ref, packed_ref, product, slab_scr, sems = refs[:5]
+    stage = refs[5] if coded else slab_scr
+    step = pl.program_id(0)
+    cols = slab_scr.shape[1]
     slab_rows = slab_scr.shape[0] // tile_total
-    coded_rows, cols = slab_rows + CODE_ROWS, coded_refs[0].shape[1]
-
-    def copy_of(part, tile):
-        at = pl.ds(pl.multiple_of(tile * coded_rows, CODE_ROWS), coded_rows)
-        return pltpu.make_async_copy(coded_refs[part].at[at, :], stage.at[part, at, :], sems.at[part, tile])
-
-    for tile in range(tile_total):
-        for part in range(CODED_PARTS):
-            copy_of(part, tile).start()
-
-    def decode(tile, carry):
-        at = pl.multiple_of(tile * coded_rows, CODE_ROWS)
-        to = pl.ds(pl.multiple_of(tile * slab_rows, slab_rows), slab_rows)
-        for part in range(CODED_PARTS):
-            copy_of(part, tile).wait()
-            code = stage[part, pl.ds(pl.multiple_of(at + slab_rows, CODE_ROWS), CODE_ROWS), :]
-            values = stage[part, pl.ds(at, slab_rows), :].astype(jnp.int32).astype(jnp.float32)
-            scale = jnp.exp2(code.astype(jnp.int32).astype(jnp.float32)[:1] - SLAB_BITS)
-            slab_scr[to, part * cols : (part + 1) * cols] = (values * scale).astype(jnp.bfloat16)
-        return carry
-
-    lax.fori_loop(0, tile_total, decode, 0)
-
-
-def ladder_kernel(tile_total, vir_count, chunks, tiles, dot_cols, coded, amp_mask, numbers, rows_ref, *refs):
-    slab_refs, refs = (refs[:CODED_PARTS], refs[CODED_PARTS:]) if coded else (refs[:1], refs[1:])
-    ladder_ref, packed_ref, product = refs[:3]
-    step = pl.program_id(0)
-    slab_ref = slab_refs[0]
-    if coded:
-        stage, slab_ref, sems = refs[3:]
-
-        @pl.when(step == 0)
-        def _():
-            decode_slab(tile_total, slab_refs, stage, slab_ref, sems)
-    cols = slab_ref.shape[1]
+    shard_rows = stage.shape[0] // tile_total
     block = cols // vir_count
     lanes = block // chunks
 
-    pair = lax.broadcasted_iota(jnp.int32, (PAIR_SQ, 1), 0)
-    own_number = numbers[lax.axis_index("occ")]
-    for n in range(tiles):
-        tile = jnp.maximum(step - 1, 0) * tiles + n
-        rows = slice(n * PAIR_SQ, (n + 1) * PAIR_SQ)
+    def masks(tile, at, width):
+        lane = lax.broadcasted_iota(jnp.int32, (1, width), 1) + at
+        left = lane % W < VT
+        keep = jnp.where(
+            lane < W * VT,
+            jnp.where(left, amp_mask[tile, 0], amp_mask[tile, 1]),
+            jnp.where(left, amp_mask[tile, 2], amp_mask[tile, 3]),
+        )
+        return keep.astype(jnp.float32).astype(jnp.bfloat16)
+
+    def finish():
+        tile = step - 1
+        pair = lax.broadcasted_iota(jnp.int32, (PAIR_SQ, 1), 0)
+        own_number = numbers[lax.axis_index("occ")]
         nonzero = (pair // ORBITALS_IN_GRP < own_number) & (pair % ORBITALS_IN_GRP < numbers[tile])
-        ladder = jnp.where(nonzero, product[rows, :], 0.0)
+        ladder = jnp.where(nonzero, product[...], 0.0)
         for h in range(chunks):
-            ladder_ref[h, rows, :] = jnp.concatenate(
+            ladder_ref[h] = jnp.concatenate(
                 [ladder[:, v * block + h * lanes : v * block + (h + 1) * lanes] for v in range(vir_count)], axis=1
             )
         by_place = ladder.reshape(ORBITALS_IN_GRP, ORBITALS_IN_GRP, cols)
@@ -149,63 +122,75 @@
         coded_rows = jnp.round(mirror * (TOP / scale_of(code))).astype(jnp.int32).astype(jnp.int16)
         code_rows = jnp.broadcast_to(code.astype(jnp.int32), (EXCHANGE_CODE_ROWS, cols)).astype(jnp.int16)
         for v in range(vir_count):
-            packed_ref[n, v, :PAIR_SQ] = coded_rows[:, v * block : (v + 1) * block]
-            packed_ref[n, v, PAIR_SQ:] = code_rows[:, v * block : (v + 1) * block]
-
-    lane = lax.broadcasted_iota(jnp.int32, (1, W * W), 1)
-    low = lane < W * VT
-    left = lane % W < VT
-    screened = []
-    for n in range(tiles):
-        tile = jnp.minimum(step * tiles + n, tile_total - 1)
-        keep = jnp.where(
-            low,
-            jnp.where(left, amp_mask[tile, 0], amp_mask[tile, 1]),
-            jnp.where(left, amp_mask[tile, 2], amp_mask[tile, 3]),
-        )
-        keep = keep.astype(jnp.float32).astype(jnp.bfloat16)
-        screened.append(rows_ref[n * PAIR_SQ : (n + 1) * PAIR_SQ, :] * keep)
-    screened = jnp.concatenate(screened, axis=0)
-    for at in range(0, cols, dot_cols):
-        product[:, at : at + dot_cols] = dot(screened, slab_ref[:, at : at + dot_cols])
-
-
-def ladder_call(tile_total, vir_count, chunks, tiles, dot_cols, amp_mask, numbers, amplitudes, slab):
-    coded = slab[0].dtype == jnp.int16
-    cols = sum(part.shape[1] for part in slab)
+            packed_ref[0, v, :PAIR_SQ] = coded_rows[:, v * block : (v + 1) * block]
+            packed_ref[0, v, PAIR_SQ:] = code_rows[:, v * block : (v + 1) * block]
+
+    @pl.when(step == 0)
+    def _():
+        def copy_of(shard):
+            at = pl.ds(pl.multiple_of(shard * shard_rows, CODE_ROWS), shard_rows)
+            return pltpu.make_async_copy(gathered_ref.at[at, :], stage.at[at, :], sems.at[shard])
+
+        for shard in range(tile_total):
+            copy_of(shard).start()
+        product[...] = jnp.zeros_like(product)
+
+        def use(shard, carry):
+            copy_of(shard).wait()
+            to = pl.ds(pl.multiple_of(shard * slab_rows, slab_rows), slab_rows)
+            if coded:
+                at = pl.multiple_of(shard * shard_rows, CODE_ROWS)
+                code = stage[pl.ds(pl.multiple_of(at + slab_rows, CODE_ROWS), CODE_ROWS), :]
+                values = stage[pl.ds(at, slab_rows), :].astype(jnp.int32).astype(jnp.float32)
+                scale = jnp.exp2(code.astype(jnp.int32).astype(jnp.float32)[:1] - SLAB_BITS)
+                slab_scr[to, :] = (values * scale).astype(jnp.bfloat16)
+            screened = rows_ref[:, to] * masks(0, shard * slab_rows, slab_rows)
+            product[...] += dot(screened, slab_scr[to, :])
+            return carry
+
+        lax.fori_loop(0, tile_total, use, 0)
+
+    @pl.when((step > 0) & (step < tile_total))
+    def _():
+        finish()
+        product[...] = dot(rows_ref[...] * masks(step, 0, W * W), slab_scr[...])
+
+    @pl.when(step == tile_total)
+    def _():
+        finish()
+
+
+def ladder_call(tile_total, vir_count, chunks, amp_mask, numbers, amplitudes, slab):
+    coded = slab.dtype == jnp.int16
+    cols = slab.shape[1]
     block = cols // vir_count
     smem = pl.BlockSpec(memory_space=pltpu.SMEM)
     rows = tile_total * PAIR_SQ
-    steps = tile_total // tiles
-    scratch = [pltpu.VMEM((tiles * PAIR_SQ, cols), jnp.float32)]
-    slab_specs = [pl.BlockSpec((W * W, cols), lambda step: (0, 0))]
-    if coded:
-        slab_specs = [pl.BlockSpec(memory_space=pl.ANY)] * CODED_PARTS
-        scratch += [
-            pltpu.VMEM((CODED_PARTS,) + slab[0].shape, slab[0].dtype),
-            pltpu.VMEM((W * W, cols), jnp.bfloat16),
-            pltpu.SemaphoreType.DMA((CODED_PARTS, tile_total)),
-        ]
     before = lambda step: jnp.maximum(step - 1, 0)
     packed_block = (vir_count, PAIR_SQ + EXCHANGE_CODE_ROWS, block)
     return pl.pallas_call(
-        functools.partial(ladder_kernel, tile_total, vir_count, chunks, tiles, min(dot_cols, cols), coded),
-        grid=(steps + 1,),
+        functools.partial(ladder_kernel, tile_total, vir_count, chunks, coded),
+        grid=(tile_total + 1,),
         in_specs=[
             smem,
             smem,
-            pl.BlockSpec((tiles * PAIR_SQ, W * W), lambda step: (jnp.minimum(step, steps - 1), 0)),
-            *slab_specs,
+            pl.BlockSpec((PAIR_SQ, W * W), lambda step: (jnp.minimum(step, tile_total - 1), 0)),
+            pl.BlockSpec(memory_space=pl.ANY),
         ],
         out_specs=[
-            pl.BlockSpec((chunks, tiles * PAIR_SQ, cols // chunks), lambda step: (0, before(step), 0)),
-            pl.BlockSpec((tiles,) + packed_block, lambda step: (before(step), 0, 0, 0)),
+            pl.BlockSpec((chunks, PAIR_SQ, cols // chunks), lambda step: (0, before(step), 0)),
+            pl.BlockSpec((1,) + packed_block, lambda step: (before(step), 0, 0, 0)),
         ],
         out_shape=[
             jax.ShapeDtypeStruct((chunks, rows, cols // chunks), jnp.float32),
             jax.ShapeDtypeStruct((tile_total,) + packed_block, jnp.int16),
         ],
-        scratch_shapes=scratch,
+        scratch_shapes=[
+            pltpu.VMEM((PAIR_SQ, cols), jnp.float32),
+            pltpu.VMEM((W * W, cols), jnp.bfloat16),
+            pltpu.SemaphoreType.DMA((tile_total,)),
+        ]
+        + [pltpu.VMEM(slab.shape, slab.dtype)] * coded,
         compiler_params=pltpu.CompilerParams(vmem_limit_bytes=VMEM_LIMIT),
         cost_estimate=pl.CostEstimate(
             flops=2 * rows * cols * W * W,
@@ -213,7 +198,7 @@
             transcendentals=0,
         ),
         name="ladder",
-    )(amp_mask, numbers, amplitudes, *slab)
+    )(amp_mask, numbers, amplitudes, slab)
 
 
 def moved_columns(values, spread_ref):
@@ -313,19 +298,15 @@
         )
         return moved.reshape(tile_total, vir_count, rows, block)
 
-    parts = screen_call(chunks, int_mask, integrals)
-    coded, later = parts[:CODED_PARTS], parts[CODED_PARTS:]
-    first = lax.all_gather(coded[0], "occ", axis=0, tiled=True)
-    *coded, first = lax.optimization_barrier((*coded[1:], first))
-    slabs = [[first] + [lax.all_gather(part, "occ", axis=0, tiled=True) for part in coded]]
+    coded, *later = screen_call(chunks, int_mask, integrals)
+    slabs = [lax.all_gather(coded, "occ", axis=0, tiled=True)]
     for part in later:
-        part, _ = lax.optimization_barrier((part, first))
-        slabs.append([lax.all_gather(part, "occ", axis=0, tiled=True)])
+        part, _ = lax.optimization_barrier((part, slabs[-1]))
+        slabs.append(lax.all_gather(part, "occ", axis=0, tiled=True))
     ladders, arrived = [], []
     for slab in slabs:
-        tiles, dot_cols = (2, 512) if ladders else (1, 256)
         ladder, packed = ladder_call(
-            tile_total, vir_count, chunks, tiles, dot_cols, amp_mask[0], group_orbital_numbers, amplitudes, slab
+            tile_total, vir_count, chunks, amp_mask[0], group_orbital_numbers, amplitudes, slab
         )
         ladders.append(ladder)
         arrived.append(exchanged(packed))
@@ -350,7 +331,7 @@
     update = None
     for chunk in range(chunks):
         direct = direct_call(chunk, direct_spread, ladders)
-        update = update_call(chunk, chunks, 4 if chunk else 1, arrived[chunk], mirror_spread, vir_sum, occ_sum, direct, update)
+        update = update_call(chunk, chunks, 4, arrived[chunk], mirror_spread, vir_sum, occ_sum, direct, update)
     return update
 
 

time: 214 us -> 214 us (level)
  waiting for transfers between devices: 74.3 us -> 78.9 us
  Pallas kernels: 68.1 us -> 63.6 us
    all_gather x1, waiting for transfers between devices: 47.6 us -> 50.6 us  [body(): slabs.append(lax.all_gather(part, 'occ', axis=0, tiled=True))]
    pallas_call x2, Pallas kernels: 15.3 us -> 12.6 us  [update_call(): pl.pallas_call(functools.partial(update_kernel, vir_count, at_once), grid...]
  transfers between devices with their start and end apart: 3 -> 3, of which waited for: 3 -> 2; matrix products, arithmetic and copies ran while one was open for 2% -> 2% of each run, Pallas kernels for 27% -> 25%
where the time goes in v14:
time: 214 us
  waiting for transfers between devices  78.9 us (37%)
  Pallas kernels  63.6 us (30%)
  blocking collectives  42.6 us (20%)
  between operations  13.5 us (6%)
  starting transfers between devices  10.1 us (5%)
  local copies, waits for them, and re-layouts  2.92 us (1%)
    all_gather x1, waiting for transfers between devices, body(): slabs.append(lax.all_gather(part, 'occ', axis=0, tiled=True))  50.6 us
    all_gather x1, blocking collectives, body(): slabs = [lax.all_gather(coded, 'occ', axis=0, tiled=True)]  42.6 us
    pallas_call x2, Pallas kernels, ladder_call(): pl.pallas_call(functools.partial(ladder_kernel, tile_total, vir_count, ch...  36.2 us
    all_to_all x2, waiting for transfers between devices, exchanged(): lax.all_to_all(packed.reshape(tile_total * vir_count, rows, block), ('occ...  28.3 us
    pallas_call x2, Pallas kernels, update_call(): pl.pallas_call(functools.partial(update_kernel, vir_count, at_once), grid...  12.6 us
    pallas_call x2, Pallas kernels, direct_call(): pl.pallas_call(direct_kernel, grid=(rows // step_rows,), in_specs=[pl.Blo...  11.2 us
    all_to_all x2, starting transfers between devices, exchanged(): lax.all_to_all(packed.reshape(tile_total * vir_count, rows, block), ('occ...  10.1 us
  transfers between devices with their start and end apart: 3, of which 2 were waited for; matrix products, arithmetic and copies ran while one was open for 2% of the time, Pallas kernels for 25%

profile of v14, /device:TPU:0, one launch (start us, length us, event | category | flops | bytes accessed | tf_op | source)
XLA Modules:
  0.0 213.7 jit_solution(14436096788705926887)
XLA Ops:
  6.5 0.0 copy-start.1
  6.5 0.0 all-gather.3.cloned.1.call-start
  6.5 3.7 %screen.1 = (s16[528,512]{1,0:T(8,128)(2,1)}, bf16[512,512]{1,0:T(8,128)(2,1)}) custom-call(s32[4,4]{1,0:T(4,128)} %int_mask.1, bf16[512,1024]{1,0:T(8,128)(2,1)} %slab_ref.1), custom_call_target="tpu_custom_call" | custom-call | tf_op jit(solution)/shard_map/screen/pallas_call | solution.py:77
  10.2 42.6 %all-gather.4.gathered_ref = s16[4224,512]{1,0:T(8,128)(2,1)} all-gather(s16[528,512]{1,0:T(8,128)(2,1)} %get-tuple-element.13), channel_id=1, replica_groups=mesh['occ'=8,'vir'=4] {'occ'}, dimensions={0}, use_global_device_ids=true | all-gather | bytes 4866048 | tf_op jit(solution)/shard_map/all_gather | solution.py:302
  52.8 0.0 all-gather.3.cloned.1.call-update
  52.8 0.0 copy-done.1
  52.8 0.7 copy.9.amp_mask
  53.5 18.5 %ladder.3 = (f32[2,2048,256]{2,1,0:T(8,128)}, s16[8,4,264,128]{3,2,1,0:T(8,128)(2,1)}) custom-call(s32[8,4]{1,0:T(8,128)} %copy.9.amp_mask, s32[8]{0:T(128)} %numbers.3, bf16[2048,4096]{1,0:T(8,128)(2,1)} %rows_ref.3, s16[4224,512]{1,0:T(8,128)(2,1)} %all-gather.4.gathered_ref), custom_call_target="tpu_custom_call" | custom-call | flops 8589934592 | bytes 27262976 | tf_op jit(solution)/shard_map/ladder/pallas_call | solution.py:171
  72.0 6.0 %all-to-all-start.1 = ((s16[32,264,128]{2,1,0:T(8,128)(2,1)}), s16[32,264,128]{2,1,0:T(8,128)(2,1)S(1)}, u32[]{:S(2)}, u32[]{:S(2)}) async-start(s16[32,264,128]{2,1,0:T(8,128)(2,1)} %bitcast.12), calls=%async_computation.1 | async-start | bytes 4325376 | tf_op jit(solution)/shard_map/all_to_all | solution.py:296
  78.0 50.6 %all-gather.3.cloned.1.call-done.gathered_ref = bf16[4096,512]{1,0:T(8,128)(2,1)} async-done(((bf16[512,512]{1,0:T(8,128)(2,1)}), bf16[4096,512]{1,0:T(8,128)(2,1)}) %all-gather.3.cloned.1.call-update) | async-done | bytes 4194320 | tf_op jit(solution)/shard_map/all_gather | solution.py:305
  128.6 17.7 %ladder.2 = (f32[2,2048,256]{2,1,0:T(8,128)}, s16[8,4,264,128]{3,2,1,0:T(8,128)(2,1)}) custom-call(s32[8,4]{1,0:T(8,128)} %copy.9.amp_mask, s32[8]{0:T(128)} %numbers.3, bf16[2048,4096]{1,0:T(8,128)(2,1)} %rows_ref.3, bf16[4096,512]{1,0:T(8,128)(2,1)} %all-gather.3.cloned.1.call-done.gathered_ref), custom_call_target="tpu_custom_call" | custom-call | flops 8589934592 | bytes 27262976 | tf_op jit(solution)/shard_map/ladder/pallas_call | solution.py:171
  146.3 0.0 copy-start.2
  146.3 0.0 copy-start.3
  146.4 0.0 all-to-all-done.1
  146.4 0.0 copy-start
  146.4 4.1 %all-to-all-start = ((s16[32,264,128]{2,1,0:T(8,128)(2,1)}), s16[32,264,128]{2,1,0:T(8,128)(2,1)}, u32[]{:S(2)}, u32[]{:S(2)}) async-start(s16[32,264,128]{2,1,0:T(8,128)(2,1)} %bitcast.11), calls=%async_computation | async-start | bytes 4325376 | tf_op jit(solution)/shard_map/all_to_all | solution.py:296
  150.5 0.0 copy-done.2
  150.5 0.1 reshape.122
  150.6 0.0 copy-done.3
  150.6 0.1 dynamic_slice.6
  150.6 0.1 broadcast_add_fusion.1
  150.7 0.7 add.167.vir_ref
  151.4 0.1 broadcast_add_fusion
  151.5 0.1 add.173
  151.6 0.9 fusion.1.spread_ref
  152.5 1.0 fusion.spread_ref
  153.5 5.5 %direct.3.refs_4_.refs_5_.refs_6_.refs_7_ = f32[2048,512]{1,0:T(8,128)} custom-call(bf16[512,512]{1,0:T(8,128)(2,1)} %fusion.1.spread_ref, f32[2,2048,256]{2,1,0:T(8,128)} %get-tuple-element.16.refs_0_, f32[2,2048,256]{2,1,0:T(8,128)} %get-tuple-element.17.refs_1_), custom_call_target="tpu_custom_call" | custom-call | flops 2147483648 | bytes 8388608 | tf_op jit(solution)/shard_map/direct/pallas_call | solution.py:216
  159.1 0.0 copy-done
  159.1 5.6 %direct.2.refs_4_.refs_5_.refs_6_.refs_7_ = f32[2048,512]{1,0:T(8,128)} custom-call(bf16[512,512]{1,0:T(8,128)(2,1)} %fusion.1.spread_ref, f32[2,2048,256]{2,1,0:T(8,128)} %get-tuple-element.16.refs_0_, f32[2,2048,256]{2,1,0:T(8,128)} %get-tuple-element.17.refs_1_), custom_call_target="tpu_custom_call" | custom-call | flops 2147483648 | bytes 8388608 | tf_op jit(solution)/shard_map/direct/pallas_call | solution.py:216
  164.7 1.3 broadcast_in_dim.2.occ_ref
  166.0 6.3 %update.2.refs_8_ = f32[2048,1024]{1,0:T(8,128)} custom-call(bf16[512,512]{1,0:T(8,128)(2,1)} %fusion.spread_ref, f32[1,1024]{1,0:T(1,128)} %add.167.vir_ref, f32[2048,128]{1,0:T(8,128)} %broadcast_in_dim.2.occ_ref, s16[8,4,264,128]{3,2,1,0:T(8,128)(2,1)} %bitcast.7, s16[8,4,264,128]{3,2,1,0:T(8,128)(2,1)} %bitcast.8, s16[8,4,264,128]{3,2,1,0:T(8,128)(2,1)} %bitcast.9, ...), custom_call_target="tpu_custom_call" | custom-call | flops 2147483648 | bytes 10485760 | tf_op jit(solution)/shard_map/update/pallas_call | solution.py:268
  172.3 28.3 %all-to-all-done = s16[32,264,128]{2,1,0:T(8,128)(2,1)} async-done(((s16[32,264,128]{2,1,0:T(8,128)(2,1)}), s16[32,264,128]{2,1,0:T(8,128)(2,1)}, u32[]{:S(2)}, u32[]{:S(2)}) %all-to-all-start) | async-done | bytes 2162720 | tf_op jit(solution)/shard_map/all_to_all | solution.py:296
  200.6 6.3 %update.3 = f32[2048,1024]{1,0:T(8,128)} custom-call(bf16[512,512]{1,0:T(8,128)(2,1)} %fusion.spread_ref, f32[1,1024]{1,0:T(1,128)} %add.167.vir_ref, f32[2048,128]{1,0:T(8,128)} %broadcast_in_dim.2.occ_ref, s16[8,4,264,128]{3,2,1,0:T(8,128)(2,1)} %bitcast.3.refs_0_.refs_1_.refs_2_.refs_3_, ...), custom_call_target="tpu_custom_call", output_to_operand_aliasing={{}: (11, {})} | custom-call | flops 2147483648 | bytes 10485760 | tf_op jit(solution)/shard_map/update/pallas_call | solution.py:268
  (4 shorter events, 0.0 us)
Async XLA Ops:
  6.5 46.3 %copy-start.1 = (s32[1,8,4]{1,2,0:T(4,128)S(1)}, s32[1,8,4]{1,2,0:T(4,128)}, u32[]{:S(2)}) copy-start(s32[1,8,4]{1,2,0:T(4,128)} %param.8) | copy-start | bytes 388
  6.5 122.1 %all-gather.3.cloned.1.call-start = ((), (), s32[]{:S(2)}) async-start(), calls=%async_computation.2 | async-start | bytes 4718592 | tf_op jit(solution)/shard_map/all_gather | solution.py:305
  72.0 74.3 %all-to-all-start.1 = ((s16[32,264,128]{2,1,0:T(8,128)(2,1)}), s16[32,264,128]{2,1,0:T(8,128)(2,1)S(1)}, u32[]{:S(2)}, u32[]{:S(2)}) async-start(s16[32,264,128]{2,1,0:T(8,128)(2,1)} %bitcast.12), calls=%async_computation.1 | async-start | bytes 4325376 | tf_op jit(solution)/shard_map/all_to_all | solution.py:296
  146.3 4.1 %copy-start.2 = (f32[128]{0:T(128)S(1)}, f32[128]{0:T(128)}, u32[]{:S(2)}) copy-start(f32[128]{0:T(128)} %param.12) | copy-start | bytes 1540
  146.3 4.2 %copy-start.3 = (f32[64]{0:T(128)S(1)}, f32[64]{0:T(128)}, u32[]{:S(2)}) copy-start(f32[64]{0:T(128)} %param.13) | copy-start | bytes 772
  146.4 12.7 %copy-start = (s16[32,264,128]{2,1,0:T(8,128)(2,1)}, s16[32,264,128]{2,1,0:T(8,128)(2,1)S(1)}, u32[]{:S(2)}) copy-start(s16[32,264,128]{2,1,0:T(8,128)(2,1)S(1)} %all-to-all-done.1) | copy-start | bytes 6488068
  146.4 54.2 %all-to-all-start = ((s16[32,264,128]{2,1,0:T(8,128)(2,1)}), s16[32,264,128]{2,1,0:T(8,128)(2,1)}, u32[]{:S(2)}, u32[]{:S(2)}) async-start(s16[32,264,128]{2,1,0:T(8,128)(2,1)} %bitcast.11), calls=%async_computation | async-start | bytes 4325376 | tf_op jit(solution)/shard_map/all_to_all | solution.py:296
Sparse Core Ops, SparseCore 0:
  52.9 75.6 all-gather.2

commit v15 on v14

--- a/solution.py
+++ b/solution.py
@@ -36,6 +36,24 @@
 
 def scale_of(code):
     return jnp.exp2(code * (1.0 / STEPS))
+
+
+def encoded(values):
+    most = jnp.maximum(jnp.max(jnp.abs(values), axis=0, keepdims=True), 1e-30)
+    code = jnp.ceil(jnp.log2(most) * STEPS)
+    coded = jnp.round(values * (TOP / scale_of(code))).astype(jnp.int32).astype(jnp.int16)
+    code_rows = jnp.broadcast_to(code.astype(jnp.int32), (EXCHANGE_CODE_ROWS, values.shape[1])).astype(jnp.int16)
+    return coded, code_rows
+
+
+def decoded(coded, code_rows):
+    scale = scale_of(code_rows.astype(jnp.int32).astype(jnp.float32)[:1]) * (1.0 / TOP)
+    return coded.astype(jnp.int32).astype(jnp.float32) * scale
+
+
+def swapped(values):
+    by_place = values.reshape(ORBITALS_IN_GRP, ORBITALS_IN_GRP, -1)
+    return jnp.swapaxes(by_place, 0, 1).reshape(values.shape)
 
 
 def screen_kernel(part, int_mask, slab_ref, coded_ref, *later_refs):
@@ -85,15 +103,14 @@
     )(int_mask, integrals)
 
 
-def ladder_kernel(tile_total, vir_count, chunks, coded, amp_mask, numbers, rows_ref, gathered_ref, *refs):
-    ladder_ref, packed_ref, product, slab_scr, sems = refs[:5]
-    stage = refs[5] if coded else slab_scr
+def ladder_kernel(tile_total, vir_count, coded, amp_mask, numbers, rows_ref, gathered_ref, *refs):
+    packed_ref, product, slab_scr, sems = refs[:4]
+    stage = refs[4] if coded else slab_scr
     step = pl.program_id(0)
     cols = slab_scr.shape[1]
     slab_rows = slab_scr.shape[0] // tile_total
     shard_rows = stage.shape[0] // tile_total
     block = cols // vir_count
-    lanes = block // chunks
 
     def masks(tile, at, width):
         lane = lax.broadcasted_iota(jnp.int32, (1, width), 1) + at
@@ -111,16 +128,7 @@
         own_number = numbers[lax.axis_index("occ")]
         nonzero = (pair // ORBITALS_IN_GRP < own_number) & (pair % ORBITALS_IN_GRP < numbers[tile])
         ladder = jnp.where(nonzero, product[...], 0.0)
-        for h in range(chunks):
-            ladder_ref[h] = jnp.concatenate(
-                [ladder[:, v * block + h * lanes : v * block + (h + 1) * lanes] for v in range(vir_count)], axis=1
-            )
-        by_place = ladder.reshape(ORBITALS_IN_GRP, ORBITALS_IN_GRP, cols)
-        mirror = jnp.swapaxes(by_place, 0, 1).reshape(PAIR_SQ, cols)
-        most = jnp.maximum(jnp.max(jnp.abs(ladder), axis=0, keepdims=True), 1e-30)
-        code = jnp.ceil(jnp.log2(most) * STEPS)
-        coded_rows = jnp.round(mirror * (TOP / scale_of(code))).astype(jnp.int32).astype(jnp.int16)
-        code_rows = jnp.broadcast_to(code.astype(jnp.int32), (EXCHANGE_CODE_ROWS, cols)).astype(jnp.int16)
+        coded_rows, code_rows = encoded(swapped(ladder))
         for v in range(vir_count):
             packed_ref[0, v, :PAIR_SQ] = coded_rows[:, v * block : (v + 1) * block]
             packed_ref[0, v, PAIR_SQ:] = code_rows[:, v * block : (v + 1) * block]
@@ -160,7 +168,7 @@
         finish()
 
 
-def ladder_call(tile_total, vir_count, chunks, amp_mask, numbers, amplitudes, slab):
+def ladder_call(tile_total, vir_count, amp_mask, numbers, amplitudes, slab):
     coded = slab.dtype == jnp.int16
     cols = slab.shape[1]
     block = cols // vir_count
@@ -169,7 +177,7 @@
     before = lambda step: jnp.maximum(step - 1, 0)
     packed_block = (vir_count, PAIR_SQ + EXCHANGE_CODE_ROWS, block)
     return pl.pallas_call(
-        functools.partial(ladder_kernel, tile_total, vir_count, chunks, coded),
+        functools.partial(ladder_kernel, tile_total, vir_count, coded),
         grid=(tile_total + 1,),
         in_specs=[
             smem,
@@ -177,14 +185,8 @@
             pl.BlockSpec((PAIR_SQ, W * W), lambda step: (jnp.minimum(step, tile_total - 1), 0)),
             pl.BlockSpec(memory_space=pl.ANY),
         ],
-        out_specs=[
-            pl.BlockSpec((chunks, PAIR_SQ, cols // chunks), lambda step: (0, before(step), 0)),
-            pl.BlockSpec((1,) + packed_block, lambda step: (before(step), 0, 0, 0)),
-        ],
-        out_shape=[
-            jax.ShapeDtypeStruct((chunks, rows, cols // chunks), jnp.float32),
-            jax.ShapeDtypeStruct((tile_total,) + packed_block, jnp.int16),
-        ],
+        out_specs=pl.BlockSpec((1,) + packed_block, lambda step: (before(step), 0, 0, 0)),
+        out_shape=jax.ShapeDtypeStruct((tile_total,) + packed_block, jnp.int16),
         scratch_shapes=[
             pltpu.VMEM((PAIR_SQ, cols), jnp.float32),
             pltpu.VMEM((W * W, cols), jnp.bfloat16),
@@ -194,7 +196,7 @@
         compiler_params=pltpu.CompilerParams(vmem_limit_bytes=VMEM_LIMIT),
         cost_estimate=pl.CostEstimate(
             flops=2 * rows * cols * W * W,
-            bytes_accessed=rows * (W * W * 2 + cols * 6) + W * W * cols * 2,
+            bytes_accessed=rows * (W * W * 2 + cols * 2) + W * W * cols * 2,
             transcendentals=0,
         ),
         name="ladder",
@@ -206,76 +208,80 @@
     return both[: values.shape[0]] + both[values.shape[0] :]
 
 
-def direct_kernel(spread_ref, *refs):
-    refs[-1][...] = moved_columns(jnp.concatenate([ref[0] for ref in refs[:-1]], axis=1), spread_ref)
-
-
-def direct_call(chunk, spread, ladders):
-    rows = ladders[0].shape[1]
-    step_rows = AT_ONCE * PAIR_SQ
+def direct_kernel(chunk, chunks, spread_ref, *refs):
+    packed_refs, direct_ref = refs[:-1], refs[-1]
+    lanes = packed_refs[0].shape[3] // chunks
+
+    def one_tile(n, carry):
+        blocks = []
+        for packed_ref in packed_refs:
+            for v in range(packed_ref.shape[1]):
+                values = decoded(packed_ref[n, v, :PAIR_SQ], packed_ref[n, v, PAIR_SQ:])
+                blocks.append(values[:, chunk * lanes : (chunk + 1) * lanes])
+        natural = moved_columns(swapped(jnp.concatenate(blocks, axis=1)), spread_ref)
+        direct_ref[n, :PAIR_SQ], direct_ref[n, PAIR_SQ:] = encoded(natural)
+        return carry
+
+    lax.fori_loop(0, AT_ONCE, one_tile, 0)
+
+
+def direct_call(chunk, spread, packed):
+    tile_total = packed[0].shape[0]
+    cols = spread.shape[1]
+    block_shape = (PAIR_SQ + EXCHANGE_CODE_ROWS, cols)
+    rows = tile_total * PAIR_SQ
     return pl.pallas_call(
-        direct_kernel,
-        grid=(rows // step_rows,),
+        functools.partial(direct_kernel, chunk, len(packed)),
+        grid=(tile_total // AT_ONCE,),
         in_specs=[pl.BlockSpec(spread.shape, lambda step: (0, 0))]
-        + [pl.BlockSpec((1, step_rows, ladder.shape[2]), lambda step: (chunk, step, 0)) for ladder in ladders],
-        out_specs=pl.BlockSpec((step_rows, spread.shape[1]), lambda step: (step, 0)),
-        out_shape=jax.ShapeDtypeStruct((rows, spread.shape[1]), jnp.float32),
+        + [pl.BlockSpec((AT_ONCE,) + each.shape[1:], lambda step: (step, 0, 0, 0)) for each in packed],
+        out_specs=pl.BlockSpec((AT_ONCE,) + block_shape, lambda step: (step, 0, 0)),
+        out_shape=jax.ShapeDtypeStruct((tile_total,) + block_shape, jnp.int16),
         compiler_params=pltpu.CompilerParams(vmem_limit_bytes=VMEM_LIMIT),
-        cost_estimate=pl.CostEstimate(
-            flops=4 * rows * spread.size, bytes_accessed=rows * spread.shape[1] * 8, transcendentals=0
-        ),
+        cost_estimate=pl.CostEstimate(flops=4 * rows * spread.size, bytes_accessed=rows * cols * 6, transcendentals=0),
         name="direct",
-    )(spread, *ladders)
-
-
-def update_kernel(vir_count, at_once, spread_ref, vir_ref, occ_ref, *refs):
-    arrived_refs, refs = refs[:vir_count], refs[vir_count:]
-    direct_refs = refs[:at_once]
+    )(spread, *packed)
+
+
+def update_kernel(vir_count, spread_ref, vir_ref, occ_ref, arrived_ref, direct_ref, *refs):
     tiles = []
-    for n in range(at_once):
-        blocks = []
-        for v in range(vir_count):
-            code = arrived_refs[v][n, 0, PAIR_SQ:].astype(jnp.int32).astype(jnp.float32)[:1]
-            values = arrived_refs[v][n, 0, :PAIR_SQ].astype(jnp.int32).astype(jnp.float32)
-            blocks.append(values * (scale_of(code) * (1.0 / TOP)))
+    for n in range(AT_ONCE):
+        blocks = [decoded(arrived_ref[n, v, :PAIR_SQ], arrived_ref[n, v, PAIR_SQ:]) for v in range(vir_count)]
         tiles.append(jnp.concatenate(blocks, axis=1))
     mirror = moved_columns(jnp.concatenate(tiles, axis=0), spread_ref)
-    for n, direct_ref in enumerate(direct_refs):
+    for n in range(AT_ONCE):
         at = slice(n * PAIR_SQ, (n + 1) * PAIR_SQ)
-        refs[-1][at, :] = (direct_ref[...] + mirror[at]) / (vir_ref[...] - occ_ref[at, :1])
-
-
-def update_call(chunk, chunks, at_once, arrived, spread, vir_sum, occ_sum, direct, earlier):
+        direct = decoded(direct_ref[n, :PAIR_SQ], direct_ref[n, PAIR_SQ:])
+        occ = jnp.transpose(jnp.broadcast_to(occ_ref[n], (128, PAIR_SQ)))[:, :1]
+        refs[-1][at, :] = (direct + mirror[at]) / (vir_ref[...] - occ)
+
+
+def update_call(chunk, chunks, arrived, spread, vir_sum, occ_sum, direct, earlier):
+    tile_total, vir_count = arrived.shape[:2]
     cols = spread.shape[1]
-    rows = direct.shape[0]
-    step_rows = at_once * PAIR_SQ
-    vir_count = arrived.shape[1]
-    args = [spread, vir_sum, occ_sum] + [arrived] * vir_count + [direct] * at_once
+    rows = tile_total * PAIR_SQ
+    args = [spread, vir_sum, occ_sum, arrived, direct]
     in_specs = [
         pl.BlockSpec(spread.shape, lambda step: (0, 0)),
         pl.BlockSpec((1, cols), lambda step: (0, chunk)),
-        pl.BlockSpec((step_rows, 128), lambda step: (step, 0)),
+        pl.BlockSpec((AT_ONCE, 1, PAIR_SQ), lambda step: (step, 0, 0)),
+        pl.BlockSpec((AT_ONCE,) + arrived.shape[1:], lambda step: (step, 0, 0, 0)),
+        pl.BlockSpec((AT_ONCE,) + direct.shape[1:], lambda step: (step, 0, 0)),
     ]
-    in_specs += [
-        pl.BlockSpec((at_once, 1) + arrived.shape[2:], lambda step, v=v: (step, v, 0, 0)) for v in range(vir_count)
-    ]
-    in_specs += [pl.BlockSpec((PAIR_SQ, cols), lambda step, n=n: (step * at_once + n, 0)) for n in range(at_once)]
     aliases = {}
     if earlier is not None:
         aliases = {len(args): 0}
         args.append(earlier)
         in_specs.append(pl.BlockSpec(memory_space=pl.ANY))
     return pl.pallas_call(
-        functools.partial(update_kernel, vir_count, at_once),
-        grid=(rows // step_rows,),
+        functools.partial(update_kernel, vir_count),
+        grid=(tile_total // AT_ONCE,),
         in_specs=in_specs,
-        out_specs=pl.BlockSpec((step_rows, cols), lambda step: (step, chunk)),
+        out_specs=pl.BlockSpec((AT_ONCE * PAIR_SQ, cols), lambda step: (step, chunk)),
         out_shape=jax.ShapeDtypeStruct((rows, chunks * cols), jnp.float32),
         input_output_aliases=aliases,
         compiler_params=pltpu.CompilerParams(vmem_limit_bytes=VMEM_LIMIT),
-        cost_estimate=pl.CostEstimate(
-            flops=4 * rows * spread.size, bytes_accessed=rows * cols * 10, transcendentals=0
-        ),
+        cost_estimate=pl.CostEstimate(flops=4 * rows * spread.size, bytes_accessed=rows * cols * 8, transcendentals=0),
         name="update",
     )(*args)
 
@@ -303,12 +309,12 @@
     for part in later:
         part, _ = lax.optimization_barrier((part, slabs[-1]))
         slabs.append(lax.all_gather(part, "occ", axis=0, tiled=True))
-    ladders, arrived = [], []
+    own, arrived = [], []
     for slab in slabs:
-        ladder, packed = ladder_call(
-            tile_total, vir_count, chunks, amp_mask[0], group_orbital_numbers, amplitudes, slab
+        packed = ladder_call(
+            tile_total, vir_count, amp_mask[0], group_orbital_numbers, amplitudes, slab
         )
-        ladders.append(ladder)
+        own.append(packed)
         arrived.append(exchanged(packed))
 
     place = jnp.arange(vir_count * block)
@@ -323,15 +329,13 @@
 
     occ_table = occ_energy.reshape(tile_total, ORBITALS_IN_GRP)
     own_energy = lax.dynamic_slice_in_dim(occ_table, row_tile, 1, 0)[0]
-    occ_sum = jnp.broadcast_to(
-        (own_energy[None, :, None] + occ_table[:, None, :]).reshape(-1, 1), (tile_total * PAIR_SQ, 128)
-    )
+    occ_sum = (own_energy[None, :, None] + occ_table[:, None, :]).reshape(tile_total, 1, PAIR_SQ)
     vir_own = lax.dynamic_slice_in_dim(vir_energy, vir_place * span, span, 0)
     vir_sum = (vir_own[:, None] + vir_energy[None, :]).reshape(1, -1)
     update = None
     for chunk in range(chunks):
-        direct = direct_call(chunk, direct_spread, ladders)
-        update = update_call(chunk, chunks, 4, arrived[chunk], mirror_spread, vir_sum, occ_sum, direct, update)
+        direct = direct_call(chunk, direct_spread, own)
+        update = update_call(chunk, chunks, arrived[chunk], mirror_spread, vir_sum, occ_sum, direct, update)
     return update
 
 

time: 214 us -> 217 us (1.014)
  Pallas kernels: 63.6 us -> 66.8 us
  waiting for transfers between devices: 78.9 us -> 76.3 us
    all_to_all x2, waiting for transfers between devices: 28.3 us -> 25 us  [exchanged(): lax.all_to_all(packed.reshape(tile_total * vir_count, rows, block), ('occ...]
    pallas_call x6, Pallas kernels: 60 us -> 63.1 us  [the longest x2 35.1 us: ladder_call(): pl.pallas_call(functools.partial(ladder_kernel, tile_total, vir_count, co...]
  transfers between devices with their start and end apart: 3 -> 3, of which waited for: 2 -> 3; matrix products, arithmetic and copies ran while one was open for 2% -> 2% of each run, Pallas kernels for 25% -> 26%
where the time goes in v15:
time: 217 us; the launch traced here: 216 us
  waiting for transfers between devices  76.3 us (35%)
  Pallas kernels  66.8 us (31%)
  blocking collectives  42.7 us (20%)
  between operations  13.5 us (6%)
  starting transfers between devices  11.3 us (5%)
  local copies, waits for them, and re-layouts  3.2 us (1%)
  other arithmetic  2.6 us (1%)
    all_gather x1, waiting for transfers between devices, body(): slabs.append(lax.all_gather(part, 'occ', axis=0, tiled=True))  51.3 us
    all_gather x1, blocking collectives, body(): slabs = [lax.all_gather(coded, 'occ', axis=0, tiled=True)]  42.7 us
    pallas_call x2, Pallas kernels, ladder_call(): pl.pallas_call(functools.partial(ladder_kernel, tile_total, vir_count, co...  35.1 us
    all_to_all x2, waiting for transfers between devices, exchanged(): lax.all_to_all(packed.reshape(tile_total * vir_count, rows, block), ('occ...  25 us
    pallas_call x2, Pallas kernels, direct_call(): pl.pallas_call(functools.partial(direct_kernel, chunk, len(packed)), grid...  15.3 us
    pallas_call x2, Pallas kernels, update_call(): pl.pallas_call(functools.partial(update_kernel, vir_count), grid=(tile_to...  12.7 us
    all_to_all x2, starting transfers between devices, exchanged(): lax.all_to_all(packed.reshape(tile_total * vir_count, rows, block), ('occ...  11.3 us
  transfers between devices with their start and end apart: 3, of which 3 were waited for; matrix products, arithmetic and copies ran while one was open for 2% of the time, Pallas kernels for 26%

profile of v15, /device:TPU:0, one launch (start us, length us, event | category | flops | bytes accessed | tf_op | source)
XLA Modules:
  0.0 216.4 jit_solution(16484487316066666703)
XLA Ops:
  6.5 0.0 all-gather.3.cloned.1.call-start
  6.5 3.7 %screen.1 = (s16[528,512]{1,0:T(8,128)(2,1)}, bf16[512,512]{1,0:T(8,128)(2,1)}) custom-call(s32[4,4]{1,0:T(4,128)} %int_mask.1, bf16[512,1024]{1,0:T(8,128)(2,1)} %slab_ref.1), custom_call_target="tpu_custom_call" | custom-call | tf_op jit(solution)/shard_map/screen/pallas_call | solution.py:95
  10.3 0.0 copy-start.1
  10.3 42.7 %all-gather.4.gathered_ref = s16[4224,512]{1,0:T(8,128)(2,1)} all-gather(s16[528,512]{1,0:T(8,128)(2,1)} %get-tuple-element.9), channel_id=1, replica_groups=mesh['occ'=8,'vir'=4] {'occ'}, dimensions={0}, use_global_device_ids=true | all-gather | bytes 4866048 | tf_op jit(solution)/shard_map/all_gather | solution.py:308
  53.0 0.0 all-gather.3.cloned.1.call-update
  53.0 0.0 copy-done.1
  53.0 0.7 copy.9.amp_mask
  53.7 17.9 %ladder.3.refs_0_ = s16[8,4,264,128]{3,2,1,0:T(8,128)(2,1)} custom-call(s32[8,4]{1,0:T(8,128)} %copy.9.amp_mask, s32[8]{0:T(128)} %numbers.3, bf16[2048,4096]{1,0:T(8,128)(2,1)} %rows_ref.3, s16[4224,512]{1,0:T(8,128)(2,1)} %all-gather.4.gathered_ref), custom_call_target="tpu_custom_call" | custom-call | flops 8589934592 | bytes 23068672 | tf_op jit(solution)/shard_map/ladder/pallas_call | solution.py:179
  71.6 6.0 %all-to-all-start.1 = ((s16[32,264,128]{2,1,0:T(8,128)(2,1)}), s16[32,264,128]{2,1,0:T(8,128)(2,1)S(1)}, u32[]{:S(2)}, u32[]{:S(2)}) async-start(s16[32,264,128]{2,1,0:T(8,128)(2,1)} %bitcast.8), calls=%async_computation.1 | async-start | bytes 4325376 | tf_op jit(solution)/shard_map/all_to_all | solution.py:302
  77.7 51.3 %all-gather.3.cloned.1.call-done.gathered_ref = bf16[4096,512]{1,0:T(8,128)(2,1)} async-done(((bf16[512,512]{1,0:T(8,128)(2,1)}), bf16[4096,512]{1,0:T(8,128)(2,1)}) %all-gather.3.cloned.1.call-update) | async-done | bytes 4194320 | tf_op jit(solution)/shard_map/all_gather | solution.py:311
  129.0 17.2 %ladder.2.refs_1_ = s16[8,4,264,128]{3,2,1,0:T(8,128)(2,1)} custom-call(s32[8,4]{1,0:T(8,128)} %copy.9.amp_mask, s32[8]{0:T(128)} %numbers.3, bf16[2048,4096]{1,0:T(8,128)(2,1)} %rows_ref.3, bf16[4096,512]{1,0:T(8,128)(2,1)} %all-gather.3.cloned.1.call-done.gathered_ref), custom_call_target="tpu_custom_call" | custom-call | flops 8589934592 | bytes 23068672 | tf_op jit(solution)/shard_map/ladder/pallas_call | solution.py:179
  146.1 0.3 all-to-all-done.1
  146.4 0.0 copy-start
  146.4 0.0 copy-start.2
  146.4 0.0 copy-start.3
  146.4 1.4 copy-done
  147.8 5.3 %all-to-all-start = ((s16[32,264,128]{2,1,0:T(8,128)(2,1)}), s16[32,264,128]{2,1,0:T(8,128)(2,1)}, u32[]{:S(2)}, u32[]{:S(2)}) async-start(s16[32,264,128]{2,1,0:T(8,128)(2,1)} %bitcast.9), calls=%async_computation | async-start | bytes 4325376 | tf_op jit(solution)/shard_map/all_to_all | solution.py:302
  153.1 0.0 copy-done.2
  153.2 0.1 reshape.142
  153.2 0.1 add.176
  153.3 0.1 add.177
  153.4 0.0 copy-done.3
  153.4 0.1 dynamic_slice.6
  153.5 0.1 broadcast_add_fusion.1
  153.6 0.7 add.173.vir_ref
  154.2 0.1 add.180
  154.4 0.6 broadcast_add_fusion.occ_ref
  155.0 0.9 fusion.1.spread_ref
  155.9 1.0 fusion.spread_ref
  156.9 7.7 %direct.3.direct_ref = s16[8,264,512]{2,1,0:T(8,128)(2,1)} custom-call(bf16[512,512]{1,0:T(8,128)(2,1)} %fusion.1.spread_ref, s16[8,4,264,128]{3,2,1,0:T(8,128)(2,1)} %ladder.3.refs_0_, s16[8,4,264,128]{3,2,1,0:T(8,128)(2,1)} %ladder.2.refs_1_), custom_call_target="tpu_custom_call" | custom-call | flops 2147483648 | bytes 6291456 | tf_op jit(solution)/shard_map/direct/pallas_call | solution.py:233
  164.5 7.6 %direct.2.direct_ref = s16[8,264,512]{2,1,0:T(8,128)(2,1)} custom-call(bf16[512,512]{1,0:T(8,128)(2,1)} %fusion.1.spread_ref, s16[8,4,264,128]{3,2,1,0:T(8,128)(2,1)} %ladder.3.refs_0_, s16[8,4,264,128]{3,2,1,0:T(8,128)(2,1)} %ladder.2.refs_1_), custom_call_target="tpu_custom_call" | custom-call | flops 2147483648 | bytes 6291456 | tf_op jit(solution)/shard_map/direct/pallas_call | solution.py:233
  172.2 6.3 %update.2.refs_0_ = f32[2048,1024]{1,0:T(8,128)} custom-call(bf16[512,512]{1,0:T(8,128)(2,1)} %fusion.spread_ref, f32[1,1024]{1,0:T(1,128)} %add.173.vir_ref, f32[8,1,256]{2,1,0:T(1,128)} %broadcast_add_fusion.occ_ref, s16[8,4,264,128]{3,2,1,0:T(8,128)(2,1)} %bitcast.7, s16[8,264,512]{2,1,0:T(8,128)(2,1)} %direct.3.direct_ref), custom_call_target="tpu_custom_call" | custom-call | flops 2147483648 | bytes 8388608 | tf_op jit(solution)/shard_map/update/pallas_call | solution.py:276
  178.5 24.7 %all-to-all-done = s16[32,264,128]{2,1,0:T(8,128)(2,1)} async-done(((s16[32,264,128]{2,1,0:T(8,128)(2,1)}), s16[32,264,128]{2,1,0:T(8,128)(2,1)}, u32[]{:S(2)}, u32[]{:S(2)}) %all-to-all-start) | async-done | bytes 2162720 | tf_op jit(solution)/shard_map/all_to_all | solution.py:302
  203.2 6.4 %update.3 = f32[2048,1024]{1,0:T(8,128)} custom-call(bf16[512,512]{1,0:T(8,128)(2,1)} %fusion.spread_ref, f32[1,1024]{1,0:T(1,128)} %add.173.vir_ref, f32[8,1,256]{2,1,0:T(1,128)} %broadcast_add_fusion.occ_ref, s16[8,4,264,128]{3,2,1,0:T(8,128)(2,1)} %bitcast.3.arrived_ref, s16[8,264,512]{2,1,0:T(8,128)(2,1)} %direct.2.direct_ref, ...), custom_call_target="tpu_custom_call", output_to_operand_aliasing={{}: (5, {})} | custom-call | flops 2147483648 | bytes 8388608 | tf_op jit(solution)/shard_map/update/pallas_call | solution.py:276
  (5 shorter events, 0.0 us)
Async XLA Ops:
  6.5 122.4 %all-gather.3.cloned.1.call-start = ((), (), s32[]{:S(2)}) async-start(), calls=%async_computation.2 | async-start | bytes 4718592 | tf_op jit(solution)/shard_map/all_gather | solution.py:311
  10.3 42.7 %copy-start.1 = (s32[1,8,4]{1,2,0:T(4,128)S(1)}, s32[1,8,4]{1,2,0:T(4,128)}, u32[]{:S(2)}) copy-start(s32[1,8,4]{1,2,0:T(4,128)} %param.8) | copy-start | bytes 388
  71.6 74.8 %all-to-all-start.1 = ((s16[32,264,128]{2,1,0:T(8,128)(2,1)}), s16[32,264,128]{2,1,0:T(8,128)(2,1)S(1)}, u32[]{:S(2)}, u32[]{:S(2)}) async-start(s16[32,264,128]{2,1,0:T(8,128)(2,1)} %bitcast.8), calls=%async_computation.1 | async-start | bytes 4325376 | tf_op jit(solution)/shard_map/all_to_all | solution.py:302
  146.4 1.4 copy-start
  146.4 6.8 %copy-start.2 = (f32[128]{0:T(128)S(1)}, f32[128]{0:T(128)}, u32[]{:S(2)}) copy-start(f32[128]{0:T(128)} %param.12) | copy-start | bytes 1540
  146.4 7.0 %copy-start.3 = (f32[64]{0:T(128)S(1)}, f32[64]{0:T(128)}, u32[]{:S(2)}) copy-start(f32[64]{0:T(128)} %param.13) | copy-start | bytes 772
  147.8 55.4 %all-to-all-start = ((s16[32,264,128]{2,1,0:T(8,128)(2,1)}), s16[32,264,128]{2,1,0:T(8,128)(2,1)}, u32[]{:S(2)}, u32[]{:S(2)}) async-start(s16[32,264,128]{2,1,0:T(8,128)(2,1)} %bitcast.9), calls=%async_computation | async-start | bytes 4325376 | tf_op jit(solution)/shard_map/all_to_all | solution.py:302
Sparse Core Ops, SparseCore 0:
  53.1 75.7 all-gather.2

commit v16 on v14

--- a/solution.py
+++ b/solution.py
@@ -86,27 +86,49 @@
 
 
 def ladder_kernel(tile_total, vir_count, chunks, coded, amp_mask, numbers, rows_ref, gathered_ref, *refs):
-    ladder_ref, packed_ref, product, slab_scr, sems = refs[:5]
-    stage = refs[5] if coded else slab_scr
+    ladder_ref, packed_ref, product = refs[:3]
+    slab_ref, stage, sems = refs[3:] if coded else (gathered_ref, None, None)
     step = pl.program_id(0)
-    cols = slab_scr.shape[1]
-    slab_rows = slab_scr.shape[0] // tile_total
-    shard_rows = stage.shape[0] // tile_total
+    cols = slab_ref.shape[1]
+    slab_rows = slab_ref.shape[0] // tile_total
+    shard_rows = slab_rows + CODE_ROWS
     block = cols // vir_count
     lanes = block // chunks
 
-    def masks(tile, at, width):
-        lane = lax.broadcasted_iota(jnp.int32, (1, width), 1) + at
+    def multiply():
+        tile = step
+        lane = lax.broadcasted_iota(jnp.int32, (1, W * W), 1)
         left = lane % W < VT
         keep = jnp.where(
             lane < W * VT,
             jnp.where(left, amp_mask[tile, 0], amp_mask[tile, 1]),
             jnp.where(left, amp_mask[tile, 2], amp_mask[tile, 3]),
         )
-        return keep.astype(jnp.float32).astype(jnp.bfloat16)
+        keep = keep.astype(jnp.float32).astype(jnp.bfloat16)
+        product[...] = dot(rows_ref[...] * keep, slab_ref[...])
+
+    def decode():
+        def copy_of(shard):
+            at = pl.ds(pl.multiple_of(shard * shard_rows, CODE_ROWS), shard_rows)
+            return pltpu.make_async_copy(gathered_ref.at[at, :], stage.at[at, :], sems.at[shard])
+
+        for shard in range(tile_total):
+            copy_of(shard).start()
+
+        def use(shard, carry):
+            copy_of(shard).wait()
+            at = pl.multiple_of(shard * shard_rows, CODE_ROWS)
+            code = stage[pl.ds(pl.multiple_of(at + slab_rows, CODE_ROWS), CODE_ROWS), :]
+            values = stage[pl.ds(at, slab_rows), :].astype(jnp.int32).astype(jnp.float32)
+            scale = jnp.exp2(code.astype(jnp.int32).astype(jnp.float32)[:1] - SLAB_BITS)
+            to = pl.ds(pl.multiple_of(shard * slab_rows, slab_rows), slab_rows)
+            slab_ref[to, :] = (values * scale).astype(jnp.bfloat16)
+            return carry
+
+        lax.fori_loop(0, tile_total, use, 0)
 
     def finish():
-        tile = step - 1
+        tile = jnp.maximum(step - 1, 0)
         pair = lax.broadcasted_iota(jnp.int32, (PAIR_SQ, 1), 0)
         own_number = numbers[lax.axis_index("occ")]
         nonzero = (pair // ORBITALS_IN_GRP < own_number) & (pair % ORBITALS_IN_GRP < numbers[tile])
@@ -125,35 +147,16 @@
             packed_ref[0, v, :PAIR_SQ] = coded_rows[:, v * block : (v + 1) * block]
             packed_ref[0, v, PAIR_SQ:] = code_rows[:, v * block : (v + 1) * block]
 
-    @pl.when(step == 0)
-    def _():
-        def copy_of(shard):
-            at = pl.ds(pl.multiple_of(shard * shard_rows, CODE_ROWS), shard_rows)
-            return pltpu.make_async_copy(gathered_ref.at[at, :], stage.at[at, :], sems.at[shard])
-
-        for shard in range(tile_total):
-            copy_of(shard).start()
-        product[...] = jnp.zeros_like(product)
-
-        def use(shard, carry):
-            copy_of(shard).wait()
-            to = pl.ds(pl.multiple_of(shard * slab_rows, slab_rows), slab_rows)
-            if coded:
-                at = pl.multiple_of(shard * shard_rows, CODE_ROWS)
-                code = stage[pl.ds(pl.multiple_of(at + slab_rows, CODE_ROWS), CODE_ROWS), :]
-                values = stage[pl.ds(at, slab_rows), :].astype(jnp.int32).astype(jnp.float32)
-                scale = jnp.exp2(code.astype(jnp.int32).astype(jnp.float32)[:1] - SLAB_BITS)
-                slab_scr[to, :] = (values * scale).astype(jnp.bfloat16)
-            screened = rows_ref[:, to] * masks(0, shard * slab_rows, slab_rows)
-            product[...] += dot(screened, slab_scr[to, :])
-            return carry
-
-        lax.fori_loop(0, tile_total, use, 0)
-
-    @pl.when((step > 0) & (step < tile_total))
+    if coded:
+
+        @pl.when(step == 0)
+        def _():
+            decode()
+
+    @pl.when(step < tile_total)
     def _():
         finish()
-        product[...] = dot(rows_ref[...] * masks(step, 0, W * W), slab_scr[...])
+        multiply()
 
     @pl.when(step == tile_total)
     def _():
@@ -175,7 +178,7 @@
             smem,
             smem,
             pl.BlockSpec((PAIR_SQ, W * W), lambda step: (jnp.minimum(step, tile_total - 1), 0)),
-            pl.BlockSpec(memory_space=pl.ANY),
+            pl.BlockSpec(memory_space=pl.ANY) if coded else pl.BlockSpec((W * W, cols), lambda step: (0, 0)),
         ],
         out_specs=[
             pl.BlockSpec((chunks, PAIR_SQ, cols // chunks), lambda step: (0, before(step), 0)),
@@ -185,12 +188,13 @@
             jax.ShapeDtypeStruct((chunks, rows, cols // chunks), jnp.float32),
             jax.ShapeDtypeStruct((tile_total,) + packed_block, jnp.int16),
         ],
-        scratch_shapes=[
-            pltpu.VMEM((PAIR_SQ, cols), jnp.float32),
+        scratch_shapes=[pltpu.VMEM((PAIR_SQ, cols), jnp.float32)]
+        + [
             pltpu.VMEM((W * W, cols), jnp.bfloat16),
+            pltpu.VMEM(slab.shape, slab.dtype),
             pltpu.SemaphoreType.DMA((tile_total,)),
         ]
-        + [pltpu.VMEM(slab.shape, slab.dtype)] * coded,
+        * coded,
         compiler_params=pltpu.CompilerParams(vmem_limit_bytes=VMEM_LIMIT),
         cost_estimate=pl.CostEstimate(
             flops=2 * rows * cols * W * W,
@@ -242,7 +246,8 @@
     mirror = moved_columns(jnp.concatenate(tiles, axis=0), spread_ref)
     for n, direct_ref in enumerate(direct_refs):
         at = slice(n * PAIR_SQ, (n + 1) * PAIR_SQ)
-        refs[-1][at, :] = (direct_ref[...] + mirror[at]) / (vir_ref[...] - occ_ref[at, :1])
+        occ = jnp.transpose(jnp.broadcast_to(occ_ref[n], (128, PAIR_SQ)))[:, :1]
+        refs[-1][at, :] = (direct_ref[...] + mirror[at]) / (vir_ref[...] - occ)
 
 
 def update_call(chunk, chunks, at_once, arrived, spread, vir_sum, occ_sum, direct, earlier):
@@ -254,7 +259,7 @@
     in_specs = [
         pl.BlockSpec(spread.shape, lambda step: (0, 0)),
         pl.BlockSpec((1, cols), lambda step: (0, chunk)),
-        pl.BlockSpec((step_rows, 128), lambda step: (step, 0)),
+        pl.BlockSpec((at_once, 1, PAIR_SQ), lambda step: (step, 0, 0)),
     ]
     in_specs += [
         pl.BlockSpec((at_once, 1) + arrived.shape[2:], lambda step, v=v: (step, v, 0, 0)) for v in range(vir_count)
@@ -323,9 +328,7 @@
 
     occ_table = occ_energy.reshape(tile_total, ORBITALS_IN_GRP)
     own_energy = lax.dynamic_slice_in_dim(occ_table, row_tile, 1, 0)[0]
-    occ_sum = jnp.broadcast_to(
-        (own_energy[None, :, None] + occ_table[:, None, :]).reshape(-1, 1), (tile_total * PAIR_SQ, 128)
-    )
+    occ_sum = (own_energy[None, :, None] + occ_table[:, None, :]).reshape(tile_total, 1, PAIR_SQ)
     vir_own = lax.dynamic_slice_in_dim(vir_energy, vir_place * span, span, 0)
     vir_sum = (vir_own[:, None] + vir_energy[None, :]).reshape(1, -1)
     update = None

time: 214 us -> 215 us (level)
  waiting for transfers between devices: 78.9 us -> 81.1 us
  transfers between devices with their start and end apart: 3 -> 3, of which waited for: 2 -> 3; matrix products, arithmetic and copies ran while one was open for 2% -> 2% of each run, Pallas kernels for 25% -> 24%
where the time goes in v16:
time: 215 us; the launch traced here: 214 us
  waiting for transfers between devices  81.1 us (38%)
  Pallas kernels  61.7 us (29%)
  blocking collectives  42.6 us (20%)
  between operations  13.5 us (6%)
  starting transfers between devices  10.5 us (5%)
  other arithmetic  2.69 us (1%)
    all_gather x1, waiting for transfers between devices, body(): slabs.append(lax.all_gather(part, 'occ', axis=0, tiled=True))  51.2 us
    all_gather x1, blocking collectives, body(): slabs = [lax.all_gather(coded, 'occ', axis=0, tiled=True)]  42.6 us
    pallas_call x2, Pallas kernels, ladder_call(): pl.pallas_call(functools.partial(ladder_kernel, tile_total, vir_count, ch...  34.5 us
    all_to_all x2, waiting for transfers between devices, exchanged(): lax.all_to_all(packed.reshape(tile_total * vir_count, rows, block), ('occ...  29.9 us
    pallas_call x2, Pallas kernels, update_call(): pl.pallas_call(functools.partial(update_kernel, vir_count, at_once), grid...  12.3 us
    pallas_call x2, Pallas kernels, direct_call(): pl.pallas_call(direct_kernel, grid=(rows // step_rows,), in_specs=[pl.Blo...  11.1 us
    all_to_all x2, starting transfers between devices, exchanged(): lax.all_to_all(packed.reshape(tile_total * vir_count, rows, block), ('occ...  10.5 us
  transfers between devices with their start and end apart: 3, of which 3 were waited for; matrix products, arithmetic and copies ran while one was open for 2% of the time, Pallas kernels for 24%

profile of v16, /device:TPU:0, one launch (start us, length us, event | category | flops | bytes accessed | tf_op | source)
XLA Modules:
  0.0 213.8 jit_solution(11373962972441430487)
XLA Ops:
  6.5 0.0 copy-start.1
  6.5 0.0 all-gather.3.cloned.1.call-start
  6.5 3.7 %screen.1 = (s16[528,512]{1,0:T(8,128)(2,1)}, bf16[512,512]{1,0:T(8,128)(2,1)}) custom-call(s32[4,4]{1,0:T(4,128)} %int_mask.1, bf16[512,1024]{1,0:T(8,128)(2,1)} %slab_ref.1), custom_call_target="tpu_custom_call" | custom-call | tf_op jit(solution)/shard_map/screen/pallas_call | solution.py:77
  10.2 42.6 %all-gather.4.gathered_ref = s16[4224,512]{1,0:T(8,128)(2,1)} all-gather(s16[528,512]{1,0:T(8,128)(2,1)} %get-tuple-element.13), channel_id=1, replica_groups=mesh['occ'=8,'vir'=4] {'occ'}, dimensions={0}, use_global_device_ids=true | all-gather | bytes 4866048 | tf_op jit(solution)/shard_map/all_gather | solution.py:307
  52.8 0.0 all-gather.3.cloned.1.call-update
  52.8 0.0 copy-done.1
  52.8 0.7 copy.9.amp_mask
  53.5 18.1 %ladder.3 = (f32[2,2048,256]{2,1,0:T(8,128)}, s16[8,4,264,128]{3,2,1,0:T(8,128)(2,1)}) custom-call(s32[8,4]{1,0:T(8,128)} %copy.9.amp_mask, s32[8]{0:T(128)} %numbers.3, bf16[2048,4096]{1,0:T(8,128)(2,1)} %rows_ref.3, s16[4224,512]{1,0:T(8,128)(2,1)} %all-gather.4.gathered_ref), custom_call_target="tpu_custom_call" | custom-call | flops 8589934592 | bytes 27262976 | tf_op jit(solution)/shard_map/ladder/pallas_call | solution.py:174
  71.6 6.0 %all-to-all-start.1 = ((s16[32,264,128]{2,1,0:T(8,128)(2,1)}), s16[32,264,128]{2,1,0:T(8,128)(2,1)S(1)}, u32[]{:S(2)}, u32[]{:S(2)}) async-start(s16[32,264,128]{2,1,0:T(8,128)(2,1)} %bitcast.12), calls=%async_computation.1 | async-start | bytes 4325376 | tf_op jit(solution)/shard_map/all_to_all | solution.py:301
  77.6 51.2 %all-gather.3.cloned.1.call-done.gathered_ref = bf16[4096,512]{1,0:T(8,128)(2,1)} async-done(((bf16[512,512]{1,0:T(8,128)(2,1)}), bf16[4096,512]{1,0:T(8,128)(2,1)}) %all-gather.3.cloned.1.call-update) | async-done | bytes 4194320 | tf_op jit(solution)/shard_map/all_gather | solution.py:310
  128.8 16.5 %ladder.2 = (f32[2,2048,256]{2,1,0:T(8,128)}, s16[8,4,264,128]{3,2,1,0:T(8,128)(2,1)}) custom-call(s32[8,4]{1,0:T(8,128)} %copy.9.amp_mask, s32[8]{0:T(128)} %numbers.3, bf16[2048,4096]{1,0:T(8,128)(2,1)} %rows_ref.3, bf16[4096,512]{1,0:T(8,128)(2,1)} %all-gather.3.cloned.1.call-done.gathered_ref), custom_call_target="tpu_custom_call" | custom-call | flops 8589934592 | bytes 27262976 | tf_op jit(solution)/shard_map/ladder/pallas_call | solution.py:174
  145.2 0.0 copy-start.2
  145.2 0.0 copy-start.3
  145.2 0.9 all-to-all-done.1
  146.2 0.0 copy-start
  146.2 4.5 %all-to-all-start = ((s16[32,264,128]{2,1,0:T(8,128)(2,1)}), s16[32,264,128]{2,1,0:T(8,128)(2,1)}, u32[]{:S(2)}, u32[]{:S(2)}) async-start(s16[32,264,128]{2,1,0:T(8,128)(2,1)} %bitcast.11), calls=%async_computation | async-start | bytes 4325376 | tf_op jit(solution)/shard_map/all_to_all | solution.py:301
  150.7 0.0 copy-done.2
  150.7 0.1 reshape.142
  150.8 0.1 add.176
  150.9 0.1 add.177
  150.9 0.0 copy-done.3
  150.9 0.1 dynamic_slice.6
  151.0 0.1 broadcast_add_fusion.1
  151.1 0.7 add.173.vir_ref
  151.8 0.1 add.180
  151.9 0.6 broadcast_add_fusion.occ_ref
  152.5 1.0 fusion.1.spread_ref
  153.5 1.0 fusion.spread_ref
  154.5 5.5 %direct.3.refs_4_.refs_5_.refs_6_.refs_7_ = f32[2048,512]{1,0:T(8,128)} custom-call(bf16[512,512]{1,0:T(8,128)(2,1)} %fusion.1.spread_ref, f32[2,2048,256]{2,1,0:T(8,128)} %get-tuple-element.16.refs_0_, f32[2,2048,256]{2,1,0:T(8,128)} %get-tuple-element.17.refs_1_), custom_call_target="tpu_custom_call" | custom-call | flops 2147483648 | bytes 8388608 | tf_op jit(solution)/shard_map/direct/pallas_call | solution.py:220
  160.0 0.0 copy-done
  160.0 5.6 %direct.2.refs_4_.refs_5_.refs_6_.refs_7_ = f32[2048,512]{1,0:T(8,128)} custom-call(bf16[512,512]{1,0:T(8,128)(2,1)} %fusion.1.spread_ref, f32[2,2048,256]{2,1,0:T(8,128)} %get-tuple-element.16.refs_0_, f32[2,2048,256]{2,1,0:T(8,128)} %get-tuple-element.17.refs_1_), custom_call_target="tpu_custom_call" | custom-call | flops 2147483648 | bytes 8388608 | tf_op jit(solution)/shard_map/direct/pallas_call | solution.py:220
  165.6 6.2 %update.2.refs_8_ = f32[2048,1024]{1,0:T(8,128)} custom-call(bf16[512,512]{1,0:T(8,128)(2,1)} %fusion.spread_ref, f32[1,1024]{1,0:T(1,128)} %add.173.vir_ref, f32[8,1,256]{2,1,0:T(1,128)} %broadcast_add_fusion.occ_ref, s16[8,4,264,128]{3,2,1,0:T(8,128)(2,1)} %bitcast.7, s16[8,4,264,128]{3,2,1,0:T(8,128)(2,1)} %bitcast.8, s16[8,4,264,128]{3,2,1,0:T(8,128)(2,1)} %bitcast.9, ...), custom_call_target="tpu_custom_call" | custom-call | flops 2147483648 | bytes 10485760 | tf_op jit(solution)/shard_map/update/pallas_call | solution.py:273
  171.8 29.0 %all-to-all-done = s16[32,264,128]{2,1,0:T(8,128)(2,1)} async-done(((s16[32,264,128]{2,1,0:T(8,128)(2,1)}), s16[32,264,128]{2,1,0:T(8,128)(2,1)}, u32[]{:S(2)}, u32[]{:S(2)}) %all-to-all-start) | async-done | bytes 2162720 | tf_op jit(solution)/shard_map/all_to_all | solution.py:301
  200.8 6.2 %update.3 = f32[2048,1024]{1,0:T(8,128)} custom-call(bf16[512,512]{1,0:T(8,128)(2,1)} %fusion.spread_ref, f32[1,1024]{1,0:T(1,128)} %add.173.vir_ref, f32[8,1,256]{2,1,0:T(1,128)} %broadcast_add_fusion.occ_ref, s16[8,4,264,128]{3,2,1,0:T(8,128)(2,1)} %bitcast.3.refs_0_.refs_1_.refs_2_.refs_3_, ...), custom_call_target="tpu_custom_call", output_to_operand_aliasing={{}: (11, {})} | custom-call | flops 2147483648 | bytes 10485760 | tf_op jit(solution)/shard_map/update/pallas_call | solution.py:273
  (5 shorter events, 0.0 us)
Async XLA Ops:
  6.5 46.3 %copy-start.1 = (s32[1,8,4]{1,2,0:T(4,128)S(1)}, s32[1,8,4]{1,2,0:T(4,128)}, u32[]{:S(2)}) copy-start(s32[1,8,4]{1,2,0:T(4,128)} %param.8) | copy-start | bytes 388
  6.5 122.2 %all-gather.3.cloned.1.call-start = ((), (), s32[]{:S(2)}) async-start(), calls=%async_computation.2 | async-start | bytes 4718592 | tf_op jit(solution)/shard_map/all_gather | solution.py:310
  71.6 74.6 %all-to-all-start.1 = ((s16[32,264,128]{2,1,0:T(8,128)(2,1)}), s16[32,264,128]{2,1,0:T(8,128)(2,1)S(1)}, u32[]{:S(2)}, u32[]{:S(2)}) async-start(s16[32,264,128]{2,1,0:T(8,128)(2,1)} %bitcast.12), calls=%async_computation.1 | async-start | bytes 4325376 | tf_op jit(solution)/shard_map/all_to_all | solution.py:301
  145.2 5.4 %copy-start.2 = (f32[128]{0:T(128)S(1)}, f32[128]{0:T(128)}, u32[]{:S(2)}) copy-start(f32[128]{0:T(128)} %param.12) | copy-start | bytes 1540
  145.2 5.7 %copy-start.3 = (f32[64]{0:T(128)S(1)}, f32[64]{0:T(128)}, u32[]{:S(2)}) copy-start(f32[64]{0:T(128)} %param.13) | copy-start | bytes 772
  146.2 13.8 %copy-start = (s16[32,264,128]{2,1,0:T(8,128)(2,1)}, s16[32,264,128]{2,1,0:T(8,128)(2,1)S(1)}, u32[]{:S(2)}) copy-start(s16[32,264,128]{2,1,0:T(8,128)(2,1)S(1)} %all-to-all-done.1) | copy-start | bytes 6488068
  146.2 54.6 %all-to-all-start = ((s16[32,264,128]{2,1,0:T(8,128)(2,1)}), s16[32,264,128]{2,1,0:T(8,128)(2,1)}, u32[]{:S(2)}, u32[]{:S(2)}) async-start(s16[32,264,128]{2,1,0:T(8,128)(2,1)} %bitcast.11), calls=%async_computation | async-start | bytes 4325376 | tf_op jit(solution)/shard_map/all_to_all | solution.py:301
Sparse Core Ops, SparseCore 0:
  52.9 75.7 all-gather.2

commit v17 on v16

--- a/solution.py
+++ b/solution.py
@@ -144,8 +144,8 @@
         coded_rows = jnp.round(mirror * (TOP / scale_of(code))).astype(jnp.int32).astype(jnp.int16)
         code_rows = jnp.broadcast_to(code.astype(jnp.int32), (EXCHANGE_CODE_ROWS, cols)).astype(jnp.int16)
         for v in range(vir_count):
-            packed_ref[0, v, :PAIR_SQ] = coded_rows[:, v * block : (v + 1) * block]
-            packed_ref[0, v, PAIR_SQ:] = code_rows[:, v * block : (v + 1) * block]
+            packed_ref[v, 0, :PAIR_SQ] = coded_rows[:, v * block : (v + 1) * block]
+            packed_ref[v, 0, PAIR_SQ:] = code_rows[:, v * block : (v + 1) * block]
 
     if coded:
 
@@ -170,7 +170,7 @@
     smem = pl.BlockSpec(memory_space=pltpu.SMEM)
     rows = tile_total * PAIR_SQ
     before = lambda step: jnp.maximum(step - 1, 0)
-    packed_block = (vir_count, PAIR_SQ + EXCHANGE_CODE_ROWS, block)
+    packed_rows = PAIR_SQ + EXCHANGE_CODE_ROWS
     return pl.pallas_call(
         functools.partial(ladder_kernel, tile_total, vir_count, chunks, coded),
         grid=(tile_total + 1,),
@@ -182,11 +182,11 @@
         ],
         out_specs=[
             pl.BlockSpec((chunks, PAIR_SQ, cols // chunks), lambda step: (0, before(step), 0)),
-            pl.BlockSpec((1,) + packed_block, lambda step: (before(step), 0, 0, 0)),
+            pl.BlockSpec((vir_count, 1, packed_rows, block), lambda step: (0, before(step), 0, 0)),
         ],
         out_shape=[
             jax.ShapeDtypeStruct((chunks, rows, cols // chunks), jnp.float32),
-            jax.ShapeDtypeStruct((tile_total,) + packed_block, jnp.int16),
+            jax.ShapeDtypeStruct((vir_count, tile_total, packed_rows, block), jnp.int16),
         ],
         scratch_shapes=[pltpu.VMEM((PAIR_SQ, cols), jnp.float32)]
         + [
@@ -239,8 +239,8 @@
     for n in range(at_once):
         blocks = []
         for v in range(vir_count):
-            code = arrived_refs[v][n, 0, PAIR_SQ:].astype(jnp.int32).astype(jnp.float32)[:1]
-            values = arrived_refs[v][n, 0, :PAIR_SQ].astype(jnp.int32).astype(jnp.float32)
+            code = arrived_refs[v][0, n, PAIR_SQ:].astype(jnp.int32).astype(jnp.float32)[:1]
+            values = arrived_refs[v][0, n, :PAIR_SQ].astype(jnp.int32).astype(jnp.float32)
             blocks.append(values * (scale_of(code) * (1.0 / TOP)))
         tiles.append(jnp.concatenate(blocks, axis=1))
     mirror = moved_columns(jnp.concatenate(tiles, axis=0), spread_ref)
@@ -254,7 +254,7 @@
     cols = spread.shape[1]
     rows = direct.shape[0]
     step_rows = at_once * PAIR_SQ
-    vir_count = arrived.shape[1]
+    vir_count = arrived.shape[0]
     args = [spread, vir_sum, occ_sum] + [arrived] * vir_count + [direct] * at_once
     in_specs = [
         pl.BlockSpec(spread.shape, lambda step: (0, 0)),
@@ -262,7 +262,7 @@
         pl.BlockSpec((at_once, 1, PAIR_SQ), lambda step: (step, 0, 0)),
     ]
     in_specs += [
-        pl.BlockSpec((at_once, 1) + arrived.shape[2:], lambda step, v=v: (step, v, 0, 0)) for v in range(vir_count)
+        pl.BlockSpec((1, at_once) + arrived.shape[2:], lambda step, v=v: (v, step, 0, 0)) for v in range(vir_count)
     ]
     in_specs += [pl.BlockSpec((PAIR_SQ, cols), lambda step, n=n: (step * at_once + n, 0)) for n in range(at_once)]
     aliases = {}
@@ -299,9 +299,9 @@
 
     def exchanged(packed):
         moved = lax.all_to_all(
-            packed.reshape(tile_total * vir_count, rows, block), ("occ", "vir"), split_axis=0, concat_axis=0, tiled=True
+            packed.reshape(vir_count * tile_total, rows, block), ("vir", "occ"), split_axis=0, concat_axis=0, tiled=True
         )
-        return moved.reshape(tile_total, vir_count, rows, block)
+        return moved.reshape(vir_count, tile_total, rows, block)
 
     coded, *later = screen_call(chunks, int_mask, integrals)
     slabs = [lax.all_gather(coded, "occ", axis=0, tiled=True)]

time: 215 us -> 218 us (1.014)
  waiting for transfers between devices: 81.1 us -> 83.9 us
    all_to_all x2, waiting for transfers between devices: 29.9 us -> 33 us  [exchanged(): lax.all_to_all(packed.reshape(vir_count * tile_total, rows, block), ('vir...]
where the time goes in v17:
time: 218 us; the launch traced here: 217 us
  waiting for transfers between devices  83.9 us (38%)
  Pallas kernels  62.6 us (29%)
  blocking collectives  42.6 us (20%)
  between operations  13.5 us (6%)
  starting transfers between devices  10 us (5%)
  other arithmetic  2.69 us (1%)
    all_gather x1, waiting for transfers between devices, body(): slabs.append(lax.all_gather(part, 'occ', axis=0, tiled=True))  50.8 us
    all_gather x1, blocking collectives, body(): slabs = [lax.all_gather(coded, 'occ', axis=0, tiled=True)]  42.6 us
    pallas_call x2, Pallas kernels, ladder_call(): pl.pallas_call(functools.partial(ladder_kernel, tile_total, vir_count, ch...  34.5 us
    all_to_all x2, waiting for transfers between devices, exchanged(): lax.all_to_all(packed.reshape(vir_count * tile_total, rows, block), ('vir...  33 us
    pallas_call x2, Pallas kernels, update_call(): pl.pallas_call(functools.partial(update_kernel, vir_count, at_once), grid...  13.3 us
    pallas_call x2, Pallas kernels, direct_call(): pl.pallas_call(direct_kernel, grid=(rows // step_rows,), in_specs=[pl.Blo...  11.1 us
    all_to_all x2, starting transfers between devices, exchanged(): lax.all_to_all(packed.reshape(vir_count * tile_total, rows, block), ('vir...  10 us
  transfers between devices with their start and end apart: 3, of which 3 were waited for; matrix products, arithmetic and copies ran while one was open for 2% of the time, Pallas kernels for 24%

profile of v17, /device:TPU:0, one launch (start us, length us, event | category | flops | bytes accessed | tf_op | source)
XLA Modules:
  0.0 217.0 jit_solution(8731142989951170263)
XLA Ops:
  6.5 0.0 copy-start.1
  6.5 0.0 all-gather.3.cloned.1.call-start
  6.5 3.7 %screen.1 = (s16[528,512]{1,0:T(8,128)(2,1)}, bf16[512,512]{1,0:T(8,128)(2,1)}) custom-call(s32[4,4]{1,0:T(4,128)} %int_mask.1, bf16[512,1024]{1,0:T(8,128)(2,1)} %slab_ref.1), custom_call_target="tpu_custom_call" | custom-call | tf_op jit(solution)/shard_map/screen/pallas_call | solution.py:77
  10.2 42.6 %all-gather.4.gathered_ref = s16[4224,512]{1,0:T(8,128)(2,1)} all-gather(s16[528,512]{1,0:T(8,128)(2,1)} %get-tuple-element.13), channel_id=1, replica_groups=mesh['occ'=8,'vir'=4] {'occ'}, dimensions={0}, use_global_device_ids=true | all-gather | bytes 4866048 | tf_op jit(solution)/shard_map/all_gather | solution.py:307
  52.8 0.0 all-gather.3.cloned.1.call-update
  52.8 0.0 copy-done.1
  52.8 0.7 copy.9.amp_mask
  53.5 18.0 %ladder.3 = (f32[2,2048,256]{2,1,0:T(8,128)}, s16[4,8,264,128]{3,2,1,0:T(8,128)(2,1)}) custom-call(s32[8,4]{1,0:T(8,128)} %copy.9.amp_mask, s32[8]{0:T(128)} %numbers.3, bf16[2048,4096]{1,0:T(8,128)(2,1)} %rows_ref.3, s16[4224,512]{1,0:T(8,128)(2,1)} %all-gather.4.gathered_ref), custom_call_target="tpu_custom_call" | custom-call | flops 8589934592 | bytes 27262976 | tf_op jit(solution)/shard_map/ladder/pallas_call | solution.py:174
  71.6 6.0 %all-to-all-start.1 = ((s16[32,264,128]{2,1,0:T(8,128)(2,1)}), s16[32,264,128]{2,1,0:T(8,128)(2,1)S(1)}, u32[]{:S(2)}, u32[]{:S(2)}) async-start(s16[32,264,128]{2,1,0:T(8,128)(2,1)} %bitcast.12), calls=%async_computation.1 | async-start | bytes 4325376 | tf_op jit(solution)/shard_map/all_to_all | solution.py:301
  77.6 50.8 %all-gather.3.cloned.1.call-done.gathered_ref = bf16[4096,512]{1,0:T(8,128)(2,1)} async-done(((bf16[512,512]{1,0:T(8,128)(2,1)}), bf16[4096,512]{1,0:T(8,128)(2,1)}) %all-gather.3.cloned.1.call-update) | async-done | bytes 4194320 | tf_op jit(solution)/shard_map/all_gather | solution.py:310
  128.4 16.5 %ladder.2 = (f32[2,2048,256]{2,1,0:T(8,128)}, s16[4,8,264,128]{3,2,1,0:T(8,128)(2,1)}) custom-call(s32[8,4]{1,0:T(8,128)} %copy.9.amp_mask, s32[8]{0:T(128)} %numbers.3, bf16[2048,4096]{1,0:T(8,128)(2,1)} %rows_ref.3, bf16[4096,512]{1,0:T(8,128)(2,1)} %all-gather.3.cloned.1.call-done.gathered_ref), custom_call_target="tpu_custom_call" | custom-call | flops 8589934592 | bytes 27262976 | tf_op jit(solution)/shard_map/ladder/pallas_call | solution.py:174
  144.9 0.0 copy-start.2
  144.9 0.0 copy-start.3
  144.9 3.1 %all-to-all-done.1 = s16[32,264,128]{2,1,0:T(8,128)(2,1)S(1)} async-done(((s16[32,264,128]{2,1,0:T(8,128)(2,1)}), s16[32,264,128]{2,1,0:T(8,128)(2,1)S(1)}, u32[]{:S(2)}, u32[]{:S(2)}) %all-to-all-start.1) | async-done | bytes 2162720 | tf_op jit(solution)/shard_map/all_to_all | solution.py:301
  148.0 0.0 copy-start
  148.0 4.0 %all-to-all-start = ((s16[32,264,128]{2,1,0:T(8,128)(2,1)}), s16[32,264,128]{2,1,0:T(8,128)(2,1)}, u32[]{:S(2)}, u32[]{:S(2)}) async-start(s16[32,264,128]{2,1,0:T(8,128)(2,1)} %bitcast.11), calls=%async_computation | async-start | bytes 4325376 | tf_op jit(solution)/shard_map/all_to_all | solution.py:301
  152.1 0.0 copy-done.2
  152.1 0.1 reshape.142
  152.2 0.1 add.176
  152.2 0.1 add.177
  152.3 0.0 copy-done.3
  152.3 0.1 dynamic_slice.6
  152.4 0.1 broadcast_add_fusion.1
  152.5 0.7 add.173.vir_ref
  153.2 0.1 add.180
  153.3 0.6 broadcast_add_fusion.occ_ref
  153.9 1.0 fusion.1.spread_ref
  154.9 1.0 fusion.spread_ref
  155.9 5.5 %direct.3.refs_4_.refs_5_.refs_6_.refs_7_ = f32[2048,512]{1,0:T(8,128)} custom-call(bf16[512,512]{1,0:T(8,128)(2,1)} %fusion.1.spread_ref, f32[2,2048,256]{2,1,0:T(8,128)} %get-tuple-element.16.refs_0_, f32[2,2048,256]{2,1,0:T(8,128)} %get-tuple-element.17.refs_1_), custom_call_target="tpu_custom_call" | custom-call | flops 2147483648 | bytes 8388608 | tf_op jit(solution)/shard_map/direct/pallas_call | solution.py:220
  161.4 0.0 copy-done
  161.4 5.6 %direct.2.refs_4_.refs_5_.refs_6_.refs_7_ = f32[2048,512]{1,0:T(8,128)} custom-call(bf16[512,512]{1,0:T(8,128)(2,1)} %fusion.1.spread_ref, f32[2,2048,256]{2,1,0:T(8,128)} %get-tuple-element.16.refs_0_, f32[2,2048,256]{2,1,0:T(8,128)} %get-tuple-element.17.refs_1_), custom_call_target="tpu_custom_call" | custom-call | flops 2147483648 | bytes 8388608 | tf_op jit(solution)/shard_map/direct/pallas_call | solution.py:220
  167.0 6.6 %update.2.refs_8_ = f32[2048,1024]{1,0:T(8,128)} custom-call(bf16[512,512]{1,0:T(8,128)(2,1)} %fusion.spread_ref, f32[1,1024]{1,0:T(1,128)} %add.173.vir_ref, f32[8,1,256]{2,1,0:T(1,128)} %broadcast_add_fusion.occ_ref, s16[4,8,264,128]{3,2,1,0:T(8,128)(2,1)} %bitcast.7, s16[4,8,264,128]{3,2,1,0:T(8,128)(2,1)} %bitcast.8, s16[4,8,264,128]{3,2,1,0:T(8,128)(2,1)} %bitcast.9, ...), custom_call_target="tpu_custom_call" | custom-call | flops 2147483648 | bytes 10485760 | tf_op jit(solution)/shard_map/update/pallas_call | solution.py:273
  173.7 29.9 %all-to-all-done = s16[32,264,128]{2,1,0:T(8,128)(2,1)} async-done(((s16[32,264,128]{2,1,0:T(8,128)(2,1)}), s16[32,264,128]{2,1,0:T(8,128)(2,1)}, u32[]{:S(2)}, u32[]{:S(2)}) %all-to-all-start) | async-done | bytes 2162720 | tf_op jit(solution)/shard_map/all_to_all | solution.py:301
  203.6 6.6 %update.3 = f32[2048,1024]{1,0:T(8,128)} custom-call(bf16[512,512]{1,0:T(8,128)(2,1)} %fusion.spread_ref, f32[1,1024]{1,0:T(1,128)} %add.173.vir_ref, f32[8,1,256]{2,1,0:T(1,128)} %broadcast_add_fusion.occ_ref, s16[4,8,264,128]{3,2,1,0:T(8,128)(2,1)} %bitcast.3.refs_0_.refs_1_.refs_2_.refs_3_, ...), custom_call_target="tpu_custom_call", output_to_operand_aliasing={{}: (11, {})} | custom-call | flops 2147483648 | bytes 10485760 | tf_op jit(solution)/shard_map/update/pallas_call | solution.py:273
  (5 shorter events, 0.0 us)
Async XLA Ops:
  6.5 46.3 %copy-start.1 = (s32[1,8,4]{1,2,0:T(4,128)S(1)}, s32[1,8,4]{1,2,0:T(4,128)}, u32[]{:S(2)}) copy-start(s32[1,8,4]{1,2,0:T(4,128)} %param.8) | copy-start | bytes 388
  6.5 121.9 %all-gather.3.cloned.1.call-start = ((), (), s32[]{:S(2)}) async-start(), calls=%async_computation.2 | async-start | bytes 4718592 | tf_op jit(solution)/shard_map/all_gather | solution.py:310
  71.6 76.5 %all-to-all-start.1 = ((s16[32,264,128]{2,1,0:T(8,128)(2,1)}), s16[32,264,128]{2,1,0:T(8,128)(2,1)S(1)}, u32[]{:S(2)}, u32[]{:S(2)}) async-start(s16[32,264,128]{2,1,0:T(8,128)(2,1)} %bitcast.12), calls=%async_computation.1 | async-start | bytes 4325376 | tf_op jit(solution)/shard_map/all_to_all | solution.py:301
  144.9 7.2 %copy-start.2 = (f32[128]{0:T(128)S(1)}, f32[128]{0:T(128)}, u32[]{:S(2)}) copy-start(f32[128]{0:T(128)} %param.12) | copy-start | bytes 1540
  144.9 7.4 %copy-start.3 = (f32[64]{0:T(128)S(1)}, f32[64]{0:T(128)}, u32[]{:S(2)}) copy-start(f32[64]{0:T(128)} %param.13) | copy-start | bytes 772
  148.0 13.4 %copy-start = (s16[32,264,128]{2,1,0:T(8,128)(2,1)}, s16[32,264,128]{2,1,0:T(8,128)(2,1)S(1)}, u32[]{:S(2)}) copy-start(s16[32,264,128]{2,1,0:T(8,128)(2,1)S(1)} %all-to-all-done.1) | copy-start | bytes 6488068
  148.0 55.5 %all-to-all-start = ((s16[32,264,128]{2,1,0:T(8,128)(2,1)}), s16[32,264,128]{2,1,0:T(8,128)(2,1)}, u32[]{:S(2)}, u32[]{:S(2)}) async-start(s16[32,264,128]{2,1,0:T(8,128)(2,1)} %bitcast.11), calls=%async_computation | async-start | bytes 4325376 | tf_op jit(solution)/shard_map/all_to_all | solution.py:301
Sparse Core Ops, SparseCore 0:
  52.9 75.4 all-gather.2

commit v18 on v16

--- a/solution.py
+++ b/solution.py
@@ -306,7 +306,6 @@
     coded, *later = screen_call(chunks, int_mask, integrals)
     slabs = [lax.all_gather(coded, "occ", axis=0, tiled=True)]
     for part in later:
-        part, _ = lax.optimization_barrier((part, slabs[-1]))
         slabs.append(lax.all_gather(part, "occ", axis=0, tiled=True))
     ladders, arrived = [], []
     for slab in slabs:

time: 215 us -> 228 us (1.060)
  blocking collectives: 42.6 us -> 72.6 us
  waiting for transfers between devices: 81.1 us -> 62.6 us
    all_gather x1, waiting for transfers between devices: 51.2 us -> 0.02 us  [body(): slabs.append(lax.all_gather(part, 'occ', axis=0, tiled=True))]
    all_to_all x2, waiting for transfers between devices: 29.9 us -> 62.6 us  [exchanged(): lax.all_to_all(packed.reshape(tile_total * vir_count, rows, block), ('occ...]
    all_gather x1, blocking collectives: 42.6 us -> 72.6 us  [body(): slabs = [lax.all_gather(coded, 'occ', axis=0, tiled=True)]]
  transfers between devices with their start and end apart: 3 -> 3, of which waited for: 3 -> 2; matrix products, arithmetic and copies ran while one was open for 2% -> 2% of each run, Pallas kernels for 24% -> 23%
where the time goes in v18:
time: 228 us; the launch traced here: 227 us
  blocking collectives  72.6 us (32%)
  waiting for transfers between devices  62.6 us (27%)
  Pallas kernels  61.5 us (27%)
  between operations  13.5 us (6%)
  starting transfers between devices  12.2 us (5%)
  other arithmetic  2.65 us (1%)
  local copies, waits for them, and re-layouts  2.46 us (1%)
    all_gather x1, blocking collectives, body(): slabs = [lax.all_gather(coded, 'occ', axis=0, tiled=True)]  72.6 us
    all_to_all x2, waiting for transfers between devices, exchanged(): lax.all_to_all(packed.reshape(tile_total * vir_count, rows, block), ('occ...  62.6 us
    pallas_call x2, Pallas kernels, ladder_call(): pl.pallas_call(functools.partial(ladder_kernel, tile_total, vir_count, ch...  34.4 us
    pallas_call x2, Pallas kernels, update_call(): pl.pallas_call(functools.partial(update_kernel, vir_count, at_once), grid...  12.3 us
    all_to_all x2, starting transfers between devices, exchanged(): lax.all_to_all(packed.reshape(tile_total * vir_count, rows, block), ('occ...  12.2 us
    pallas_call x2, Pallas kernels, direct_call(): pl.pallas_call(direct_kernel, grid=(rows // step_rows,), in_specs=[pl.Blo...  11.2 us
  transfers between devices with their start and end apart: 3, of which 2 were waited for; matrix products, arithmetic and copies ran while one was open for 2% of the time, Pallas kernels for 23%

profile of v18, /device:TPU:0, one launch (start us, length us, event | category | flops | bytes accessed | tf_op | source)
XLA Modules:
  0.0 227.5 jit_solution(16546900817941251106)
XLA Ops:
  6.5 0.0 all-gather.3.cloned.1.call-start
  6.5 3.7 %screen.1 = (s16[528,512]{1,0:T(8,128)(2,1)}, bf16[512,512]{1,0:T(8,128)(2,1)}) custom-call(s32[4,4]{1,0:T(4,128)} %int_mask.1, bf16[512,1024]{1,0:T(8,128)(2,1)} %slab_ref.1), custom_call_target="tpu_custom_call" | custom-call | tf_op jit(solution)/shard_map/screen/pallas_call | solution.py:77
  10.2 0.0 all-gather.3.cloned.1.call-update
  10.2 1.4 copy.9.amp_mask
  11.6 72.6 %all-gather.4.gathered_ref = s16[4224,512]{1,0:T(8,128)(2,1)} all-gather(s16[528,512]{1,0:T(8,128)(2,1)} %get-tuple-element.13), channel_id=1, replica_groups=mesh['occ'=8,'vir'=4] {'occ'}, dimensions={0}, use_global_device_ids=true | all-gather | bytes 4866048 | tf_op jit(solution)/shard_map/all_gather | solution.py:307
  84.2 17.9 %ladder.3 = (f32[2,2048,256]{2,1,0:T(8,128)}, s16[8,4,264,128]{3,2,1,0:T(8,128)(2,1)}) custom-call(s32[8,4]{1,0:T(8,128)} %copy.9.amp_mask, s32[8]{0:T(128)} %numbers.3, bf16[2048,4096]{1,0:T(8,128)(2,1)} %rows_ref.3, s16[4224,512]{1,0:T(8,128)(2,1)} %all-gather.4.gathered_ref), custom_call_target="tpu_custom_call" | custom-call | flops 8589934592 | bytes 27262976 | tf_op jit(solution)/shard_map/ladder/pallas_call | solution.py:174
  102.1 7.6 %all-to-all-start.1 = ((s16[32,264,128]{2,1,0:T(8,128)(2,1)}), s16[32,264,128]{2,1,0:T(8,128)(2,1)S(1)}, u32[]{:S(2)}, u32[]{:S(2)}) async-start(s16[32,264,128]{2,1,0:T(8,128)(2,1)} %bitcast.12), calls=%async_computation.1 | async-start | bytes 4325376 | tf_op jit(solution)/shard_map/all_to_all | solution.py:301
  109.7 0.0 all-gather.3.cloned.1.call-done.gathered_ref
  109.8 16.5 %ladder.2 = (f32[2,2048,256]{2,1,0:T(8,128)}, s16[8,4,264,128]{3,2,1,0:T(8,128)(2,1)}) custom-call(s32[8,4]{1,0:T(8,128)} %copy.9.amp_mask, s32[8]{0:T(128)} %numbers.3, bf16[2048,4096]{1,0:T(8,128)(2,1)} %rows_ref.3, bf16[4096,512]{1,0:T(8,128)(2,1)} %all-gather.3.cloned.1.call-done.gathered_ref), custom_call_target="tpu_custom_call" | custom-call | flops 8589934592 | bytes 27262976 | tf_op jit(solution)/shard_map/ladder/pallas_call | solution.py:174
  126.3 0.0 copy-start.1
  126.3 0.0 copy-start.2
  126.3 33.6 %all-to-all-done.1 = s16[32,264,128]{2,1,0:T(8,128)(2,1)S(1)} async-done(((s16[32,264,128]{2,1,0:T(8,128)(2,1)}), s16[32,264,128]{2,1,0:T(8,128)(2,1)S(1)}, u32[]{:S(2)}, u32[]{:S(2)}) %all-to-all-start.1) | async-done | bytes 2162720 | tf_op jit(solution)/shard_map/all_to_all | solution.py:301
  159.8 0.0 copy-start
  159.8 4.5 %all-to-all-start = ((s16[32,264,128]{2,1,0:T(8,128)(2,1)}), s16[32,264,128]{2,1,0:T(8,128)(2,1)}, u32[]{:S(2)}, u32[]{:S(2)}) async-start(s16[32,264,128]{2,1,0:T(8,128)(2,1)} %bitcast.11), calls=%async_computation | async-start | bytes 4325376 | tf_op jit(solution)/shard_map/all_to_all | solution.py:301
  164.4 0.0 copy-done.1
  164.4 0.1 reshape.142
  164.5 0.1 add.176
  164.5 0.1 add.177
  164.6 0.0 copy-done.2
  164.6 0.1 dynamic_slice.6
  164.7 0.1 broadcast_add_fusion.1
  164.8 0.7 add.173.vir_ref
  165.5 0.1 add.180
  165.6 0.6 broadcast_add_fusion.occ_ref
  166.2 0.9 fusion.1.spread_ref
  167.1 1.0 fusion.spread_ref
  168.1 5.5 %direct.3.refs_4_.refs_5_.refs_6_.refs_7_ = f32[2048,512]{1,0:T(8,128)} custom-call(bf16[512,512]{1,0:T(8,128)(2,1)} %fusion.1.spread_ref, f32[2,2048,256]{2,1,0:T(8,128)} %get-tuple-element.14.refs_0_, f32[2,2048,256]{2,1,0:T(8,128)} %get-tuple-element.15.refs_1_), custom_call_target="tpu_custom_call" | custom-call | flops 2147483648 | bytes 8388608 | tf_op jit(solution)/shard_map/direct/pallas_call | solution.py:220
  173.7 0.0 copy-done
  173.7 5.6 %direct.2.refs_4_.refs_5_.refs_6_.refs_7_ = f32[2048,512]{1,0:T(8,128)} custom-call(bf16[512,512]{1,0:T(8,128)(2,1)} %fusion.1.spread_ref, f32[2,2048,256]{2,1,0:T(8,128)} %get-tuple-element.14.refs_0_, f32[2,2048,256]{2,1,0:T(8,128)} %get-tuple-element.15.refs_1_), custom_call_target="tpu_custom_call" | custom-call | flops 2147483648 | bytes 8388608 | tf_op jit(solution)/shard_map/direct/pallas_call | solution.py:220
  179.3 6.2 %update.2.refs_8_ = f32[2048,1024]{1,0:T(8,128)} custom-call(bf16[512,512]{1,0:T(8,128)(2,1)} %fusion.spread_ref, f32[1,1024]{1,0:T(1,128)} %add.173.vir_ref, f32[8,1,256]{2,1,0:T(1,128)} %broadcast_add_fusion.occ_ref, s16[8,4,264,128]{3,2,1,0:T(8,128)(2,1)} %bitcast.7, s16[8,4,264,128]{3,2,1,0:T(8,128)(2,1)} %bitcast.8, s16[8,4,264,128]{3,2,1,0:T(8,128)(2,1)} %bitcast.9, ...), custom_call_target="tpu_custom_call" | custom-call | flops 2147483648 | bytes 10485760 | tf_op jit(solution)/shard_map/update/pallas_call | solution.py:273
  185.5 29.0 %all-to-all-done = s16[32,264,128]{2,1,0:T(8,128)(2,1)} async-done(((s16[32,264,128]{2,1,0:T(8,128)(2,1)}), s16[32,264,128]{2,1,0:T(8,128)(2,1)}, u32[]{:S(2)}, u32[]{:S(2)}) %all-to-all-start) | async-done | bytes 2162720 | tf_op jit(solution)/shard_map/all_to_all | solution.py:301
  214.5 6.2 %update.3 = f32[2048,1024]{1,0:T(8,128)} custom-call(bf16[512,512]{1,0:T(8,128)(2,1)} %fusion.spread_ref, f32[1,1024]{1,0:T(1,128)} %add.173.vir_ref, f32[8,1,256]{2,1,0:T(1,128)} %broadcast_add_fusion.occ_ref, s16[8,4,264,128]{3,2,1,0:T(8,128)(2,1)} %bitcast.3.refs_0_.refs_1_.refs_2_.refs_3_, ...), custom_call_target="tpu_custom_call", output_to_operand_aliasing={{}: (11, {})} | custom-call | flops 2147483648 | bytes 10485760 | tf_op jit(solution)/shard_map/update/pallas_call | solution.py:273
  (5 shorter events, 0.0 us)
Async XLA Ops:
  6.5 103.2 %all-gather.3.cloned.1.call-start = ((), (), s32[]{:S(2)}) async-start(), calls=%async_computation.2 | async-start | bytes 4718592 | tf_op jit(solution)/shard_map/all_gather | solution.py:309
  102.1 57.8 %all-to-all-start.1 = ((s16[32,264,128]{2,1,0:T(8,128)(2,1)}), s16[32,264,128]{2,1,0:T(8,128)(2,1)S(1)}, u32[]{:S(2)}, u32[]{:S(2)}) async-start(s16[32,264,128]{2,1,0:T(8,128)(2,1)} %bitcast.12), calls=%async_computation.1 | async-start | bytes 4325376 | tf_op jit(solution)/shard_map/all_to_all | solution.py:301
  126.3 38.1 %copy-start.1 = (f32[128]{0:T(128)S(1)}, f32[128]{0:T(128)}, u32[]{:S(2)}) copy-start(f32[128]{0:T(128)} %param.12) | copy-start | bytes 1540
  126.3 38.3 %copy-start.2 = (f32[64]{0:T(128)S(1)}, f32[64]{0:T(128)}, u32[]{:S(2)}) copy-start(f32[64]{0:T(128)} %param.13) | copy-start | bytes 772
  159.8 13.8 %copy-start = (s16[32,264,128]{2,1,0:T(8,128)(2,1)}, s16[32,264,128]{2,1,0:T(8,128)(2,1)S(1)}, u32[]{:S(2)}) copy-start(s16[32,264,128]{2,1,0:T(8,128)(2,1)S(1)} %all-to-all-done.1) | copy-start | bytes 6488068
  159.8 54.6 %all-to-all-start = ((s16[32,264,128]{2,1,0:T(8,128)(2,1)}), s16[32,264,128]{2,1,0:T(8,128)(2,1)}, u32[]{:S(2)}, u32[]{:S(2)}) async-start(s16[32,264,128]{2,1,0:T(8,128)(2,1)} %bitcast.11), calls=%async_computation | async-start | bytes 4325376 | tf_op jit(solution)/shard_map/all_to_all | solution.py:301
Sparse Core Ops, SparseCore 0:
  10.4 78.0 all-gather.2

commit v19 on v18

--- a/solution.py
+++ b/solution.py
@@ -50,7 +50,7 @@
     place = lax.broadcasted_iota(jnp.int32, (slab_cols, cols), 1)
     to = lax.broadcasted_iota(jnp.int32, (1, cols), 1)
     second = lax.broadcasted_iota(jnp.int32, (slab_rows, 1), 0) % W >= VT
-    for chunk in range(1 + len(later_refs)):
+    for chunk in range(span // part):
         right = to // (part * span) * span + chunk * part + to // part % part >= VT
         kept = [
             jnp.where(right, int_mask[label, col_label + 1], int_mask[label, col_label])
@@ -60,7 +60,10 @@
         moved = dot(slab_ref[...], ones.astype(jnp.float32).astype(jnp.bfloat16))
         moved = jnp.where(jnp.where(second, kept[1], kept[0]) > 0, moved, 0.0)
         if chunk:
-            later_refs[chunk - 1][...] = moved.astype(jnp.bfloat16)
+            at = 0
+            for later_ref in later_refs:
+                later_ref[...] = moved[:, at : at + later_ref.shape[1]].astype(jnp.bfloat16)
+                at += later_ref.shape[1]
         else:
             most = jnp.maximum(jnp.max(jnp.abs(moved), axis=0, keepdims=True), 1e-30)
             code = jnp.floor(jnp.log2(most)) + 1.0
@@ -73,24 +76,28 @@
 def screen_call(chunks, int_mask, integrals):
     slab_rows, slab_cols = integrals.shape
     cols = slab_cols // chunks
+    later_cols = [cols // 4, cols - cols // 4] if chunks > 1 else []
     vmem = pl.BlockSpec(memory_space=pltpu.VMEM)
     return pl.pallas_call(
         functools.partial(screen_kernel, slab_cols // W // chunks),
         in_specs=[pl.BlockSpec(memory_space=pltpu.SMEM), vmem],
-        out_specs=[vmem] * chunks,
+        out_specs=[vmem] * (1 + len(later_cols)),
         out_shape=[jax.ShapeDtypeStruct((slab_rows + CODE_ROWS, cols), jnp.int16)]
-        + [jax.ShapeDtypeStruct((slab_rows, cols), integrals.dtype)] * (chunks - 1),
+        + [jax.ShapeDtypeStruct((slab_rows, each), integrals.dtype) for each in later_cols],
         compiler_params=pltpu.CompilerParams(vmem_limit_bytes=VMEM_LIMIT),
         name="screen",
     )(int_mask, integrals)
 
 
-def ladder_kernel(tile_total, vir_count, chunks, coded, amp_mask, numbers, rows_ref, gathered_ref, *refs):
+def ladder_kernel(tile_total, vir_count, chunks, coded, parts, amp_mask, numbers, rows_ref, *refs):
+    gathered_refs, refs = refs[:parts], refs[parts:]
     ladder_ref, packed_ref, product = refs[:3]
-    slab_ref, stage, sems = refs[3:] if coded else (gathered_ref, None, None)
+    slab_refs = gathered_refs
+    if coded:
+        slab_refs, stage, sems = refs[3:4], refs[4], refs[5]
     step = pl.program_id(0)
-    cols = slab_ref.shape[1]
-    slab_rows = slab_ref.shape[0] // tile_total
+    cols = product.shape[1]
+    slab_rows = slab_refs[0].shape[0] // tile_total
     shard_rows = slab_rows + CODE_ROWS
     block = cols // vir_count
     lanes = block // chunks
@@ -105,12 +112,16 @@
             jnp.where(left, amp_mask[tile, 2], amp_mask[tile, 3]),
         )
         keep = keep.astype(jnp.float32).astype(jnp.bfloat16)
-        product[...] = dot(rows_ref[...] * keep, slab_ref[...])
+        screened = rows_ref[...] * keep
+        at = 0
+        for slab_ref in slab_refs:
+            product[:, at : at + slab_ref.shape[1]] = dot(screened, slab_ref[...])
+            at += slab_ref.shape[1]
 
     def decode():
         def copy_of(shard):
             at = pl.ds(pl.multiple_of(shard * shard_rows, CODE_ROWS), shard_rows)
-            return pltpu.make_async_copy(gathered_ref.at[at, :], stage.at[at, :], sems.at[shard])
+            return pltpu.make_async_copy(gathered_refs[0].at[at, :], stage.at[at, :], sems.at[shard])
 
         for shard in range(tile_total):
             copy_of(shard).start()
@@ -122,7 +133,7 @@
             values = stage[pl.ds(at, slab_rows), :].astype(jnp.int32).astype(jnp.float32)
             scale = jnp.exp2(code.astype(jnp.int32).astype(jnp.float32)[:1] - SLAB_BITS)
             to = pl.ds(pl.multiple_of(shard * slab_rows, slab_rows), slab_rows)
-            slab_ref[to, :] = (values * scale).astype(jnp.bfloat16)
+            slab_refs[0][to, :] = (values * scale).astype(jnp.bfloat16)
             return carry
 
         lax.fori_loop(0, tile_total, use, 0)
@@ -164,21 +175,24 @@
 
 
 def ladder_call(tile_total, vir_count, chunks, amp_mask, numbers, amplitudes, slab):
-    coded = slab.dtype == jnp.int16
-    cols = slab.shape[1]
+    coded = slab[0].dtype == jnp.int16
+    cols = sum(part.shape[1] for part in slab)
     block = cols // vir_count
     smem = pl.BlockSpec(memory_space=pltpu.SMEM)
     rows = tile_total * PAIR_SQ
     before = lambda step: jnp.maximum(step - 1, 0)
     packed_block = (vir_count, PAIR_SQ + EXCHANGE_CODE_ROWS, block)
     return pl.pallas_call(
-        functools.partial(ladder_kernel, tile_total, vir_count, chunks, coded),
+        functools.partial(ladder_kernel, tile_total, vir_count, chunks, coded, len(slab)),
         grid=(tile_total + 1,),
         in_specs=[
             smem,
             smem,
             pl.BlockSpec((PAIR_SQ, W * W), lambda step: (jnp.minimum(step, tile_total - 1), 0)),
-            pl.BlockSpec(memory_space=pl.ANY) if coded else pl.BlockSpec((W * W, cols), lambda step: (0, 0)),
+            *[
+                pl.BlockSpec(memory_space=pl.ANY) if coded else pl.BlockSpec(part.shape, lambda step: (0, 0))
+                for part in slab
+            ],
         ],
         out_specs=[
             pl.BlockSpec((chunks, PAIR_SQ, cols // chunks), lambda step: (0, before(step), 0)),
@@ -191,7 +205,7 @@
         scratch_shapes=[pltpu.VMEM((PAIR_SQ, cols), jnp.float32)]
         + [
             pltpu.VMEM((W * W, cols), jnp.bfloat16),
-            pltpu.VMEM(slab.shape, slab.dtype),
+            pltpu.VMEM(slab[0].shape, slab[0].dtype),
             pltpu.SemaphoreType.DMA((tile_total,)),
         ]
         * coded,
@@ -202,7 +216,7 @@
             transcendentals=0,
         ),
         name="ladder",
-    )(amp_mask, numbers, amplitudes, slab)
+    )(amp_mask, numbers, amplitudes, *slab)
 
 
 def moved_columns(values, spread_ref):
@@ -304,9 +318,8 @@
         return moved.reshape(tile_total, vir_count, rows, block)
 
     coded, *later = screen_call(chunks, int_mask, integrals)
-    slabs = [lax.all_gather(coded, "occ", axis=0, tiled=True)]
-    for part in later:
-        slabs.append(lax.all_gather(part, "occ", axis=0, tiled=True))
+    later = [lax.all_gather(part, "occ", axis=0, tiled=True) for part in later]
+    slabs = [[lax.all_gather(coded, "occ", axis=0, tiled=True)]] + [later] * (chunks - 1)
     ladders, arrived = [], []
     for slab in slabs:
         ladder, packed = ladder_call(

time: 228 us -> 216 us (0.947)
  blocking collectives: 72.6 us -> 59.9 us
  Pallas kernels: 61.5 us -> 64.2 us
    all_gather x1, blocking collectives: 72.6 us -> 59.9 us  [body(): lax.all_gather(coded, 'occ', axis=0, tiled=True)]
    all_to_all x2, waiting for transfers between devices: 62.6 us -> 59.9 us  [exchanged(): lax.all_to_all(packed.reshape(tile_total * vir_count, rows, block), ('occ...]
    pallas_call x2, Pallas kernels: 34.4 us -> 37 us  [ladder_call(): pl.pallas_call(functools.partial(ladder_kernel, tile_total, vir_count, ch...]
  transfers between devices with their start and end apart: 3 -> 4, of which waited for: 2 -> 2; matrix products, arithmetic and copies ran while one was open for 2% -> 2% of each run, Pallas kernels for 23% -> 25%
where the time goes in v19:
time: 216 us
  Pallas kernels  64.2 us (30%)
  waiting for transfers between devices  60.6 us (28%)
  blocking collectives  59.9 us (28%)
  between operations  13.5 us (6%)
  starting transfers between devices  12.3 us (6%)
  other arithmetic  2.65 us (1%)
  local copies, waits for them, and re-layouts  2.44 us (1%)
    all_gather x1, blocking collectives, body(): lax.all_gather(coded, 'occ', axis=0, tiled=True)  59.9 us
    all_to_all x2, waiting for transfers between devices, exchanged(): lax.all_to_all(packed.reshape(tile_total * vir_count, rows, block), ('occ...  59.9 us
    pallas_call x2, Pallas kernels, ladder_call(): pl.pallas_call(functools.partial(ladder_kernel, tile_total, vir_count, ch...  37 us
    pallas_call x2, Pallas kernels, update_call(): pl.pallas_call(functools.partial(update_kernel, vir_count, at_once), grid...  12.3 us
    all_to_all x2, starting transfers between devices, exchanged(): lax.all_to_all(packed.reshape(tile_total * vir_count, rows, block), ('occ...  12.2 us
    pallas_call x2, Pallas kernels, direct_call(): pl.pallas_call(direct_kernel, grid=(rows // step_rows,), in_specs=[pl.Blo...  11.1 us
  transfers between devices with their start and end apart: 4, of which 2 were waited for; matrix products, arithmetic and copies ran while one was open for 2% of the time, Pallas kernels for 25%

profile of v19, /device:TPU:0, one launch (start us, length us, event | category | flops | bytes accessed | tf_op | source)
XLA Modules:
  0.0 215.6 jit_solution(16938059132760722511)
XLA Ops:
  6.5 0.0 all-gather.4.cloned.1.call-start
  6.5 3.7 %screen.1 = (s16[528,512]{1,0:T(8,128)(2,1)}, bf16[512,128]{1,0:T(8,128)(2,1)}, bf16[512,384]{1,0:T(8,128)(2,1)}) custom-call(s32[4,4]{1,0:T(4,128)} %int_mask.1, bf16[512,1024]{1,0:T(8,128)(2,1)} %slab_ref.1), custom_call_target="tpu_custom_call" | custom-call | tf_op jit(solution)/shard_map/screen/pallas_call | solution.py:81
  10.2 0.0 all-gather.4.cloned.1.call-update
  10.2 0.0 all-gather.6.cloned.1.call-start
  10.3 0.7 all-gather.6.cloned.1.call-update
  11.0 1.3 copy.9.amp_mask
  12.3 59.9 %all-gather.7.refs_0_ = s16[4224,512]{1,0:T(8,128)(2,1)} all-gather(s16[528,512]{1,0:T(8,128)(2,1)} %get-tuple-element.15), channel_id=1, replica_groups=mesh['occ'=8,'vir'=4] {'occ'}, dimensions={0}, use_global_device_ids=true | all-gather | bytes 4866048 | tf_op jit(solution)/shard_map/all_gather | solution.py:322
  72.2 17.8 %ladder.3 = (f32[2,2048,256]{2,1,0:T(8,128)}, s16[8,4,264,128]{3,2,1,0:T(8,128)(2,1)}) custom-call(s32[8,4]{1,0:T(8,128)} %copy.9.amp_mask, s32[8]{0:T(128)} %numbers.3, bf16[2048,4096]{1,0:T(8,128)(2,1)} %rows_ref.3, s16[4224,512]{1,0:T(8,128)(2,1)} %all-gather.7.refs_0_), custom_call_target="tpu_custom_call" | custom-call | flops 8589934592 | bytes 27262976 | tf_op jit(solution)/shard_map/ladder/pallas_call | solution.py:185
  90.1 7.7 %all-to-all-start.1 = ((s16[32,264,128]{2,1,0:T(8,128)(2,1)}), s16[32,264,128]{2,1,0:T(8,128)(2,1)S(1)}, u32[]{:S(2)}, u32[]{:S(2)}) async-start(s16[32,264,128]{2,1,0:T(8,128)(2,1)} %bitcast.12), calls=%async_computation.1 | async-start | bytes 4325376 | tf_op jit(solution)/shard_map/all_to_all | solution.py:315
  97.8 0.0 all-gather.4.cloned.1.call-done.refs_0_
  97.9 0.0 all-gather.6.cloned.1.call-done.refs_1_
  97.9 19.2 %ladder.2 = (f32[2,2048,256]{2,1,0:T(8,128)}, s16[8,4,264,128]{3,2,1,0:T(8,128)(2,1)}) custom-call(s32[8,4]{1,0:T(8,128)} %copy.9.amp_mask, s32[8]{0:T(128)} %numbers.3, bf16[2048,4096]{1,0:T(8,128)(2,1)} %rows_ref.3, bf16[4096,128]{1,0:T(8,128)(2,1)} %all-gather.4.cloned.1.call-done.refs_0_, bf16[4096,384]{1,0:T(8,128)(2,1)} %all-gather.6.cloned.1.call-done.refs_1_), custom_call_target="tpu_custom_call" | custom-call | flops 8589934592 | bytes 27262976 | tf_op jit(solution)/shard_map/ladder/pallas_call | solution.py:185
  117.1 0.0 copy-start.1
  117.1 0.0 copy-start.2
  117.1 30.9 %all-to-all-done.1 = s16[32,264,128]{2,1,0:T(8,128)(2,1)S(1)} async-done(((s16[32,264,128]{2,1,0:T(8,128)(2,1)}), s16[32,264,128]{2,1,0:T(8,128)(2,1)S(1)}, u32[]{:S(2)}, u32[]{:S(2)}) %all-to-all-start.1) | async-done | bytes 2162720 | tf_op jit(solution)/shard_map/all_to_all | solution.py:315
  147.9 0.0 copy-start
  147.9 4.5 %all-to-all-start = ((s16[32,264,128]{2,1,0:T(8,128)(2,1)}), s16[32,264,128]{2,1,0:T(8,128)(2,1)}, u32[]{:S(2)}, u32[]{:S(2)}) async-start(s16[32,264,128]{2,1,0:T(8,128)(2,1)} %bitcast.11), calls=%async_computation | async-start | bytes 4325376 | tf_op jit(solution)/shard_map/all_to_all | solution.py:315
  152.5 0.0 copy-done.1
  152.5 0.1 reshape.142
  152.6 0.1 add.176
  152.6 0.1 add.177
  152.7 0.0 copy-done.2
  152.7 0.1 dynamic_slice.6
  152.8 0.1 broadcast_add_fusion.1
  152.9 0.7 add.173.vir_ref
  153.6 0.1 add.180
  153.7 0.6 broadcast_add_fusion.occ_ref
  154.3 0.9 fusion.1.spread_ref
  155.2 1.0 fusion.spread_ref
  156.2 5.5 %direct.3.refs_4_.refs_5_.refs_6_.refs_7_ = f32[2048,512]{1,0:T(8,128)} custom-call(bf16[512,512]{1,0:T(8,128)(2,1)} %fusion.1.spread_ref, f32[2,2048,256]{2,1,0:T(8,128)} %get-tuple-element.16.refs_0_, f32[2,2048,256]{2,1,0:T(8,128)} %get-tuple-element.17.refs_1_), custom_call_target="tpu_custom_call" | custom-call | flops 2147483648 | bytes 8388608 | tf_op jit(solution)/shard_map/direct/pallas_call | solution.py:234
  161.8 0.0 copy-done
  161.8 5.6 %direct.2.refs_4_.refs_5_.refs_6_.refs_7_ = f32[2048,512]{1,0:T(8,128)} custom-call(bf16[512,512]{1,0:T(8,128)(2,1)} %fusion.1.spread_ref, f32[2,2048,256]{2,1,0:T(8,128)} %get-tuple-element.16.refs_0_, f32[2,2048,256]{2,1,0:T(8,128)} %get-tuple-element.17.refs_1_), custom_call_target="tpu_custom_call" | custom-call | flops 2147483648 | bytes 8388608 | tf_op jit(solution)/shard_map/direct/pallas_call | solution.py:234
  167.4 6.2 %update.2.refs_8_ = f32[2048,1024]{1,0:T(8,128)} custom-call(bf16[512,512]{1,0:T(8,128)(2,1)} %fusion.spread_ref, f32[1,1024]{1,0:T(1,128)} %add.173.vir_ref, f32[8,1,256]{2,1,0:T(1,128)} %broadcast_add_fusion.occ_ref, s16[8,4,264,128]{3,2,1,0:T(8,128)(2,1)} %bitcast.7, s16[8,4,264,128]{3,2,1,0:T(8,128)(2,1)} %bitcast.8, s16[8,4,264,128]{3,2,1,0:T(8,128)(2,1)} %bitcast.9, ...), custom_call_target="tpu_custom_call" | custom-call | flops 2147483648 | bytes 10485760 | tf_op jit(solution)/shard_map/update/pallas_call | solution.py:287
  173.5 29.0 %all-to-all-done = s16[32,264,128]{2,1,0:T(8,128)(2,1)} async-done(((s16[32,264,128]{2,1,0:T(8,128)(2,1)}), s16[32,264,128]{2,1,0:T(8,128)(2,1)}, u32[]{:S(2)}, u32[]{:S(2)}) %all-to-all-start) | async-done | bytes 2162720 | tf_op jit(solution)/shard_map/all_to_all | solution.py:315
  202.6 6.2 %update.3 = f32[2048,1024]{1,0:T(8,128)} custom-call(bf16[512,512]{1,0:T(8,128)(2,1)} %fusion.spread_ref, f32[1,1024]{1,0:T(1,128)} %add.173.vir_ref, f32[8,1,256]{2,1,0:T(1,128)} %broadcast_add_fusion.occ_ref, s16[8,4,264,128]{3,2,1,0:T(8,128)(2,1)} %bitcast.3.refs_0_.refs_1_.refs_2_.refs_3_, ...), custom_call_target="tpu_custom_call", output_to_operand_aliasing={{}: (11, {})} | custom-call | flops 2147483648 | bytes 10485760 | tf_op jit(solution)/shard_map/update/pallas_call | solution.py:287
  (5 shorter events, 0.0 us)
Async XLA Ops:
  6.5 91.3 %all-gather.4.cloned.1.call-start = ((), (), s32[]{:S(2)}) async-start(), calls=%async_computation.2 | async-start | bytes 1179648 | tf_op jit(solution)/shard_map/all_gather | solution.py:321
  10.2 87.6 %all-gather.6.cloned.1.call-start = ((), (), s32[]{:S(2)}) async-start(), calls=%async_computation.3 | async-start | bytes 3538944 | tf_op jit(solution)/shard_map/all_gather | solution.py:321
  90.1 57.8 %all-to-all-start.1 = ((s16[32,264,128]{2,1,0:T(8,128)(2,1)}), s16[32,264,128]{2,1,0:T(8,128)(2,1)S(1)}, u32[]{:S(2)}, u32[]{:S(2)}) async-start(s16[32,264,128]{2,1,0:T(8,128)(2,1)} %bitcast.12), calls=%async_computation.1 | async-start | bytes 4325376 | tf_op jit(solution)/shard_map/all_to_all | solution.py:315
  117.1 35.4 %copy-start.1 = (f32[128]{0:T(128)S(1)}, f32[128]{0:T(128)}, u32[]{:S(2)}) copy-start(f32[128]{0:T(128)} %param.12) | copy-start | bytes 1540
  117.1 35.6 %copy-start.2 = (f32[64]{0:T(128)S(1)}, f32[64]{0:T(128)}, u32[]{:S(2)}) copy-start(f32[64]{0:T(128)} %param.13) | copy-start | bytes 772
  147.9 13.8 %copy-start = (s16[32,264,128]{2,1,0:T(8,128)(2,1)}, s16[32,264,128]{2,1,0:T(8,128)(2,1)S(1)}, u32[]{:S(2)}) copy-start(s16[32,264,128]{2,1,0:T(8,128)(2,1)S(1)} %all-to-all-done.1) | copy-start | bytes 6488068
  147.9 54.6 %all-to-all-start = ((s16[32,264,128]{2,1,0:T(8,128)(2,1)}), s16[32,264,128]{2,1,0:T(8,128)(2,1)}, u32[]{:S(2)}, u32[]{:S(2)}) async-start(s16[32,264,128]{2,1,0:T(8,128)(2,1)} %bitcast.11), calls=%async_computation | async-start | bytes 4325376 | tf_op jit(solution)/shard_map/all_to_all | solution.py:315
Sparse Core Ops, SparseCore 0:
  10.4 32.5 all-gather.3
  44.6 44.7 all-gather.5

commit v20 on v19

--- a/solution.py
+++ b/solution.py
@@ -15,6 +15,7 @@
 CODE_ROWS = 16
 EXCHANGE_CODE_ROWS = 8
 AT_ONCE = 4
+CODED_PARTS = 2
 SLAB_BITS = 14.0
 TOP = 32700.0
 STEPS = 8.0
@@ -38,9 +39,10 @@
     return jnp.exp2(code * (1.0 / STEPS))
 
 
-def screen_kernel(part, int_mask, slab_ref, coded_ref, *later_refs):
+def screen_kernel(part, int_mask, slab_ref, *refs):
+    coded_refs, later_refs = refs[:CODED_PARTS], refs[CODED_PARTS:]
     slab_rows, slab_cols = slab_ref.shape
-    cols = coded_ref.shape[1]
+    cols = sum(ref.shape[1] for ref in coded_refs)
     span = slab_cols // W
     row_label = lax.axis_index("occ") * slab_rows // W // VT * NVT
     col_label = lax.axis_index("vir") * slab_cols // W // VT * NVT
@@ -60,30 +62,31 @@
         moved = dot(slab_ref[...], ones.astype(jnp.float32).astype(jnp.bfloat16))
         moved = jnp.where(jnp.where(second, kept[1], kept[0]) > 0, moved, 0.0)
         if chunk:
-            at = 0
-            for later_ref in later_refs:
-                later_ref[...] = moved[:, at : at + later_ref.shape[1]].astype(jnp.bfloat16)
-                at += later_ref.shape[1]
+            later_refs[chunk - 1][...] = moved.astype(jnp.bfloat16)
         else:
             most = jnp.maximum(jnp.max(jnp.abs(moved), axis=0, keepdims=True), 1e-30)
             code = jnp.floor(jnp.log2(most)) + 1.0
             coded = jnp.round(moved * jnp.exp2(SLAB_BITS - code)).astype(jnp.int32).astype(jnp.int16)
             code_rows = jnp.broadcast_to(code.astype(jnp.int32), (CODE_ROWS, cols)).astype(jnp.int16)
-            coded_ref[:slab_rows, :] = coded
-            coded_ref[slab_rows:, :] = code_rows
+            at = 0
+            for coded_ref in coded_refs:
+                end = at + coded_ref.shape[1]
+                coded_ref[:slab_rows, :] = coded[:, at:end]
+                coded_ref[slab_rows:, :] = code_rows[:, at:end]
+                at = end
 
 
 def screen_call(chunks, int_mask, integrals):
     slab_rows, slab_cols = integrals.shape
     cols = slab_cols // chunks
-    later_cols = [cols // 4, cols - cols // 4] if chunks > 1 else []
+    coded_cols = [cols - cols // 4, cols // 4]
     vmem = pl.BlockSpec(memory_space=pltpu.VMEM)
     return pl.pallas_call(
         functools.partial(screen_kernel, slab_cols // W // chunks),
         in_specs=[pl.BlockSpec(memory_space=pltpu.SMEM), vmem],
-        out_specs=[vmem] * (1 + len(later_cols)),
-        out_shape=[jax.ShapeDtypeStruct((slab_rows + CODE_ROWS, cols), jnp.int16)]
-        + [jax.ShapeDtypeStruct((slab_rows, each), integrals.dtype) for each in later_cols],
+        out_specs=[vmem] * (CODED_PARTS + chunks - 1),
+        out_shape=[jax.ShapeDtypeStruct((slab_rows + CODE_ROWS, each), jnp.int16) for each in coded_cols]
+        + [jax.ShapeDtypeStruct((slab_rows, cols), integrals.dtype)] * (chunks - 1),
         compiler_params=pltpu.CompilerParams(vmem_limit_bytes=VMEM_LIMIT),
         name="screen",
     )(int_mask, integrals)
@@ -94,7 +97,7 @@
     ladder_ref, packed_ref, product = refs[:3]
     slab_refs = gathered_refs
     if coded:
-        slab_refs, stage, sems = refs[3:4], refs[4], refs[5]
+        slab_refs, sems, stages = refs[3:4], refs[4], refs[5:]
     step = pl.program_id(0)
     cols = product.shape[1]
     slab_rows = slab_refs[0].shape[0] // tile_total
@@ -119,21 +122,25 @@
             at += slab_ref.shape[1]
 
     def decode():
-        def copy_of(shard):
+        def copy_of(n, shard):
             at = pl.ds(pl.multiple_of(shard * shard_rows, CODE_ROWS), shard_rows)
-            return pltpu.make_async_copy(gathered_refs[0].at[at, :], stage.at[at, :], sems.at[shard])
+            return pltpu.make_async_copy(gathered_refs[n].at[at, :], stages[n].at[at, :], sems.at[n, shard])
 
         for shard in range(tile_total):
-            copy_of(shard).start()
+            for n in range(parts):
+                copy_of(n, shard).start()
 
         def use(shard, carry):
-            copy_of(shard).wait()
             at = pl.multiple_of(shard * shard_rows, CODE_ROWS)
-            code = stage[pl.ds(pl.multiple_of(at + slab_rows, CODE_ROWS), CODE_ROWS), :]
-            values = stage[pl.ds(at, slab_rows), :].astype(jnp.int32).astype(jnp.float32)
-            scale = jnp.exp2(code.astype(jnp.int32).astype(jnp.float32)[:1] - SLAB_BITS)
             to = pl.ds(pl.multiple_of(shard * slab_rows, slab_rows), slab_rows)
-            slab_refs[0][to, :] = (values * scale).astype(jnp.bfloat16)
+            col = 0
+            for n, stage in enumerate(stages):
+                copy_of(n, shard).wait()
+                code = stage[pl.ds(pl.multiple_of(at + slab_rows, CODE_ROWS), CODE_ROWS), :]
+                values = stage[pl.ds(at, slab_rows), :].astype(jnp.int32).astype(jnp.float32)
+                scale = jnp.exp2(code.astype(jnp.int32).astype(jnp.float32)[:1] - SLAB_BITS)
+                slab_refs[0][to, col : col + stage.shape[1]] = (values * scale).astype(jnp.bfloat16)
+                col += stage.shape[1]
             return carry
 
         lax.fori_loop(0, tile_total, use, 0)
@@ -205,8 +212,8 @@
         scratch_shapes=[pltpu.VMEM((PAIR_SQ, cols), jnp.float32)]
         + [
             pltpu.VMEM((W * W, cols), jnp.bfloat16),
-            pltpu.VMEM(slab[0].shape, slab[0].dtype),
-            pltpu.SemaphoreType.DMA((tile_total,)),
+            pltpu.SemaphoreType.DMA((len(slab), tile_total)),
+            *[pltpu.VMEM(part.shape, part.dtype) for part in slab],
         ]
         * coded,
         compiler_params=pltpu.CompilerParams(vmem_limit_bytes=VMEM_LIMIT),
@@ -317,9 +324,11 @@
         )
         return moved.reshape(tile_total, vir_count, rows, block)
 
-    coded, *later = screen_call(chunks, int_mask, integrals)
-    later = [lax.all_gather(part, "occ", axis=0, tiled=True) for part in later]
-    slabs = [[lax.all_gather(coded, "occ", axis=0, tiled=True)]] + [later] * (chunks - 1)
+    screened = screen_call(chunks, int_mask, integrals)
+    first = lax.all_gather(screened[0], "occ", axis=0, tiled=True)
+    *screened, first = lax.optimization_barrier((*screened[1:], first))
+    rest = [lax.all_gather(part, "occ", axis=0, tiled=True) for part in screened]
+    slabs = [[first, rest[0]]] + [[part] for part in rest[1:]]
     ladders, arrived = [], []
     for slab in slabs:
         ladder, packed = ladder_call(

time: 216 us -> 210 us (0.972)
  starting transfers between devices: 12.3 us -> 7.76 us
  waiting for transfers between devices: 60.6 us -> 64.6 us
  blocking collectives: 59.9 us -> 57.1 us
  Pallas kernels: 64.2 us -> 61.5 us
    all_gather x2 -> x1, waiting for transfers between devices: 0.04 us -> 7.89 us  [body(): lax.all_gather(part, 'occ', axis=0, tiled=True)]
    all_to_all x2, starting transfers between devices: 12.2 us -> 7.76 us  [exchanged(): lax.all_to_all(packed.reshape(tile_total * vir_count, rows, block), ('occ...]
    all_to_all x2, waiting for transfers between devices: 59.9 us -> 56.7 us  [exchanged(): lax.all_to_all(packed.reshape(tile_total * vir_count, rows, block), ('occ...]
    all_gather x1 -> x2, blocking collectives: 59.9 us -> 57.1 us  [the longest x1 34.3 us: body(): first = lax.all_gather(screened[0], 'occ', axis=0, tiled=True)]
    pallas_call x2, Pallas kernels: 37 us -> 34.4 us  [ladder_call(): pl.pallas_call(functools.partial(ladder_kernel, tile_total, vir_count, ch...]
  transfers between devices with their start and end apart: 4 -> 3, of which waited for: 2 -> 3; matrix products, arithmetic and copies ran while one was open for 2% -> 2% of each run, Pallas kernels for 25% -> 25%
where the time goes in v20:
time: 210 us; the launch traced here: 209 us
  waiting for transfers between devices  64.6 us (31%)
  Pallas kernels  61.5 us (29%)
  blocking collectives  57.1 us (27%)
  between operations  13.5 us (6%)
  starting transfers between devices  7.76 us (4%)
  other arithmetic  2.6 us (1%)
    all_to_all x2, waiting for transfers between devices, exchanged(): lax.all_to_all(packed.reshape(tile_total * vir_count, rows, block), ('occ...  56.7 us
    pallas_call x2, Pallas kernels, ladder_call(): pl.pallas_call(functools.partial(ladder_kernel, tile_total, vir_count, ch...  34.4 us
    all_gather x1, blocking collectives, body(): first = lax.all_gather(screened[0], 'occ', axis=0, tiled=True)  34.3 us
    all_gather x1, blocking collectives, body(): lax.all_gather(part, 'occ', axis=0, tiled=True)  22.8 us
    pallas_call x2, Pallas kernels, update_call(): pl.pallas_call(functools.partial(update_kernel, vir_count, at_once), grid...  12.3 us
    pallas_call x2, Pallas kernels, direct_call(): pl.pallas_call(direct_kernel, grid=(rows // step_rows,), in_specs=[pl.Blo...  11 us
    all_gather x1, waiting for transfers between devices, body(): lax.all_gather(part, 'occ', axis=0, tiled=True)  7.89 us
    all_to_all x2, starting transfers between devices, exchanged(): lax.all_to_all(packed.reshape(tile_total * vir_count, rows, block), ('occ...  7.76 us
  transfers between devices with their start and end apart: 3, of which 3 were waited for; matrix products, arithmetic and copies ran while one was open for 2% of the time, Pallas kernels for 25%

profile of v20, /device:TPU:0, one launch (start us, length us, event | category | flops | bytes accessed | tf_op | source)
XLA Modules:
  0.0 208.8 jit_solution(10190557069503576455)
XLA Ops:
  6.5 0.0 copy-start.2
  6.5 0.0 all-gather.4.cloned.1.call-start
  6.5 3.7 %screen.1 = (s16[528,384]{1,0:T(8,128)(2,1)}, s16[528,128]{1,0:T(8,128)(2,1)}, bf16[512,512]{1,0:T(8,128)(2,1)}) custom-call(s32[4,4]{1,0:T(4,128)} %int_mask.1, bf16[512,1024]{1,0:T(8,128)(2,1)} %slab_ref.1), custom_call_target="tpu_custom_call" | custom-call | tf_op jit(solution)/shard_map/screen/pallas_call | solution.py:84
  10.2 0.0 copy-start.1
  10.2 34.3 %all-gather.5.refs_0_ = s16[4224,384]{1,0:T(8,128)(2,1)} all-gather(s16[528,384]{1,0:T(8,128)(2,1)} %get-tuple-element.17), channel_id=1, replica_groups=mesh['occ'=8,'vir'=4] {'occ'}, dimensions={0}, use_global_device_ids=true | all-gather | bytes 3649536 | tf_op jit(solution)/shard_map/all_gather | solution.py:328
  44.5 0.0 all-gather.4.cloned.1.call-update
  44.6 0.0 copy-done.2
  44.6 0.7 copy.9.amp_mask
  45.2 0.0 copy-done.1
  45.3 22.8 %all-gather.6.refs_1_ = s16[4224,128]{1,0:T(8,128)(2,1)} all-gather(s16[528,128]{1,0:T(8,128)(2,1)S(1)} %copy-done.1), channel_id=1, replica_groups=mesh['occ'=8,'vir'=4] {'occ'}, dimensions={0}, use_global_device_ids=true | all-gather | bytes 1216512 | tf_op jit(solution)/shard_map/all_gather | solution.py:330
  68.1 18.0 %ladder.3 = (f32[2,2048,256]{2,1,0:T(8,128)}, s16[8,4,264,128]{3,2,1,0:T(8,128)(2,1)}) custom-call(s32[8,4]{1,0:T(8,128)} %copy.9.amp_mask, s32[8]{0:T(128)} %numbers.3, bf16[2048,4096]{1,0:T(8,128)(2,1)} %rows_ref.3, s16[4224,384]{1,0:T(8,128)(2,1)} %all-gather.5.refs_0_, s16[4224,128]{1,0:T(8,128)(2,1)} %all-gather.6.refs_1_), custom_call_target="tpu_custom_call" | custom-call | flops 8589934592 | bytes 27262976 | tf_op jit(solution)/shard_map/ladder/pallas_call | solution.py:192
  86.0 4.0 %all-to-all-start.1 = ((s16[32,264,128]{2,1,0:T(8,128)(2,1)}), s16[32,264,128]{2,1,0:T(8,128)(2,1)S(1)}, u32[]{:S(2)}, u32[]{:S(2)}) async-start(s16[32,264,128]{2,1,0:T(8,128)(2,1)} %bitcast.12), calls=%async_computation.1 | async-start | bytes 4325376 | tf_op jit(solution)/shard_map/all_to_all | solution.py:322
  90.1 7.9 %all-gather.4.cloned.1.call-done.refs_0_ = bf16[4096,512]{1,0:T(8,128)(2,1)} async-done(((bf16[512,512]{1,0:T(8,128)(2,1)}), bf16[4096,512]{1,0:T(8,128)(2,1)}) %all-gather.4.cloned.1.call-update) | async-done | bytes 4194320 | tf_op jit(solution)/shard_map/all_gather | solution.py:330
  97.9 16.5 %ladder.2 = (f32[2,2048,256]{2,1,0:T(8,128)}, s16[8,4,264,128]{3,2,1,0:T(8,128)(2,1)}) custom-call(s32[8,4]{1,0:T(8,128)} %copy.9.amp_mask, s32[8]{0:T(128)} %numbers.3, bf16[2048,4096]{1,0:T(8,128)(2,1)} %rows_ref.3, bf16[4096,512]{1,0:T(8,128)(2,1)} %all-gather.4.cloned.1.call-done.refs_0_), custom_call_target="tpu_custom_call" | custom-call | flops 8589934592 | bytes 27262976 | tf_op jit(solution)/shard_map/ladder/pallas_call | solution.py:192
  114.4 0.0 copy-start.3
  114.4 0.0 copy-start.4
  114.4 27.5 %all-to-all-done.1 = s16[32,264,128]{2,1,0:T(8,128)(2,1)S(1)} async-done(((s16[32,264,128]{2,1,0:T(8,128)(2,1)}), s16[32,264,128]{2,1,0:T(8,128)(2,1)S(1)}, u32[]{:S(2)}, u32[]{:S(2)}) %all-to-all-start.1) | async-done | bytes 2162720 | tf_op jit(solution)/shard_map/all_to_all | solution.py:322
  141.9 0.0 copy-start
  141.9 3.8 %all-to-all-start = ((s16[32,264,128]{2,1,0:T(8,128)(2,1)}), s16[32,264,128]{2,1,0:T(8,128)(2,1)}, u32[]{:S(2)}, u32[]{:S(2)}) async-start(s16[32,264,128]{2,1,0:T(8,128)(2,1)} %bitcast.11), calls=%async_computation | async-start | bytes 4325376 | tf_op jit(solution)/shard_map/all_to_all | solution.py:322
  145.7 0.0 copy-done.3
  145.7 0.1 reshape.142
  145.8 0.1 add.176
  145.8 0.1 add.177
  145.9 0.0 copy-done.4
  145.9 0.1 dynamic_slice.6
  146.0 0.1 broadcast_add_fusion.1
  146.1 0.7 add.173.vir_ref
  146.8 0.1 add.180
  146.9 0.6 broadcast_add_fusion.occ_ref
  147.5 0.9 fusion.1.spread_ref
  148.5 1.0 fusion.spread_ref
  149.4 5.5 %direct.3.refs_4_.refs_5_.refs_6_.refs_7_ = f32[2048,512]{1,0:T(8,128)} custom-call(bf16[512,512]{1,0:T(8,128)(2,1)} %fusion.1.spread_ref, f32[2,2048,256]{2,1,0:T(8,128)} %get-tuple-element.22.refs_0_, f32[2,2048,256]{2,1,0:T(8,128)} %get-tuple-element.23.refs_1_), custom_call_target="tpu_custom_call" | custom-call | flops 2147483648 | bytes 8388608 | tf_op jit(solution)/shard_map/direct/pallas_call | solution.py:241
  154.9 0.0 copy-done
  154.9 5.5 %direct.2.refs_4_.refs_5_.refs_6_.refs_7_ = f32[2048,512]{1,0:T(8,128)} custom-call(bf16[512,512]{1,0:T(8,128)(2,1)} %fusion.1.spread_ref, f32[2,2048,256]{2,1,0:T(8,128)} %get-tuple-element.22.refs_0_, f32[2,2048,256]{2,1,0:T(8,128)} %get-tuple-element.23.refs_1_), custom_call_target="tpu_custom_call" | custom-call | flops 2147483648 | bytes 8388608 | tf_op jit(solution)/shard_map/direct/pallas_call | solution.py:241
  160.5 6.2 %update.2.refs_8_ = f32[2048,1024]{1,0:T(8,128)} custom-call(bf16[512,512]{1,0:T(8,128)(2,1)} %fusion.spread_ref, f32[1,1024]{1,0:T(1,128)} %add.173.vir_ref, f32[8,1,256]{2,1,0:T(1,128)} %broadcast_add_fusion.occ_ref, s16[8,4,264,128]{3,2,1,0:T(8,128)(2,1)} %bitcast.7, s16[8,4,264,128]{3,2,1,0:T(8,128)(2,1)} %bitcast.8, s16[8,4,264,128]{3,2,1,0:T(8,128)(2,1)} %bitcast.9, ...), custom_call_target="tpu_custom_call" | custom-call | flops 2147483648 | bytes 10485760 | tf_op jit(solution)/shard_map/update/pallas_call | solution.py:294
  166.6 29.2 %all-to-all-done = s16[32,264,128]{2,1,0:T(8,128)(2,1)} async-done(((s16[32,264,128]{2,1,0:T(8,128)(2,1)}), s16[32,264,128]{2,1,0:T(8,128)(2,1)}, u32[]{:S(2)}, u32[]{:S(2)}) %all-to-all-start) | async-done | bytes 2162720 | tf_op jit(solution)/shard_map/all_to_all | solution.py:322
  195.8 6.2 %update.3 = f32[2048,1024]{1,0:T(8,128)} custom-call(bf16[512,512]{1,0:T(8,128)(2,1)} %fusion.spread_ref, f32[1,1024]{1,0:T(1,128)} %add.173.vir_ref, f32[8,1,256]{2,1,0:T(1,128)} %broadcast_add_fusion.occ_ref, s16[8,4,264,128]{3,2,1,0:T(8,128)(2,1)} %bitcast.3.refs_0_.refs_1_.refs_2_.refs_3_, ...), custom_call_target="tpu_custom_call", output_to_operand_aliasing={{}: (11, {})} | custom-call | flops 2147483648 | bytes 10485760 | tf_op jit(solution)/shard_map/update/pallas_call | solution.py:294
  (5 shorter events, 0.0 us)
Async XLA Ops:
  6.5 38.0 %copy-start.2 = (s32[1,8,4]{1,2,0:T(4,128)S(1)}, s32[1,8,4]{1,2,0:T(4,128)}, u32[]{:S(2)}) copy-start(s32[1,8,4]{1,2,0:T(4,128)} %param.8) | copy-start | bytes 388
  6.5 91.4 %all-gather.4.cloned.1.call-start = ((), (), s32[]{:S(2)}) async-start(), calls=%async_computation.2 | async-start | bytes 4718592 | tf_op jit(solution)/shard_map/all_gather | solution.py:330
  10.2 35.0 %copy-start.1 = (s16[528,128]{1,0:T(8,128)(2,1)S(1)}, s16[528,128]{1,0:T(8,128)(2,1)}, u32[]{:S(2)}) copy-start(s16[528,128]{1,0:T(8,128)(2,1)} %get-tuple-element.21) | copy-start | bytes 405508
  86.0 55.9 %all-to-all-start.1 = ((s16[32,264,128]{2,1,0:T(8,128)(2,1)}), s16[32,264,128]{2,1,0:T(8,128)(2,1)S(1)}, u32[]{:S(2)}, u32[]{:S(2)}) async-start(s16[32,264,128]{2,1,0:T(8,128)(2,1)} %bitcast.12), calls=%async_computation.1 | async-start | bytes 4325376 | tf_op jit(solution)/shard_map/all_to_all | solution.py:322
  114.4 31.3 %copy-start.3 = (f32[128]{0:T(128)S(1)}, f32[128]{0:T(128)}, u32[]{:S(2)}) copy-start(f32[128]{0:T(128)} %param.12) | copy-start | bytes 1540
  114.4 31.5 %copy-start.4 = (f32[64]{0:T(128)S(1)}, f32[64]{0:T(128)}, u32[]{:S(2)}) copy-start(f32[64]{0:T(128)} %param.13) | copy-start | bytes 772
  141.9 13.0 %copy-start = (s16[32,264,128]{2,1,0:T(8,128)(2,1)}, s16[32,264,128]{2,1,0:T(8,128)(2,1)S(1)}, u32[]{:S(2)}) copy-start(s16[32,264,128]{2,1,0:T(8,128)(2,1)S(1)} %all-to-all-done.1) | copy-start | bytes 6488068
  141.9 53.9 %all-to-all-start = ((s16[32,264,128]{2,1,0:T(8,128)(2,1)}), s16[32,264,128]{2,1,0:T(8,128)(2,1)}, u32[]{:S(2)}, u32[]{:S(2)}) async-start(s16[32,264,128]{2,1,0:T(8,128)(2,1)} %bitcast.11), calls=%async_computation | async-start | bytes 4325376 | tf_op jit(solution)/shard_map/all_to_all | solution.py:322
Sparse Core Ops, SparseCore 0:
  44.7 53.2 all-gather.3

commit v21 on v20

--- a/solution.py
+++ b/solution.py
@@ -42,7 +42,7 @@
 def screen_kernel(part, int_mask, slab_ref, *refs):
     coded_refs, later_refs = refs[:CODED_PARTS], refs[CODED_PARTS:]
     slab_rows, slab_cols = slab_ref.shape
-    cols = sum(ref.shape[1] for ref in coded_refs)
+    cols = coded_refs[0].shape[1]
     span = slab_cols // W
     row_label = lax.axis_index("occ") * slab_rows // W // VT * NVT
     col_label = lax.axis_index("vir") * slab_cols // W // VT * NVT
@@ -70,22 +70,22 @@
             code_rows = jnp.broadcast_to(code.astype(jnp.int32), (CODE_ROWS, cols)).astype(jnp.int16)
             at = 0
             for coded_ref in coded_refs:
-                end = at + coded_ref.shape[1]
-                coded_ref[:slab_rows, :] = coded[:, at:end]
-                coded_ref[slab_rows:, :] = code_rows[:, at:end]
-                at = end
+                rows = coded_ref.shape[0] - CODE_ROWS
+                coded_ref[:rows, :] = coded[at : at + rows]
+                coded_ref[rows:, :] = code_rows
+                at += rows
 
 
 def screen_call(chunks, int_mask, integrals):
     slab_rows, slab_cols = integrals.shape
     cols = slab_cols // chunks
-    coded_cols = [cols - cols // 4, cols // 4]
+    coded_rows = [slab_rows - slab_rows // 8, slab_rows // 8]
     vmem = pl.BlockSpec(memory_space=pltpu.VMEM)
     return pl.pallas_call(
         functools.partial(screen_kernel, slab_cols // W // chunks),
         in_specs=[pl.BlockSpec(memory_space=pltpu.SMEM), vmem],
         out_specs=[vmem] * (CODED_PARTS + chunks - 1),
-        out_shape=[jax.ShapeDtypeStruct((slab_rows + CODE_ROWS, each), jnp.int16) for each in coded_cols]
+        out_shape=[jax.ShapeDtypeStruct((each + CODE_ROWS, cols), jnp.int16) for each in coded_rows]
         + [jax.ShapeDtypeStruct((slab_rows, cols), integrals.dtype)] * (chunks - 1),
         compiler_params=pltpu.CompilerParams(vmem_limit_bytes=VMEM_LIMIT),
         name="screen",
@@ -101,7 +101,6 @@
     step = pl.program_id(0)
     cols = product.shape[1]
     slab_rows = slab_refs[0].shape[0] // tile_total
-    shard_rows = slab_rows + CODE_ROWS
     block = cols // vir_count
     lanes = block // chunks
 
@@ -122,8 +121,10 @@
             at += slab_ref.shape[1]
 
     def decode():
+        shard_rows = [stage.shape[0] // tile_total for stage in stages]
+
         def copy_of(n, shard):
-            at = pl.ds(pl.multiple_of(shard * shard_rows, CODE_ROWS), shard_rows)
+            at = pl.ds(pl.multiple_of(shard * shard_rows[n], CODE_ROWS), shard_rows[n])
             return pltpu.make_async_copy(gathered_refs[n].at[at, :], stages[n].at[at, :], sems.at[n, shard])
 
         for shard in range(tile_total):
@@ -131,16 +132,17 @@
                 copy_of(n, shard).start()
 
         def use(shard, carry):
-            at = pl.multiple_of(shard * shard_rows, CODE_ROWS)
-            to = pl.ds(pl.multiple_of(shard * slab_rows, slab_rows), slab_rows)
-            col = 0
+            first = 0
             for n, stage in enumerate(stages):
                 copy_of(n, shard).wait()
-                code = stage[pl.ds(pl.multiple_of(at + slab_rows, CODE_ROWS), CODE_ROWS), :]
-                values = stage[pl.ds(at, slab_rows), :].astype(jnp.int32).astype(jnp.float32)
+                rows = shard_rows[n] - CODE_ROWS
+                at = pl.multiple_of(shard * shard_rows[n], CODE_ROWS)
+                code = stage[pl.ds(pl.multiple_of(at + rows, CODE_ROWS), CODE_ROWS), :]
+                values = stage[pl.ds(at, rows), :].astype(jnp.int32).astype(jnp.float32)
                 scale = jnp.exp2(code.astype(jnp.int32).astype(jnp.float32)[:1] - SLAB_BITS)
-                slab_refs[0][to, col : col + stage.shape[1]] = (values * scale).astype(jnp.bfloat16)
-                col += stage.shape[1]
+                to = pl.ds(pl.multiple_of(shard * slab_rows + first, CODE_ROWS), rows)
+                slab_refs[0][to, :] = (values * scale).astype(jnp.bfloat16)
+                first += rows
             return carry
 
         lax.fori_loop(0, tile_total, use, 0)
@@ -183,7 +185,7 @@
 
 def ladder_call(tile_total, vir_count, chunks, amp_mask, numbers, amplitudes, slab):
     coded = slab[0].dtype == jnp.int16
-    cols = sum(part.shape[1] for part in slab)
+    cols = slab[0].shape[1]
     block = cols // vir_count
     smem = pl.BlockSpec(memory_space=pltpu.SMEM)
     rows = tile_total * PAIR_SQ

time: 210 us -> 212 us (level)
  starting transfers between devices: 7.76 us -> 10.3 us
    all_gather x1, blocking collectives: 22.8 us -> 17.9 us  [body(): lax.all_gather(part, 'occ', axis=0, tiled=True)]
    all_gather x1, blocking collectives: 34.3 us -> 38.7 us  [body(): first = lax.all_gather(screened[0], 'occ', axis=0, tiled=True)]
    all_to_all x2, starting transfers between devices: 7.76 us -> 10.2 us  [exchanged(): lax.all_to_all(packed.reshape(tile_total * vir_count, rows, block), ('occ...]
  transfers between devices with their start and end apart: 3 -> 3, of which waited for: 3 -> 3; matrix products, arithmetic and copies ran while one was open for 2% -> 2% of each run, Pallas kernels for 25% -> 24%
where the time goes in v21:
time: 212 us; the launch traced here: 211 us
  waiting for transfers between devices  65.4 us (31%)
  Pallas kernels  61.4 us (29%)
  blocking collectives  56.5 us (27%)
  between operations  13.5 us (6%)
  starting transfers between devices  10.3 us (5%)
  other arithmetic  2.6 us (1%)
    all_to_all x2, waiting for transfers between devices, exchanged(): lax.all_to_all(packed.reshape(tile_total * vir_count, rows, block), ('occ...  55.7 us
    all_gather x1, blocking collectives, body(): first = lax.all_gather(screened[0], 'occ', axis=0, tiled=True)  38.7 us
    pallas_call x2, Pallas kernels, ladder_call(): pl.pallas_call(functools.partial(ladder_kernel, tile_total, vir_count, ch...  34.4 us
    all_gather x1, blocking collectives, body(): lax.all_gather(part, 'occ', axis=0, tiled=True)  17.9 us
    pallas_call x2, Pallas kernels, update_call(): pl.pallas_call(functools.partial(update_kernel, vir_count, at_once), grid...  12.3 us
    pallas_call x2, Pallas kernels, direct_call(): pl.pallas_call(direct_kernel, grid=(rows // step_rows,), in_specs=[pl.Blo...  11 us
    all_to_all x2, starting transfers between devices, exchanged(): lax.all_to_all(packed.reshape(tile_total * vir_count, rows, block), ('occ...  10.2 us
    all_gather x1, waiting for transfers between devices, body(): lax.all_gather(part, 'occ', axis=0, tiled=True)  9.65 us
  transfers between devices with their start and end apart: 3, of which 3 were waited for; matrix products, arithmetic and copies ran while one was open for 2% of the time, Pallas kernels for 24%

profile of v21, /device:TPU:0, one launch (start us, length us, event | category | flops | bytes accessed | tf_op | source)
XLA Modules:
  0.0 211.4 jit_solution(3640695792127844676)
XLA Ops:
  6.5 0.0 copy-start.2
  6.5 0.0 all-gather.3.cloned.1.call-start
  6.5 3.7 %screen.1 = (s16[464,512]{1,0:T(8,128)(2,1)}, s16[80,512]{1,0:T(8,128)(2,1)}, bf16[512,512]{1,0:T(8,128)(2,1)}) custom-call(s32[4,4]{1,0:T(4,128)} %int_mask.1, bf16[512,1024]{1,0:T(8,128)(2,1)} %slab_ref.1), custom_call_target="tpu_custom_call" | custom-call | tf_op jit(solution)/shard_map/screen/pallas_call | solution.py:84
  10.2 0.0 copy-start.1
  10.2 38.7 %all-gather.4.refs_0_ = s16[3712,512]{1,0:T(8,128)(2,1)} all-gather(s16[464,512]{1,0:T(8,128)(2,1)} %get-tuple-element.17), channel_id=1, replica_groups=mesh['occ'=8,'vir'=4] {'occ'}, dimensions={0}, use_global_device_ids=true | all-gather | bytes 4276224 | tf_op jit(solution)/shard_map/all_gather | solution.py:330
  48.9 0.0 all-gather.3.cloned.1.call-update
  48.9 0.0 copy-done.2
  48.9 0.7 copy.9.amp_mask
  49.6 0.0 copy-done.1
  49.6 17.9 %all_gather.11.refs_1_ = s16[640,512]{1,0:T(8,128)(2,1)} all-gather(s16[80,512]{1,0:T(8,128)(2,1)S(1)} %copy-done.1), channel_id=1, replica_groups=mesh['occ'=8,'vir'=4] {'occ'}, dimensions={0}, use_global_device_ids=true | all-gather | bytes 737280 | tf_op jit(solution)/shard_map/all_gather | solution.py:332
  67.5 18.0 %ladder.3 = (f32[2,2048,256]{2,1,0:T(8,128)}, s16[8,4,264,128]{3,2,1,0:T(8,128)(2,1)}) custom-call(s32[8,4]{1,0:T(8,128)} %copy.9.amp_mask, s32[8]{0:T(128)} %numbers.3, bf16[2048,4096]{1,0:T(8,128)(2,1)} %rows_ref.3, s16[3712,512]{1,0:T(8,128)(2,1)} %all-gather.4.refs_0_, s16[640,512]{1,0:T(8,128)(2,1)} %all_gather.11.refs_1_), custom_call_target="tpu_custom_call" | custom-call | flops 8589934592 | bytes 27262976 | tf_op jit(solution)/shard_map/ladder/pallas_call | solution.py:194
  85.4 6.5 %all-to-all-start.1 = ((s16[32,264,128]{2,1,0:T(8,128)(2,1)}), s16[32,264,128]{2,1,0:T(8,128)(2,1)S(1)}, u32[]{:S(2)}, u32[]{:S(2)}) async-start(s16[32,264,128]{2,1,0:T(8,128)(2,1)} %bitcast.12), calls=%async_computation.1 | async-start | bytes 4325376 | tf_op jit(solution)/shard_map/all_to_all | solution.py:324
  92.0 9.6 %all-gather.3.cloned.1.call-done.refs_0_ = bf16[4096,512]{1,0:T(8,128)(2,1)} async-done(((bf16[512,512]{1,0:T(8,128)(2,1)}), bf16[4096,512]{1,0:T(8,128)(2,1)}) %all-gather.3.cloned.1.call-update) | async-done | bytes 4194320 | tf_op jit(solution)/shard_map/all_gather | solution.py:332
  101.6 16.5 %ladder.2 = (f32[2,2048,256]{2,1,0:T(8,128)}, s16[8,4,264,128]{3,2,1,0:T(8,128)(2,1)}) custom-call(s32[8,4]{1,0:T(8,128)} %copy.9.amp_mask, s32[8]{0:T(128)} %numbers.3, bf16[2048,4096]{1,0:T(8,128)(2,1)} %rows_ref.3, bf16[4096,512]{1,0:T(8,128)(2,1)} %all-gather.3.cloned.1.call-done.refs_0_), custom_call_target="tpu_custom_call" | custom-call | flops 8589934592 | bytes 27262976 | tf_op jit(solution)/shard_map/ladder/pallas_call | solution.py:194
  118.1 0.0 copy-start.3
  118.1 0.0 copy-start.4
  118.1 26.5 %all-to-all-done.1 = s16[32,264,128]{2,1,0:T(8,128)(2,1)S(1)} async-done(((s16[32,264,128]{2,1,0:T(8,128)(2,1)}), s16[32,264,128]{2,1,0:T(8,128)(2,1)S(1)}, u32[]{:S(2)}, u32[]{:S(2)}) %all-to-all-start.1) | async-done | bytes 2162720 | tf_op jit(solution)/shard_map/all_to_all | solution.py:324
  144.6 0.0 copy-start
  144.6 3.7 %all-to-all-start = ((s16[32,264,128]{2,1,0:T(8,128)(2,1)}), s16[32,264,128]{2,1,0:T(8,128)(2,1)}, u32[]{:S(2)}, u32[]{:S(2)}) async-start(s16[32,264,128]{2,1,0:T(8,128)(2,1)} %bitcast.11), calls=%async_computation | async-start | bytes 4325376 | tf_op jit(solution)/shard_map/all_to_all | solution.py:324
  148.3 0.0 copy-done.3
  148.4 0.1 reshape.142
  148.4 0.1 add.176
  148.5 0.1 add.177
  148.6 0.0 copy-done.4
  148.6 0.1 dynamic_slice.6
  148.7 0.1 broadcast_add_fusion.1
  148.8 0.7 add.173.vir_ref
  149.4 0.1 add.180
  149.6 0.6 broadcast_add_fusion.occ_ref
  150.2 0.9 fusion.1.spread_ref
  151.1 1.0 fusion.spread_ref
  152.1 5.5 %direct.3.refs_4_.refs_5_.refs_6_.refs_7_ = f32[2048,512]{1,0:T(8,128)} custom-call(bf16[512,512]{1,0:T(8,128)(2,1)} %fusion.1.spread_ref, f32[2,2048,256]{2,1,0:T(8,128)} %get-tuple-element.22.refs_0_, f32[2,2048,256]{2,1,0:T(8,128)} %get-tuple-element.23.refs_1_), custom_call_target="tpu_custom_call" | custom-call | flops 2147483648 | bytes 8388608 | tf_op jit(solution)/shard_map/direct/pallas_call | solution.py:243
  157.6 0.0 copy-done
  157.6 5.5 %direct.2.refs_4_.refs_5_.refs_6_.refs_7_ = f32[2048,512]{1,0:T(8,128)} custom-call(bf16[512,512]{1,0:T(8,128)(2,1)} %fusion.1.spread_ref, f32[2,2048,256]{2,1,0:T(8,128)} %get-tuple-element.22.refs_0_, f32[2,2048,256]{2,1,0:T(8,128)} %get-tuple-element.23.refs_1_), custom_call_target="tpu_custom_call" | custom-call | flops 2147483648 | bytes 8388608 | tf_op jit(solution)/shard_map/direct/pallas_call | solution.py:243
  163.1 6.2 %update.2.refs_8_ = f32[2048,1024]{1,0:T(8,128)} custom-call(bf16[512,512]{1,0:T(8,128)(2,1)} %fusion.spread_ref, f32[1,1024]{1,0:T(1,128)} %add.173.vir_ref, f32[8,1,256]{2,1,0:T(1,128)} %broadcast_add_fusion.occ_ref, s16[8,4,264,128]{3,2,1,0:T(8,128)(2,1)} %bitcast.7, s16[8,4,264,128]{3,2,1,0:T(8,128)(2,1)} %bitcast.8, s16[8,4,264,128]{3,2,1,0:T(8,128)(2,1)} %bitcast.9, ...), custom_call_target="tpu_custom_call" | custom-call | flops 2147483648 | bytes 10485760 | tf_op jit(solution)/shard_map/update/pallas_call | solution.py:296
  169.3 29.2 %all-to-all-done = s16[32,264,128]{2,1,0:T(8,128)(2,1)} async-done(((s16[32,264,128]{2,1,0:T(8,128)(2,1)}), s16[32,264,128]{2,1,0:T(8,128)(2,1)}, u32[]{:S(2)}, u32[]{:S(2)}) %all-to-all-start) | async-done | bytes 2162720 | tf_op jit(solution)/shard_map/all_to_all | solution.py:324
  198.4 6.2 %update.3 = f32[2048,1024]{1,0:T(8,128)} custom-call(bf16[512,512]{1,0:T(8,128)(2,1)} %fusion.spread_ref, f32[1,1024]{1,0:T(1,128)} %add.173.vir_ref, f32[8,1,256]{2,1,0:T(1,128)} %broadcast_add_fusion.occ_ref, s16[8,4,264,128]{3,2,1,0:T(8,128)(2,1)} %bitcast.3.refs_0_.refs_1_.refs_2_.refs_3_, ...), custom_call_target="tpu_custom_call", output_to_operand_aliasing={{}: (11, {})} | custom-call | flops 2147483648 | bytes 10485760 | tf_op jit(solution)/shard_map/update/pallas_call | solution.py:296
  (5 shorter events, 0.0 us)
Async XLA Ops:
  6.5 42.4 %copy-start.2 = (s32[1,8,4]{1,2,0:T(4,128)S(1)}, s32[1,8,4]{1,2,0:T(4,128)}, u32[]{:S(2)}) copy-start(s32[1,8,4]{1,2,0:T(4,128)} %param.8) | copy-start | bytes 388
  6.5 95.1 %all-gather.3.cloned.1.call-start = ((), (), s32[]{:S(2)}) async-start(), calls=%async_computation.2 | async-start | bytes 4718592 | tf_op jit(solution)/shard_map/all_gather | solution.py:332
  10.2 39.4 %copy-start.1 = (s16[80,512]{1,0:T(8,128)(2,1)S(1)}, s16[80,512]{1,0:T(8,128)(2,1)}, u32[]{:S(2)}) copy-start(s16[80,512]{1,0:T(8,128)(2,1)} %get-tuple-element.21) | copy-start | bytes 245764
  85.4 59.2 %all-to-all-start.1 = ((s16[32,264,128]{2,1,0:T(8,128)(2,1)}), s16[32,264,128]{2,1,0:T(8,128)(2,1)S(1)}, u32[]{:S(2)}, u32[]{:S(2)}) async-start(s16[32,264,128]{2,1,0:T(8,128)(2,1)} %bitcast.12), calls=%async_computation.1 | async-start | bytes 4325376 | tf_op jit(solution)/shard_map/all_to_all | solution.py:324
  118.1 30.3 %copy-start.3 = (f32[128]{0:T(128)S(1)}, f32[128]{0:T(128)}, u32[]{:S(2)}) copy-start(f32[128]{0:T(128)} %param.12) | copy-start | bytes 1540
  118.1 30.5 %copy-start.4 = (f32[64]{0:T(128)S(1)}, f32[64]{0:T(128)}, u32[]{:S(2)}) copy-start(f32[64]{0:T(128)} %param.13) | copy-start | bytes 772
  144.6 13.0 %copy-start = (s16[32,264,128]{2,1,0:T(8,128)(2,1)}, s16[32,264,128]{2,1,0:T(8,128)(2,1)S(1)}, u32[]{:S(2)}) copy-start(s16[32,264,128]{2,1,0:T(8,128)(2,1)S(1)} %all-to-all-done.1) | copy-start | bytes 6488068
  144.6 53.8 %all-to-all-start = ((s16[32,264,128]{2,1,0:T(8,128)(2,1)}), s16[32,264,128]{2,1,0:T(8,128)(2,1)}, u32[]{:S(2)}, u32[]{:S(2)}) async-start(s16[32,264,128]{2,1,0:T(8,128)(2,1)} %bitcast.11), calls=%async_computation | async-start | bytes 4325376 | tf_op jit(solution)/shard_map/all_to_all | solution.py:324
Sparse Core Ops, SparseCore 0:
  49.0 52.5 all-gather.2

commit v22 on v19

--- a/solution.py
+++ b/solution.py
@@ -38,9 +38,10 @@
     return jnp.exp2(code * (1.0 / STEPS))
 
 
-def screen_kernel(part, int_mask, slab_ref, coded_ref, *later_refs):
+def screen_kernel(part, int_mask, slab_ref, coded_ref, plain_ref, *later_refs):
     slab_rows, slab_cols = slab_ref.shape
-    cols = coded_ref.shape[1]
+    coded_cols = coded_ref.shape[1]
+    cols = coded_cols + plain_ref.shape[1]
     span = slab_cols // W
     row_label = lax.axis_index("occ") * slab_rows // W // VT * NVT
     col_label = lax.axis_index("vir") * slab_cols // W // VT * NVT
@@ -60,30 +61,30 @@
         moved = dot(slab_ref[...], ones.astype(jnp.float32).astype(jnp.bfloat16))
         moved = jnp.where(jnp.where(second, kept[1], kept[0]) > 0, moved, 0.0)
         if chunk:
-            at = 0
-            for later_ref in later_refs:
-                later_ref[...] = moved[:, at : at + later_ref.shape[1]].astype(jnp.bfloat16)
-                at += later_ref.shape[1]
+            later_refs[chunk - 1][...] = moved.astype(jnp.bfloat16)
         else:
+            plain_ref[...] = moved[:, coded_cols:].astype(jnp.bfloat16)
+            moved = moved[:, :coded_cols]
             most = jnp.maximum(jnp.max(jnp.abs(moved), axis=0, keepdims=True), 1e-30)
             code = jnp.floor(jnp.log2(most)) + 1.0
-            coded = jnp.round(moved * jnp.exp2(SLAB_BITS - code)).astype(jnp.int32).astype(jnp.int16)
-            code_rows = jnp.broadcast_to(code.astype(jnp.int32), (CODE_ROWS, cols)).astype(jnp.int16)
-            coded_ref[:slab_rows, :] = coded
-            coded_ref[slab_rows:, :] = code_rows
+            coded_ref[:slab_rows, :] = jnp.round(moved * jnp.exp2(SLAB_BITS - code)).astype(jnp.int32).astype(jnp.int16)
+            coded_ref[slab_rows:, :] = jnp.broadcast_to(
+                code.astype(jnp.int32), (CODE_ROWS, coded_cols)
+            ).astype(jnp.int16)
 
 
 def screen_call(chunks, int_mask, integrals):
     slab_rows, slab_cols = integrals.shape
     cols = slab_cols // chunks
-    later_cols = [cols // 4, cols - cols // 4] if chunks > 1 else []
+    coded_cols = cols - cols // 4
+    plain_cols = [cols // 4] + [cols] * (chunks - 1)
     vmem = pl.BlockSpec(memory_space=pltpu.VMEM)
     return pl.pallas_call(
         functools.partial(screen_kernel, slab_cols // W // chunks),
         in_specs=[pl.BlockSpec(memory_space=pltpu.SMEM), vmem],
-        out_specs=[vmem] * (1 + len(later_cols)),
-        out_shape=[jax.ShapeDtypeStruct((slab_rows + CODE_ROWS, cols), jnp.int16)]
-        + [jax.ShapeDtypeStruct((slab_rows, each), integrals.dtype) for each in later_cols],
+        out_specs=[vmem] * (1 + len(plain_cols)),
+        out_shape=[jax.ShapeDtypeStruct((slab_rows + CODE_ROWS, coded_cols), jnp.int16)]
+        + [jax.ShapeDtypeStruct((slab_rows, each), integrals.dtype) for each in plain_cols],
         compiler_params=pltpu.CompilerParams(vmem_limit_bytes=VMEM_LIMIT),
         name="screen",
     )(int_mask, integrals)
@@ -94,7 +95,7 @@
     ladder_ref, packed_ref, product = refs[:3]
     slab_refs = gathered_refs
     if coded:
-        slab_refs, stage, sems = refs[3:4], refs[4], refs[5]
+        slab_refs, stage, sems = (refs[3], *gathered_refs[1:]), refs[4], refs[5]
     step = pl.program_id(0)
     cols = product.shape[1]
     slab_rows = slab_refs[0].shape[0] // tile_total
@@ -190,7 +191,9 @@
             smem,
             pl.BlockSpec((PAIR_SQ, W * W), lambda step: (jnp.minimum(step, tile_total - 1), 0)),
             *[
-                pl.BlockSpec(memory_space=pl.ANY) if coded else pl.BlockSpec(part.shape, lambda step: (0, 0))
+                pl.BlockSpec(memory_space=pl.ANY)
+                if part.dtype == jnp.int16
+                else pl.BlockSpec(part.shape, lambda step: (0, 0))
                 for part in slab
             ],
         ],
@@ -204,7 +207,7 @@
         ],
         scratch_shapes=[pltpu.VMEM((PAIR_SQ, cols), jnp.float32)]
         + [
-            pltpu.VMEM((W * W, cols), jnp.bfloat16),
+            pltpu.VMEM((W * W, slab[0].shape[1]), jnp.bfloat16),
             pltpu.VMEM(slab[0].shape, slab[0].dtype),
             pltpu.SemaphoreType.DMA((tile_total,)),
         ]
@@ -317,9 +320,9 @@
         )
         return moved.reshape(tile_total, vir_count, rows, block)
 
-    coded, *later = screen_call(chunks, int_mask, integrals)
-    later = [lax.all_gather(part, "occ", axis=0, tiled=True) for part in later]
-    slabs = [[lax.all_gather(coded, "occ", axis=0, tiled=True)]] + [later] * (chunks - 1)
+    coded, *plain = screen_call(chunks, int_mask, integrals)
+    plain = [lax.all_gather(part, "occ", axis=0, tiled=True) for part in plain]
+    slabs = [[lax.all_gather(coded, "occ", axis=0, tiled=True), plain[0]]] + [[part] for part in plain[1:]]
     ladders, arrived = [], []
     for slab in slabs:
         ladder, packed = ladder_call(

time: 216 us -> 203 us (0.940)
  blocking collectives: 59.9 us -> 43 us
  waiting for transfers between devices: 60.6 us -> 64.9 us
    all_gather x1, blocking collectives: 59.9 us -> 43 us  [body(): lax.all_gather(coded, 'occ', axis=0, tiled=True)]
    all_gather x2, waiting for transfers between devices: 0.04 us -> 8.61 us  [body(): plain = [lax.all_gather(part, 'occ', axis=0, tiled=True) for part in plain]]
    all_to_all x2, waiting for transfers between devices: 59.9 us -> 55.6 us  [exchanged(): lax.all_to_all(packed.reshape(tile_total * vir_count, rows, block), ('occ...]
  transfers between devices with their start and end apart: 4 -> 4, of which waited for: 2 -> 3; matrix products, arithmetic and copies ran while one was open for 2% -> 2% of each run, Pallas kernels for 25% -> 27%
where the time goes in v22:
time: 203 us
  waiting for transfers between devices  64.9 us (32%)
  Pallas kernels  64 us (32%)
  blocking collectives  43 us (21%)
  between operations  13.5 us (7%)
  starting transfers between devices  12.3 us (6%)
  other arithmetic  2.63 us (1%)
  local copies, waits for them, and re-layouts  2.44 us (1%)
    all_to_all x2, waiting for transfers between devices, exchanged(): lax.all_to_all(packed.reshape(tile_total * vir_count, rows, block), ('occ...  55.6 us
    all_gather x1, blocking collectives, body(): lax.all_gather(coded, 'occ', axis=0, tiled=True)  43 us
    pallas_call x2, Pallas kernels, ladder_call(): pl.pallas_call(functools.partial(ladder_kernel, tile_total, vir_count, ch...  37 us
    pallas_call x2, Pallas kernels, update_call(): pl.pallas_call(functools.partial(update_kernel, vir_count, at_once), grid...  12.3 us
    all_to_all x2, starting transfers between devices, exchanged(): lax.all_to_all(packed.reshape(tile_total * vir_count, rows, block), ('occ...  12.2 us
    pallas_call x2, Pallas kernels, direct_call(): pl.pallas_call(direct_kernel, grid=(rows // step_rows,), in_specs=[pl.Blo...  11.1 us
    all_gather x2, waiting for transfers between devices, body(): plain = [lax.all_gather(part, 'occ', axis=0, tiled=True) for part in plain]  8.61 us
  transfers between devices with their start and end apart: 4, of which 3 were waited for; matrix products, arithmetic and copies ran while one was open for 2% of the time, Pallas kernels for 27%

profile of v22, /device:TPU:0, one launch (start us, length us, event | category | flops | bytes accessed | tf_op | source)
XLA Modules:
  0.0 202.7 jit_solution(12756223644961981936)
XLA Ops:
  6.5 0.0 all-gather.6.cloned.1.call-start
  6.5 3.6 %screen.1 = (s16[528,384]{1,0:T(8,128)(2,1)}, bf16[512,128]{1,0:T(8,128)(2,1)}, bf16[512,512]{1,0:T(8,128)(2,1)}) custom-call(s32[4,4]{1,0:T(4,128)} %int_mask.1, bf16[512,1024]{1,0:T(8,128)(2,1)} %slab_ref.1), custom_call_target="tpu_custom_call" | custom-call | tf_op jit(solution)/shard_map/screen/pallas_call | solution.py:82
  10.2 0.0 all-gather.6.cloned.1.call-update
  10.2 0.0 all-gather.4.cloned.1.call-start
  10.2 0.7 all-gather.4.cloned.1.call-update
  10.9 1.3 copy.9.amp_mask
  12.3 43.0 %all-gather.7.refs_0_ = s16[4224,384]{1,0:T(8,128)(2,1)} all-gather(s16[528,384]{1,0:T(8,128)(2,1)} %get-tuple-element.14), channel_id=1, replica_groups=mesh['occ'=8,'vir'=4] {'occ'}, dimensions={0}, use_global_device_ids=true | all-gather | bytes 3649536 | tf_op jit(solution)/shard_map/all_gather | solution.py:325
  55.3 0.0 all-gather.6.cloned.1.call-done.refs_1_
  55.3 20.5 %ladder.3 = (f32[2,2048,256]{2,1,0:T(8,128)}, s16[8,4,264,128]{3,2,1,0:T(8,128)(2,1)}) custom-call(s32[8,4]{1,0:T(8,128)} %copy.9.amp_mask, s32[8]{0:T(128)} %numbers.3, bf16[2048,4096]{1,0:T(8,128)(2,1)} %rows_ref.3, s16[4224,384]{1,0:T(8,128)(2,1)} %all-gather.7.refs_0_, bf16[4096,128]{1,0:T(8,128)(2,1)} %all-gather.6.cloned.1.call-done.refs_1_), custom_call_target="tpu_custom_call" | custom-call | flops 8589934592 | bytes 27262976 | tf_op jit(solution)/shard_map/ladder/pallas_call | solution.py:186
  75.8 7.8 %all-to-all-start.1 = ((s16[32,264,128]{2,1,0:T(8,128)(2,1)}), s16[32,264,128]{2,1,0:T(8,128)(2,1)S(1)}, u32[]{:S(2)}, u32[]{:S(2)}) async-start(s16[32,264,128]{2,1,0:T(8,128)(2,1)} %bitcast.12), calls=%async_computation.1 | async-start | bytes 4325376 | tf_op jit(solution)/shard_map/all_to_all | solution.py:318
  83.6 8.6 %all-gather.4.cloned.1.call-done.refs_0_ = bf16[4096,512]{1,0:T(8,128)(2,1)} async-done(((bf16[512,512]{1,0:T(8,128)(2,1)}), bf16[4096,512]{1,0:T(8,128)(2,1)}) %all-gather.4.cloned.1.call-update) | async-done | bytes 4194320 | tf_op jit(solution)/shard_map/all_gather | solution.py:324
  92.2 16.5 %ladder.2 = (f32[2,2048,256]{2,1,0:T(8,128)}, s16[8,4,264,128]{3,2,1,0:T(8,128)(2,1)}) custom-call(s32[8,4]{1,0:T(8,128)} %copy.9.amp_mask, s32[8]{0:T(128)} %numbers.3, bf16[2048,4096]{1,0:T(8,128)(2,1)} %rows_ref.3, bf16[4096,512]{1,0:T(8,128)(2,1)} %all-gather.4.cloned.1.call-done.refs_0_), custom_call_target="tpu_custom_call" | custom-call | flops 8589934592 | bytes 27262976 | tf_op jit(solution)/shard_map/ladder/pallas_call | solution.py:186
  108.7 0.0 copy-start.1
  108.7 0.0 copy-start.2
  108.7 26.5 %all-to-all-done.1 = s16[32,264,128]{2,1,0:T(8,128)(2,1)S(1)} async-done(((s16[32,264,128]{2,1,0:T(8,128)(2,1)}), s16[32,264,128]{2,1,0:T(8,128)(2,1)S(1)}, u32[]{:S(2)}, u32[]{:S(2)}) %all-to-all-start.1) | async-done | bytes 2162720 | tf_op jit(solution)/shard_map/all_to_all | solution.py:318
  135.1 0.0 copy-start
  135.1 4.5 %all-to-all-start = ((s16[32,264,128]{2,1,0:T(8,128)(2,1)}), s16[32,264,128]{2,1,0:T(8,128)(2,1)}, u32[]{:S(2)}, u32[]{:S(2)}) async-start(s16[32,264,128]{2,1,0:T(8,128)(2,1)} %bitcast.11), calls=%async_computation | async-start | bytes 4325376 | tf_op jit(solution)/shard_map/all_to_all | solution.py:318
  139.6 0.0 copy-done.1
  139.6 0.1 reshape.142
  139.7 0.1 add.176
  139.8 0.1 add.177
  139.8 0.0 copy-done.2
  139.9 0.1 dynamic_slice.6
  139.9 0.1 broadcast_add_fusion.1
  140.0 0.7 add.173.vir_ref
  140.7 0.1 add.180
  140.8 0.6 broadcast_add_fusion.occ_ref
  141.4 1.0 fusion.1.spread_ref
  142.4 1.0 fusion.spread_ref
  143.3 5.5 %direct.3.refs_4_.refs_5_.refs_6_.refs_7_ = f32[2048,512]{1,0:T(8,128)} custom-call(bf16[512,512]{1,0:T(8,128)(2,1)} %fusion.1.spread_ref, f32[2,2048,256]{2,1,0:T(8,128)} %get-tuple-element.16.refs_0_, f32[2,2048,256]{2,1,0:T(8,128)} %get-tuple-element.17.refs_1_), custom_call_target="tpu_custom_call" | custom-call | flops 2147483648 | bytes 8388608 | tf_op jit(solution)/shard_map/direct/pallas_call | solution.py:237
  148.9 0.0 copy-done
  148.9 5.5 %direct.2.refs_4_.refs_5_.refs_6_.refs_7_ = f32[2048,512]{1,0:T(8,128)} custom-call(bf16[512,512]{1,0:T(8,128)(2,1)} %fusion.1.spread_ref, f32[2,2048,256]{2,1,0:T(8,128)} %get-tuple-element.16.refs_0_, f32[2,2048,256]{2,1,0:T(8,128)} %get-tuple-element.17.refs_1_), custom_call_target="tpu_custom_call" | custom-call | flops 2147483648 | bytes 8388608 | tf_op jit(solution)/shard_map/direct/pallas_call | solution.py:237
  154.4 6.2 %update.2.refs_8_ = f32[2048,1024]{1,0:T(8,128)} custom-call(bf16[512,512]{1,0:T(8,128)(2,1)} %fusion.spread_ref, f32[1,1024]{1,0:T(1,128)} %add.173.vir_ref, f32[8,1,256]{2,1,0:T(1,128)} %broadcast_add_fusion.occ_ref, s16[8,4,264,128]{3,2,1,0:T(8,128)(2,1)} %bitcast.7, s16[8,4,264,128]{3,2,1,0:T(8,128)(2,1)} %bitcast.8, s16[8,4,264,128]{3,2,1,0:T(8,128)(2,1)} %bitcast.9, ...), custom_call_target="tpu_custom_call" | custom-call | flops 2147483648 | bytes 10485760 | tf_op jit(solution)/shard_map/update/pallas_call | solution.py:290
  160.6 29.1 %all-to-all-done = s16[32,264,128]{2,1,0:T(8,128)(2,1)} async-done(((s16[32,264,128]{2,1,0:T(8,128)(2,1)}), s16[32,264,128]{2,1,0:T(8,128)(2,1)}, u32[]{:S(2)}, u32[]{:S(2)}) %all-to-all-start) | async-done | bytes 2162720 | tf_op jit(solution)/shard_map/all_to_all | solution.py:318
  189.7 6.2 %update.3 = f32[2048,1024]{1,0:T(8,128)} custom-call(bf16[512,512]{1,0:T(8,128)(2,1)} %fusion.spread_ref, f32[1,1024]{1,0:T(1,128)} %add.173.vir_ref, f32[8,1,256]{2,1,0:T(1,128)} %broadcast_add_fusion.occ_ref, s16[8,4,264,128]{3,2,1,0:T(8,128)(2,1)} %bitcast.3.refs_0_.refs_1_.refs_2_.refs_3_, ...), custom_call_target="tpu_custom_call", output_to_operand_aliasing={{}: (11, {})} | custom-call | flops 2147483648 | bytes 10485760 | tf_op jit(solution)/shard_map/update/pallas_call | solution.py:290
  (5 shorter events, 0.0 us)
Async XLA Ops:
  6.5 48.8 %all-gather.6.cloned.1.call-start = ((), (), s32[]{:S(2)}) async-start(), calls=%async_computation.3 | async-start | bytes 1179648 | tf_op jit(solution)/shard_map/all_gather | solution.py:324
  10.2 82.0 %all-gather.4.cloned.1.call-start = ((), (), s32[]{:S(2)}) async-start(), calls=%async_computation.2 | async-start | bytes 4718592 | tf_op jit(solution)/shard_map/all_gather | solution.py:324
  75.8 59.3 %all-to-all-start.1 = ((s16[32,264,128]{2,1,0:T(8,128)(2,1)}), s16[32,264,128]{2,1,0:T(8,128)(2,1)S(1)}, u32[]{:S(2)}, u32[]{:S(2)}) async-start(s16[32,264,128]{2,1,0:T(8,128)(2,1)} %bitcast.12), calls=%async_computation.1 | async-start | bytes 4325376 | tf_op jit(solution)/shard_map/all_to_all | solution.py:318
  108.7 30.9 %copy-start.1 = (f32[128]{0:T(128)S(1)}, f32[128]{0:T(128)}, u32[]{:S(2)}) copy-start(f32[128]{0:T(128)} %param.12) | copy-start | bytes 1540
  108.7 31.2 %copy-start.2 = (f32[64]{0:T(128)S(1)}, f32[64]{0:T(128)}, u32[]{:S(2)}) copy-start(f32[64]{0:T(128)} %param.13) | copy-start | bytes 772
  135.1 13.7 %copy-start = (s16[32,264,128]{2,1,0:T(8,128)(2,1)}, s16[32,264,128]{2,1,0:T(8,128)(2,1)S(1)}, u32[]{:S(2)}) copy-start(s16[32,264,128]{2,1,0:T(8,128)(2,1)S(1)} %all-to-all-done.1) | copy-start | bytes 6488068
  135.1 54.6 %all-to-all-start = ((s16[32,264,128]{2,1,0:T(8,128)(2,1)}), s16[32,264,128]{2,1,0:T(8,128)(2,1)}, u32[]{:S(2)}, u32[]{:S(2)}) async-start(s16[32,264,128]{2,1,0:T(8,128)(2,1)} %bitcast.11), calls=%async_computation | async-start | bytes 4325376 | tf_op jit(solution)/shard_map/all_to_all | solution.py:318
Sparse Core Ops, SparseCore 0:
  10.3 32.5 all-gather.5
  44.5 47.6 all-gather.3

commit v23 on v22

--- a/solution.py
+++ b/solution.py
@@ -95,7 +95,7 @@
     ladder_ref, packed_ref, product = refs[:3]
     slab_refs = gathered_refs
     if coded:
-        slab_refs, stage, sems = (refs[3], *gathered_refs[1:]), refs[4], refs[5]
+        slab_refs, stage, sems = refs[3:4], refs[4], refs[5]
     step = pl.program_id(0)
     cols = product.shape[1]
     slab_rows = slab_refs[0].shape[0] // tile_total
@@ -124,6 +124,7 @@
             at = pl.ds(pl.multiple_of(shard * shard_rows, CODE_ROWS), shard_rows)
             return pltpu.make_async_copy(gathered_refs[0].at[at, :], stage.at[at, :], sems.at[shard])
 
+        coded_cols = stage.shape[1]
         for shard in range(tile_total):
             copy_of(shard).start()
 
@@ -134,7 +135,8 @@
             values = stage[pl.ds(at, slab_rows), :].astype(jnp.int32).astype(jnp.float32)
             scale = jnp.exp2(code.astype(jnp.int32).astype(jnp.float32)[:1] - SLAB_BITS)
             to = pl.ds(pl.multiple_of(shard * slab_rows, slab_rows), slab_rows)
-            slab_refs[0][to, :] = (values * scale).astype(jnp.bfloat16)
+            slab_refs[0][to, coded_cols:] = gathered_refs[1][to, :]
+            slab_refs[0][to, :coded_cols] = (values * scale).astype(jnp.bfloat16)
             return carry
 
         lax.fori_loop(0, tile_total, use, 0)
@@ -207,7 +209,7 @@
         ],
         scratch_shapes=[pltpu.VMEM((PAIR_SQ, cols), jnp.float32)]
         + [
-            pltpu.VMEM((W * W, slab[0].shape[1]), jnp.bfloat16),
+            pltpu.VMEM((W * W, cols), jnp.bfloat16),
             pltpu.VMEM(slab[0].shape, slab[0].dtype),
             pltpu.SemaphoreType.DMA((tile_total,)),
         ]

time: 203 us -> 203 us (level)
  Pallas kernels: 64 us -> 61.3 us
  waiting for transfers between devices: 64.9 us -> 67.6 us
    all_gather x2, waiting for transfers between devices: 8.61 us -> 14.3 us  [body(): plain = [lax.all_gather(part, 'occ', axis=0, tiled=True) for part in plain]]
    all_to_all x2, waiting for transfers between devices: 55.6 us -> 52.5 us  [exchanged(): lax.all_to_all(packed.reshape(tile_total * vir_count, rows, block), ('occ...]
    pallas_call x2, Pallas kernels: 37 us -> 34.2 us  [ladder_call(): pl.pallas_call(functools.partial(ladder_kernel, tile_total, vir_count, ch...]
  transfers between devices with their start and end apart: 4 -> 4, of which waited for: 3 -> 3; matrix products, arithmetic and copies ran while one was open for 2% -> 2% of each run, Pallas kernels for 27% -> 25%
where the time goes in v23:
time: 203 us
  waiting for transfers between devices  67.6 us (33%)
  Pallas kernels  61.3 us (30%)
  blocking collectives  43 us (21%)
  between operations  13.5 us (7%)
  starting transfers between devices  12.1 us (6%)
  other arithmetic  2.63 us (1%)
  local copies, waits for them, and re-layouts  2.44 us (1%)
    all_to_all x2, waiting for transfers between devices, exchanged(): lax.all_to_all(packed.reshape(tile_total * vir_count, rows, block), ('occ...  52.5 us
    all_gather x1, blocking collectives, body(): lax.all_gather(coded, 'occ', axis=0, tiled=True)  43 us
    pallas_call x2, Pallas kernels, ladder_call(): pl.pallas_call(functools.partial(ladder_kernel, tile_total, vir_count, ch...  34.2 us
    all_gather x2, waiting for transfers between devices, body(): plain = [lax.all_gather(part, 'occ', axis=0, tiled=True) for part in plain]  14.3 us
    pallas_call x2, Pallas kernels, update_call(): pl.pallas_call(functools.partial(update_kernel, vir_count, at_once), grid...  12.3 us
    all_to_all x2, starting transfers between devices, exchanged(): lax.all_to_all(packed.reshape(tile_total * vir_count, rows, block), ('occ...  12.1 us
    pallas_call x2, Pallas kernels, direct_call(): pl.pallas_call(direct_kernel, grid=(rows // step_rows,), in_specs=[pl.Blo...  11.1 us
  transfers between devices with their start and end apart: 4, of which 3 were waited for; matrix products, arithmetic and copies ran while one was open for 2% of the time, Pallas kernels for 25%

profile of v23, /device:TPU:0, one launch (start us, length us, event | category | flops | bytes accessed | tf_op | source)
XLA Modules:
  0.0 202.6 jit_solution(16744116872517537945)
XLA Ops:
  6.5 0.0 all-gather.6.cloned.1.call-start
  6.5 3.6 %screen.1 = (s16[528,384]{1,0:T(8,128)(2,1)}, bf16[512,128]{1,0:T(8,128)(2,1)}, bf16[512,512]{1,0:T(8,128)(2,1)}) custom-call(s32[4,4]{1,0:T(4,128)} %int_mask.1, bf16[512,1024]{1,0:T(8,128)(2,1)} %slab_ref.1), custom_call_target="tpu_custom_call" | custom-call | tf_op jit(solution)/shard_map/screen/pallas_call | solution.py:82
  10.2 0.0 all-gather.6.cloned.1.call-update
  10.2 0.0 all-gather.4.cloned.1.call-start
  10.2 0.7 all-gather.4.cloned.1.call-update
  10.9 1.3 copy.9.amp_mask
  12.3 43.0 %all-gather.7.refs_0_ = s16[4224,384]{1,0:T(8,128)(2,1)} all-gather(s16[528,384]{1,0:T(8,128)(2,1)} %get-tuple-element.14), channel_id=1, replica_groups=mesh['occ'=8,'vir'=4] {'occ'}, dimensions={0}, use_global_device_ids=true | all-gather | bytes 3649536 | tf_op jit(solution)/shard_map/all_gather | solution.py:327
  55.3 0.0 all-gather.6.cloned.1.call-done.refs_1_
  55.3 17.8 %ladder.3 = (f32[2,2048,256]{2,1,0:T(8,128)}, s16[8,4,264,128]{3,2,1,0:T(8,128)(2,1)}) custom-call(s32[8,4]{1,0:T(8,128)} %copy.9.amp_mask, s32[8]{0:T(128)} %numbers.3, bf16[2048,4096]{1,0:T(8,128)(2,1)} %rows_ref.3, s16[4224,384]{1,0:T(8,128)(2,1)} %all-gather.7.refs_0_, bf16[4096,128]{1,0:T(8,128)(2,1)} %all-gather.6.cloned.1.call-done.refs_1_), custom_call_target="tpu_custom_call" | custom-call | flops 8589934592 | bytes 27262976 | tf_op jit(solution)/shard_map/ladder/pallas_call | solution.py:188
  73.1 7.8 %all-to-all-start.1 = ((s16[32,264,128]{2,1,0:T(8,128)(2,1)}), s16[32,264,128]{2,1,0:T(8,128)(2,1)S(1)}, u32[]{:S(2)}, u32[]{:S(2)}) async-start(s16[32,264,128]{2,1,0:T(8,128)(2,1)} %bitcast.12), calls=%async_computation.1 | async-start | bytes 4325376 | tf_op jit(solution)/shard_map/all_to_all | solution.py:320
  80.9 14.3 %all-gather.4.cloned.1.call-done.refs_0_ = bf16[4096,512]{1,0:T(8,128)(2,1)} async-done(((bf16[512,512]{1,0:T(8,128)(2,1)}), bf16[4096,512]{1,0:T(8,128)(2,1)}) %all-gather.4.cloned.1.call-update) | async-done | bytes 4194320 | tf_op jit(solution)/shard_map/all_gather | solution.py:326
  95.2 16.5 %ladder.2 = (f32[2,2048,256]{2,1,0:T(8,128)}, s16[8,4,264,128]{3,2,1,0:T(8,128)(2,1)}) custom-call(s32[8,4]{1,0:T(8,128)} %copy.9.amp_mask, s32[8]{0:T(128)} %numbers.3, bf16[2048,4096]{1,0:T(8,128)(2,1)} %rows_ref.3, bf16[4096,512]{1,0:T(8,128)(2,1)} %all-gather.4.cloned.1.call-done.refs_0_), custom_call_target="tpu_custom_call" | custom-call | flops 8589934592 | bytes 27262976 | tf_op jit(solution)/shard_map/ladder/pallas_call | solution.py:188
  111.7 0.0 copy-start.1
  111.7 0.0 copy-start.2
  111.7 23.4 %all-to-all-done.1 = s16[32,264,128]{2,1,0:T(8,128)(2,1)S(1)} async-done(((s16[32,264,128]{2,1,0:T(8,128)(2,1)}), s16[32,264,128]{2,1,0:T(8,128)(2,1)S(1)}, u32[]{:S(2)}, u32[]{:S(2)}) %all-to-all-start.1) | async-done | bytes 2162720 | tf_op jit(solution)/shard_map/all_to_all | solution.py:320
  135.1 0.0 copy-start
  135.1 4.3 %all-to-all-start = ((s16[32,264,128]{2,1,0:T(8,128)(2,1)}), s16[32,264,128]{2,1,0:T(8,128)(2,1)}, u32[]{:S(2)}, u32[]{:S(2)}) async-start(s16[32,264,128]{2,1,0:T(8,128)(2,1)} %bitcast.11), calls=%async_computation | async-start | bytes 4325376 | tf_op jit(solution)/shard_map/all_to_all | solution.py:320
  139.5 0.0 copy-done.1
  139.5 0.1 reshape.142
  139.6 0.1 add.176
  139.6 0.1 add.177
  139.7 0.0 copy-done.2
  139.7 0.1 dynamic_slice.6
  139.8 0.1 broadcast_add_fusion.1
  139.9 0.7 add.173.vir_ref
  140.6 0.1 add.180
  140.7 0.6 broadcast_add_fusion.occ_ref
  141.3 1.0 fusion.1.spread_ref
  142.3 1.0 fusion.spread_ref
  143.2 5.5 %direct.3.refs_4_.refs_5_.refs_6_.refs_7_ = f32[2048,512]{1,0:T(8,128)} custom-call(bf16[512,512]{1,0:T(8,128)(2,1)} %fusion.1.spread_ref, f32[2,2048,256]{2,1,0:T(8,128)} %get-tuple-element.16.refs_0_, f32[2,2048,256]{2,1,0:T(8,128)} %get-tuple-element.17.refs_1_), custom_call_target="tpu_custom_call" | custom-call | flops 2147483648 | bytes 8388608 | tf_op jit(solution)/shard_map/direct/pallas_call | solution.py:239
  148.7 0.0 copy-done
  148.8 5.5 %direct.2.refs_4_.refs_5_.refs_6_.refs_7_ = f32[2048,512]{1,0:T(8,128)} custom-call(bf16[512,512]{1,0:T(8,128)(2,1)} %fusion.1.spread_ref, f32[2,2048,256]{2,1,0:T(8,128)} %get-tuple-element.16.refs_0_, f32[2,2048,256]{2,1,0:T(8,128)} %get-tuple-element.17.refs_1_), custom_call_target="tpu_custom_call" | custom-call | flops 2147483648 | bytes 8388608 | tf_op jit(solution)/shard_map/direct/pallas_call | solution.py:239
  154.3 6.2 %update.2.refs_8_ = f32[2048,1024]{1,0:T(8,128)} custom-call(bf16[512,512]{1,0:T(8,128)(2,1)} %fusion.spread_ref, f32[1,1024]{1,0:T(1,128)} %add.173.vir_ref, f32[8,1,256]{2,1,0:T(1,128)} %broadcast_add_fusion.occ_ref, s16[8,4,264,128]{3,2,1,0:T(8,128)(2,1)} %bitcast.7, s16[8,4,264,128]{3,2,1,0:T(8,128)(2,1)} %bitcast.8, s16[8,4,264,128]{3,2,1,0:T(8,128)(2,1)} %bitcast.9, ...), custom_call_target="tpu_custom_call" | custom-call | flops 2147483648 | bytes 10485760 | tf_op jit(solution)/shard_map/update/pallas_call | solution.py:292
  160.5 29.1 %all-to-all-done = s16[32,264,128]{2,1,0:T(8,128)(2,1)} async-done(((s16[32,264,128]{2,1,0:T(8,128)(2,1)}), s16[32,264,128]{2,1,0:T(8,128)(2,1)}, u32[]{:S(2)}, u32[]{:S(2)}) %all-to-all-start) | async-done | bytes 2162720 | tf_op jit(solution)/shard_map/all_to_all | solution.py:320
  189.6 6.2 %update.3 = f32[2048,1024]{1,0:T(8,128)} custom-call(bf16[512,512]{1,0:T(8,128)(2,1)} %fusion.spread_ref, f32[1,1024]{1,0:T(1,128)} %add.173.vir_ref, f32[8,1,256]{2,1,0:T(1,128)} %broadcast_add_fusion.occ_ref, s16[8,4,264,128]{3,2,1,0:T(8,128)(2,1)} %bitcast.3.refs_0_.refs_1_.refs_2_.refs_3_, ...), custom_call_target="tpu_custom_call", output_to_operand_aliasing={{}: (11, {})} | custom-call | flops 2147483648 | bytes 10485760 | tf_op jit(solution)/shard_map/update/pallas_call | solution.py:292
  (5 shorter events, 0.0 us)
Async XLA Ops:
  6.5 48.8 %all-gather.6.cloned.1.call-start = ((), (), s32[]{:S(2)}) async-start(), calls=%async_computation.3 | async-start | bytes 1179648 | tf_op jit(solution)/shard_map/all_gather | solution.py:326
  10.2 85.0 %all-gather.4.cloned.1.call-start = ((), (), s32[]{:S(2)}) async-start(), calls=%async_computation.2 | async-start | bytes 4718592 | tf_op jit(solution)/shard_map/all_gather | solution.py:326
  73.1 62.0 %all-to-all-start.1 = ((s16[32,264,128]{2,1,0:T(8,128)(2,1)}), s16[32,264,128]{2,1,0:T(8,128)(2,1)S(1)}, u32[]{:S(2)}, u32[]{:S(2)}) async-start(s16[32,264,128]{2,1,0:T(8,128)(2,1)} %bitcast.12), calls=%async_computation.1 | async-start | bytes 4325376 | tf_op jit(solution)/shard_map/all_to_all | solution.py:320
  111.7 27.8 %copy-start.1 = (f32[128]{0:T(128)S(1)}, f32[128]{0:T(128)}, u32[]{:S(2)}) copy-start(f32[128]{0:T(128)} %param.12) | copy-start | bytes 1540
  111.7 28.0 %copy-start.2 = (f32[64]{0:T(128)S(1)}, f32[64]{0:T(128)}, u32[]{:S(2)}) copy-start(f32[64]{0:T(128)} %param.13) | copy-start | bytes 772
  135.1 13.6 %copy-start = (s16[32,264,128]{2,1,0:T(8,128)(2,1)}, s16[32,264,128]{2,1,0:T(8,128)(2,1)S(1)}, u32[]{:S(2)}) copy-start(s16[32,264,128]{2,1,0:T(8,128)(2,1)S(1)} %all-to-all-done.1) | copy-start | bytes 6488068
  135.1 54.4 %all-to-all-start = ((s16[32,264,128]{2,1,0:T(8,128)(2,1)}), s16[32,264,128]{2,1,0:T(8,128)(2,1)}, u32[]{:S(2)}, u32[]{:S(2)}) async-start(s16[32,264,128]{2,1,0:T(8,128)(2,1)} %bitcast.11), calls=%async_computation | async-start | bytes 4325376 | tf_op jit(solution)/shard_map/all_to_all | solution.py:320
Sparse Core Ops, SparseCore 0:
  10.3 32.5 all-gather.5
  44.5 50.6 all-gather.3

commit v24 on v23

--- a/solution.py
+++ b/solution.py
@@ -76,8 +76,8 @@
 def screen_call(chunks, int_mask, integrals):
     slab_rows, slab_cols = integrals.shape
     cols = slab_cols // chunks
-    coded_cols = cols - cols // 4
-    plain_cols = [cols // 4] + [cols] * (chunks - 1)
+    coded_cols = cols - cols // 2
+    plain_cols = [cols // 2] + [cols] * (chunks - 1)
     vmem = pl.BlockSpec(memory_space=pltpu.VMEM)
     return pl.pallas_call(
         functools.partial(screen_kernel, slab_cols // W // chunks),

time: 203 us -> 218 us (1.074)
  waiting for transfers between devices: 67.6 us -> 90.2 us
  blocking collectives: 43 us -> 38.8 us
  starting transfers between devices: 12.1 us -> 8.32 us
    all_gather x2, waiting for transfers between devices: 14.3 us -> 60.4 us  [body(): plain = [lax.all_gather(part, 'occ', axis=0, tiled=True) for part in plain]]
    all_to_all x2, waiting for transfers between devices: 52.5 us -> 29.1 us  [exchanged(): lax.all_to_all(packed.reshape(tile_total * vir_count, rows, block), ('occ...]
    all_gather x1, blocking collectives: 43 us -> 38.8 us  [body(): lax.all_gather(coded, 'occ', axis=0, tiled=True)]
    all_to_all x2, starting transfers between devices: 12.1 us -> 8.27 us  [exchanged(): lax.all_to_all(packed.reshape(tile_total * vir_count, rows, block), ('occ...]
  transfers between devices with their start and end apart: 4 -> 4, of which waited for: 3 -> 3; matrix products, arithmetic and copies ran while one was open for 2% -> 2% of each run, Pallas kernels for 25% -> 24%
where the time goes in v24:
time: 218 us; the launch traced here: 217 us
  waiting for transfers between devices  90.2 us (41%)
  Pallas kernels  61.4 us (28%)
  blocking collectives  38.8 us (18%)
  between operations  13.5 us (6%)
  starting transfers between devices  8.32 us (4%)
  other arithmetic  2.63 us (1%)
  local copies, waits for them, and re-layouts  2.45 us (1%)
    all_gather x2, waiting for transfers between devices, body(): plain = [lax.all_gather(part, 'occ', axis=0, tiled=True) for part in plain]  60.4 us
    all_gather x1, blocking collectives, body(): lax.all_gather(coded, 'occ', axis=0, tiled=True)  38.8 us
    pallas_call x2, Pallas kernels, ladder_call(): pl.pallas_call(functools.partial(ladder_kernel, tile_total, vir_count, ch...  34.5 us
    all_to_all x2, waiting for transfers between devices, exchanged(): lax.all_to_all(packed.reshape(tile_total * vir_count, rows, block), ('occ...  29.1 us
    pallas_call x2, Pallas kernels, update_call(): pl.pallas_call(functools.partial(update_kernel, vir_count, at_once), grid...  12.3 us
    pallas_call x2, Pallas kernels, direct_call(): pl.pallas_call(direct_kernel, grid=(rows // step_rows,), in_specs=[pl.Blo...  11.1 us
    all_to_all x2, starting transfers between devices, exchanged(): lax.all_to_all(packed.reshape(tile_total * vir_count, rows, block), ('occ...  8.27 us
  transfers between devices with their start and end apart: 4, of which 3 were waited for; matrix products, arithmetic and copies ran while one was open for 2% of the time, Pallas kernels for 24%

profile of v24, /device:TPU:0, one launch (start us, length us, event | category | flops | bytes accessed | tf_op | source)
XLA Modules:
  0.0 217.2 jit_solution(2549996686921025532)
XLA Ops:
  6.5 0.0 all-gather.6.cloned.1.call-start
  6.5 3.5 %screen.1 = (s16[528,256]{1,0:T(8,128)(2,1)}, bf16[512,256]{1,0:T(8,128)(2,1)}, bf16[512,512]{1,0:T(8,128)(2,1)}) custom-call(s32[4,4]{1,0:T(4,128)} %int_mask.1, bf16[512,1024]{1,0:T(8,128)(2,1)} %slab_ref.1), custom_call_target="tpu_custom_call" | custom-call | tf_op jit(solution)/shard_map/screen/pallas_call | solution.py:82
  10.1 0.0 all-gather.6.cloned.1.call-update
  10.1 0.0 all-gather.4.cloned.1.call-start
  10.2 0.7 all-gather.4.cloned.1.call-update
  10.9 1.4 copy.9.amp_mask
  12.2 38.8 %all-gather.7.refs_0_ = s16[4224,256]{1,0:T(8,128)(2,1)} all-gather(s16[528,256]{1,0:T(8,128)(2,1)} %get-tuple-element.14), channel_id=1, replica_groups=mesh['occ'=8,'vir'=4] {'occ'}, dimensions={0}, use_global_device_ids=true | all-gather | bytes 2433024 | tf_op jit(solution)/shard_map/all_gather | solution.py:327
  51.0 3.9 %all-gather.6.cloned.1.call-done.refs_1_ = bf16[4096,256]{1,0:T(8,128)(2,1)} async-done(((bf16[512,256]{1,0:T(8,128)(2,1)}), bf16[4096,256]{1,0:T(8,128)(2,1)}) %all-gather.6.cloned.1.call-update) | async-done | bytes 2097168 | tf_op jit(solution)/shard_map/all_gather | solution.py:326
  54.9 18.0 %ladder.3 = (f32[2,2048,256]{2,1,0:T(8,128)}, s16[8,4,264,128]{3,2,1,0:T(8,128)(2,1)}) custom-call(s32[8,4]{1,0:T(8,128)} %copy.9.amp_mask, s32[8]{0:T(128)} %numbers.3, bf16[2048,4096]{1,0:T(8,128)(2,1)} %rows_ref.3, s16[4224,256]{1,0:T(8,128)(2,1)} %all-gather.7.refs_0_, bf16[4096,256]{1,0:T(8,128)(2,1)} %all-gather.6.cloned.1.call-done.refs_1_), custom_call_target="tpu_custom_call" | custom-call | flops 8589934592 | bytes 27262976 | tf_op jit(solution)/shard_map/ladder/pallas_call | solution.py:188
  72.8 3.9 %all-to-all-start.1 = ((s16[32,264,128]{2,1,0:T(8,128)(2,1)}), s16[32,264,128]{2,1,0:T(8,128)(2,1)S(1)}, u32[]{:S(2)}, u32[]{:S(2)}) async-start(s16[32,264,128]{2,1,0:T(8,128)(2,1)} %bitcast.12), calls=%async_computation.1 | async-start | bytes 4325376 | tf_op jit(solution)/shard_map/all_to_all | solution.py:320
  76.7 56.5 %all-gather.4.cloned.1.call-done.refs_0_ = bf16[4096,512]{1,0:T(8,128)(2,1)} async-done(((bf16[512,512]{1,0:T(8,128)(2,1)}), bf16[4096,512]{1,0:T(8,128)(2,1)}) %all-gather.4.cloned.1.call-update) | async-done | bytes 4194320 | tf_op jit(solution)/shard_map/all_gather | solution.py:326
  133.2 16.5 %ladder.2 = (f32[2,2048,256]{2,1,0:T(8,128)}, s16[8,4,264,128]{3,2,1,0:T(8,128)(2,1)}) custom-call(s32[8,4]{1,0:T(8,128)} %copy.9.amp_mask, s32[8]{0:T(128)} %numbers.3, bf16[2048,4096]{1,0:T(8,128)(2,1)} %rows_ref.3, bf16[4096,512]{1,0:T(8,128)(2,1)} %all-gather.4.cloned.1.call-done.refs_0_), custom_call_target="tpu_custom_call" | custom-call | flops 8589934592 | bytes 27262976 | tf_op jit(solution)/shard_map/ladder/pallas_call | solution.py:188
  149.7 0.0 copy-start.1
  149.7 0.0 copy-start.2
  149.7 0.0 all-to-all-done.1
  149.7 0.0 copy-start
  149.7 4.4 %all-to-all-start = ((s16[32,264,128]{2,1,0:T(8,128)(2,1)}), s16[32,264,128]{2,1,0:T(8,128)(2,1)}, u32[]{:S(2)}, u32[]{:S(2)}) async-start(s16[32,264,128]{2,1,0:T(8,128)(2,1)} %bitcast.11), calls=%async_computation | async-start | bytes 4325376 | tf_op jit(solution)/shard_map/all_to_all | solution.py:320
  154.1 0.0 copy-done.1
  154.1 0.1 reshape.142
  154.2 0.1 add.176
  154.3 0.1 add.177
  154.4 0.0 copy-done.2
  154.4 0.1 dynamic_slice.6
  154.5 0.1 broadcast_add_fusion.1
  154.5 0.7 add.173.vir_ref
  155.2 0.1 add.180
  155.4 0.6 broadcast_add_fusion.occ_ref
  156.0 1.0 fusion.1.spread_ref
  156.9 1.0 fusion.spread_ref
  157.9 5.5 %direct.3.refs_4_.refs_5_.refs_6_.refs_7_ = f32[2048,512]{1,0:T(8,128)} custom-call(bf16[512,512]{1,0:T(8,128)(2,1)} %fusion.1.spread_ref, f32[2,2048,256]{2,1,0:T(8,128)} %get-tuple-element.16.refs_0_, f32[2,2048,256]{2,1,0:T(8,128)} %get-tuple-element.17.refs_1_), custom_call_target="tpu_custom_call" | custom-call | flops 2147483648 | bytes 8388608 | tf_op jit(solution)/shard_map/direct/pallas_call | solution.py:239
  163.4 0.0 copy-done
  163.4 5.5 %direct.2.refs_4_.refs_5_.refs_6_.refs_7_ = f32[2048,512]{1,0:T(8,128)} custom-call(bf16[512,512]{1,0:T(8,128)(2,1)} %fusion.1.spread_ref, f32[2,2048,256]{2,1,0:T(8,128)} %get-tuple-element.16.refs_0_, f32[2,2048,256]{2,1,0:T(8,128)} %get-tuple-element.17.refs_1_), custom_call_target="tpu_custom_call" | custom-call | flops 2147483648 | bytes 8388608 | tf_op jit(solution)/shard_map/direct/pallas_call | solution.py:239
  169.0 6.2 %update.2.refs_8_ = f32[2048,1024]{1,0:T(8,128)} custom-call(bf16[512,512]{1,0:T(8,128)(2,1)} %fusion.spread_ref, f32[1,1024]{1,0:T(1,128)} %add.173.vir_ref, f32[8,1,256]{2,1,0:T(1,128)} %broadcast_add_fusion.occ_ref, s16[8,4,264,128]{3,2,1,0:T(8,128)(2,1)} %bitcast.7, s16[8,4,264,128]{3,2,1,0:T(8,128)(2,1)} %bitcast.8, s16[8,4,264,128]{3,2,1,0:T(8,128)(2,1)} %bitcast.9, ...), custom_call_target="tpu_custom_call" | custom-call | flops 2147483648 | bytes 10485760 | tf_op jit(solution)/shard_map/update/pallas_call | solution.py:292
  175.1 29.1 %all-to-all-done = s16[32,264,128]{2,1,0:T(8,128)(2,1)} async-done(((s16[32,264,128]{2,1,0:T(8,128)(2,1)}), s16[32,264,128]{2,1,0:T(8,128)(2,1)}, u32[]{:S(2)}, u32[]{:S(2)}) %all-to-all-start) | async-done | bytes 2162720 | tf_op jit(solution)/shard_map/all_to_all | solution.py:320
  204.2 6.2 %update.3 = f32[2048,1024]{1,0:T(8,128)} custom-call(bf16[512,512]{1,0:T(8,128)(2,1)} %fusion.spread_ref, f32[1,1024]{1,0:T(1,128)} %add.173.vir_ref, f32[8,1,256]{2,1,0:T(1,128)} %broadcast_add_fusion.occ_ref, s16[8,4,264,128]{3,2,1,0:T(8,128)(2,1)} %bitcast.3.refs_0_.refs_1_.refs_2_.refs_3_, ...), custom_call_target="tpu_custom_call", output_to_operand_aliasing={{}: (11, {})} | custom-call | flops 2147483648 | bytes 10485760 | tf_op jit(solution)/shard_map/update/pallas_call | solution.py:292
  (5 shorter events, 0.0 us)
Async XLA Ops:
  6.5 48.3 %all-gather.6.cloned.1.call-start = ((), (), s32[]{:S(2)}) async-start(), calls=%async_computation.3 | async-start | bytes 2359296 | tf_op jit(solution)/shard_map/all_gather | solution.py:326
  10.1 123.1 %all-gather.4.cloned.1.call-start = ((), (), s32[]{:S(2)}) async-start(), calls=%async_computation.2 | async-start | bytes 4718592 | tf_op jit(solution)/shard_map/all_gather | solution.py:326
  72.8 76.9 %all-to-all-start.1 = ((s16[32,264,128]{2,1,0:T(8,128)(2,1)}), s16[32,264,128]{2,1,0:T(8,128)(2,1)S(1)}, u32[]{:S(2)}, u32[]{:S(2)}) async-start(s16[32,264,128]{2,1,0:T(8,128)(2,1)} %bitcast.12), calls=%async_computation.1 | async-start | bytes 4325376 | tf_op jit(solution)/shard_map/all_to_all | solution.py:320
  149.7 4.5 %copy-start.1 = (f32[128]{0:T(128)S(1)}, f32[128]{0:T(128)}, u32[]{:S(2)}) copy-start(f32[128]{0:T(128)} %param.12) | copy-start | bytes 1540
  149.7 4.7 %copy-start.2 = (f32[64]{0:T(128)S(1)}, f32[64]{0:T(128)}, u32[]{:S(2)}) copy-start(f32[64]{0:T(128)} %param.13) | copy-start | bytes 772
  149.7 13.7 %copy-start = (s16[32,264,128]{2,1,0:T(8,128)(2,1)}, s16[32,264,128]{2,1,0:T(8,128)(2,1)S(1)}, u32[]{:S(2)}) copy-start(s16[32,264,128]{2,1,0:T(8,128)(2,1)S(1)} %all-to-all-done.1) | copy-start | bytes 6488068
  149.7 54.5 %all-to-all-start = ((s16[32,264,128]{2,1,0:T(8,128)(2,1)}), s16[32,264,128]{2,1,0:T(8,128)(2,1)}, u32[]{:S(2)}, u32[]{:S(2)}) async-start(s16[32,264,128]{2,1,0:T(8,128)(2,1)} %bitcast.11), calls=%async_computation | async-start | bytes 4325376 | tf_op jit(solution)/shard_map/all_to_all | solution.py:320
Sparse Core Ops, SparseCore 0:
  10.2 44.5 all-gather.5
  56.4 76.6 all-gather.3

commit v25 on v23

--- a/solution.py
+++ b/solution.py
@@ -266,7 +266,11 @@
     for n, direct_ref in enumerate(direct_refs):
         at = slice(n * PAIR_SQ, (n + 1) * PAIR_SQ)
         occ = jnp.transpose(jnp.broadcast_to(occ_ref[n], (128, PAIR_SQ)))[:, :1]
-        refs[-1][at, :] = (direct_ref[...] + mirror[at]) / (vir_ref[...] - occ)
+        denominator = vir_ref[...] - occ
+        inverse = pl.reciprocal(denominator, approx=True)
+        for _ in range(2):
+            inverse = inverse * (2.0 - denominator * inverse)
+        refs[-1][at, :] = (direct_ref[...] + mirror[at]) * inverse
 
 
 def update_call(chunk, chunks, at_once, arrived, spread, vir_sum, occ_sum, direct, earlier):

time: 203 us -> 204 us (level)
  transfers between devices with their start and end apart: 4 -> 4, of which waited for: 3 -> 3; matrix products, arithmetic and copies ran while one was open for 2% -> 2% of each run, Pallas kernels for 25% -> 26%
where the time goes in v25:
time: 204 us; the launch traced here: 203 us
  waiting for transfers between devices  66.9 us (33%)
  Pallas kernels  62.6 us (31%)
  blocking collectives  43 us (21%)
  between operations  13.5 us (7%)
  starting transfers between devices  12.1 us (6%)
  other arithmetic  2.63 us (1%)
  local copies, waits for them, and re-layouts  2.44 us (1%)
    all_to_all x2, waiting for transfers between devices, exchanged(): lax.all_to_all(packed.reshape(tile_total * vir_count, rows, block), ('occ...  51.9 us
    all_gather x1, blocking collectives, body(): lax.all_gather(coded, 'occ', axis=0, tiled=True)  43 us
    pallas_call x2, Pallas kernels, ladder_call(): pl.pallas_call(functools.partial(ladder_kernel, tile_total, vir_count, ch...  34.2 us
    all_gather x2, waiting for transfers between devices, body(): plain = [lax.all_gather(part, 'occ', axis=0, tiled=True) for part in plain]  14.3 us
    pallas_call x2, Pallas kernels, update_call(): pl.pallas_call(functools.partial(update_kernel, vir_count, at_once), grid...  13.6 us
    all_to_all x2, starting transfers between devices, exchanged(): lax.all_to_all(packed.reshape(tile_total * vir_count, rows, block), ('occ...  12.1 us
    pallas_call x2, Pallas kernels, direct_call(): pl.pallas_call(direct_kernel, grid=(rows // step_rows,), in_specs=[pl.Blo...  11.1 us
  transfers between devices with their start and end apart: 4, of which 3 were waited for; matrix products, arithmetic and copies ran while one was open for 2% of the time, Pallas kernels for 26%

profile of v25, /device:TPU:0, one launch (start us, length us, event | category | flops | bytes accessed | tf_op | source)
XLA Modules:
  0.0 203.2 jit_solution(16787618294612020478)
XLA Ops:
  6.5 0.0 all-gather.6.cloned.1.call-start
  6.5 3.6 %screen.1 = (s16[528,384]{1,0:T(8,128)(2,1)}, bf16[512,128]{1,0:T(8,128)(2,1)}, bf16[512,512]{1,0:T(8,128)(2,1)}) custom-call(s32[4,4]{1,0:T(4,128)} %int_mask.1, bf16[512,1024]{1,0:T(8,128)(2,1)} %slab_ref.1), custom_call_target="tpu_custom_call" | custom-call | tf_op jit(solution)/shard_map/screen/pallas_call | solution.py:82
  10.2 0.0 all-gather.6.cloned.1.call-update
  10.2 0.0 all-gather.4.cloned.1.call-start
  10.2 0.7 all-gather.4.cloned.1.call-update
  10.9 1.3 copy.9.amp_mask
  12.3 43.0 %all-gather.7.refs_0_ = s16[4224,384]{1,0:T(8,128)(2,1)} all-gather(s16[528,384]{1,0:T(8,128)(2,1)} %get-tuple-element.14), channel_id=1, replica_groups=mesh['occ'=8,'vir'=4] {'occ'}, dimensions={0}, use_global_device_ids=true | all-gather | bytes 3649536 | tf_op jit(solution)/shard_map/all_gather | solution.py:331
  55.3 0.0 all-gather.6.cloned.1.call-done.refs_1_
  55.3 17.8 %ladder.3 = (f32[2,2048,256]{2,1,0:T(8,128)}, s16[8,4,264,128]{3,2,1,0:T(8,128)(2,1)}) custom-call(s32[8,4]{1,0:T(8,128)} %copy.9.amp_mask, s32[8]{0:T(128)} %numbers.3, bf16[2048,4096]{1,0:T(8,128)(2,1)} %rows_ref.3, s16[4224,384]{1,0:T(8,128)(2,1)} %all-gather.7.refs_0_, bf16[4096,128]{1,0:T(8,128)(2,1)} %all-gather.6.cloned.1.call-done.refs_1_), custom_call_target="tpu_custom_call" | custom-call | flops 8589934592 | bytes 27262976 | tf_op jit(solution)/shard_map/ladder/pallas_call | solution.py:188
  73.1 7.8 %all-to-all-start.1 = ((s16[32,264,128]{2,1,0:T(8,128)(2,1)}), s16[32,264,128]{2,1,0:T(8,128)(2,1)S(1)}, u32[]{:S(2)}, u32[]{:S(2)}) async-start(s16[32,264,128]{2,1,0:T(8,128)(2,1)} %bitcast.12), calls=%async_computation.1 | async-start | bytes 4325376 | tf_op jit(solution)/shard_map/all_to_all | solution.py:324
  80.9 14.3 %all-gather.4.cloned.1.call-done.refs_0_ = bf16[4096,512]{1,0:T(8,128)(2,1)} async-done(((bf16[512,512]{1,0:T(8,128)(2,1)}), bf16[4096,512]{1,0:T(8,128)(2,1)}) %all-gather.4.cloned.1.call-update) | async-done | bytes 4194320 | tf_op jit(solution)/shard_map/all_gather | solution.py:330
  95.2 16.5 %ladder.2 = (f32[2,2048,256]{2,1,0:T(8,128)}, s16[8,4,264,128]{3,2,1,0:T(8,128)(2,1)}) custom-call(s32[8,4]{1,0:T(8,128)} %copy.9.amp_mask, s32[8]{0:T(128)} %numbers.3, bf16[2048,4096]{1,0:T(8,128)(2,1)} %rows_ref.3, bf16[4096,512]{1,0:T(8,128)(2,1)} %all-gather.4.cloned.1.call-done.refs_0_), custom_call_target="tpu_custom_call" | custom-call | flops 8589934592 | bytes 27262976 | tf_op jit(solution)/shard_map/ladder/pallas_call | solution.py:188
  111.7 0.0 copy-start.1
  111.7 0.0 copy-start.2
  111.7 23.4 %all-to-all-done.1 = s16[32,264,128]{2,1,0:T(8,128)(2,1)S(1)} async-done(((s16[32,264,128]{2,1,0:T(8,128)(2,1)}), s16[32,264,128]{2,1,0:T(8,128)(2,1)S(1)}, u32[]{:S(2)}, u32[]{:S(2)}) %all-to-all-start.1) | async-done | bytes 2162720 | tf_op jit(solution)/shard_map/all_to_all | solution.py:324
  135.1 0.0 copy-start
  135.1 4.3 %all-to-all-start = ((s16[32,264,128]{2,1,0:T(8,128)(2,1)}), s16[32,264,128]{2,1,0:T(8,128)(2,1)}, u32[]{:S(2)}, u32[]{:S(2)}) async-start(s16[32,264,128]{2,1,0:T(8,128)(2,1)} %bitcast.11), calls=%async_computation | async-start | bytes 4325376 | tf_op jit(solution)/shard_map/all_to_all | solution.py:324
  139.5 0.0 copy-done.1
  139.5 0.1 reshape.142
  139.6 0.1 add.176
  139.6 0.1 add.177
  139.7 0.0 copy-done.2
  139.7 0.1 dynamic_slice.6
  139.8 0.1 broadcast_add_fusion.1
  139.9 0.7 add.173.vir_ref
  140.6 0.1 add.180
  140.7 0.6 broadcast_add_fusion.occ_ref
  141.3 1.0 fusion.1.spread_ref
  142.3 1.0 fusion.spread_ref
  143.2 5.5 %direct.3.refs_4_.refs_5_.refs_6_.refs_7_ = f32[2048,512]{1,0:T(8,128)} custom-call(bf16[512,512]{1,0:T(8,128)(2,1)} %fusion.1.spread_ref, f32[2,2048,256]{2,1,0:T(8,128)} %get-tuple-element.16.refs_0_, f32[2,2048,256]{2,1,0:T(8,128)} %get-tuple-element.17.refs_1_), custom_call_target="tpu_custom_call" | custom-call | flops 2147483648 | bytes 8388608 | tf_op jit(solution)/shard_map/direct/pallas_call | solution.py:239
  148.7 0.0 copy-done
  148.8 5.5 %direct.2.refs_4_.refs_5_.refs_6_.refs_7_ = f32[2048,512]{1,0:T(8,128)} custom-call(bf16[512,512]{1,0:T(8,128)(2,1)} %fusion.1.spread_ref, f32[2,2048,256]{2,1,0:T(8,128)} %get-tuple-element.16.refs_0_, f32[2,2048,256]{2,1,0:T(8,128)} %get-tuple-element.17.refs_1_), custom_call_target="tpu_custom_call" | custom-call | flops 2147483648 | bytes 8388608 | tf_op jit(solution)/shard_map/direct/pallas_call | solution.py:239
  154.3 6.8 %update.2.refs_8_ = f32[2048,1024]{1,0:T(8,128)} custom-call(bf16[512,512]{1,0:T(8,128)(2,1)} %fusion.spread_ref, f32[1,1024]{1,0:T(1,128)} %add.173.vir_ref, f32[8,1,256]{2,1,0:T(1,128)} %broadcast_add_fusion.occ_ref, s16[8,4,264,128]{3,2,1,0:T(8,128)(2,1)} %bitcast.7, s16[8,4,264,128]{3,2,1,0:T(8,128)(2,1)} %bitcast.8, s16[8,4,264,128]{3,2,1,0:T(8,128)(2,1)} %bitcast.9, ...), custom_call_target="tpu_custom_call" | custom-call | flops 2147483648 | bytes 10485760 | tf_op jit(solution)/shard_map/update/pallas_call | solution.py:296
  161.1 28.4 %all-to-all-done = s16[32,264,128]{2,1,0:T(8,128)(2,1)} async-done(((s16[32,264,128]{2,1,0:T(8,128)(2,1)}), s16[32,264,128]{2,1,0:T(8,128)(2,1)}, u32[]{:S(2)}, u32[]{:S(2)}) %all-to-all-start) | async-done | bytes 2162720 | tf_op jit(solution)/shard_map/all_to_all | solution.py:324
  189.6 6.8 %update.3 = f32[2048,1024]{1,0:T(8,128)} custom-call(bf16[512,512]{1,0:T(8,128)(2,1)} %fusion.spread_ref, f32[1,1024]{1,0:T(1,128)} %add.173.vir_ref, f32[8,1,256]{2,1,0:T(1,128)} %broadcast_add_fusion.occ_ref, s16[8,4,264,128]{3,2,1,0:T(8,128)(2,1)} %bitcast.3.refs_0_.refs_1_.refs_2_.refs_3_, ...), custom_call_target="tpu_custom_call", output_to_operand_aliasing={{}: (11, {})} | custom-call | flops 2147483648 | bytes 10485760 | tf_op jit(solution)/shard_map/update/pallas_call | solution.py:296
  (5 shorter events, 0.0 us)
Async XLA Ops:
  6.5 48.8 %all-gather.6.cloned.1.call-start = ((), (), s32[]{:S(2)}) async-start(), calls=%async_computation.3 | async-start | bytes 1179648 | tf_op jit(solution)/shard_map/all_gather | solution.py:330
  10.2 85.0 %all-gather.4.cloned.1.call-start = ((), (), s32[]{:S(2)}) async-start(), calls=%async_computation.2 | async-start | bytes 4718592 | tf_op jit(solution)/shard_map/all_gather | solution.py:330
  73.1 62.0 %all-to-all-start.1 = ((s16[32,264,128]{2,1,0:T(8,128)(2,1)}), s16[32,264,128]{2,1,0:T(8,128)(2,1)S(1)}, u32[]{:S(2)}, u32[]{:S(2)}) async-start(s16[32,264,128]{2,1,0:T(8,128)(2,1)} %bitcast.12), calls=%async_computation.1 | async-start | bytes 4325376 | tf_op jit(solution)/shard_map/all_to_all | solution.py:324
  111.7 27.8 %copy-start.1 = (f32[128]{0:T(128)S(1)}, f32[128]{0:T(128)}, u32[]{:S(2)}) copy-start(f32[128]{0:T(128)} %param.12) | copy-start | bytes 1540
  111.7 28.0 %copy-start.2 = (f32[64]{0:T(128)S(1)}, f32[64]{0:T(128)}, u32[]{:S(2)}) copy-start(f32[64]{0:T(128)} %param.13) | copy-start | bytes 772
  135.1 13.6 %copy-start = (s16[32,264,128]{2,1,0:T(8,128)(2,1)}, s16[32,264,128]{2,1,0:T(8,128)(2,1)S(1)}, u32[]{:S(2)}) copy-start(s16[32,264,128]{2,1,0:T(8,128)(2,1)S(1)} %all-to-all-done.1) | copy-start | bytes 6488068
  135.1 54.4 %all-to-all-start = ((s16[32,264,128]{2,1,0:T(8,128)(2,1)}), s16[32,264,128]{2,1,0:T(8,128)(2,1)}, u32[]{:S(2)}, u32[]{:S(2)}) async-start(s16[32,264,128]{2,1,0:T(8,128)(2,1)} %bitcast.11), calls=%async_computation | async-start | bytes 4325376 | tf_op jit(solution)/shard_map/all_to_all | solution.py:324
Sparse Core Ops, SparseCore 0:
  10.3 32.5 all-gather.5
  44.5 50.6 all-gather.3
